TPU v7x, 32 devices: a whole 2x2x4 slice. The times are simulated.
32 devices in a mesh: dp: 8 (over z, y), row: 2 (over core), col: 2 (over x).
Axes of the slice: x: 2, y: 2, z: 4, core: 2. Of those that a mesh axis runs over, the one named last changes fastest.
Arguments:
- tokens: bfloat16 [8192, 2048], P('dp', 'row'), may hold values from -6 to 6
- segment_ids: int32 [8192], P('dp'), may hold values from 0 to 31, never falling along the last dimension, each value on 1 to 1024 neighbouring positions
- cotangent: bfloat16 [8192, 2048], P('dp', 'row'), may hold values from -6 to 6
- g_attn: float32 [2048], P('row'), may hold values from 0.5 to 1.5
- query_weight: bfloat16 [2048, 2048], P('row', 'col'), may hold values from -0.125 to 0.125
- key_weight: bfloat16 [2048, 256], P('row', 'col'), may hold values from -0.125 to 0.125
- value_weight: bfloat16 [2048, 256], P('row', 'col'), may hold values from -0.125 to 0.125
- w_o: bfloat16 [2048, 2048], P('col', 'row'), may hold values from -0.5 to 0.5
- g_mlp: float32 [2048], P('row'), may hold values from 0.5 to 1.5
- w_gate: bfloat16 [2048, 5632], P('row', 'col'), may hold values from -0.125 to 0.125
- w_up: bfloat16 [2048, 5632], P('row', 'col'), may hold values from -0.125 to 0.125
- w_down: bfloat16 [5632, 2048], P('col', 'row'), may hold values from -0.15625 to 0.15625
Outputs:
- mixed: bfloat16 [8192, 2048], P('dp', 'row')
- d_tokens: float32 [8192, 2048], P('dp', 'row')
- d_g_attn: float32 [2048], P(('row', 'dp'))
- d_w_q: float32 [2048, 2048], P(('row', 'dp'), 'col')
- d_w_k: float32 [2048, 256], P(('row', 'dp'), 'col')
- d_w_v: float32 [2048, 256], P(('row', 'dp'), 'col')
- d_w_o: float32 [2048, 2048], P('col', ('row', 'dp'))
- d_g_mlp: float32 [2048], P(('row', 'dp'))
- d_w_gate: float32 [2048, 5632], P(('row', 'dp'), 'col')
- d_w_up: float32 [2048, 5632], P(('row', 'dp'), 'col')
- d_w_down: float32 [5632, 2048], P('col', ('row', 'dp'))
Inputs may be any that keep to these rules, and one draw needn't show every extreme that they name: `segment_ids`: segment ids never fall along the tokens; each segment has 1 to 1024 tokens and one has exactly 1024.
All inputs are finite; a program needn't handle non-finite values.
Results may differ from a plain program's by a relative error of at most 0.033.
Values may be sent and summed in bfloat16 or wider, within the bound.
No kernel may reach another device: no remote copies, remote signals or barrier semaphores. Data moves between devices by JAX's collectives and lax.ppermute only.
A program may use at most 256 MiB of HBM per device.

v0:
```python
import math

import jax
import jax.numpy as jnp
from jax import lax
from jax.sharding import PartitionSpec as P

MODEL_WIDTH = 2048
QUERY_HEADS = 32
KEY_VALUE_HEADS = 4
HEAD_SIZE = 64
SEQ = 1024


EPS = 1e-05
THETA = 10000.0


def dot_plain(left, right):
    return jnp.dot(left, right, preferred_element_type=jnp.float32)


def dot_right(left, right):
    return lax.dot_general(
        left, right, (((1,), (1,)), ((), ())), preferred_element_type=jnp.float32
    )


def dot_left(left, right):
    return lax.dot_general(
        left, right, (((0,), (0,)), ((), ())), preferred_element_type=jnp.float32
    )


def row_total(value_rows):
    return lax.psum(value_rows, "row")


def col_total(value_rows):
    return lax.psum(value_rows.astype(jnp.bfloat16), "col").astype(jnp.float32)


def angles(places):
    half = HEAD_SIZE // 2
    freq = jnp.exp(jnp.arange(half, dtype=jnp.float32) * (-2.0 * math.log(THETA) / HEAD_SIZE))
    turn = places.astype(jnp.float32)[:, None] * freq
    return (jnp.cos(turn), jnp.sin(turn))


def rotate(value_rows, cosine, sine):
    half = value_rows.shape[-1] // 2
    first = value_rows[..., :half]
    second = value_rows[..., half:]
    return jnp.concatenate(
        [first * cosine - second * sine, second * cosine + first * sine], axis=-1
    )


def unrotate(grad, cosine, sine):
    half = grad.shape[-1] // 2
    first = grad[..., :half]
    second = grad[..., half:]
    return jnp.concatenate(
        [first * cosine + second * sine, second * cosine - first * sine], axis=-1
    )


def masked_scores(query, key, seg, scale):
    sequence_length = seg.shape[0]
    raw = jnp.einsum("ikrd,jkd->krij", query, key, preferred_element_type=jnp.float32) * scale
    index = lax.broadcasted_iota(jnp.int32, (sequence_length, sequence_length), 0)
    other = lax.broadcasted_iota(jnp.int32, (sequence_length, sequence_length), 1)
    allowed = (seg[:, None] == seg[None, :]) & (other <= index)
    return jnp.where(allowed, raw, -1e30)


def shards(
    tokens,
    segment_ids,
    cotangent,
    g_attn,
    query_weight,
    key_weight,
    value_weight,
    w_o,
    g_mlp,
    w_gate,
    w_up,
    w_down,
):
    rows = tokens.shape[0]
    seqs = rows // SEQ
    repeat_heads = QUERY_HEADS // KEY_VALUE_HEADS
    scale = HEAD_SIZE ** (-0.5)
    segs = segment_ids.reshape(seqs, SEQ)
    index = lax.broadcasted_iota(jnp.int32, (seqs, SEQ), 1)
    change = jnp.concatenate(
        [jnp.ones((seqs, 1), jnp.int32), (segs[:, 1:] != segs[:, :-1]).astype(jnp.int32)], axis=1
    )
    places = index - lax.cummax(jnp.where(change > 0, index, 0), axis=1)
    cosine, sine = angles(places.reshape(rows))
    cos_q = cosine[:, None, None, :]
    sin_q = sine[:, None, None, :]
    cos_k = cosine[:, None, :]
    sin_k = sine[:, None, :]
    x = tokens.astype(jnp.float32)
    inv_one = lax.rsqrt(row_total(jnp.sum(x * x, axis=-1))[:, None] / MODEL_WIDTH + EPS)
    unit_one = x * inv_one
    xn_one = (unit_one * g_attn).astype(jnp.bfloat16)
    query_rotated, key_rotated, vp = (
        lax.psum_scatter(
            dot_plain(xn_one, query_weight).astype(jnp.bfloat16),
            "row",
            scatter_dimension=1,
            tiled=True,
        ).astype(jnp.float32),
        lax.psum_scatter(
            dot_plain(xn_one, key_weight).astype(jnp.bfloat16),
            "row",
            scatter_dimension=1,
            tiled=True,
        ).astype(jnp.float32),
        lax.psum_scatter(
            dot_plain(xn_one, value_weight).astype(jnp.bfloat16),
            "row",
            scatter_dimension=1,
            tiled=True,
        ).astype(jnp.float32),
    )
    kv_heads = key_rotated.shape[1] // HEAD_SIZE
    query = rotate(
        query_rotated.reshape(rows, kv_heads, repeat_heads, HEAD_SIZE), cos_q, sin_q
    ).astype(jnp.bfloat16)
    key = rotate(key_rotated.reshape(rows, kv_heads, HEAD_SIZE), cos_k, sin_k).astype(jnp.bfloat16)
    values = vp.astype(jnp.bfloat16).reshape(rows, kv_heads, HEAD_SIZE)
    query_seq = query.reshape(seqs, SEQ, kv_heads, repeat_heads, HEAD_SIZE)
    key_seq = key.reshape(seqs, SEQ, kv_heads, HEAD_SIZE)
    value_seq = values.reshape(seqs, SEQ, kv_heads, HEAD_SIZE)

    def forward_one(item):
        qs, ks, vs, sg = item
        raw = masked_scores(qs, ks, sg, scale)
        top = jnp.max(raw, axis=-1, keepdims=True)
        expo = jnp.exp(raw - top)
        total = jnp.sum(expo, axis=-1, keepdims=True)
        probs = (expo / total).astype(jnp.bfloat16)
        heads = jnp.einsum("krij,jkd->ikrd", probs, vs, preferred_element_type=jnp.float32)
        return (heads.astype(jnp.bfloat16), top + jnp.log(total))

    heads_seq, logsum = lax.map(forward_one, (query_seq, key_seq, value_seq, segs))
    heads = heads_seq.reshape(rows, -1)
    heads_group = lax.all_gather(heads, "row", axis=1, tiled=True)
    hidden = x + col_total(dot_plain(heads_group, w_o))
    inv_two = lax.rsqrt(row_total(jnp.sum(hidden * hidden, axis=-1))[:, None] / MODEL_WIDTH + EPS)
    unit_two = hidden * inv_two
    xn_two = (unit_two * g_mlp).astype(jnp.bfloat16)
    gate, up = (
        lax.psum_scatter(
            dot_plain(xn_two, w_gate).astype(jnp.bfloat16), "row", scatter_dimension=1, tiled=True
        ).astype(jnp.float32),
        lax.psum_scatter(
            dot_plain(xn_two, w_up).astype(jnp.bfloat16), "row", scatter_dimension=1, tiled=True
        ).astype(jnp.float32),
    )
    sigma = jax.nn.sigmoid(gate)
    swish = gate * sigma
    act = (swish * up).astype(jnp.bfloat16)
    act_group = lax.all_gather(act, "row", axis=1, tiled=True)
    mlp = col_total(dot_plain(act_group, w_down))
    result = (hidden + mlp).astype(jnp.bfloat16)
    gw_down = dot_left(act_group, cotangent)
    d_act = lax.psum_scatter(
        dot_right(cotangent, w_down).astype(jnp.bfloat16), "row", scatter_dimension=1, tiled=True
    ).astype(jnp.float32)
    d_gate = (d_act * up * (sigma * (1.0 + gate * (1.0 - sigma)))).astype(jnp.bfloat16)
    d_up = (d_act * swish).astype(jnp.bfloat16)
    gate_group, up_group = (
        lax.all_gather(d_gate, "row", axis=1, tiled=True),
        lax.all_gather(d_up, "row", axis=1, tiled=True),
    )
    gw_gate = dot_left(xn_two, gate_group)
    gw_up = dot_left(xn_two, up_group)
    d_xn_two = col_total(dot_right(gate_group, w_gate) + dot_right(up_group, w_up))
    gg_mlp = jnp.sum(d_xn_two * unit_two, axis=0)
    e_two = d_xn_two * g_mlp
    mean_two = row_total(jnp.sum(e_two * unit_two, axis=-1))[:, None] / MODEL_WIDTH
    d_hidden = cotangent.astype(jnp.float32) + inv_two * (e_two - unit_two * mean_two)
    d_attn = d_hidden.astype(jnp.bfloat16)
    gw_o = dot_left(heads_group, d_attn)
    d_heads = lax.psum_scatter(
        dot_right(d_attn, w_o).astype(jnp.bfloat16), "row", scatter_dimension=1, tiled=True
    ).astype(jnp.float32)
    d_heads = d_heads.astype(jnp.bfloat16).reshape(seqs, SEQ, kv_heads, repeat_heads, HEAD_SIZE)

    def backward_one(item):
        qs, ks, vs, sg, lse, dm = item
        raw = masked_scores(qs, ks, sg, scale)
        probs = jnp.exp(raw - lse)
        d_value = jnp.einsum(
            "krij,ikrd->jkd", probs.astype(jnp.bfloat16), dm, preferred_element_type=jnp.float32
        )
        d_probs = jnp.einsum("ikrd,jkd->krij", dm, vs, preferred_element_type=jnp.float32)
        delta = jnp.sum(d_probs * probs, axis=-1, keepdims=True)
        d_raw = (probs * (d_probs - delta)).astype(jnp.bfloat16)
        d_query = (
            jnp.einsum("krij,jkd->ikrd", d_raw, ks, preferred_element_type=jnp.float32) * scale
        )
        d_key = jnp.einsum("krij,ikrd->jkd", d_raw, qs, preferred_element_type=jnp.float32) * scale
        return (d_query, d_key, d_value)

    d_query, d_key, d_value = lax.map(
        backward_one, (query_seq, key_seq, value_seq, segs, logsum, d_heads)
    )
    d_qp = (
        unrotate(d_query.reshape(rows, kv_heads, repeat_heads, HEAD_SIZE), cos_q, sin_q)
        .reshape(rows, -1)
        .astype(jnp.bfloat16)
    )
    d_kp = (
        unrotate(d_key.reshape(rows, kv_heads, HEAD_SIZE), cos_k, sin_k)
        .reshape(rows, -1)
        .astype(jnp.bfloat16)
    )
    d_vp = d_value.reshape(rows, -1).astype(jnp.bfloat16)
    query_grad, key_grad, value_grad = (
        lax.all_gather(d_qp, "row", axis=1, tiled=True),
        lax.all_gather(d_kp, "row", axis=1, tiled=True),
        lax.all_gather(d_vp, "row", axis=1, tiled=True),
    )
    gw_q = dot_left(xn_one, query_grad)
    gw_k = dot_left(xn_one, key_grad)
    gw_v = dot_left(xn_one, value_grad)
    d_xn_one = col_total(
        dot_right(query_grad, query_weight)
        + dot_right(key_grad, key_weight)
        + dot_right(value_grad, value_weight)
    )
    gg_attn = jnp.sum(d_xn_one * unit_one, axis=0)
    e_one = d_xn_one * g_attn
    mean_one = row_total(jnp.sum(e_one * unit_one, axis=-1))[:, None] / MODEL_WIDTH
    d_tokens = d_hidden + inv_one * (e_one - unit_one * mean_one)
    sent_gattn, sent_q, sent_k, sent_v, sent_o, sent_gmlp, sent_gate, sent_up, sent_down = (
        lax.psum_scatter(gg_attn, "dp", scatter_dimension=0, tiled=True),
        lax.psum_scatter(gw_q, "dp", scatter_dimension=0, tiled=True),
        lax.psum_scatter(gw_k, "dp", scatter_dimension=0, tiled=True),
        lax.psum_scatter(gw_v, "dp", scatter_dimension=0, tiled=True),
        lax.psum_scatter(gw_o, "dp", scatter_dimension=1, tiled=True),
        lax.psum_scatter(gg_mlp, "dp", scatter_dimension=0, tiled=True),
        lax.psum_scatter(gw_gate, "dp", scatter_dimension=0, tiled=True),
        lax.psum_scatter(gw_up, "dp", scatter_dimension=0, tiled=True),
        lax.psum_scatter(gw_down, "dp", scatter_dimension=1, tiled=True),
    )
    return (
        result,
        d_tokens,
        sent_gattn,
        sent_q,
        sent_k,
        sent_v,
        sent_o,
        sent_gmlp,
        sent_gate,
        sent_up,
        sent_down,
    )


def solution(mesh):
    placed = (
        P("dp", "row"),
        P("dp"),
        P("dp", "row"),
        P("row"),
        P("row", "col"),
        P("row", "col"),
        P("row", "col"),
        P("col", "row"),
        P("row"),
        P("row", "col"),
        P("row", "col"),
        P("col", "row"),
    )
    return jax.shard_map(
        shards,
        mesh=mesh,
        in_specs=placed,
        out_specs=(
            P("dp", "row"),
            P("dp", "row"),
            P(("row", "dp")),
            P(("row", "dp"), "col"),
            P(("row", "dp"), "col"),
            P(("row", "dp"), "col"),
            P("col", ("row", "dp")),
            P(("row", "dp")),
            P(("row", "dp"), "col"),
            P(("row", "dp"), "col"),
            P("col", ("row", "dp")),
        ),
        check_vma=False,
    )
```

profile of v0, /device:TPU:0, one launch (start us, length us, event | category | flops | bytes accessed | tf_op | source)
XLA Modules:
  0.0 1510.7 jit_solution(5444379542869375600)
XLA Ops:
  46.3 13.5 fusion.94
  60.5 13.0 fusion.3
  73.6 14.5 fusion.40
  88.2 11.9 all-gather.8.cloned.1.call-done
  125.0 44.7 %all-reduce.8.cloned.1.call-done = bf16[1024,1024]{1,0:T(8,128)(2,1)} async-done(((bf16[1024,1024]{1,0:T(8,128)(2,1)}), bf16[1024,1024]{1,0:T(8,128)(2,1)}) %all-reduce.8.cloned.1.call-update) | async-done | bytes 2097168 | tf_op jit(solution)/shard_map/psum | solution.py:40
  179.4 12.0 convolution_convert_fusion.1
  247.0 16.7 %all-gather.12.cloned.1.call-done = bf16[1024,2816]{1,0:T(8,128)(2,1)} async-done(((bf16[1024,1408]{1,0:T(8,128)(2,1)}), bf16[1024,2816]{1,0:T(8,128)(2,1)}) %all-gather.12.cloned.1.call-update) | async-done | bytes 5767184 | tf_op jit(solution)/shard_map/all_gather | solution.py:178
  282.3 11.6 add_convert_fusion.1
  294.5 63.6 %all-reduce.10.cloned.1.call-done = bf16[1024,1024]{1,0:T(8,128)(2,1)} async-done(((bf16[1024,1024]{1,0:T(8,128)(2,1)}), bf16[1024,1024]{1,0:T(8,128)(2,1)}) %all-reduce.10.cloned.1.call-update) | async-done | bytes 2097168 | tf_op jit(solution)/shard_map/psum | solution.py:40
  390.6 21.5 %fusion = (f32[8,1024]{1,0:T(8,128)S(1)}, f32[1024,1024,8]{1,0,2:T(8,128)}) fusion(f32[1,8,1024,1024]{2,3,1,0:T(8,128)} %get-tuple-element.86, f32[8,1024]{1,0:T(8,128)S(1)} %log_add_fusion, bf16[1024,8,64]{0,2,1:T(8,128)(2,1)S(1)} %bitcast.162, bf16[1024,64]{0,1:T(8,128)(2,1)S(1)} %copy-done.22), kind=kOutput, calls=%fused_computation.3 | convolution fusion | flops 1098899456 | bytes 68354048 | tf_op jit(solution)/shard_map/while/body/eval_jaxpr/ikrd,jkd->krij/dot_general | solution.py:202
  412.1 28.2 %fusion.8 = bf16[8,1024,1024]{1,2,0:T(8,128)(2,1)} fusion(f32[1024,1024,8]{1,0,2:T(8,128)} %get-tuple-element.88, f32[1,8,1024,1024]{2,3,1,0:T(8,128)} %get-tuple-element.86, f32[8,1024]{1,0:T(8,128)S(1)} %get-tuple-element.87, f32[8,1024]{1,0:T(8,128)S(1)} %log_add_fusion), kind=kLoop, calls=%fused_computation.13 | loop fusion | flops 33554432 | bytes 83951616 | tf_op jit(solution)/shard_map/reshape.58
  450.7 14.4 fusion.51
  512.9 11.9 fusion.99
  524.9 11.9 fusion.98
  537.0 11.9 fusion.100
  550.8 49.3 %all-reduce.12.cloned.1.call-done = (bf16[1024,1024]{1,0:T(8,128)(2,1)}, bf16[1024,1024]{1,0:T(8,128)(2,1)}) async-done(((bf16[1024,1024]{1,0:T(8,128)(2,1)}, bf16[1024,1024]{1,0:T(8,128)(2,1)}), (bf16[1024,1024]{1,0:T(8,128)(2,1)}, bf16[1024,1024]{1,0:T(8,128)(2,1)})) %all-reduce.12.cloned.1.call-update) | async-done | bytes 4194320 | tf_op jit(solution)/shard_map/psum | solution.py:40
  603.1 21.7 %all-reduce.2 = (f32[1024]{0:T(1024)S(1)}, f32[1024]{0:T(1024)S(1)}) all-reduce(f32[1024]{0:T(1024)S(1)} %get-tuple-element.54, f32[1024]{0:T(1024)S(1)} %copy-done.32), channel_id=11, replica_groups=mesh['dp'=8,'row'=2,'col'=2] {'dp'}, use_global_device_ids=true, to_apply=%region_25.26.clone | all-reduce | flops 2048 | bytes 16384
  636.6 29.2 %reduce-scatter.33.cloned.1.call-done = f32[128,128]{1,0:T(8,128)} async-done(((f32[1024,128]{1,0:T(8,128)}), f32[128,128]{1,0:T(8,128)}) %reduce-scatter.33.cloned.1.call-update) | async-done | bytes 65552 | tf_op jit(solution)/shard_map/reduce_scatter | solution.py:246
  665.8 65.0 %reduce-scatter.31.cloned.1.call-done = f32[128,128]{1,0:T(8,128)} async-done(((f32[1024,128]{1,0:T(8,128)}), f32[128,128]{1,0:T(8,128)}) %reduce-scatter.31.cloned.1.call-update) | async-done | bytes 65552 | tf_op jit(solution)/shard_map/reduce_scatter | solution.py:245
  730.8 91.4 %reduce-scatter.35.cloned.1.call-done = f32[1024,128]{1,0:T(8,128)} async-done(((f32[1024,1024]{1,0:T(8,128)}), f32[1024,128]{1,0:T(8,128)}) %reduce-scatter.35.cloned.1.call-update) | async-done | bytes 524304 | tf_op jit(solution)/shard_map/reduce_scatter | solution.py:247
  822.2 92.5 %reduce-scatter.29.cloned.1.call-done = f32[128,1024]{1,0:T(8,128)} async-done(((f32[1024,1024]{1,0:T(8,128)}), f32[128,1024]{1,0:T(8,128)}) %reduce-scatter.29.cloned.1.call-update) | async-done | bytes 524304 | tf_op jit(solution)/shard_map/reduce_scatter | solution.py:244
  914.8 196.5 %reduce-scatter.39.cloned.1.call-done = f32[128,2816]{1,0:T(8,128)} async-done(((f32[1024,2816]{1,0:T(8,128)}), f32[128,2816]{1,0:T(8,128)}) %reduce-scatter.39.cloned.1.call-update) | async-done | bytes 1441808 | tf_op jit(solution)/shard_map/reduce_scatter | solution.py:250
  1111.3 196.0 %reduce-scatter.37.cloned.1.call-done = f32[128,2816]{1,0:T(8,128)} async-done(((f32[1024,2816]{1,0:T(8,128)}), f32[128,2816]{1,0:T(8,128)}) %reduce-scatter.37.cloned.1.call-update) | async-done | bytes 1441808 | tf_op jit(solution)/shard_map/reduce_scatter | solution.py:249
  1307.3 196.4 %reduce-scatter.41.cloned.1.call-done = f32[2816,128]{1,0:T(8,128)} async-done(((f32[2816,1024]{1,0:T(8,128)}), f32[2816,128]{1,0:T(8,128)}) %reduce-scatter.41.cloned.1.call-update) | async-done | bytes 1441808 | tf_op jit(solution)/shard_map/reduce_scatter | solution.py:251
  (193 shorter events, 255.7 us)
Async XLA Ops:
  7.2 92.9 %copy-start = (bf16[1024,1024]{1,0:T(8,128)(2,1)S(1)}, bf16[1024,1024]{1,0:T(8,128)(2,1)}, u32[]{:S(2)}) copy-start(bf16[1024,1024]{1,0:T(8,128)(2,1)} %param.19) | copy-start | bytes 6291460
  7.2 22.1 %reduce-scatter.23.cloned.1.call-start = ((), (), s32[]{:S(2)}) async-start(), calls=%async_computation.15 | async-start | bytes 393216 | tf_op jit(solution)/shard_map/reduce_scatter | solution.py:117
  17.7 24.1 %reduce-scatter.25.cloned.1.call-start = ((), (), s32[]{:S(2)}) async-start(), calls=%async_computation.16 | async-start | bytes 3145728 | tf_op jit(solution)/shard_map/reduce_scatter | solution.py:111
  23.7 49.8 %reduce-scatter.21.cloned.1.call-start = ((), (), s32[]{:S(2)}) async-start(), calls=%async_computation.14 | async-start | bytes 393216 | tf_op jit(solution)/shard_map/reduce_scatter | solution.py:123
  26.9 73.1 %all-gather.8.cloned.1.call-start = ((), (), s32[]{:S(2)}) async-start(), calls=%async_computation.17 | async-start | bytes 3145728 | tf_op jit(solution)/shard_map/all_gather | solution.py:152
  88.1 81.5 %all-reduce.8.cloned.1.call-start = ((), (), s32[]{:S(2)}) async-start(), calls=%async_computation.18 | async-start | bytes 4194304 | tf_op jit(solution)/shard_map/psum | solution.py:40
  105.4 114.2 %reduce-scatter.47.cloned.1.call-start = ((), (), s32[]{:S(2)}) async-start(), calls=%async_computation.34 | async-start | bytes 8650752
  124.9 99.2 %reduce-scatter.45.cloned.1.call-start = ((), (), s32[]{:S(2)}) async-start(), calls=%async_computation.33 | async-start | bytes 8650752
  199.8 33.3 %reduce-scatter.43.cloned.1.call-start = ((), (), s32[]{:S(2)}) async-start(), calls=%async_computation.32 | async-start | bytes 8650752
  219.1 44.6 %all-gather.12.cloned.1.call-start = ((), (), s32[]{:S(2)}) async-start(), calls=%async_computation.20 | async-start | bytes 8650752 | tf_op jit(solution)/shard_map/all_gather | solution.py:178
  246.3 35.9 %all-gather.14.cloned.1.call-start = ((), (), s32[]{:S(2)}) async-start(), calls=%async_computation.21 | async-start | bytes 8650752 | tf_op jit(solution)/shard_map/all_gather | solution.py:179
  246.9 111.2 %all-reduce.10.cloned.1.call-start = ((), (), s32[]{:S(2)}) async-start(), calls=%async_computation.22 | async-start | bytes 4194304 | tf_op jit(solution)/shard_map/psum | solution.py:40
  293.8 81.6 %all-gather.10.cloned.1.call-start = ((), (), s32[]{:S(2)}) async-start(), calls=%async_computation.19 | async-start | bytes 8650752 | tf_op jit(solution)/shard_map/all_gather | solution.py:168
  294.4 94.7 %reduce-scatter.27.cloned.1.call-start = ((), (), s32[]{:S(2)}) async-start(), calls=%async_computation.23 | async-start | bytes 3145728 | tf_op jit(solution)/shard_map/reduce_scatter | solution.py:190
  374.8 108.8 %all-gather.16.cloned.1.call-start = ((), (), s32[]{:S(2)}) async-start(), calls=%async_computation.24 | async-start | bytes 3145728 | tf_op jit(solution)/shard_map/all_gather | solution.py:226
  450.6 149.5 %all-reduce.12.cloned.1.call-start = ((), (), s32[]{:S(2)}) async-start(), calls=%async_computation.35 | async-start | bytes 8388608 | tf_op jit(solution)/shard_map/psum | solution.py:40
  490.6 175.2 %reduce-scatter.33.cloned.1.call-start = ((), (), s32[]{:S(2)}) async-start(), calls=%async_computation.27 | async-start | bytes 589824 | tf_op jit(solution)/shard_map/reduce_scatter | solution.py:246
  493.9 236.9 %reduce-scatter.31.cloned.1.call-start = ((), (), s32[]{:S(2)}) async-start(), calls=%async_computation.26 | async-start | bytes 589824 | tf_op jit(solution)/shard_map/reduce_scatter | solution.py:245
  497.1 325.1 %reduce-scatter.35.cloned.1.call-start = ((), (), s32[]{:S(2)}) async-start(), calls=%async_computation.28 | async-start | bytes 4718592 | tf_op jit(solution)/shard_map/reduce_scatter | solution.py:247
  505.6 409.1 %reduce-scatter.29.cloned.1.call-start = ((), (), s32[]{:S(2)}) async-start(), calls=%async_computation.25 | async-start | bytes 4718592 | tf_op jit(solution)/shard_map/reduce_scatter | solution.py:244
  512.8 598.4 %reduce-scatter.39.cloned.1.call-start = ((), (), s32[]{:S(2)}) async-start(), calls=%async_computation.30 | async-start | bytes 12976128 | tf_op jit(solution)/shard_map/reduce_scatter | solution.py:250
  524.8 782.4 %reduce-scatter.37.cloned.1.call-start = ((), (), s32[]{:S(2)}) async-start(), calls=%async_computation.29 | async-start | bytes 12976128 | tf_op jit(solution)/shard_map/reduce_scatter | solution.py:249
  536.8 966.8 %reduce-scatter.41.cloned.1.call-start = ((), (), s32[]{:S(2)}) async-start(), calls=%async_computation.31 | async-start | bytes 12976128 | tf_op jit(solution)/shard_map/reduce_scatter | solution.py:251
  628.4 875.2 %copy-start.1 = (bf16[1024,1024]{1,0:T(8,128)(2,1)S(1)}, bf16[1024,1024]{1,0:T(8,128)(2,1)}, u32[]{:S(2)}) copy-start(bf16[1024,1024]{1,0:T(8,128)(2,1)} %param.19) | copy-start | bytes 6291460
  (34 other events, 610.3 us)
Sparse Core Ops, SparseCore 0:
  17.8 10.2 reduce-scatter.22
  31.0 10.7 reduce-scatter.24
  44.7 8.8 reduce-scatter.20
  88.2 11.7 all-gather.7
  105.5 64.0 all-reduce.7
  171.8 13.8 reduce-scatter.46
  199.9 13.5 reduce-scatter.44
  219.2 13.7 reduce-scatter.42
  246.4 17.1 all-gather.11
  265.1 17.1 all-gather.13
  294.0 64.0 all-reduce.9
  359.5 15.9 all-gather.9
  378.3 10.7 reduce-scatter.26
  450.7 11.7 all-gather.15
  490.7 109.3 all-reduce.11
  603.9 61.8 reduce-scatter.32
  669.9 60.8 reduce-scatter.30
  734.9 87.3 reduce-scatter.34
  826.9 87.8 reduce-scatter.28
  918.8 192.4 reduce-scatter.38
  1115.4 191.7 reduce-scatter.36
  1311.5 192.1 reduce-scatter.40
where the time goes:
time: 1520 us; the launch traced here: 1510 us
  waiting for transfers between devices  1080 us (71%)
  matrix products  243 us (16%)
  other arithmetic  83.8 us (6%)
  local copies, waits for them, and re-layouts  49.5 us (3%)
  blocking collectives  35.8 us (2%)
  between operations  15.7 us (1%)
    reduce_scatter x1, waiting for transfers between devices, shards(): lax.psum_scatter(gw_up, 'dp', scatter_dimension=0, tiled=True)  196 us
    reduce_scatter x1, waiting for transfers between devices, shards(): lax.psum_scatter(gw_down, 'dp', scatter_dimension=1, tiled=True)  196 us
    reduce_scatter x1, waiting for transfers between devices, shards(): lax.psum_scatter(gw_gate, 'dp', scatter_dimension=0, tiled=True)  196 us
    psum x3, waiting for transfers between devices, col_total(): return lax.psum(value_rows.astype(jnp.bfloat16), 'col').astype(jnp.float32)  158 us
    reduce_scatter x1, waiting for transfers between devices, shards(): lax.psum_scatter(gw_q, 'dp', scatter_dimension=0, tiled=True)  92.5 us
    reduce_scatter x1, waiting for transfers between devices, shards(): lax.psum_scatter(gw_o, 'dp', scatter_dimension=1, tiled=True)  91.4 us
    reduce_scatter x1, waiting for transfers between devices, shards(): lax.psum_scatter(gw_k, 'dp', scatter_dimension=0, tiled=True)  65 us
    dot_general x7, matrix products, dot_left(): lax.dot_general(left, right, (((0,), (0,)), ((), ())), preferred_element_...  57.3 us
  transfers between devices with their start and end apart: 22, of which 17 were waited for; matrix products, arithmetic and copies ran while one was open for 17% of the time, Pallas kernels for 0%

commit v1 on v0

v1 whole, which is shorter than its diff:
```python
import math

import jax
import jax.numpy as jnp
from jax import lax
from jax.experimental import pallas as pl
from jax.experimental.pallas import tpu as pltpu
from jax.sharding import PartitionSpec as P

MODEL_WIDTH = 2048
QUERY_HEADS = 32
KEY_VALUE_HEADS = 4
HEAD_SIZE = 64
SEQ = 1024

EPS = 1e-05
THETA = 10000.0
HALF = HEAD_SIZE // 2
CHUNK = SEQ // 4
OWN = SEQ // 2
PAIR = 2 * HEAD_SIZE
SCALE = HEAD_SIZE ** (-0.5)
NEG = -1e30
F32 = jnp.float32
BF16 = jnp.bfloat16


def dot_plain(left, right):
    return jnp.dot(left, right, preferred_element_type=F32)


def dot_right(left, right):
    return lax.dot_general(left, right, (((1,), (1,)), ((), ())), preferred_element_type=F32)


def dot_left(left, right):
    return lax.dot_general(left, right, (((0,), (0,)), ((), ())), preferred_element_type=F32)


def own_rows(value, row):
    a, b, c, d = (value[i * CHUNK : (i + 1) * CHUNK] for i in range(4))
    return jnp.concatenate([jnp.where(row == 0, a, b), jnp.where(row == 0, d, c)], axis=0)


def other_rows(value, row):
    a, b, c, d = (value[i * CHUNK : (i + 1) * CHUNK] for i in range(4))
    return jnp.concatenate([jnp.where(row == 0, b, a), jnp.where(row == 0, c, d)], axis=0)


def merge_rows(own, other, row):
    a, b = own[:CHUNK], own[CHUNK:]
    c, d = other[:CHUNK], other[CHUNK:]
    return jnp.concatenate(
        [
            jnp.where(row == 0, a, c),
            jnp.where(row == 0, c, a),
            jnp.where(row == 0, d, b),
            jnp.where(row == 0, b, d),
        ],
        axis=0,
    )


def chunk_bias(start_ref, bias, row):
    for c in range(2):
        place = jnp.where(row == 0, 3 * c, 1 + c) * CHUNK
        lanes = slice(c * CHUNK, (c + 1) * CHUNK)
        keys = lax.broadcasted_iota(jnp.int32, (SEQ, CHUNK), 0)
        queries = lax.broadcasted_iota(jnp.int32, (SEQ, CHUNK), 1) + place
        allowed = (keys >= start_ref[:, lanes]) & (keys <= queries)
        bias[:, lanes] = jnp.where(allowed, 0.0, NEG)


def place_keys(own_ref, other_ref, row, put):
    @pl.when(row == 0)
    def _():
        for i, (ref, half) in enumerate(((own_ref, 0), (other_ref, 0), (other_ref, 1), (own_ref, 1))):
            put(i, ref[half * CHUNK : (half + 1) * CHUNK, :])

    @pl.when(row == 1)
    def _():
        for i, (ref, half) in enumerate(((other_ref, 0), (own_ref, 0), (own_ref, 1), (other_ref, 1))):
            put(i, ref[half * CHUNK : (half + 1) * CHUNK, :])


def attend_kernel(
    row_ref, q_ref, cos_ref, sin_ref, start_ref, own_ref, other_ref, o_ref, lse_ref, qt_ref, bias, keys, values_t
):
    step = pl.program_id(0)
    kv = step // 4
    row = row_ref[0]

    @pl.when(step == 0)
    def _():
        chunk_bias(start_ref, bias, row)

        def put(i, block):
            span = slice(i * CHUNK, (i + 1) * CHUNK)
            for h in range(2):
                keys[h, span, :] = block[:, h * HEAD_SIZE : (h + 1) * HEAD_SIZE]
            turned = jnp.transpose(block[:, PAIR:].astype(F32)).astype(BF16)
            for h in range(2):
                values_t[h, :, span] = turned[h * HEAD_SIZE : (h + 1) * HEAD_SIZE]

        place_keys(own_ref, other_ref, row, put)

    turned = jnp.transpose(q_ref[...])
    cosine, sine = cos_ref[...], sin_ref[...]
    for h in range(2):
        a = turned[h * HEAD_SIZE : h * HEAD_SIZE + HALF]
        b = turned[h * HEAD_SIZE + HALF : (h + 1) * HEAD_SIZE]
        rot = jnp.concatenate([a * cosine - b * sine, b * cosine + a * sine], axis=0)
        qt_ref[h * HEAD_SIZE : (h + 1) * HEAD_SIZE, :] = (rot * SCALE).astype(BF16)

    def unit(c, blocks):
        lanes = slice(c * CHUNK, (c + 1) * CHUNK)
        count = blocks * CHUNK
        outs, sums = [], []
        for h in range(2):
            query = qt_ref[h * HEAD_SIZE : (h + 1) * HEAD_SIZE, lanes]
            scores = dot_plain(keys[kv, :count, :], query) + bias[:count, lanes]
            top = jnp.max(scores, axis=0, keepdims=True)
            expo = jnp.exp(scores - top)
            total = jnp.sum(expo, axis=0, keepdims=True)
            head = dot_plain(values_t[kv, :, :count], expo.astype(BF16))
            outs.append(head * (1.0 / total))
            sums.append(top + jnp.log(total))
        o_ref[lanes, :] = jnp.transpose(jnp.concatenate(outs, axis=0)).astype(BF16)
        lse_ref[0, :, lanes] = jnp.concatenate(sums, axis=0)

    @pl.when(row == 0)
    def _():
        unit(0, 1)
        unit(1, 4)

    @pl.when(row == 1)
    def _():
        unit(0, 2)
        unit(1, 3)


def attend(row, q, cosine, sine, start, own_kv, other_kv):
    heads = q.shape[1] // HEAD_SIZE
    pairs = heads // 2
    whole = lambda shape: pl.BlockSpec(shape, lambda i: (0,) * len(shape))
    return pl.pallas_call(
        attend_kernel,
        grid=(pairs,),
        in_specs=[
            pl.BlockSpec(memory_space=pltpu.SMEM),
            pl.BlockSpec((OWN, PAIR), lambda i: (0, i)),
            whole((HALF, OWN)),
            whole((HALF, OWN)),
            whole((1, OWN)),
            whole((OWN, 2 * PAIR)),
            whole((OWN, 2 * PAIR)),
        ],
        out_specs=[
            pl.BlockSpec((OWN, PAIR), lambda i: (0, i)),
            pl.BlockSpec((1, 2, OWN), lambda i: (i, 0, 0)),
            pl.BlockSpec((PAIR, OWN), lambda i: (i, 0)),
        ],
        out_shape=[
            jax.ShapeDtypeStruct((OWN, heads * HEAD_SIZE), BF16),
            jax.ShapeDtypeStruct((pairs, 2, OWN), F32),
            jax.ShapeDtypeStruct((heads * HEAD_SIZE, OWN), BF16),
        ],
        scratch_shapes=[
            pltpu.VMEM((SEQ, OWN), F32),
            pltpu.VMEM((2, SEQ, HEAD_SIZE), BF16),
            pltpu.VMEM((2, HEAD_SIZE, SEQ), BF16),
        ],
        compiler_params=pltpu.CompilerParams(vmem_limit_bytes=40 * 1024 * 1024),
        cost_estimate=pl.CostEstimate(flops=20_000_000_000, bytes_accessed=8_000_000, transcendentals=0),
        name="attend",
    )(row, q, cosine, sine, start, own_kv, other_kv)


def attend_back_kernel(
    row_ref,
    qt_ref,
    do_ref,
    o_ref,
    lse_ref,
    cos_ref,
    sin_ref,
    start_ref,
    own_ref,
    other_ref,
    dq_ref,
    dk_ref,
    dv_ref,
    bias,
    keys,
    keys_t,
    values,
):
    step = pl.program_id(0)
    kv = step // 4
    row = row_ref[0]

    @pl.when(step == 0)
    def _():
        chunk_bias(start_ref, bias, row)

        def put(i, block):
            span = slice(i * CHUNK, (i + 1) * CHUNK)
            for h in range(2):
                keys[h, span, :] = block[:, h * HEAD_SIZE : (h + 1) * HEAD_SIZE]
                values[h, span, :] = block[:, PAIR + h * HEAD_SIZE : PAIR + (h + 1) * HEAD_SIZE]
            turned = jnp.transpose(block[:, :PAIR].astype(F32)).astype(BF16)
            for h in range(2):
                keys_t[h, :, span] = turned[h * HEAD_SIZE : (h + 1) * HEAD_SIZE]

        place_keys(own_ref, other_ref, row, put)

    @pl.when(step % 4 == 0)
    def _():
        dk_ref[...] = jnp.zeros_like(dk_ref)
        dv_ref[...] = jnp.zeros_like(dv_ref)

    grad = do_ref[...].astype(F32)
    grad_t = jnp.transpose(grad)
    mixed_t = jnp.transpose(grad * o_ref[...].astype(F32))
    cosine, sine = cos_ref[...], sin_ref[...]

    def unit(c, blocks):
        lanes = slice(c * CHUNK, (c + 1) * CHUNK)
        count = blocks * CHUNK
        outs = []
        for h in range(2):
            rows = slice(h * HEAD_SIZE, (h + 1) * HEAD_SIZE)
            query = qt_ref[rows, lanes]
            d_head = grad_t[rows, lanes].astype(BF16)
            delta = jnp.sum(mixed_t[rows, lanes], axis=0, keepdims=True)
            scores = dot_plain(keys[kv, :count, :], query) + bias[:count, lanes]
            probs = jnp.exp(scores - lse_ref[0, h : h + 1, lanes])
            dv_ref[0, :count, :] += dot_right(probs.astype(BF16), d_head)
            d_probs = dot_plain(values[kv, :count, :], d_head)
            d_raw = (probs * (d_probs - delta)).astype(BF16)
            d_query = dot_plain(keys_t[kv, :, :count], d_raw) * SCALE
            dk_ref[0, :count, :] += dot_right(d_raw, query)
            a, b = d_query[:HALF], d_query[HALF:]
            co, si = cosine[:, lanes], sine[:, lanes]
            outs.append(a * co + b * si)
            outs.append(b * co - a * si)
        dq_ref[lanes, :] = jnp.transpose(jnp.concatenate(outs, axis=0)).astype(BF16)

    @pl.when(row == 0)
    def _():
        unit(0, 1)
        unit(1, 4)

    @pl.when(row == 1)
    def _():
        unit(0, 2)
        unit(1, 3)


def attend_back(row, qt, d_o, o, lse, cosine, sine, start, own_kv, other_kv):
    heads = qt.shape[0] // HEAD_SIZE
    pairs = heads // 2
    whole = lambda shape: pl.BlockSpec(shape, lambda i: (0,) * len(shape))
    return pl.pallas_call(
        attend_back_kernel,
        grid=(pairs,),
        in_specs=[
            pl.BlockSpec(memory_space=pltpu.SMEM),
            pl.BlockSpec((PAIR, OWN), lambda i: (i, 0)),
            pl.BlockSpec((OWN, PAIR), lambda i: (0, i)),
            pl.BlockSpec((OWN, PAIR), lambda i: (0, i)),
            pl.BlockSpec((1, 2, OWN), lambda i: (i, 0, 0)),
            whole((HALF, OWN)),
            whole((HALF, OWN)),
            whole((1, OWN)),
            whole((OWN, 2 * PAIR)),
            whole((OWN, 2 * PAIR)),
        ],
        out_specs=[
            pl.BlockSpec((OWN, PAIR), lambda i: (0, i)),
            pl.BlockSpec((1, SEQ, HEAD_SIZE), lambda i: (i // 4, 0, 0)),
            pl.BlockSpec((1, SEQ, HEAD_SIZE), lambda i: (i // 4, 0, 0)),
        ],
        out_shape=[
            jax.ShapeDtypeStruct((OWN, heads * HEAD_SIZE), BF16),
            jax.ShapeDtypeStruct((2, SEQ, HEAD_SIZE), F32),
            jax.ShapeDtypeStruct((2, SEQ, HEAD_SIZE), F32),
        ],
        scratch_shapes=[
            pltpu.VMEM((SEQ, OWN), F32),
            pltpu.VMEM((2, SEQ, HEAD_SIZE), BF16),
            pltpu.VMEM((2, HEAD_SIZE, SEQ), BF16),
            pltpu.VMEM((2, SEQ, HEAD_SIZE), BF16),
        ],
        compiler_params=pltpu.CompilerParams(vmem_limit_bytes=40 * 1024 * 1024),
        cost_estimate=pl.CostEstimate(flops=40_000_000_000, bytes_accessed=8_000_000, transcendentals=0),
        name="attend_back",
    )(row, qt, d_o, o, lse, cosine, sine, start, own_kv, other_kv)


def shards(
    count,
    tokens,
    segment_ids,
    cotangent,
    g_attn,
    query_weight,
    key_weight,
    value_weight,
    w_o,
    g_mlp,
    w_gate,
    w_up,
    w_down,
):
    row = lax.axis_index("row")
    dp = lax.axis_index("dp")
    bits = count.bit_length() - 1

    def swap(value):
        return lax.ppermute(value, "row", [(0, 1), (1, 0)])

    def cross(value):
        return lax.ppermute(value, "col", [(0, 1), (1, 0)])

    def flip(value, bit):
        return lax.ppermute(value, "dp", [(i, i ^ (1 << bit)) for i in range(count)])

    def order_of(first):
        return ([first] + [b for b in range(bits) if b != first]) if bits else []

    def relative(value, order):
        width = value.shape[1] // count
        blocks = []
        for place in range(count):
            differs = 0
            for at, bit in enumerate(order):
                differs |= ((place >> (len(order) - 1 - at)) & 1) << bit
            blocks.append(lax.dynamic_slice_in_dim(value, (dp ^ differs) * width, width, axis=1))
        return jnp.concatenate(blocks, axis=1)

    def half_of(value, axis, upper):
        size = value.shape[axis] // 2
        return lax.slice_in_dim(value, size if upper else 0, 2 * size if upper else size, axis=axis)

    def scatter_sum(left, right, axis, order):
        if not order:
            return dot_left(left, right)
        if axis == 0:
            send = dot_left(half_of(left, 1, True), right)
            keep = dot_left(half_of(left, 1, False), right)
        else:
            send = dot_left(left, half_of(right, 1, True))
            keep = dot_left(left, half_of(right, 1, False))
        for at, bit in enumerate(order):
            came = flip(send.astype(BF16), bit)
            total = keep + came.astype(F32)
            if at + 1 < len(order):
                send = half_of(total, axis, True)
                keep = half_of(total, axis, False)
        return total

    wqkv = jnp.concatenate([query_weight, key_weight, value_weight], axis=1)
    x_m = own_rows(tokens, row)
    x_o = swap(other_rows(tokens, row))
    wqkv_o = swap(wqkv)
    gains = jnp.stack([g_attn, g_mlp])
    gains_o = swap(gains)
    w_o_x = cross(w_o)
    c_m = own_rows(cotangent, row)
    c_t = other_rows(cotangent, row)
    c_o = swap(c_t)
    w_o_o = swap(w_o)
    wg_o = swap(w_gate)
    wu_o = swap(w_up)
    wd_o = swap(w_down)
    w_o_xo = swap(w_o_x)

    start = jnp.sum((segment_ids[None, :] < segment_ids[:, None]).astype(jnp.int32), axis=1)
    index = lax.iota(jnp.int32, SEQ)
    start_own = own_rows(start, row)
    places = own_rows(index, row) - start_own
    freq = jnp.exp(jnp.arange(HALF, dtype=F32) * (-2.0 * math.log(THETA) / HEAD_SIZE))
    turn_t = freq[:, None] * places.astype(F32)[None, :]
    cosine_t, sine_t = jnp.cos(turn_t), jnp.sin(turn_t)
    cosine, sine = cosine_t.T[:, None, :], sine_t.T[:, None, :]

    x_m, x_o = x_m.astype(F32), x_o.astype(F32)
    square = jnp.sum(x_m * x_m, axis=-1, keepdims=True) + jnp.sum(x_o * x_o, axis=-1, keepdims=True)
    inv_one = lax.rsqrt(square / MODEL_WIDTH + EPS)
    xn_m = (x_m * inv_one * gains[0]).astype(BF16)
    xn_o = (x_o * inv_one * gains_o[0]).astype(BF16)
    qkv = dot_plain(xn_m, wqkv) + dot_plain(xn_o, wqkv_o)
    wide = query_weight.shape[1]
    narrow = key_weight.shape[1]
    q = qkv[:, :wide]
    kp = qkv[:, wide : wide + narrow].reshape(OWN, -1, HEAD_SIZE)
    first, second = kp[..., :HALF], kp[..., HALF:]
    key = jnp.concatenate([first * cosine - second * sine, second * cosine + first * sine], axis=-1)
    own_kv = jnp.concatenate([key.reshape(OWN, narrow), qkv[:, wide + narrow :]], axis=1).astype(BF16)
    other_kv = swap(own_kv)
    row_arg = row.astype(jnp.int32).reshape(1)
    start_arg = start_own.reshape(1, OWN)
    o, lse, qt = attend(row_arg, q, cosine_t, sine_t, start_arg, own_kv, other_kv)

    o_x = cross(o)
    hidden_m = x_m + (dot_plain(o, w_o) + dot_plain(o_x, w_o_x))
    hidden_o = x_o + (dot_plain(o, w_o_o) + dot_plain(o_x, w_o_xo))
    square = jnp.sum(hidden_m * hidden_m, axis=-1, keepdims=True) + jnp.sum(
        hidden_o * hidden_o, axis=-1, keepdims=True
    )
    inv_two = lax.rsqrt(square / MODEL_WIDTH + EPS)
    unit_m, unit_o = hidden_m * inv_two, hidden_o * inv_two
    xn2_m = (unit_m * gains[1]).astype(BF16)
    xn2_o = (unit_o * gains_o[1]).astype(BF16)

    d_act = dot_right(c_m, w_down) + dot_right(c_o, wd_o)
    gate = dot_plain(xn2_m, w_gate) + dot_plain(xn2_o, wg_o)
    up = dot_plain(xn2_m, w_up) + dot_plain(xn2_o, wu_o)
    sigma = jax.nn.sigmoid(gate)
    swish = gate * sigma
    act = (swish * up).astype(BF16)
    d_gate = (d_act * up * (sigma * (1.0 + gate * (1.0 - sigma)))).astype(BF16)
    d_up = (d_act * swish).astype(BF16)
    part_m = (dot_right(d_gate, w_gate) + dot_right(d_up, w_up)).astype(BF16)
    part_o = (dot_right(d_gate, wg_o) + dot_right(d_up, wu_o)).astype(BF16)
    d_xn2_m = part_m.astype(F32) + cross(part_m).astype(F32)
    d_xn2_o = part_o.astype(F32) + cross(part_o).astype(F32)

    order_y, order_z = order_of(0), order_of(min(1, max(bits - 1, 0)))
    both = lambda own, other: jnp.concatenate([own, other], axis=0)
    act_all = both(act, swap(act))
    gw_down = scatter_sum(act_all, relative(both(c_m, c_t), order_y), 1, order_y)
    xn2_all = both(xn2_m, swap(xn2_o))
    gw_gate = scatter_sum(relative(xn2_all, order_y), both(d_gate, swap(d_gate)), 0, order_y)
    gw_up = scatter_sum(relative(xn2_all, order_z), both(d_up, swap(d_up)), 0, order_z)

    mix_m = dot_plain(act, w_down).astype(BF16)
    mix_o = dot_plain(act, wd_o).astype(BF16)

    e_m, e_o = d_xn2_m * gains[1], d_xn2_o * gains_o[1]
    mean = (
        jnp.sum(e_m * unit_m, axis=-1, keepdims=True) + jnp.sum(e_o * unit_o, axis=-1, keepdims=True)
    ) / MODEL_WIDTH
    gg_mlp_m = jnp.sum(d_xn2_m * unit_m, axis=0)
    gg_mlp_o = jnp.sum(d_xn2_o * unit_o, axis=0)
    d_hid_m = c_m.astype(F32) + inv_two * (e_m - unit_m * mean)
    d_hid_o = c_o.astype(F32) + inv_two * (e_o - unit_o * mean)
    dh_m, dh_o = d_hid_m.astype(BF16), d_hid_o.astype(BF16)
    d_o = (dot_right(dh_m, w_o) + dot_right(dh_o, w_o_o)).astype(BF16)
    gw_o = scatter_sum(both(o, swap(o)), relative(both(dh_m, swap(dh_o)), order_y), 1, order_y)

    d_q, d_k, d_v = attend_back(row_arg, qt, d_o, o, lse, cosine_t, sine_t, start_arg, own_kv, other_kv)
    d_kv = jnp.concatenate([d_k[0], d_k[1], d_v[0], d_v[1]], axis=1)
    d_kv = own_rows(d_kv, row) + swap(other_rows(d_kv, row))
    d_key = d_kv[:, :narrow].reshape(OWN, -1, HEAD_SIZE)
    first, second = d_key[..., :HALF], d_key[..., HALF:]
    d_key = jnp.concatenate([first * cosine + second * sine, second * cosine - first * sine], axis=-1)
    d_qkv = jnp.concatenate(
        [d_q, d_key.reshape(OWN, narrow).astype(BF16), d_kv[:, narrow:].astype(BF16)], axis=1
    )
    part_m = dot_right(d_qkv, wqkv).astype(BF16)
    part_o = dot_right(d_qkv, wqkv_o).astype(BF16)
    d_xn_m = part_m.astype(F32) + cross(part_m).astype(F32)
    d_xn_o = part_o.astype(F32) + cross(part_o).astype(F32)
    xn_all = both(xn_m, swap(xn_o))
    gw_qkv = scatter_sum(relative(xn_all, order_y), both(d_qkv, swap(d_qkv)), 0, order_y)

    out_m = (hidden_m + (mix_m.astype(F32) + cross(mix_m).astype(F32))).astype(BF16)
    out_o = (hidden_o + (mix_o.astype(F32) + cross(mix_o).astype(F32))).astype(BF16)
    mixed = merge_rows(out_m, swap(out_o), row)

    unit_m, unit_o = x_m * inv_one, x_o * inv_one
    e_m, e_o = d_xn_m * gains[0], d_xn_o * gains_o[0]
    mean = (
        jnp.sum(e_m * unit_m, axis=-1, keepdims=True) + jnp.sum(e_o * unit_o, axis=-1, keepdims=True)
    ) / MODEL_WIDTH
    gg_attn_m = jnp.sum(d_xn_m * unit_m, axis=0)
    gg_attn_o = jnp.sum(d_xn_o * unit_o, axis=0)
    d_tok_m = d_hid_m + inv_one * (e_m - unit_m * mean)
    d_tok_o = d_hid_o + inv_one * (e_o - unit_o * mean)
    d_tokens = merge_rows(d_tok_m, swap(d_tok_o), row)

    gg = jnp.stack([gg_attn_m, gg_mlp_m]) + swap(jnp.stack([gg_attn_o, gg_mlp_o]))
    gg = lax.psum_scatter(gg, "dp", scatter_dimension=1, tiled=True)
    return (
        mixed,
        d_tokens,
        gg[0],
        gw_qkv[:, :wide],
        gw_qkv[:, wide : wide + narrow],
        gw_qkv[:, wide + narrow :],
        gw_o,
        gg[1],
        gw_gate,
        gw_up,
        gw_down,
    )


def solution(mesh):
    count = mesh.shape["dp"]
    placed = (
        P("dp", "row"),
        P("dp"),
        P("dp", "row"),
        P("row"),
        P("row", "col"),
        P("row", "col"),
        P("row", "col"),
        P("col", "row"),
        P("row"),
        P("row", "col"),
        P("row", "col"),
        P("col", "row"),
    )

    def body(*args):
        return shards(count, *args)

    return jax.shard_map(
        body,
        mesh=mesh,
        in_specs=placed,
        out_specs=(
            P("dp", "row"),
            P("dp", "row"),
            P(("row", "dp")),
            P(("row", "dp"), "col"),
            P(("row", "dp"), "col"),
            P(("row", "dp"), "col"),
            P("col", ("row", "dp")),
            P(("row", "dp")),
            P(("row", "dp"), "col"),
            P(("row", "dp"), "col"),
            P("col", ("row", "dp")),
        ),
        check_vma=False,
    )
```

time: 1520 us -> 723 us (0.48)
  waiting for transfers between devices: 1080 us -> 404 us
  matrix products: 243 us -> 160 us
  Pallas kernels: 0 us -> 38.9 us
  other arithmetic: 83.8 us -> 45.7 us
  blocking collectives: 35.8 us -> 0 us
  starting transfers between devices: 2.45 us -> 34.2 us
  local copies, waits for them, and re-layouts: 49.5 us -> 18.4 us
    reduce_scatter x11 -> x0, waiting for transfers between devices: 881 us -> none  [the longest x1 196 us: shards(): lax.psum_scatter(gw_up, 'dp', scatter_dimension=0, tiled=True)]
    ppermute x0 -> x45, waiting for transfers between devices: none -> 345 us  [the longest x15 215 us: flip(): return lax.ppermute(value, 'dp', [(i, i ^ 1 << bit) for i in range(count)])]
    psum x3 -> x0, waiting for transfers between devices: 158 us -> none  [col_total(): return lax.psum(value_rows.astype(jnp.bfloat16), 'col').astype(jnp.float32)]
    dot_general x13 -> x12, matrix products: 134 us -> 54.9 us  [dot_plain(): return jnp.dot(left, right, preferred_element_type=F32)]
    unnamed x25 -> x2, waiting for transfers between devices: 5.57 us -> 59.3 us
    pallas_call x0 -> x2, Pallas kernels: none -> 38.9 us  [the longest x1 20 us: attend(): pl.pallas_call(attend_kernel, grid=(pairs,), in_specs=[pl.BlockSpec(memor...]
    all_gather x5 -> x0, waiting for transfers between devices: 36.4 us -> none  [the longest x1 16.7 us: shards(): lax.all_gather(d_gate, 'row', axis=1, tiled=True)]
    unnamed x81 -> x174, local copies, waits for them, and re-layouts: 45.2 us -> 9.23 us
  transfers between devices with their start and end apart: 22 -> 46, of which waited for: 17 -> 19; matrix products, arithmetic and copies ran while one was open for 17% -> 30% of each run, Pallas kernels for 0% -> 5%
where the time goes in v1:
time: 723 us; the launch traced here: 717 us
  waiting for transfers between devices  404 us (56%)
  matrix products  160 us (22%)
  other arithmetic  45.7 us (6%)
  Pallas kernels  38.9 us (5%)
  starting transfers between devices  34.2 us (5%)
  local copies, waits for them, and re-layouts  18.4 us (3%)
  between operations  15.9 us (2%)
    ppermute x15, waiting for transfers between devices, flip(): return lax.ppermute(value, 'dp', [(i, i ^ 1 << bit) for i in range(count)])  215 us
    ppermute x8, waiting for transfers between devices, cross(): return lax.ppermute(value, 'col', [(0, 1), (1, 0)])  129 us
    unnamed x2, waiting for transfers between devices  59.3 us
    dot_general x10, matrix products, dot_right(): lax.dot_general(left, right, (((1,), (1,)), ((), ())), preferred_element_...  56.5 us
    dot_general x12, matrix products, dot_plain(): return jnp.dot(left, right, preferred_element_type=F32)  54.9 us
    dot_general x10, matrix products, dot_left(): lax.dot_general(left, right, (((0,), (0,)), ((), ())), preferred_element_...  48.4 us
    pallas_call x1, Pallas kernels, attend(): pl.pallas_call(attend_kernel, grid=(pairs,), in_specs=[pl.BlockSpec(memor...  20 us
    pallas_call x1, Pallas kernels, attend_back(): pl.pallas_call(attend_back_kernel, grid=(pairs,), in_specs=[pl.BlockSpec(...  18.9 us
  transfers between devices with their start and end apart: 46, of which 19 were waited for; matrix products, arithmetic and copies ran while one was open for 30% of the time, Pallas kernels for 5%

profile of v1, /device:TPU:0, one launch (start us, length us, event | category | flops | bytes accessed | tf_op | source)
XLA Modules:
  0.0 716.8 jit_solution(1925622938263896910)
XLA Ops:
  35.8 20.4 %collective-permute-done.5 = bf16[1024,1024]{1,0:T(8,128)(2,1)} collective-permute-done((bf16[1024,1024]{1,0:T(8,128)(2,1)}, bf16[1024,1024]{1,0:T(8,128)(2,1)}, u32[]{:S(2)}, u32[]{:S(2)}) %collective-permute-start.5) | collective-permute-done | bytes 2097184 | tf_op jit(solution)/shard_map/ppermute | solution.py:324
  56.5 20.0 %attend.1 = (bf16[512,1024]{1,0:T(8,128)(2,1)S(1)}, f32[8,2,512]{2,1,0:T(2,128)S(1)}, bf16[1024,512]{1,0:T(8,128)(2,1)S(1)}) custom-call(s32[1]{0:T(128)} %bitcast.row_ref, f32[512,1024]{1,0:T(8,128)S(1)} %slice.319.q_ref, f32[32,512]{1,0:T(8,128)S(1)} %get-tuple-element.115.cos_ref, f32[32,512]{1,0:T(8,128)S(1)} %get-tuple-element.114.sin_ref, ...), custom_call_target="tpu_custom_call" | custom-call | flops 20000000000 | bytes 8000000 | tf_op jit(solution)/shard_map/attend/pallas_call | solution.py:146
  86.8 14.4 %collective-permute-done.4 = bf16[512,1024]{1,0:T(8,128)(2,1)S(1)} collective-permute-done((bf16[512,1024]{1,0:T(8,128)(2,1)S(1)}, bf16[512,1024]{1,0:T(8,128)(2,1)S(1)}, u32[]{:S(2)}, u32[]{:S(2)}) %collective-permute-start.4) | collective-permute-done | bytes 1048608 | tf_op jit(solution)/shard_map/ppermute | solution.py:324
  119.6 7.6 %convolution_add_fusion.1 = f32[512,2816]{1,0:T(8,128)} fusion(f32[512,2816]{1,0:T(8,128)S(1)} %fusion.129, bf16[512,1024]{1,0:T(8,128)(2,1)S(1)} %get-tuple-element.116, bf16[1024,2816]{1,0:T(8,128)(2,1)} %collective-permute-done.9), kind=kOutput, calls=%fused_computation.12 | convolution fusion | flops 2954231808 | bytes 18350080 | tf_op jit(solution)/shard_map/dot_general | solution.py:29
  127.3 8.2 %convolution_add_fusion.2 = f32[512,2816]{1,0:T(8,128)} fusion(f32[512,2816]{1,0:T(8,128)S(1)} %fusion.128, bf16[512,1024]{1,0:T(8,128)(2,1)S(1)} %get-tuple-element.116, bf16[1024,2816]{1,0:T(8,128)(2,1)} %collective-permute-done.8), kind=kOutput, calls=%fused_computation.13 | convolution fusion | flops 2954231808 | bytes 18350080 | tf_op jit(solution)/shard_map/dot_general | solution.py:29
  135.4 13.7 %multiply_convert_fusion = (bf16[512,2816]{1,0:T(8,128)(2,1)}, bf16[512,2816]{1,0:T(8,128)(2,1)}, bf16[512,2816]{1,0:T(8,128)(2,1)}) fusion(f32[512,2816]{1,0:T(8,128)} %convolution_add_fusion.2, f32[512,2816]{1,0:T(8,128)} %convolution_add_fusion.1, f32[512,2816]{1,0:T(8,128)} %fusion.83, bf16[512,1024]{1,0:T(8,128)(2,1)S(1)} %collective-permute-done.14, ...), kind=kOutput, calls=%fused_computation.6 | convolution fusion | flops 2975858688 | bytes 32768000 | tf_op jit(solution)/shard_map/dot_general | solution.py:33
  161.4 6.8 add_convert_fusion.1
  170.0 6.7 add_convert_fusion.2
  194.3 22.5 %collective-permute-done.15 = bf16[512,1024]{1,0:T(8,128)(2,1)S(1)} collective-permute-done((bf16[512,1024]{1,0:T(8,128)(2,1)S(1)}, bf16[512,1024]{1,0:T(8,128)(2,1)S(1)}, u32[]{:S(2)}, u32[]{:S(2)}) %collective-permute-start.15) | collective-permute-done | bytes 1048608 | tf_op jit(solution)/shard_map/ppermute | solution.py:324
  218.7 19.6 %collective-permute-done.10 = bf16[512,1024]{1,0:T(8,128)(2,1)S(1)} collective-permute-done((bf16[512,1024]{1,0:T(8,128)(2,1)S(1)}, bf16[512,1024]{1,0:T(8,128)(2,1)S(1)}, u32[]{:S(2)}, u32[]{:S(2)}) %collective-permute-start.10) | collective-permute-done | bytes 1048608 | tf_op jit(solution)/shard_map/ppermute | solution.py:324
  247.7 18.9 %attend_back.1 = (bf16[512,1024]{1,0:T(8,128)(2,1)S(1)}, f32[2,1024,64]{2,1,0:T(8,128)S(1)}, f32[2,1024,64]{2,1,0:T(8,128)S(1)}) custom-call(s32[1]{0:T(128)} %bitcast.row_ref, bf16[1024,512]{1,0:T(8,128)(2,1)S(1)} %get-tuple-element.18.qt_ref, bf16[512,1024]{1,0:T(8,128)(2,1)S(1)} %add_convert_fusion.do_ref, bf16[512,1024]{1,0:T(8,128)(2,1)S(1)} %get-tuple-element.17.o_ref, ...), custom_call_target="tpu_custom_call" | custom-call | flops 40000000000 | bytes 8000000 | tf_op jit(solution)/shard_map/attend_back/pallas_call | solution.py:264
  303.4 22.5 %collective-permute-done.19 = bf16[512,1024]{1,0:T(8,128)(2,1)S(1)} collective-permute-done((bf16[512,1024]{1,0:T(8,128)(2,1)S(1)}, bf16[512,1024]{1,0:T(8,128)(2,1)S(1)}, u32[]{:S(2)}, u32[]{:S(2)}) %collective-permute-start.19) | collective-permute-done | bytes 1048608 | tf_op jit(solution)/shard_map/ppermute | solution.py:324
  327.4 20.0 %collective-permute-done.12 = bf16[512,1024]{1,0:T(8,128)(2,1)S(1)} collective-permute-done((bf16[512,1024]{1,0:T(8,128)(2,1)S(1)}, bf16[512,1024]{1,0:T(8,128)(2,1)S(1)}, u32[]{:S(2)}, u32[]{:S(2)}) %collective-permute-start.12) | collective-permute-done | bytes 1048608 | tf_op jit(solution)/shard_map/ppermute | solution.py:324
  357.0 59.3 %reduce-scatter.4.cloned.1.call-done = f32[128,2]{1,0:T(8,128)} async-done(((f32[1024,2]{1,0:T(8,128)}), f32[128,2]{1,0:T(8,128)}) %reduce-scatter.4.cloned.1.call-update) | async-done | bytes 1040
  454.3 66.6 %collective-permute-done.24 = bf16[512,1280]{1,0:T(8,128)(2,1)S(1)} collective-permute-done((bf16[512,1280]{1,0:T(8,128)(2,1)S(1)}, bf16[512,1280]{1,0:T(8,128)(2,1)S(1)}, u32[]{:S(2)}, u32[]{:S(2)}) %collective-permute-start.24) | collective-permute-done | bytes 1310752 | tf_op jit(solution)/shard_map/ppermute | solution.py:327
  537.1 8.7 %collective-permute-done.25 = bf16[256,1280]{1,0:T(8,128)(2,1)S(1)} collective-permute-done((bf16[256,1280]{1,0:T(8,128)(2,1)S(1)}, bf16[256,1280]{1,0:T(8,128)(2,1)S(1)}, u32[]{:S(2)}, u32[]{:S(2)}) %collective-permute-start.25) | collective-permute-done | bytes 655392 | tf_op jit(solution)/shard_map/ppermute | solution.py:327
  550.2 11.7 %collective-permute-done.26 = bf16[128,1280]{1,0:T(8,128)(2,1)S(1)} collective-permute-done((bf16[128,1280]{1,0:T(8,128)(2,1)S(1)}, bf16[128,1280]{1,0:T(8,128)(2,1)S(1)}, u32[]{:S(2)}, u32[]{:S(2)}) %collective-permute-start.26) | collective-permute-done | bytes 327712 | tf_op jit(solution)/shard_map/ppermute | solution.py:327
  569.9 7.0 convert_add_fusion.1
  578.4 22.1 %collective-permute-done.34 = bf16[512,2816]{1,0:T(8,128)(2,1)} collective-permute-done((bf16[512,2816]{1,0:T(8,128)(2,1)S(1)}, bf16[512,2816]{1,0:T(8,128)(2,1)}, u32[]{:S(2)}, u32[]{:S(2)}) %collective-permute-start.34) | collective-permute-done | bytes 2883616 | tf_op jit(solution)/shard_map/ppermute | solution.py:327
  600.4 7.0 convert_add_fusion.2
  611.1 18.2 %collective-permute-done.39 = bf16[256,2816]{1,0:T(8,128)(2,1)S(1)} collective-permute-done((bf16[256,2816]{1,0:T(8,128)(2,1)S(1)}, bf16[256,2816]{1,0:T(8,128)(2,1)S(1)}, u32[]{:S(2)}, u32[]{:S(2)}) %collective-permute-start.39) | collective-permute-done | bytes 1441824 | tf_op jit(solution)/shard_map/ppermute | solution.py:327
  629.6 31.4 %collective-permute-done.35 = bf16[256,2816]{1,0:T(8,128)(2,1)S(1)} collective-permute-done((bf16[256,2816]{1,0:T(8,128)(2,1)S(1)}, bf16[256,2816]{1,0:T(8,128)(2,1)S(1)}, u32[]{:S(2)}, u32[]{:S(2)}) %collective-permute-start.35) | collective-permute-done | bytes 1441824 | tf_op jit(solution)/shard_map/ppermute | solution.py:327
  662.7 33.2 %collective-permute-done.40 = bf16[128,2816]{1,0:T(8,128)(2,1)S(1)} collective-permute-done((bf16[128,2816]{1,0:T(8,128)(2,1)S(1)}, bf16[128,2816]{1,0:T(8,128)(2,1)S(1)}, u32[]{:S(2)}, u32[]{:S(2)}) %collective-permute-start.40) | collective-permute-done | bytes 720928 | tf_op jit(solution)/shard_map/ppermute | solution.py:327
  697.2 11.3 %collective-permute-done.36 = bf16[128,2816]{1,0:T(8,128)(2,1)S(1)} collective-permute-done((bf16[128,2816]{1,0:T(8,128)(2,1)S(1)}, bf16[128,2816]{1,0:T(8,128)(2,1)S(1)}, u32[]{:S(2)}, u32[]{:S(2)}) %collective-permute-start.36) | collective-permute-done | bytes 720928 | tf_op jit(solution)/shard_map/ppermute | solution.py:327
  (367 shorter events, 223.3 us)
Async XLA Ops:
  7.2 409.1 %reduce-scatter.4.cloned.1.call-start = ((), (), s32[]{:S(2)}) async-start(), calls=%async_computation.1 | async-start | bytes 589824
  10.2 73.6 %collective-permute-start.6 = (bf16[1024,1024]{1,0:T(8,128)(2,1)}, bf16[1024,1024]{1,0:T(8,128)(2,1)}, u32[]{:S(2)}, u32[]{:S(2)}) collective-permute-start(bf16[1024,1024]{1,0:T(8,128)(2,1)} %param.19), channel_id=1, source_target_pairs={{0,2},{2,0},{1,3},{3,1},{4,6},{6,4},{5,7},{7,5},{8,10},{10,8},{9,1... | collective-permute-start | bytes 6291464 | tf_op jit(solution)/shard_map/ppermute | solution.py:321
  23.6 96.0 %collective-permute-start.9 = (bf16[1024,2816]{1,0:T(8,128)(2,1)}, bf16[1024,2816]{1,0:T(8,128)(2,1)}, u32[]{:S(2)}, u32[]{:S(2)}) collective-permute-start(bf16[1024,2816]{1,0:T(8,128)(2,1)} %param.22), channel_id=1, source_target_pairs={{0,2},{2,0},{1,3},{3,1},{4,6},{6,4},{5,7},{7,5},{8,10},{10,8},{9,1... | collective-permute-start | bytes 17301512 | tf_op jit(solution)/shard_map/ppermute | solution.py:321
  23.7 103.5 %collective-permute-start.8 = (bf16[1024,2816]{1,0:T(8,128)(2,1)}, bf16[1024,2816]{1,0:T(8,128)(2,1)}, u32[]{:S(2)}, u32[]{:S(2)}) collective-permute-start(bf16[1024,2816]{1,0:T(8,128)(2,1)} %param.21), channel_id=1, source_target_pairs={{0,2},{2,0},{1,3},{3,1},{4,6},{6,4},{5,7},{7,5},{8,10},{10,8},{9,1... | collective-permute-start | bytes 17301512 | tf_op jit(solution)/shard_map/ppermute | solution.py:321
  105.6 78.4 %collective-permute-start.22 = (bf16[512,1024]{1,0:T(8,128)(2,1)}, bf16[512,1024]{1,0:T(8,128)(2,1)}, u32[]{:S(2)}, u32[]{:S(2)}) collective-permute-start(bf16[512,1024]{1,0:T(8,128)(2,1)} %get-tuple-element.120), channel_id=1, source_target_pairs={{0,2},{2,0},{1,3},{3,1},{4,6},{6,4},{5,7},{7,5},{8,10},{10,8},{9,1... | collective-permute-start | bytes 3145736 | tf_op jit(solution)/shard_map/ppermute | solution.py:321
  182.6 55.7 %collective-permute-start.10 = (bf16[512,1024]{1,0:T(8,128)(2,1)S(1)}, bf16[512,1024]{1,0:T(8,128)(2,1)S(1)}, u32[]{:S(2)}, u32[]{:S(2)}) collective-permute-start(bf16[512,1024]{1,0:T(8,128)(2,1)S(1)} %convolution_convert_fusion.5), channel_id=1, source_target_pairs={{0,1},{1,0},{2,3},{3,2},{4,5},{5,4},{6,7},{7,6},{8,9},{9,8},{10,11... | collective-permute-start | bytes 3145736 | tf_op jit(solution)/shard_map/ppermute | solution.py:324
  188.3 79.1 %collective-permute-start.27 = (bf16[512,1024]{1,0:T(8,128)(2,1)S(1)}, bf16[512,1024]{1,0:T(8,128)(2,1)S(1)}, u32[]{:S(2)}, u32[]{:S(2)}) collective-permute-start(bf16[512,1024]{1,0:T(8,128)(2,1)S(1)} %get-tuple-element.17.o_ref), channel_id=1, source_target_pairs={{0,2},{2,0},{1,3},{3,1},{4,6},{6,4},{5,7},{7,5},{8,10},{10,8},{9,1... | collective-permute-start | bytes 3145736 | tf_op jit(solution)/shard_map/ppermute | solution.py:321
  188.4 79.2 %collective-permute-start.32 = (bf16[512,1024]{1,0:T(8,128)(2,1)S(1)}, bf16[512,1024]{1,0:T(8,128)(2,1)S(1)}, u32[]{:S(2)}, u32[]{:S(2)}) collective-permute-start(bf16[512,1024]{1,0:T(8,128)(2,1)S(1)} %get-tuple-element.116), channel_id=1, source_target_pairs={{0,2},{2,0},{1,3},{3,1},{4,6},{6,4},{5,7},{7,5},{8,10},{10,8},{9,1... | collective-permute-start | bytes 3145736 | tf_op jit(solution)/shard_map/ppermute | solution.py:321
  270.0 148.4 %collective-permute-start.41 = (bf16[512,2816]{1,0:T(8,128)(2,1)}, bf16[512,2816]{1,0:T(8,128)(2,1)}, u32[]{:S(2)}, u32[]{:S(2)}) collective-permute-start(bf16[512,2816]{1,0:T(8,128)(2,1)} %get-tuple-element.39), channel_id=1, source_target_pairs={{0,2},{2,0},{1,3},{3,1},{4,6},{6,4},{5,7},{7,5},{8,10},{10,8},{9,1... | collective-permute-start | bytes 8650760 | tf_op jit(solution)/shard_map/ppermute | solution.py:321
  270.6 157.7 %collective-permute-start.37 = (bf16[512,2816]{1,0:T(8,128)(2,1)}, bf16[512,2816]{1,0:T(8,128)(2,1)}, u32[]{:S(2)}, u32[]{:S(2)}) collective-permute-start(bf16[512,2816]{1,0:T(8,128)(2,1)} %get-tuple-element.37), channel_id=1, source_target_pairs={{0,2},{2,0},{1,3},{3,1},{4,6},{6,4},{5,7},{7,5},{8,10},{10,8},{9,1... | collective-permute-start | bytes 8650760 | tf_op jit(solution)/shard_map/ppermute | solution.py:321
  290.6 56.9 %collective-permute-start.12 = (bf16[512,1024]{1,0:T(8,128)(2,1)S(1)}, bf16[512,1024]{1,0:T(8,128)(2,1)S(1)}, u32[]{:S(2)}, u32[]{:S(2)}) collective-permute-start(bf16[512,1024]{1,0:T(8,128)(2,1)S(1)} %convolution_convert_fusion.4), channel_id=1, source_target_pairs={{0,1},{1,0},{2,3},{3,2},{4,5},{5,4},{6,7},{7,6},{8,9},{9,8},{10,11... | collective-permute-start | bytes 3145736 | tf_op jit(solution)/shard_map/ppermute | solution.py:324
  303.4 135.9 %collective-permute-start.33 = (bf16[512,2816]{1,0:T(8,128)(2,1)}, bf16[512,2816]{1,0:T(8,128)(2,1)}, u32[]{:S(2)}, u32[]{:S(2)}) collective-permute-start(bf16[512,2816]{1,0:T(8,128)(2,1)} %get-tuple-element.38), channel_id=1, source_target_pairs={{0,2},{2,0},{1,3},{3,1},{4,6},{6,4},{5,7},{7,5},{8,10},{10,8},{9,1... | collective-permute-start | bytes 8650760 | tf_op jit(solution)/shard_map/ppermute | solution.py:321
  325.8 98.8 %collective-permute-start.23 = (bf16[512,1280]{1,0:T(8,128)(2,1)}, bf16[512,1280]{1,0:T(8,128)(2,1)}, u32[]{:S(2)}, u32[]{:S(2)}) collective-permute-start(bf16[512,1280]{1,0:T(8,128)(2,1)} %pad_maximum_fusion.17), channel_id=1, source_target_pairs={{0,2},{2,0},{1,3},{3,1},{4,6},{6,4},{5,7},{7,5},{8,10},{10,8},{9,1... | collective-permute-start | bytes 3932168 | tf_op jit(solution)/shard_map/ppermute | solution.py:321
  350.9 84.9 %collective-permute-start.29 = (bf16[1024,512]{1,0:T(8,128)(2,1)}, bf16[1024,512]{1,0:T(8,128)(2,1)}, u32[]{:S(2)}, u32[]{:S(2)}) collective-permute-start(bf16[1024,512]{1,0:T(8,128)(2,1)} %convolution_convert_fusion.6), channel_id=1, source_target_pairs={{0,4},{4,0},{8,12},{12,8},{16,20},{20,16},{24,28},{28,24},{1,5},{5... | collective-permute-start | bytes 3145736 | tf_op jit(solution)/shard_map/ppermute | solution.py:327
  418.4 128.7 %collective-permute-start.20 = (f32[512,1024]{1,0:T(8,128)}, f32[512,1024]{1,0:T(8,128)S(1)}, u32[]{:S(2)}, u32[]{:S(2)}) collective-permute-start(f32[512,1024]{1,0:T(8,128)} %get-tuple-element.76), channel_id=1, source_target_pairs={{0,2},{2,0},{1,3},{3,1},{4,6},{6,4},{5,7},{7,5},{8,10},{10,8},{9,1... | collective-permute-start | bytes 6291464 | tf_op jit(solution)/shard_map/ppermute | solution.py:321
  424.7 100.7 %collective-permute-start.13 = (bf16[512,1024]{1,0:T(8,128)(2,1)S(1)}, bf16[512,1024]{1,0:T(8,128)(2,1)S(1)}, u32[]{:S(2)}, u32[]{:S(2)}) collective-permute-start(bf16[512,1024]{1,0:T(8,128)(2,1)S(1)} %copy-done.34), channel_id=1, source_target_pairs={{0,2},{2,0},{1,3},{3,1},{4,6},{6,4},{5,7},{7,5},{8,10},{10,8},{9,1... | collective-permute-start | bytes 3145736 | tf_op jit(solution)/shard_map/ppermute | solution.py:321
  428.3 135.2 %collective-permute-start.42 = (bf16[2816,512]{1,0:T(8,128)(2,1)S(1)}, bf16[2816,512]{1,0:T(8,128)(2,1)S(1)}, u32[]{:S(2)}, u32[]{:S(2)}) collective-permute-start(bf16[2816,512]{1,0:T(8,128)(2,1)S(1)} %convolution_convert_fusion), channel_id=1, source_target_pairs={{0,4},{4,0},{8,12},{12,8},{16,20},{20,16},{24,28},{28,24},{1,5},{5... | collective-permute-start | bytes 8650760 | tf_op jit(solution)/shard_map/ppermute | solution.py:327
  435.8 85.1 %collective-permute-start.24 = (bf16[512,1280]{1,0:T(8,128)(2,1)S(1)}, bf16[512,1280]{1,0:T(8,128)(2,1)S(1)}, u32[]{:S(2)}, u32[]{:S(2)}) collective-permute-start(bf16[512,1280]{1,0:T(8,128)(2,1)S(1)} %convolution_convert_fusion.3), channel_id=1, source_target_pairs={{0,4},{4,0},{8,12},{12,8},{16,20},{20,16},{24,28},{28,24},{1,5},{5... | collective-permute-start | bytes 3932168 | tf_op jit(solution)/shard_map/ppermute | solution.py:327
  452.7 116.5 %collective-permute-start.38 = (bf16[512,2816]{1,0:T(8,128)(2,1)S(1)}, bf16[512,2816]{1,0:T(8,128)(2,1)}, u32[]{:S(2)}, u32[]{:S(2)}) collective-permute-start(bf16[512,2816]{1,0:T(8,128)(2,1)S(1)} %convolution_convert_fusion.1), channel_id=1, source_target_pairs={{0,8},{4,12},{8,0},{12,4},{16,24},{20,28},{24,16},{28,20},{1,9},{5... | collective-permute-start | bytes 8650760 | tf_op jit(solution)/shard_map/ppermute | solution.py:327
  534.9 65.5 %collective-permute-start.34 = (bf16[512,2816]{1,0:T(8,128)(2,1)S(1)}, bf16[512,2816]{1,0:T(8,128)(2,1)}, u32[]{:S(2)}, u32[]{:S(2)}) collective-permute-start(bf16[512,2816]{1,0:T(8,128)(2,1)S(1)} %convolution_convert_fusion.2), channel_id=1, source_target_pairs={{0,4},{4,0},{8,12},{12,8},{16,20},{20,16},{24,28},{28,24},{1,5},{5... | collective-permute-start | bytes 8650760 | tf_op jit(solution)/shard_map/ppermute | solution.py:327
  577.0 52.2 %collective-permute-start.39 = (bf16[256,2816]{1,0:T(8,128)(2,1)S(1)}, bf16[256,2816]{1,0:T(8,128)(2,1)S(1)}, u32[]{:S(2)}, u32[]{:S(2)}) collective-permute-start(bf16[256,2816]{1,0:T(8,128)(2,1)S(1)} %slice.449), channel_id=1, source_target_pairs={{0,4},{4,0},{8,12},{12,8},{16,20},{20,16},{24,28},{28,24},{1,5},{5... | collective-permute-start | bytes 4325384 | tf_op jit(solution)/shard_map/ppermute | solution.py:327
  607.6 53.5 %collective-permute-start.35 = (bf16[256,2816]{1,0:T(8,128)(2,1)S(1)}, bf16[256,2816]{1,0:T(8,128)(2,1)S(1)}, u32[]{:S(2)}, u32[]{:S(2)}) collective-permute-start(bf16[256,2816]{1,0:T(8,128)(2,1)S(1)} %slice.450), channel_id=1, source_target_pairs={{0,8},{4,12},{8,0},{12,4},{16,24},{20,28},{24,16},{28,20},{1,9},{5... | collective-permute-start | bytes 4325384 | tf_op jit(solution)/shard_map/ppermute | solution.py:327
  608.2 53.2 %collective-permute-start.44 = (bf16[2816,128]{1,0:T(8,128)(2,1)S(1)}, bf16[2816,128]{1,0:T(8,128)(2,1)S(1)}, u32[]{:S(2)}, u32[]{:S(2)}) collective-permute-start(bf16[2816,128]{1,0:T(8,128)(2,1)S(1)} %slice.451), channel_id=1, source_target_pairs={{0,16},{4,20},{8,24},{12,28},{16,0},{20,4},{24,8},{28,12},{1,17},{... | collective-permute-start | bytes 2162696 | tf_op jit(solution)/shard_map/ppermute | solution.py:327
  629.6 66.4 %collective-permute-start.40 = (bf16[128,2816]{1,0:T(8,128)(2,1)S(1)}, bf16[128,2816]{1,0:T(8,128)(2,1)S(1)}, u32[]{:S(2)}, u32[]{:S(2)}) collective-permute-start(bf16[128,2816]{1,0:T(8,128)(2,1)S(1)} %slice.452), channel_id=1, source_target_pairs={{0,16},{4,20},{8,24},{12,28},{16,0},{20,4},{24,8},{28,12},{1,17},{... | collective-permute-start | bytes 2162696 | tf_op jit(solution)/shard_map/ppermute | solution.py:327
  (106 other events, 2067.6 us)
Sparse Core Ops, SparseCore 0:
  353.9 62.2 reduce-scatter.3

commit v2 on v1

--- a/solution.py
+++ b/solution.py
@@ -298,6 +298,117 @@
     )(row, qt, d_o, o, lse, cosine, sine, start, own_kv, other_kv)
 
 
+def hidden_units_kernel(
+    xm_ref, xo_ref, cm_ref, co_ref, gm_ref, go_ref, um_ref, uo_ref, dm_ref, do_ref, act_ref, dg_ref, du_ref
+):
+    gate = dot_plain(xm_ref[...], gm_ref[...]) + dot_plain(xo_ref[...], go_ref[...])
+    up = dot_plain(xm_ref[...], um_ref[...]) + dot_plain(xo_ref[...], uo_ref[...])
+    d_act = dot_right(cm_ref[...], dm_ref[...]) + dot_right(co_ref[...], do_ref[...])
+    sigma = jax.nn.sigmoid(gate)
+    swish = gate * sigma
+    act_ref[...] = (swish * up).astype(BF16)
+    dg_ref[...] = (d_act * up * (sigma * (1.0 + gate * (1.0 - sigma)))).astype(BF16)
+    du_ref[...] = (d_act * swish).astype(BF16)
+
+
+def hidden_units(xm, xo, cm, co, gm, go, um, uo, dm, do):
+    rows, depth = xm.shape
+    wide = gm.shape[1]
+    tile = 256
+    full = pl.BlockSpec((rows, depth), lambda i: (0, 0))
+    column = pl.BlockSpec((depth, tile), lambda i: (0, i))
+    line = pl.BlockSpec((tile, depth), lambda i: (i, 0))
+    out = pl.BlockSpec((rows, tile), lambda i: (0, i))
+    return pl.pallas_call(
+        hidden_units_kernel,
+        grid=(wide // tile,),
+        in_specs=[full] * 4 + [column] * 4 + [line] * 2,
+        out_specs=[out] * 3,
+        out_shape=[jax.ShapeDtypeStruct((rows, wide), BF16)] * 3,
+        compiler_params=pltpu.CompilerParams(vmem_limit_bytes=48 * 1024 * 1024),
+        cost_estimate=pl.CostEstimate(
+            flops=12 * rows * depth * wide, bytes_accessed=12 * depth * wide, transcendentals=0
+        ),
+        name="hidden_units",
+    )(xm, xo, cm, co, gm, go, um, uo, dm, do)
+
+
+def input_grad_kernel(dg_ref, du_ref, g_ref, u_ref, out_ref):
+    out_ref[...] = (dot_right(dg_ref[...], g_ref[...]) + dot_right(du_ref[...], u_ref[...])).astype(BF16)
+
+
+def input_grad(dg, du, g, u):
+    rows, wide = dg.shape
+    depth = g.shape[0]
+    tile = 256
+    full = pl.BlockSpec((rows, wide), lambda i: (0, 0))
+    line = pl.BlockSpec((tile, wide), lambda i: (i, 0))
+    return pl.pallas_call(
+        input_grad_kernel,
+        grid=(depth // tile,),
+        in_specs=[full] * 2 + [line] * 2,
+        out_specs=pl.BlockSpec((rows, tile), lambda i: (0, i)),
+        out_shape=jax.ShapeDtypeStruct((rows, depth), BF16),
+        compiler_params=pltpu.CompilerParams(vmem_limit_bytes=48 * 1024 * 1024),
+        cost_estimate=pl.CostEstimate(flops=4 * rows * depth * wide, bytes_accessed=4 * depth * wide, transcendentals=0),
+        name="input_grad",
+    )(dg, du, g, u)
+
+
+class Halving:
+    def __init__(self, left, right, axis, order, flip):
+        self.left, self.right, self.axis, self.order, self.flip = left, right, axis, list(order), flip
+        self.at = 0
+
+    def part(self, upper):
+        if not self.order:
+            return dot_left(self.left, self.right)
+        if self.axis == 0:
+            return dot_left(half_of(self.left, 1, upper), self.right)
+        return dot_left(self.left, half_of(self.right, 1, upper))
+
+    def begin(self):
+        self.send = self.part(True).astype(BF16)
+        return self.send
+
+    def stay(self):
+        self.keep = self.part(False)
+        return self.keep
+
+    def go(self):
+        if self.at < len(self.order):
+            self.came = self.flip(self.send, self.order[self.at])
+        else:
+            self.came = self.send
+        return self.came
+
+    def add(self):
+        if self.at < len(self.order):
+            self.total = self.keep + self.came.astype(F32)
+            self.at += 1
+            if self.at < len(self.order):
+                self.send = half_of(self.total, self.axis, True).astype(BF16)
+                self.keep = half_of(self.total, self.axis, False)
+        elif not self.order:
+            self.total = self.keep
+
+    def rest(self):
+        self.add()
+        while self.at < len(self.order):
+            self.go()
+            self.add()
+        return self.total
+
+
+def half_of(value, axis, upper):
+    size = value.shape[axis] // 2
+    return lax.slice_in_dim(value, size if upper else 0, 2 * size if upper else size, axis=axis)
+
+
+def tie(*values):
+    return lax.optimization_barrier(values)
+
+
 def shards(
     count,
     tokens,
@@ -339,42 +450,19 @@
             blocks.append(lax.dynamic_slice_in_dim(value, (dp ^ differs) * width, width, axis=1))
         return jnp.concatenate(blocks, axis=1)
 
-    def half_of(value, axis, upper):
-        size = value.shape[axis] // 2
-        return lax.slice_in_dim(value, size if upper else 0, 2 * size if upper else size, axis=axis)
-
-    def scatter_sum(left, right, axis, order):
-        if not order:
-            return dot_left(left, right)
-        if axis == 0:
-            send = dot_left(half_of(left, 1, True), right)
-            keep = dot_left(half_of(left, 1, False), right)
-        else:
-            send = dot_left(left, half_of(right, 1, True))
-            keep = dot_left(left, half_of(right, 1, False))
-        for at, bit in enumerate(order):
-            came = flip(send.astype(BF16), bit)
-            total = keep + came.astype(F32)
-            if at + 1 < len(order):
-                send = half_of(total, axis, True)
-                keep = half_of(total, axis, False)
-        return total
-
-    wqkv = jnp.concatenate([query_weight, key_weight, value_weight], axis=1)
     x_m = own_rows(tokens, row)
     x_o = swap(other_rows(tokens, row))
-    wqkv_o = swap(wqkv)
+    wkv = jnp.concatenate([key_weight, value_weight], axis=1)
+    wkv_o = swap(wkv)
+    wq_o = swap(query_weight)
     gains = jnp.stack([g_attn, g_mlp])
     gains_o = swap(gains)
     w_o_x = cross(w_o)
-    c_m = own_rows(cotangent, row)
-    c_t = other_rows(cotangent, row)
-    c_o = swap(c_t)
-    w_o_o = swap(w_o)
-    wg_o = swap(w_gate)
-    wu_o = swap(w_up)
-    wd_o = swap(w_down)
-    w_o_xo = swap(w_o_x)
+    x_m, x_o = x_m.astype(F32), x_o.astype(F32)
+    square = jnp.sum(x_m * x_m, axis=-1, keepdims=True) + jnp.sum(x_o * x_o, axis=-1, keepdims=True)
+    inv_one = lax.rsqrt(square / MODEL_WIDTH + EPS)
+    xn_m = (x_m * inv_one * gains[0]).astype(BF16)
+    xn_o = (x_o * inv_one * gains_o[0]).astype(BF16)
 
     start = jnp.sum((segment_ids[None, :] < segment_ids[:, None]).astype(jnp.int32), axis=1)
     index = lax.iota(jnp.int32, SEQ)
@@ -385,27 +473,39 @@
     cosine_t, sine_t = jnp.cos(turn_t), jnp.sin(turn_t)
     cosine, sine = cosine_t.T[:, None, :], sine_t.T[:, None, :]
 
-    x_m, x_o = x_m.astype(F32), x_o.astype(F32)
-    square = jnp.sum(x_m * x_m, axis=-1, keepdims=True) + jnp.sum(x_o * x_o, axis=-1, keepdims=True)
-    inv_one = lax.rsqrt(square / MODEL_WIDTH + EPS)
-    xn_m = (x_m * inv_one * gains[0]).astype(BF16)
-    xn_o = (x_o * inv_one * gains_o[0]).astype(BF16)
-    qkv = dot_plain(xn_m, wqkv) + dot_plain(xn_o, wqkv_o)
+    kv = dot_plain(xn_m, wkv) + dot_plain(xn_o, wkv_o)
+    narrow = key_weight.shape[1]
     wide = query_weight.shape[1]
-    narrow = key_weight.shape[1]
-    q = qkv[:, :wide]
-    kp = qkv[:, wide : wide + narrow].reshape(OWN, -1, HEAD_SIZE)
+    kp = kv[:, :narrow].reshape(OWN, -1, HEAD_SIZE)
     first, second = kp[..., :HALF], kp[..., HALF:]
     key = jnp.concatenate([first * cosine - second * sine, second * cosine + first * sine], axis=-1)
-    own_kv = jnp.concatenate([key.reshape(OWN, narrow), qkv[:, wide + narrow :]], axis=1).astype(BF16)
+    own_kv = jnp.concatenate([key.reshape(OWN, narrow), kv[:, narrow:]], axis=1).astype(BF16)
     other_kv = swap(own_kv)
+    xn_m, xn_o, own_kv = tie(xn_m, xn_o, own_kv)
+    q = dot_plain(xn_m, query_weight) + dot_plain(xn_o, wq_o)
+
+    cotangent, w_gate, w_up, w_down, w_o, xn_o = tie(cotangent, w_gate, w_up, w_down, w_o, xn_o)
+    w_o_o = swap(w_o)
+    wg_o = swap(w_gate)
+    wu_o = swap(w_up)
+    c_m = own_rows(cotangent, row)
+    c_t = other_rows(cotangent, row)
+    c_o = swap(c_t)
+    wd_o = swap(w_down)
+    xn_t = swap(xn_o)
+
     row_arg = row.astype(jnp.int32).reshape(1)
     start_arg = start_own.reshape(1, OWN)
     o, lse, qt = attend(row_arg, q, cosine_t, sine_t, start_arg, own_kv, other_kv)
+    o, w_o_x = tie(o, w_o_x)
+    w_o_xo = swap(w_o_x)
 
     o_x = cross(o)
-    hidden_m = x_m + (dot_plain(o, w_o) + dot_plain(o_x, w_o_x))
-    hidden_o = x_o + (dot_plain(o, w_o_o) + dot_plain(o_x, w_o_xo))
+    o_t = swap(o)
+    near_m, near_o = dot_plain(o, w_o), dot_plain(o, w_o_o)
+    near_m, near_o, o_x = tie(near_m, near_o, o_x)
+    hidden_m = x_m + (near_m + dot_plain(o_x, w_o_x))
+    hidden_o = x_o + (near_o + dot_plain(o_x, w_o_xo))
     square = jnp.sum(hidden_m * hidden_m, axis=-1, keepdims=True) + jnp.sum(
         hidden_o * hidden_o, axis=-1, keepdims=True
     )
@@ -414,30 +514,39 @@
     xn2_m = (unit_m * gains[1]).astype(BF16)
     xn2_o = (unit_o * gains_o[1]).astype(BF16)
 
-    d_act = dot_right(c_m, w_down) + dot_right(c_o, wd_o)
-    gate = dot_plain(xn2_m, w_gate) + dot_plain(xn2_o, wg_o)
-    up = dot_plain(xn2_m, w_up) + dot_plain(xn2_o, wu_o)
-    sigma = jax.nn.sigmoid(gate)
-    swish = gate * sigma
-    act = (swish * up).astype(BF16)
-    d_gate = (d_act * up * (sigma * (1.0 + gate * (1.0 - sigma)))).astype(BF16)
-    d_up = (d_act * swish).astype(BF16)
-    part_m = (dot_right(d_gate, w_gate) + dot_right(d_up, w_up)).astype(BF16)
-    part_o = (dot_right(d_gate, wg_o) + dot_right(d_up, wu_o)).astype(BF16)
-    d_xn2_m = part_m.astype(F32) + cross(part_m).astype(F32)
-    d_xn2_o = part_o.astype(F32) + cross(part_o).astype(F32)
-
     order_y, order_z = order_of(0), order_of(min(1, max(bits - 1, 0)))
     both = lambda own, other: jnp.concatenate([own, other], axis=0)
-    act_all = both(act, swap(act))
-    gw_down = scatter_sum(act_all, relative(both(c_m, c_t), order_y), 1, order_y)
     xn2_all = both(xn2_m, swap(xn2_o))
-    gw_gate = scatter_sum(relative(xn2_all, order_y), both(d_gate, swap(d_gate)), 0, order_y)
-    gw_up = scatter_sum(relative(xn2_all, order_z), both(d_up, swap(d_up)), 0, order_z)
-
+    xn2_y, xn2_z = relative(xn2_all, order_y), relative(xn2_all, order_z)
+    c_y = relative(both(c_m, c_t), order_y)
+    act, d_gate, d_up = hidden_units(xn2_m, xn2_o, c_m, c_o, w_gate, wg_o, w_up, wu_o, w_down, wd_o)
+    act_t, d_up_t, d_gate_t = swap(act), swap(d_up), swap(d_gate)
+    part_m = input_grad(d_gate, d_up, w_gate, w_up)
+    came_m = cross(part_m)
+    act_t, d_up_t, part_m = tie(act_t, d_up_t, part_m)
+    down = Halving(both(act, act_t), c_y, 1, order_y, flip)
+    upper = Halving(xn2_z, both(d_up, d_up_t), 0, order_z, flip)
+    gater = Halving(xn2_y, both(d_gate, d_gate_t), 0, order_y, flip)
+    down.begin()
+    down.go()
+    upper.begin()
+    upper.go()
+    down.send, upper.send, d_gate_late = tie(down.send, upper.send, d_gate)
+    part_o = input_grad(d_gate_late, d_up, wg_o, wu_o)
+    came_o = cross(part_o)
+    down.left, upper.left, part_o = tie(down.left, upper.left, part_o)
+    down.stay()
+    upper.stay()
+    gater.begin()
+    gater.stay()
     mix_m = dot_plain(act, w_down).astype(BF16)
     mix_o = dot_plain(act, wd_o).astype(BF16)
 
+    came_m, came_o, down.keep, upper.keep, gater.send, gater.keep, mix_m, mix_o = tie(
+        came_m, came_o, down.keep, upper.keep, gater.send, gater.keep, mix_m, mix_o
+    )
+    d_xn2_m = part_m.astype(F32) + came_m.astype(F32)
+    d_xn2_o = part_o.astype(F32) + came_o.astype(F32)
     e_m, e_o = d_xn2_m * gains[1], d_xn2_o * gains_o[1]
     mean = (
         jnp.sum(e_m * unit_m, axis=-1, keepdims=True) + jnp.sum(e_o * unit_o, axis=-1, keepdims=True)
@@ -447,29 +556,51 @@
     d_hid_m = c_m.astype(F32) + inv_two * (e_m - unit_m * mean)
     d_hid_o = c_o.astype(F32) + inv_two * (e_o - unit_o * mean)
     dh_m, dh_o = d_hid_m.astype(BF16), d_hid_o.astype(BF16)
+    dh_t = swap(dh_o)
     d_o = (dot_right(dh_m, w_o) + dot_right(dh_o, w_o_o)).astype(BF16)
-    gw_o = scatter_sum(both(o, swap(o)), relative(both(dh_m, swap(dh_o)), order_y), 1, order_y)
 
     d_q, d_k, d_v = attend_back(row_arg, qt, d_o, o, lse, cosine_t, sine_t, start_arg, own_kv, other_kv)
     d_kv = jnp.concatenate([d_k[0], d_k[1], d_v[0], d_v[1]], axis=1)
-    d_kv = own_rows(d_kv, row) + swap(other_rows(d_kv, row))
+    d_kv_t = swap(other_rows(d_kv, row))
+    d_kv_own = own_rows(d_kv, row)
+    d_kv_own, down.came, upper.came, gater.send = tie(d_kv_own, down.came, upper.came, gater.send)
+    gater.go()
+    down.add()
+    down.go()
+    upper.add()
+    upper.go()
+    d_kv_t, down.send, down.keep, upper.send, upper.keep = tie(
+        d_kv_t, down.send, down.keep, upper.send, upper.keep
+    )
+    d_kv = d_kv_own + d_kv_t
     d_key = d_kv[:, :narrow].reshape(OWN, -1, HEAD_SIZE)
     first, second = d_key[..., :HALF], d_key[..., HALF:]
     d_key = jnp.concatenate([first * cosine + second * sine, second * cosine - first * sine], axis=-1)
-    d_qkv = jnp.concatenate(
-        [d_q, d_key.reshape(OWN, narrow).astype(BF16), d_kv[:, narrow:].astype(BF16)], axis=1
-    )
-    part_m = dot_right(d_qkv, wqkv).astype(BF16)
-    part_o = dot_right(d_qkv, wqkv_o).astype(BF16)
-    d_xn_m = part_m.astype(F32) + cross(part_m).astype(F32)
-    d_xn_o = part_o.astype(F32) + cross(part_o).astype(F32)
-    xn_all = both(xn_m, swap(xn_o))
-    gw_qkv = scatter_sum(relative(xn_all, order_y), both(d_qkv, swap(d_qkv)), 0, order_y)
-
-    out_m = (hidden_m + (mix_m.astype(F32) + cross(mix_m).astype(F32))).astype(BF16)
-    out_o = (hidden_o + (mix_o.astype(F32) + cross(mix_o).astype(F32))).astype(BF16)
-    mixed = merge_rows(out_m, swap(out_o), row)
-
+    d_kv = jnp.concatenate([d_key.reshape(OWN, narrow).astype(BF16), d_kv[:, narrow:].astype(BF16)], axis=1)
+    d_qkv = jnp.concatenate([d_q, d_kv], axis=1)
+    part_m = (dot_right(d_q, query_weight) + dot_right(d_kv, wkv)).astype(BF16)
+    came_m = cross(part_m)
+    part_o = (dot_right(d_q, wq_o) + dot_right(d_kv, wkv_o)).astype(BF16)
+    came_o = cross(part_o)
+    d_qkv_t = swap(d_qkv)
+    d_qkv_t, dh_t, part_o = tie(d_qkv_t, dh_t, part_o)
+    outer = Halving(both(o, o_t), relative(both(dh_m, dh_t), order_y), 1, order_y, flip)
+    inner = Halving(relative(both(xn_m, xn_t), order_y), both(d_qkv, d_qkv_t), 0, order_y, flip)
+    inner.begin()
+    inner.go()
+    outer.begin()
+    outer.go()
+    inner.stay()
+    outer.stay()
+
+    came_m, came_o, inner.keep, outer.keep, gater.came, mix_m, mix_o = tie(
+        came_m, came_o, inner.keep, outer.keep, gater.came, mix_m, mix_o
+    )
+    gater.add()
+    gater.go()
+    mix_cm, mix_co = cross(mix_m), cross(mix_o)
+    d_xn_m = part_m.astype(F32) + came_m.astype(F32)
+    d_xn_o = part_o.astype(F32) + came_o.astype(F32)
     unit_m, unit_o = x_m * inv_one, x_o * inv_one
     e_m, e_o = d_xn_m * gains[0], d_xn_o * gains_o[0]
     mean = (
@@ -481,8 +612,16 @@
     d_tok_o = d_hid_o + inv_one * (e_o - unit_o * mean)
     d_tokens = merge_rows(d_tok_m, swap(d_tok_o), row)
 
+    out_m = (hidden_m + (mix_m.astype(F32) + mix_cm.astype(F32))).astype(BF16)
+    out_o = (hidden_o + (mix_o.astype(F32) + mix_co.astype(F32))).astype(BF16)
+    mixed = merge_rows(out_m, swap(out_o), row)
+
     gg = jnp.stack([gg_attn_m, gg_mlp_m]) + swap(jnp.stack([gg_attn_o, gg_mlp_o]))
-    gg = lax.psum_scatter(gg, "dp", scatter_dimension=1, tiled=True)
+    gg = relative(gg, order_y)
+    for bit in order_y:
+        gg = half_of(gg, 1, False) + flip(half_of(gg, 1, True), bit)
+
+    gw_down, gw_up, gw_gate, gw_o, gw_qkv = (h.rest() for h in (down, upper, gater, outer, inner))
     return (
         mixed,
         d_tokens,

time: 723 us -> 520 us (0.72)
  waiting for transfers between devices: 404 us -> 208 us
  matrix products: 160 us -> 84.4 us
  Pallas kernels: 38.9 us -> 83.4 us
  local copies, waits for them, and re-layouts: 18.4 us -> 38.1 us
  between operations: 15.9 us -> 2.55 us
  other arithmetic: 45.7 us -> 54.6 us
    ppermute x8, waiting for transfers between devices: 129 us -> 24.7 us  [cross(): return lax.ppermute(value, 'col', [(0, 1), (1, 0)])]
    unnamed x2 -> x0, waiting for transfers between devices: 59.3 us -> none
    pallas_call x0 -> x3, Pallas kernels: none -> 44.4 us  [the longest x1 24.7 us: hidden_units(): pl.pallas_call(hidden_units_kernel, grid=(wide // tile,), in_specs=[full]...]
    dot_general x10 -> x6, matrix products: 56.5 us -> 13.5 us  [dot_right(): lax.dot_general(left, right, (((1,), (1,)), ((), ())), preferred_element_...]
    ppermute x15 -> x18, waiting for transfers between devices: 215 us -> 184 us  [flip(): return lax.ppermute(value, 'dp', [(i, i ^ 1 << bit) for i in range(count)])]
    dot_general x12 -> x10, matrix products: 54.9 us -> 31.7 us  [dot_plain(): return jnp.dot(left, right, preferred_element_type=F32)]
    add x11 -> x19, other arithmetic: 5.93 us -> 18.6 us  [the longest x15 18.5 us: add(): self.total = self.keep + self.came.astype(F32)]
    dot_general x10, matrix products: 48.4 us -> 39.2 us  [dot_left(): lax.dot_general(left, right, (((0,), (0,)), ((), ())), preferred_element_...]
  transfers between devices with their start and end apart: 46 -> 49, of which waited for: 19 -> 13; matrix products, arithmetic and copies ran while one was open for 30% -> 31% of each run, Pallas kernels for 5% -> 11%
where the time goes in v2:
time: 520 us; the launch traced here: 511 us
  waiting for transfers between devices  208 us (40%)
  matrix products  84.4 us (16%)
  Pallas kernels  83.4 us (16%)
  other arithmetic  54.6 us (10%)
  starting transfers between devices  40 us (8%)
  local copies, waits for them, and re-layouts  38.1 us (7%)
    ppermute x18, waiting for transfers between devices, flip(): return lax.ppermute(value, 'dp', [(i, i ^ 1 << bit) for i in range(count)])  184 us
    dot_general x10, matrix products, dot_left(): lax.dot_general(left, right, (((0,), (0,)), ((), ())), preferred_element_...  39.2 us
    dot_general x10, matrix products, dot_plain(): return jnp.dot(left, right, preferred_element_type=F32)  31.7 us
    pallas_call x1, Pallas kernels, hidden_units(): pl.pallas_call(hidden_units_kernel, grid=(wide // tile,), in_specs=[full]...  24.7 us
    ppermute x8, waiting for transfers between devices, cross(): return lax.ppermute(value, 'col', [(0, 1), (1, 0)])  24.7 us
    ppermute x18, starting transfers between devices, flip(): return lax.ppermute(value, 'dp', [(i, i ^ 1 << bit) for i in range(count)])  22.7 us
    pallas_call x2, Pallas kernels, input_grad(): pl.pallas_call(input_grad_kernel, grid=(depth // tile,), in_specs=[full]...  19.7 us
    pallas_call x1, Pallas kernels, attend(): pl.pallas_call(attend_kernel, grid=(pairs,), in_specs=[pl.BlockSpec(memor...  19.7 us
  transfers between devices with their start and end apart: 49, of which 13 were waited for; matrix products, arithmetic and copies ran while one was open for 31% of the time, Pallas kernels for 11%

profile of v2, /device:TPU:0, one launch (start us, length us, event | category | flops | bytes accessed | tf_op | source)
XLA Modules:
  0.0 511.5 jit_solution(7649181550466464147)
XLA Ops:
  23.8 19.7 %attend.1 = (bf16[512,1024]{1,0:T(8,128)(2,1)S(1)}, f32[8,2,512]{2,1,0:T(2,128)S(1)}, bf16[1024,512]{1,0:T(8,128)(2,1)S(1)}) custom-call(s32[1]{0:T(128)} %bitcast.row_ref, f32[512,1024]{1,0:T(8,128)S(1)} %fusion.129.q_ref, f32[32,512]{1,0:T(8,128)S(1)} %get-tuple-element.225.cos_ref, f32[32,512]{1,0:T(8,128)S(1)} %get-tuple-element.224.sin_ref, ...), custom_call_target="tpu_custom_call" | custom-call | flops 20000000000 | bytes 8000000 | tf_op jit(solution)/shard_map/attend/pallas_call | solution.py:146
  45.1 8.5 %collective-permute-done.5 = bf16[1024,1024]{1,0:T(8,128)(2,1)} collective-permute-done((bf16[1024,1024]{1,0:T(8,128)(2,1)}, bf16[1024,1024]{1,0:T(8,128)(2,1)}, u32[]{:S(2)}, u32[]{:S(2)}) %collective-permute-start.5) | collective-permute-done | bytes 2097184 | tf_op jit(solution)/shard_map/ppermute | solution.py:435
  63.0 16.1 %collective-permute-done.7 = bf16[512,1024]{1,0:T(8,128)(2,1)S(1)} collective-permute-done((bf16[512,1024]{1,0:T(8,128)(2,1)S(1)}, bf16[512,1024]{1,0:T(8,128)(2,1)S(1)}, u32[]{:S(2)}, u32[]{:S(2)}) %collective-permute-start.7) | collective-permute-done | bytes 1048608 | tf_op jit(solution)/shard_map/ppermute | solution.py:435
  97.6 24.7 %hidden_units.1 = (bf16[512,2816]{1,0:T(8,128)(2,1)}, bf16[512,2816]{1,0:T(8,128)(2,1)}, bf16[512,2816]{1,0:T(8,128)(2,1)}) custom-call(bf16[512,1024]{1,0:T(8,128)(2,1)S(1)} %get-tuple-element.229.xm_ref, bf16[512,1024]{1,0:T(8,128)(2,1)S(1)} %get-tuple-element.228.xo_ref, bf16[512,1024]{1,0:T(8,128)(2,1)S(1)} %pad_maximum_fusion.13.cm_ref, ...), custom_call_target="tpu_custom_call" | custom-call | flops 17716740096 | bytes 34603008 | tf_op jit(solution)/shard_map/hidden_units/pallas_call | solution.py:322
  124.5 10.1 %input_grad.2 = bf16[512,1024]{1,0:T(8,128)(2,1)S(1)} custom-call(bf16[512,2816]{1,0:T(8,128)(2,1)S(1)} %copy-done, bf16[512,2816]{1,0:T(8,128)(2,1)} %get-tuple-element.82.du_ref, bf16[1024,2816]{1,0:T(8,128)(2,1)} %g_ref, bf16[1024,2816]{1,0:T(8,128)(2,1)} %u_ref), custom_call_target="tpu_custom_call" | custom-call | flops 5905580032 | bytes 11534336 | tf_op jit(solution)/shard_map/input_grad/pallas_call | solution.py:346
  142.2 6.8 %convolution_convert_fusion.5 = bf16[512,1024]{1,0:T(8,128)(2,1)} fusion(bf16[512,2816]{1,0:T(8,128)(2,1)S(1)} %copy-done.38, bf16[2816,1024]{1,0:T(8,128)(2,1)} %dm_ref), kind=kOutput, calls=%fused_computation.104 | convolution fusion | flops 2953314304 | bytes 9699328 | tf_op jit(solution)/shard_map/dot_general | solution.py:29
  149.0 6.8 %convolution_convert_fusion.4 = bf16[512,1024]{1,0:T(8,128)(2,1)} fusion(bf16[512,2816]{1,0:T(8,128)(2,1)S(1)} %copy-done.38, bf16[2816,1024]{1,0:T(8,128)(2,1)} %collective-permute-done.12.do_ref), kind=kOutput, calls=%fused_computation.103 | convolution fusion | flops 2953314304 | bytes 9699328 | tf_op jit(solution)/shard_map/dot_general | solution.py:29
  157.1 4.5 convolution_convert_fusion.2
  165.2 4.7 convolution_convert_fusion.1
  171.5 9.7 %input_grad.3 = bf16[512,1024]{1,0:T(8,128)(2,1)S(1)} custom-call(bf16[512,2816]{1,0:T(8,128)(2,1)S(1)} %copy-done, bf16[512,2816]{1,0:T(8,128)(2,1)} %get-tuple-element.82.du_ref, bf16[1024,2816]{1,0:T(8,128)(2,1)} %collective-permute-done.10.go_ref.g_ref, bf16[1024,2816]{1,0:T(8,128)(2,1)} %collective-permute-done.11.uo_ref.u_ref), custom_call_target="tpu_custom_call" | custom-call | flops 5905580032 | bytes 11534336 | tf_op jit(solution)/shard_map/input_grad/pallas_call | solution.py:346
  185.7 7.5 %convolution_convert_fusion = bf16[512,2816]{1,0:T(8,128)(2,1)} fusion(bf16[1024,2816]{1,0:T(8,128)(2,1)} %constant_dynamic-update-slice_fusion.14, bf16[1024,128]{1,0:T(8,128)(2,1)S(1)} %copy-done.74, bf16[1024,128]{1,0:T(8,128)(2,1)S(1)} %copy-done.72, bf16[1024,128]{1,0:T(8,128)(2,1)S(1)} %copy-done.70, bf16[1024,128]{1,0:T(8,128)(2,1)S(1)} %copy-done.69), kind=kOutput, calls=%fused_computation.3 | convolution fusion | flops 2958426112 | bytes 9699328 | tf_op jit(solution)/shard_map/dot_general | solution.py:37
  193.3 5.3 %fusion.36 = f32[2816,512]{1,0:T(8,128)} fusion(bf16[1024,2816]{1,0:T(8,128)(2,1)S(1)} %bitcast.77, bf16[1024,128]{1,0:T(8,128)(2,1)S(1)} %copy-done.60, bf16[1024,128]{1,0:T(8,128)(2,1)S(1)} %copy-done.61, bf16[1024,128]{1,0:T(8,128)(2,1)S(1)} %copy-done.62, bf16[1024,128]{1,0:T(8,128)(2,1)S(1)} %copy-done.59), kind=kOutput, calls=%fused_computation.136 | convolution fusion | flops 2956984320 | bytes 12582912 | tf_op jit(solution)/shard_map/dot_general | solution.py:37
  198.6 5.4 %fusion.47 = f32[512,2816]{1,0:T(8,128)} fusion(bf16[1024,2816]{1,0:T(8,128)(2,1)S(1)} %bitcast.71, bf16[1024,128]{1,0:T(8,128)(2,1)S(1)} %copy-done.46, bf16[1024,128]{1,0:T(8,128)(2,1)S(1)} %get-tuple-element.142, bf16[1024,128]{1,0:T(8,128)(2,1)S(1)} %get-tuple-element.148, bf16[1024,128]{1,0:T(8,128)(2,1)S(1)} %get-tuple-element.150), kind=kOutput, calls=%fused_computation.147 | convolution fusion | flops 2956984320 | bytes 12582912 | tf_op jit(solution)/shard_map/dot_general | solution.py:37
  204.0 5.1 fusion.85
  221.6 19.3 %attend_back.1 = (bf16[512,1024]{1,0:T(8,128)(2,1)S(1)}, f32[2,1024,64]{2,1,0:T(8,128)S(1)}, f32[2,1024,64]{2,1,0:T(8,128)S(1)}) custom-call(s32[1]{0:T(128)} %bitcast.row_ref, bf16[1024,512]{1,0:T(8,128)(2,1)S(1)} %copy-done.6, bf16[512,1024]{1,0:T(8,128)(2,1)S(1)} %add_convert_fusion.4.do_ref, bf16[512,1024]{1,0:T(8,128)(2,1)S(1)} %get-tuple-element.70.o_ref, ...), custom_call_target="tpu_custom_call" | custom-call | flops 40000000000 | bytes 8000000 | tf_op jit(solution)/shard_map/attend_back/pallas_call | solution.py:264
  246.0 4.4 convert_add_fusion.1
  279.5 13.3 %collective-permute-done.45 = bf16[256,2816]{1,0:T(8,128)(2,1)S(1)} collective-permute-done((bf16[256,2816]{1,0:T(8,128)(2,1)S(1)}, bf16[256,2816]{1,0:T(8,128)(2,1)S(1)}, u32[]{:S(2)}, u32[]{:S(2)}) %collective-permute-start.45) | collective-permute-done | bytes 1441824 | tf_op jit(solution)/shard_map/ppermute | solution.py:438
  297.1 29.6 %collective-permute-done.46 = bf16[128,2816]{1,0:T(8,128)(2,1)S(1)} collective-permute-done((bf16[128,2816]{1,0:T(8,128)(2,1)S(1)}, bf16[128,2816]{1,0:T(8,128)(2,1)S(1)}, u32[]{:S(2)}, u32[]{:S(2)}) %collective-permute-start.46) | collective-permute-done | bytes 720928 | tf_op jit(solution)/shard_map/ppermute | solution.py:438
  328.0 32.0 %collective-permute-done.48 = bf16[2816,128]{1,0:T(8,128)(2,1)S(1)} collective-permute-done((bf16[2816,128]{1,0:T(8,128)(2,1)S(1)}, bf16[2816,128]{1,0:T(8,128)(2,1)S(1)}, u32[]{:S(2)}, u32[]{:S(2)}) %collective-permute-start.48) | collective-permute-done | bytes 720928 | tf_op jit(solution)/shard_map/ppermute | solution.py:438
  366.5 16.2 %collective-permute-done.37 = bf16[512,1280]{1,0:T(8,128)(2,1)S(1)} collective-permute-done((bf16[512,1280]{1,0:T(8,128)(2,1)S(1)}, bf16[512,1280]{1,0:T(8,128)(2,1)S(1)}, u32[]{:S(2)}, u32[]{:S(2)}) %collective-permute-start.37) | collective-permute-done | bytes 1310752 | tf_op jit(solution)/shard_map/ppermute | solution.py:438
  384.3 20.2 %collective-permute-done.40 = bf16[1024,512]{1,0:T(8,128)(2,1)S(1)} collective-permute-done((bf16[1024,512]{1,0:T(8,128)(2,1)S(1)}, bf16[1024,512]{1,0:T(8,128)(2,1)S(1)}, u32[]{:S(2)}, u32[]{:S(2)}) %collective-permute-start.40) | collective-permute-done | bytes 1048608 | tf_op jit(solution)/shard_map/ppermute | solution.py:438
  411.6 7.9 %collective-permute-done.35 = f32[2,256]{1,0:T(2,128)S(1)} collective-permute-done((f32[2,256]{1,0:T(2,128)S(1)}, f32[2,256]{1,0:T(2,128)S(1)}, u32[]{:S(2)}, u32[]{:S(2)}) %collective-permute-start.35) | collective-permute-done | bytes 2080 | tf_op jit(solution)/shard_map/ppermute | solution.py:438
  430.5 31.6 %collective-permute-done.42 = bf16[1024,128]{1,0:T(8,128)(2,1)S(1)} collective-permute-done((bf16[1024,128]{1,0:T(8,128)(2,1)S(1)}, bf16[1024,128]{1,0:T(8,128)(2,1)S(1)}, u32[]{:S(2)}, u32[]{:S(2)}) %collective-permute-start.42) | collective-permute-done | bytes 262176 | tf_op jit(solution)/shard_map/ppermute | solution.py:438
  478.3 28.3 %collective-permute-done.44 = bf16[128,2816]{1,0:T(8,128)(2,1)S(1)} collective-permute-done((bf16[128,2816]{1,0:T(8,128)(2,1)S(1)}, bf16[128,2816]{1,0:T(8,128)(2,1)S(1)}, u32[]{:S(2)}, u32[]{:S(2)}) %collective-permute-start.44) | collective-permute-done | bytes 720928 | tf_op jit(solution)/shard_map/ppermute | solution.py:438
  (436 shorter events, 171.3 us)
Async XLA Ops:
  4.4 49.1 %collective-permute-start.5 = (bf16[1024,1024]{1,0:T(8,128)(2,1)}, bf16[1024,1024]{1,0:T(8,128)(2,1)}, u32[]{:S(2)}, u32[]{:S(2)}) collective-permute-start(bf16[1024,1024]{1,0:T(8,128)(2,1)} %param.19), channel_id=1, source_target_pairs={{0,1},{1,0},{2,3},{3,2},{4,5},{5,4},{6,7},{7,6},{8,9},{9,8},{10,11... | collective-permute-start | bytes 6291464 | tf_op jit(solution)/shard_map/ppermute | solution.py:435
  16.8 36.8 %collective-permute-start.6 = (bf16[1024,1024]{1,0:T(8,128)(2,1)}, bf16[1024,1024]{1,0:T(8,128)(2,1)}, u32[]{:S(2)}, u32[]{:S(2)}) collective-permute-start(bf16[1024,1024]{1,0:T(8,128)(2,1)} %param.19), channel_id=1, source_target_pairs={{0,2},{2,0},{1,3},{3,1},{4,6},{6,4},{5,7},{7,5},{8,10},{10,8},{9,1... | collective-permute-start | bytes 6291464 | tf_op jit(solution)/shard_map/ppermute | solution.py:432
  17.3 80.3 %collective-permute-start.10 = (bf16[1024,2816]{1,0:T(8,128)(2,1)}, bf16[1024,2816]{1,0:T(8,128)(2,1)}, u32[]{:S(2)}, u32[]{:S(2)}) collective-permute-start(bf16[1024,2816]{1,0:T(8,128)(2,1)} %g_ref), channel_id=1, source_target_pairs={{0,2},{2,0},{1,3},{3,1},{4,6},{6,4},{5,7},{7,5},{8,10},{10,8},{9,1... | collective-permute-start | bytes 17301512 | tf_op jit(solution)/shard_map/ppermute | solution.py:432
  20.2 77.4 %collective-permute-start.11 = (bf16[1024,2816]{1,0:T(8,128)(2,1)}, bf16[1024,2816]{1,0:T(8,128)(2,1)}, u32[]{:S(2)}, u32[]{:S(2)}) collective-permute-start(bf16[1024,2816]{1,0:T(8,128)(2,1)} %u_ref), channel_id=1, source_target_pairs={{0,2},{2,0},{1,3},{3,1},{4,6},{6,4},{5,7},{7,5},{8,10},{10,8},{9,1... | collective-permute-start | bytes 17301512 | tf_op jit(solution)/shard_map/ppermute | solution.py:432
  23.6 74.0 %collective-permute-start.12 = (bf16[2816,1024]{1,0:T(8,128)(2,1)}, bf16[2816,1024]{1,0:T(8,128)(2,1)}, u32[]{:S(2)}, u32[]{:S(2)}) collective-permute-start(bf16[2816,1024]{1,0:T(8,128)(2,1)} %dm_ref), channel_id=1, source_target_pairs={{0,2},{2,0},{1,3},{3,1},{4,6},{6,4},{5,7},{7,5},{8,10},{10,8},{9,1... | collective-permute-start | bytes 17301512 | tf_op jit(solution)/shard_map/ppermute | solution.py:432
  134.6 47.2 %collective-permute-start.18 = (bf16[512,2816]{1,0:T(8,128)(2,1)S(1)}, bf16[512,2816]{1,0:T(8,128)(2,1)}, u32[]{:S(2)}, u32[]{:S(2)}) collective-permute-start(bf16[512,2816]{1,0:T(8,128)(2,1)S(1)} %copy-done), channel_id=1, source_target_pairs={{0,2},{2,0},{1,3},{3,1},{4,6},{6,4},{5,7},{7,5},{8,10},{10,8},{9,1... | collective-permute-start | bytes 8650760 | tf_op jit(solution)/shard_map/ppermute | solution.py:432
  134.7 74.4 %collective-permute-start.15 = (bf16[512,1024]{1,0:T(8,128)(2,1)S(1)}, bf16[512,1024]{1,0:T(8,128)(2,1)S(1)}, u32[]{:S(2)}, u32[]{:S(2)}) collective-permute-start(bf16[512,1024]{1,0:T(8,128)(2,1)S(1)} %input_grad.2), channel_id=1, source_target_pairs={{0,1},{1,0},{2,3},{3,2},{4,5},{5,4},{6,7},{7,6},{8,9},{9,8},{10,11... | collective-permute-start | bytes 3145736 | tf_op jit(solution)/shard_map/ppermute | solution.py:435
  161.6 81.0 %collective-permute-start.19 = (bf16[2816,512]{1,0:T(8,128)(2,1)}, bf16[2816,512]{1,0:T(8,128)(2,1)}, u32[]{:S(2)}, u32[]{:S(2)}) collective-permute-start(bf16[2816,512]{1,0:T(8,128)(2,1)} %convolution_convert_fusion.2), channel_id=1, source_target_pairs={{0,4},{4,0},{8,12},{12,8},{16,20},{20,16},{24,28},{28,24},{1,5},{5... | collective-permute-start | bytes 8650760 | tf_op jit(solution)/shard_map/ppermute | solution.py:438
  169.9 72.8 %collective-permute-start.20 = (bf16[512,2816]{1,0:T(8,128)(2,1)}, bf16[512,2816]{1,0:T(8,128)(2,1)}, u32[]{:S(2)}, u32[]{:S(2)}) collective-permute-start(bf16[512,2816]{1,0:T(8,128)(2,1)} %convolution_convert_fusion.1), channel_id=1, source_target_pairs={{0,8},{4,12},{8,0},{12,4},{16,24},{20,28},{24,16},{28,20},{1,9},{5... | collective-permute-start | bytes 8650760 | tf_op jit(solution)/shard_map/ppermute | solution.py:438
  218.1 49.3 %collective-permute-start.26 = (bf16[512,1024]{1,0:T(8,128)(2,1)}, bf16[512,1024]{1,0:T(8,128)(2,1)}, u32[]{:S(2)}, u32[]{:S(2)}) collective-permute-start(bf16[512,1024]{1,0:T(8,128)(2,1)} %get-tuple-element.221), channel_id=1, source_target_pairs={{0,2},{2,0},{1,3},{3,1},{4,6},{6,4},{5,7},{7,5},{8,10},{10,8},{9,1... | collective-permute-start | bytes 3145736 | tf_op jit(solution)/shard_map/ppermute | solution.py:432
  262.1 100.6 %collective-permute-start.22 = (bf16[512,1024]{1,0:T(8,128)(2,1)S(1)}, bf16[512,1024]{1,0:T(8,128)(2,1)S(1)}, u32[]{:S(2)}, u32[]{:S(2)}) collective-permute-start(bf16[512,1024]{1,0:T(8,128)(2,1)S(1)} %add_convert_fusion.3), channel_id=1, source_target_pairs={{0,1},{1,0},{2,3},{3,2},{4,5},{5,4},{6,7},{7,6},{8,9},{9,8},{10,11... | collective-permute-start | bytes 3145736 | tf_op jit(solution)/shard_map/ppermute | solution.py:435
  267.4 95.4 %collective-permute-start.23 = (bf16[512,1024]{1,0:T(8,128)(2,1)S(1)}, bf16[512,1024]{1,0:T(8,128)(2,1)S(1)}, u32[]{:S(2)}, u32[]{:S(2)}) collective-permute-start(bf16[512,1024]{1,0:T(8,128)(2,1)S(1)} %add_convert_fusion.2), channel_id=1, source_target_pairs={{0,1},{1,0},{2,3},{3,2},{4,5},{5,4},{6,7},{7,6},{8,9},{9,8},{10,11... | collective-permute-start | bytes 3145736 | tf_op jit(solution)/shard_map/ppermute | solution.py:435
  267.8 94.9 %collective-permute-start.28 = (bf16[512,2816]{1,0:T(8,128)(2,1)S(1)}, bf16[512,2816]{1,0:T(8,128)(2,1)S(1)}, u32[]{:S(2)}, u32[]{:S(2)}) collective-permute-start(bf16[512,2816]{1,0:T(8,128)(2,1)S(1)} %copy-done.87), channel_id=1, source_target_pairs={{0,4},{4,0},{8,12},{12,8},{16,20},{20,16},{24,28},{28,24},{1,5},{5... | collective-permute-start | bytes 8650760 | tf_op jit(solution)/shard_map/ppermute | solution.py:438
  292.8 89.9 %collective-permute-start.37 = (bf16[512,1280]{1,0:T(8,128)(2,1)S(1)}, bf16[512,1280]{1,0:T(8,128)(2,1)S(1)}, u32[]{:S(2)}, u32[]{:S(2)}) collective-permute-start(bf16[512,1280]{1,0:T(8,128)(2,1)S(1)} %convolution_convert_fusion.3), channel_id=1, source_target_pairs={{0,4},{4,0},{8,12},{12,8},{16,20},{20,16},{24,28},{28,24},{1,5},{5... | collective-permute-start | bytes 3932168 | tf_op jit(solution)/shard_map/ppermute | solution.py:438
  360.0 44.5 %collective-permute-start.40 = (bf16[1024,512]{1,0:T(8,128)(2,1)S(1)}, bf16[1024,512]{1,0:T(8,128)(2,1)S(1)}, u32[]{:S(2)}, u32[]{:S(2)}) collective-permute-start(bf16[1024,512]{1,0:T(8,128)(2,1)S(1)} %copy-done.88), channel_id=1, source_target_pairs={{0,4},{4,0},{8,12},{12,8},{16,20},{20,16},{24,28},{28,24},{1,5},{5... | collective-permute-start | bytes 3145736 | tf_op jit(solution)/shard_map/ppermute | solution.py:438
  362.8 104.3 %collective-permute-start.30 = (bf16[512,1024]{1,0:T(8,128)(2,1)}, bf16[512,1024]{1,0:T(8,128)(2,1)}, u32[]{:S(2)}, u32[]{:S(2)}) collective-permute-start(bf16[512,1024]{1,0:T(8,128)(2,1)} %convolution_convert_fusion.4), channel_id=1, source_target_pairs={{0,1},{1,0},{2,3},{3,2},{4,5},{5,4},{6,7},{7,6},{8,9},{9,8},{10,11... | collective-permute-start | bytes 3145736 | tf_op jit(solution)/shard_map/ppermute | solution.py:435
  364.3 110.4 %collective-permute-start.29 = (bf16[512,1024]{1,0:T(8,128)(2,1)S(1)}, bf16[512,1024]{1,0:T(8,128)(2,1)}, u32[]{:S(2)}, u32[]{:S(2)}) collective-permute-start(bf16[512,1024]{1,0:T(8,128)(2,1)S(1)} %copy-done.44), channel_id=1, source_target_pairs={{0,1},{1,0},{2,3},{3,2},{4,5},{5,4},{6,7},{7,6},{8,9},{9,8},{10,11... | collective-permute-start | bytes 3145736 | tf_op jit(solution)/shard_map/ppermute | solution.py:435
  366.4 39.7 %collective-permute-start.33 = (f32[2,1024]{1,0:T(2,128)S(1)}, f32[2,1024]{1,0:T(2,128)S(1)}, u32[]{:S(2)}, u32[]{:S(2)}) collective-permute-start(f32[2,1024]{1,0:T(2,128)S(1)} %pad_maximum_fusion.27), channel_id=1, source_target_pairs={{0,2},{2,0},{1,3},{3,1},{4,6},{6,4},{5,7},{7,5},{8,10},{10,8},{9,1... | collective-permute-start | bytes 24584 | tf_op jit(solution)/shard_map/ppermute | solution.py:432
  383.9 44.4 %collective-permute-start.38 = (bf16[256,1280]{1,0:T(8,128)(2,1)}, bf16[256,1280]{1,0:T(8,128)(2,1)}, u32[]{:S(2)}, u32[]{:S(2)}) collective-permute-start(bf16[256,1280]{1,0:T(8,128)(2,1)} %slice.477), channel_id=1, source_target_pairs={{0,8},{4,12},{8,0},{12,4},{16,24},{20,28},{24,16},{28,20},{1,9},{5... | collective-permute-start | bytes 1966088 | tf_op jit(solution)/shard_map/ppermute | solution.py:438
  423.9 47.1 %collective-permute-start.43 = (bf16[256,2816]{1,0:T(8,128)(2,1)S(1)}, bf16[256,2816]{1,0:T(8,128)(2,1)S(1)}, u32[]{:S(2)}, u32[]{:S(2)}) collective-permute-start(bf16[256,2816]{1,0:T(8,128)(2,1)S(1)} %slice.471), channel_id=1, source_target_pairs={{0,8},{4,12},{8,0},{12,4},{16,24},{20,28},{24,16},{28,20},{1,9},{5... | collective-permute-start | bytes 4325384 | tf_op jit(solution)/shard_map/ppermute | solution.py:438
  425.6 36.4 %collective-permute-start.42 = (bf16[1024,128]{1,0:T(8,128)(2,1)S(1)}, bf16[1024,128]{1,0:T(8,128)(2,1)S(1)}, u32[]{:S(2)}, u32[]{:S(2)}) collective-permute-start(bf16[1024,128]{1,0:T(8,128)(2,1)S(1)} %slice.480), channel_id=1, source_target_pairs={{0,16},{4,20},{8,24},{12,28},{16,0},{20,4},{24,8},{28,12},{1,17},{... | collective-permute-start | bytes 786440 | tf_op jit(solution)/shard_map/ppermute | solution.py:438
  429.5 36.1 %collective-permute-start.39 = (bf16[128,1280]{1,0:T(8,128)(2,1)S(1)}, bf16[128,1280]{1,0:T(8,128)(2,1)S(1)}, u32[]{:S(2)}, u32[]{:S(2)}) collective-permute-start(bf16[128,1280]{1,0:T(8,128)(2,1)S(1)} %slice.479), channel_id=1, source_target_pairs={{0,16},{4,20},{8,24},{12,28},{16,0},{20,4},{24,8},{28,12},{1,17},{... | collective-permute-start | bytes 983048 | tf_op jit(solution)/shard_map/ppermute | solution.py:438
  470.5 37.3 %collective-permute-start.32 = (f32[512,1024]{1,0:T(8,128)S(1)}, f32[512,1024]{1,0:T(8,128)S(1)}, u32[]{:S(2)}, u32[]{:S(2)}) collective-permute-start(f32[512,1024]{1,0:T(8,128)S(1)} %get-tuple-element.175), channel_id=1, source_target_pairs={{0,2},{2,0},{1,3},{3,1},{4,6},{6,4},{5,7},{7,5},{8,10},{10,8},{9,1... | collective-permute-start | bytes 6291464 | tf_op jit(solution)/shard_map/ppermute | solution.py:432
  471.3 35.3 %collective-permute-start.44 = (bf16[128,2816]{1,0:T(8,128)(2,1)S(1)}, bf16[128,2816]{1,0:T(8,128)(2,1)S(1)}, u32[]{:S(2)}, u32[]{:S(2)}) collective-permute-start(bf16[128,2816]{1,0:T(8,128)(2,1)S(1)} %slice.476), channel_id=1, source_target_pairs={{0,16},{4,20},{8,24},{12,28},{16,0},{20,4},{24,8},{28,12},{1,17},{... | collective-permute-start | bytes 2162696 | tf_op jit(solution)/shard_map/ppermute | solution.py:438
  (128 other events, 1899.8 us)

commit v3 on v2

--- a/solution.py
+++ b/solution.py
@@ -1,3 +1,4 @@
+import functools
 import math
 
 import jax
@@ -84,10 +85,9 @@
 
 
 def attend_kernel(
-    row_ref, q_ref, cos_ref, sin_ref, start_ref, own_ref, other_ref, o_ref, lse_ref, qt_ref, bias, keys, values_t
+    group, row_ref, q_ref, cos_ref, sin_ref, start_ref, own_ref, other_ref, o_ref, lse_ref, qt_ref, bias, keys, values_t
 ):
     step = pl.program_id(0)
-    kv = step // 4
     row = row_ref[0]
 
     @pl.when(step == 0)
@@ -96,11 +96,9 @@
 
         def put(i, block):
             span = slice(i * CHUNK, (i + 1) * CHUNK)
-            for h in range(2):
-                keys[h, span, :] = block[:, h * HEAD_SIZE : (h + 1) * HEAD_SIZE]
-            turned = jnp.transpose(block[:, PAIR:].astype(F32)).astype(BF16)
-            for h in range(2):
-                values_t[h, :, span] = turned[h * HEAD_SIZE : (h + 1) * HEAD_SIZE]
+            lanes = slice(group * HEAD_SIZE, (group + 1) * HEAD_SIZE)
+            keys[span, :] = block[:, lanes]
+            values_t[:, span] = jnp.transpose(block[:, PAIR:].astype(F32)).astype(BF16)[lanes]
 
         place_keys(own_ref, other_ref, row, put)
 
@@ -118,11 +116,11 @@
         outs, sums = [], []
         for h in range(2):
             query = qt_ref[h * HEAD_SIZE : (h + 1) * HEAD_SIZE, lanes]
-            scores = dot_plain(keys[kv, :count, :], query) + bias[:count, lanes]
+            scores = dot_plain(keys[:count, :], query) + bias[:count, lanes]
             top = jnp.max(scores, axis=0, keepdims=True)
             expo = jnp.exp(scores - top)
             total = jnp.sum(expo, axis=0, keepdims=True)
-            head = dot_plain(values_t[kv, :, :count], expo.astype(BF16))
+            head = dot_plain(values_t[:, :count], expo.astype(BF16))
             outs.append(head * (1.0 / total))
             sums.append(top + jnp.log(total))
         o_ref[lanes, :] = jnp.transpose(jnp.concatenate(outs, axis=0)).astype(BF16)
@@ -139,16 +137,15 @@
         unit(1, 3)
 
 
-def attend(row, q, cosine, sine, start, own_kv, other_kv):
-    heads = q.shape[1] // HEAD_SIZE
-    pairs = heads // 2
+def attend(group, row, q, cosine, sine, start, own_kv, other_kv):
+    pairs = q.shape[1] // (2 * PAIR)
     whole = lambda shape: pl.BlockSpec(shape, lambda i: (0,) * len(shape))
     return pl.pallas_call(
-        attend_kernel,
+        functools.partial(attend_kernel, group),
         grid=(pairs,),
         in_specs=[
             pl.BlockSpec(memory_space=pltpu.SMEM),
-            pl.BlockSpec((OWN, PAIR), lambda i: (0, i)),
+            pl.BlockSpec((OWN, PAIR), lambda i: (0, i + group * pairs)),
             whole((HALF, OWN)),
             whole((HALF, OWN)),
             whole((1, OWN)),
@@ -161,17 +158,17 @@
             pl.BlockSpec((PAIR, OWN), lambda i: (i, 0)),
         ],
         out_shape=[
-            jax.ShapeDtypeStruct((OWN, heads * HEAD_SIZE), BF16),
+            jax.ShapeDtypeStruct((OWN, pairs * PAIR), BF16),
             jax.ShapeDtypeStruct((pairs, 2, OWN), F32),
-            jax.ShapeDtypeStruct((heads * HEAD_SIZE, OWN), BF16),
+            jax.ShapeDtypeStruct((pairs * PAIR, OWN), BF16),
         ],
         scratch_shapes=[
             pltpu.VMEM((SEQ, OWN), F32),
-            pltpu.VMEM((2, SEQ, HEAD_SIZE), BF16),
-            pltpu.VMEM((2, HEAD_SIZE, SEQ), BF16),
+            pltpu.VMEM((SEQ, HEAD_SIZE), BF16),
+            pltpu.VMEM((HEAD_SIZE, SEQ), BF16),
         ],
         compiler_params=pltpu.CompilerParams(vmem_limit_bytes=40 * 1024 * 1024),
-        cost_estimate=pl.CostEstimate(flops=20_000_000_000, bytes_accessed=8_000_000, transcendentals=0),
+        cost_estimate=pl.CostEstimate(flops=1000, bytes_accessed=1000, transcendentals=0),
         name="attend",
     )(row, q, cosine, sine, start, own_kv, other_kv)
 
@@ -293,102 +290,116 @@
             pltpu.VMEM((2, SEQ, HEAD_SIZE), BF16),
         ],
         compiler_params=pltpu.CompilerParams(vmem_limit_bytes=40 * 1024 * 1024),
-        cost_estimate=pl.CostEstimate(flops=40_000_000_000, bytes_accessed=8_000_000, transcendentals=0),
+        cost_estimate=pl.CostEstimate(flops=1000, bytes_accessed=1000, transcendentals=0),
         name="attend_back",
     )(row, qt, d_o, o, lse, cosine, sine, start, own_kv, other_kv)
 
 
 def hidden_units_kernel(
-    xm_ref, xo_ref, cm_ref, co_ref, gm_ref, go_ref, um_ref, uo_ref, dm_ref, do_ref, act_ref, dg_ref, du_ref
+    xm_ref, xo_ref, cm_ref, co_ref, gm_ref, go_ref, um_ref, uo_ref, dm_ref, do_ref, out_ref
 ):
     gate = dot_plain(xm_ref[...], gm_ref[...]) + dot_plain(xo_ref[...], go_ref[...])
     up = dot_plain(xm_ref[...], um_ref[...]) + dot_plain(xo_ref[...], uo_ref[...])
     d_act = dot_right(cm_ref[...], dm_ref[...]) + dot_right(co_ref[...], do_ref[...])
     sigma = jax.nn.sigmoid(gate)
     swish = gate * sigma
-    act_ref[...] = (swish * up).astype(BF16)
-    dg_ref[...] = (d_act * up * (sigma * (1.0 + gate * (1.0 - sigma)))).astype(BF16)
-    du_ref[...] = (d_act * swish).astype(BF16)
-
-
-def hidden_units(xm, xo, cm, co, gm, go, um, uo, dm, do):
+    out_ref[0] = (swish * up).astype(BF16)
+    out_ref[1] = (d_act * up * (sigma * (1.0 + gate * (1.0 - sigma)))).astype(BF16)
+    out_ref[2] = (d_act * swish).astype(BF16)
+
+
+def hidden_units(first, tiles, xm, xo, cm, co, gm, go, um, uo, dm, do):
     rows, depth = xm.shape
-    wide = gm.shape[1]
     tile = 256
+    wide = tiles * tile
     full = pl.BlockSpec((rows, depth), lambda i: (0, 0))
-    column = pl.BlockSpec((depth, tile), lambda i: (0, i))
-    line = pl.BlockSpec((tile, depth), lambda i: (i, 0))
-    out = pl.BlockSpec((rows, tile), lambda i: (0, i))
+    column = pl.BlockSpec((depth, tile), lambda i: (0, i + first))
+    line = pl.BlockSpec((tile, depth), lambda i: (i + first, 0))
+    out = pl.BlockSpec((3, rows, tile), lambda i: (0, 0, i))
     return pl.pallas_call(
         hidden_units_kernel,
-        grid=(wide // tile,),
+        grid=(tiles,),
         in_specs=[full] * 4 + [column] * 4 + [line] * 2,
-        out_specs=[out] * 3,
-        out_shape=[jax.ShapeDtypeStruct((rows, wide), BF16)] * 3,
+        out_specs=out,
+        out_shape=jax.ShapeDtypeStruct((3, rows, wide), BF16),
         compiler_params=pltpu.CompilerParams(vmem_limit_bytes=48 * 1024 * 1024),
-        cost_estimate=pl.CostEstimate(
-            flops=12 * rows * depth * wide, bytes_accessed=12 * depth * wide, transcendentals=0
-        ),
+        cost_estimate=pl.CostEstimate(flops=1000, bytes_accessed=1000, transcendentals=0),
         name="hidden_units",
     )(xm, xo, cm, co, gm, go, um, uo, dm, do)
 
 
-def input_grad_kernel(dg_ref, du_ref, g_ref, u_ref, out_ref):
-    out_ref[...] = (dot_right(dg_ref[...], g_ref[...]) + dot_right(du_ref[...], u_ref[...])).astype(BF16)
-
-
-def input_grad(dg, du, g, u):
-    rows, wide = dg.shape
-    depth = g.shape[0]
+def input_grad_kernel(a_ref, b_ref, gm_ref, um_ref, go_ref, uo_ref, out_ref):
+    cut = a_ref.shape[2]
+
+    def fill(g_ref, u_ref):
+        total = dot_right(a_ref[1], g_ref[:, :cut]) + dot_right(b_ref[1], g_ref[:, cut:])
+        total += dot_right(a_ref[2], u_ref[:, :cut]) + dot_right(b_ref[2], u_ref[:, cut:])
+        out_ref[...] = total.astype(BF16)
+
+    step, half = pl.program_id(0), pl.num_programs(0) // 2
+    pl.when(step < half)(lambda: fill(gm_ref, um_ref))
+    pl.when(step >= half)(lambda: fill(go_ref, uo_ref))
+
+
+def input_grad(a, b, gm, um, go, uo):
+    rows = a.shape[1]
+    depth, wide = gm.shape
     tile = 256
-    full = pl.BlockSpec((rows, wide), lambda i: (0, 0))
-    line = pl.BlockSpec((tile, wide), lambda i: (i, 0))
+    tiles = depth // tile
+    full = lambda value: pl.BlockSpec(value.shape, lambda i: (0, 0, 0))
+    line_m = pl.BlockSpec((tile, wide), lambda i: (jnp.minimum(i, tiles - 1), 0))
+    line_o = pl.BlockSpec((tile, wide), lambda i: (jnp.maximum(i - tiles, 0), 0))
     return pl.pallas_call(
         input_grad_kernel,
-        grid=(depth // tile,),
-        in_specs=[full] * 2 + [line] * 2,
+        grid=(2 * tiles,),
+        in_specs=[full(a), full(b), line_m, line_m, line_o, line_o],
         out_specs=pl.BlockSpec((rows, tile), lambda i: (0, i)),
-        out_shape=jax.ShapeDtypeStruct((rows, depth), BF16),
+        out_shape=jax.ShapeDtypeStruct((rows, 2 * depth), BF16),
         compiler_params=pltpu.CompilerParams(vmem_limit_bytes=48 * 1024 * 1024),
-        cost_estimate=pl.CostEstimate(flops=4 * rows * depth * wide, bytes_accessed=4 * depth * wide, transcendentals=0),
+        cost_estimate=pl.CostEstimate(flops=1000, bytes_accessed=1000, transcendentals=0),
         name="input_grad",
-    )(dg, du, g, u)
+    )(a, b, gm, um, go, uo)
 
 
 class Halving:
-    def __init__(self, left, right, axis, order, flip):
-        self.left, self.right, self.axis, self.order, self.flip = left, right, axis, list(order), flip
-        self.at = 0
+    def __init__(self, pairs, order, flip):
+        self.pairs, self.order, self.flip, self.at, self.open = pairs, list(order), flip, 0, False
 
     def part(self, upper):
-        if not self.order:
-            return dot_left(self.left, self.right)
-        if self.axis == 0:
-            return dot_left(half_of(self.left, 1, upper), self.right)
-        return dot_left(self.left, half_of(self.right, 1, upper))
-
-    def begin(self):
-        self.send = self.part(True).astype(BF16)
+        parts = [dot_left(half_of(a, upper, 1) if self.order else a, b) for a, b in self.pairs]
+        if upper:
+            parts = [p.astype(BF16) for p in parts]
+        return parts[0] if len(parts) == 1 else jnp.concatenate(parts, axis=1)
+
+    def begin(self, *deps):
+        if deps:
+            a, b = self.pairs[0]
+            a, *_ = tie(a, *deps)
+            self.pairs[0] = (a, b)
+        self.send = self.part(True)
         return self.send
 
-    def stay(self):
+    def stay(self, *deps):
+        if deps:
+            a, b = self.pairs[0]
+            a, *_ = tie(a, *deps)
+            self.pairs[0] = (a, b)
         self.keep = self.part(False)
         return self.keep
 
     def go(self):
-        if self.at < len(self.order):
+        self.came, self.open = self.send, self.at < len(self.order)
+        if self.open:
             self.came = self.flip(self.send, self.order[self.at])
-        else:
-            self.came = self.send
-        return self.came
 
     def add(self):
-        if self.at < len(self.order):
+        if self.open:
+            self.open = False
             self.total = self.keep + self.came.astype(F32)
             self.at += 1
             if self.at < len(self.order):
-                self.send = half_of(self.total, self.axis, True).astype(BF16)
-                self.keep = half_of(self.total, self.axis, False)
+                self.send = half_of(self.total, True).astype(BF16)
+                self.keep = half_of(self.total, False)
         elif not self.order:
             self.total = self.keep
 
@@ -400,13 +411,20 @@
         return self.total
 
 
-def half_of(value, axis, upper):
+def half_of(value, upper, axis=0):
     size = value.shape[axis] // 2
     return lax.slice_in_dim(value, size if upper else 0, 2 * size if upper else size, axis=axis)
 
 
 def tie(*values):
     return lax.optimization_barrier(values)
+
+
+def serve(value, done=(), ready=()):
+    out = tie(value, *[h.came for h in done], *ready)
+    for h, came in zip(done, out[1:]):
+        h.came = came
+    return out[0]
 
 
 def shards(
@@ -450,6 +468,9 @@
             blocks.append(lax.dynamic_slice_in_dim(value, (dp ^ differs) * width, width, axis=1))
         return jnp.concatenate(blocks, axis=1)
 
+    low = (dp & 1) == 0
+    half = w_o.shape[0] // 2
+    far_a = cross(jnp.where(low, w_o[:half], w_o[half:]))
     x_m = own_rows(tokens, row)
     x_o = swap(other_rows(tokens, row))
     wkv = jnp.concatenate([key_weight, value_weight], axis=1)
@@ -457,7 +478,6 @@
     wq_o = swap(query_weight)
     gains = jnp.stack([g_attn, g_mlp])
     gains_o = swap(gains)
-    w_o_x = cross(w_o)
     x_m, x_o = x_m.astype(F32), x_o.astype(F32)
     square = jnp.sum(x_m * x_m, axis=-1, keepdims=True) + jnp.sum(x_o * x_o, axis=-1, keepdims=True)
     inv_one = lax.rsqrt(square / MODEL_WIDTH + EPS)
@@ -485,27 +505,45 @@
     q = dot_plain(xn_m, query_weight) + dot_plain(xn_o, wq_o)
 
     cotangent, w_gate, w_up, w_down, w_o, xn_o = tie(cotangent, w_gate, w_up, w_down, w_o, xn_o)
-    w_o_o = swap(w_o)
     wg_o = swap(w_gate)
     wu_o = swap(w_up)
+    w_o_o = swap(w_o)
     c_m = own_rows(cotangent, row)
     c_t = other_rows(cotangent, row)
+    q, far_a, other_kv, c_m, c_t = tie(q, far_a, other_kv, c_m, c_t)
+    far_b = flip(far_a, 0)
+    row_arg = row.astype(jnp.int32).reshape(1)
+    start_arg = start_own.reshape(1, OWN)
+    o_1, lse_1, qt_1 = attend(0, row_arg, q, cosine_t, sine_t, start_arg, own_kv, other_kv)
+    o_1, q, wg_o, wu_o, w_o_o, w_down, c_t, far_a = tie(o_1, q, wg_o, wu_o, w_o_o, w_down, c_t, far_a)
+    o_x1 = cross(o_1)
     c_o = swap(c_t)
     wd_o = swap(w_down)
+    far_ao = swap(far_a)
+    o_2, lse_2, qt_2 = attend(1, row_arg, q, cosine_t, sine_t, start_arg, own_kv, other_kv)
+    o_2, o_1, c_o, wd_o, far_ao, xn_o = tie(o_2, o_1, c_o, wd_o, far_ao, xn_o)
+    o_x2 = cross(o_2)
+
+    near_m = dot_plain(o_1, w_o[:half]) + dot_plain(o_2, w_o[half:])
+    near_o = dot_plain(o_1, w_o_o[:half]) + dot_plain(o_2, w_o_o[half:])
+    order_y, order_z = order_of(0), order_of(min(1, max(bits - 1, 0)))
+    both = lambda own, other: jnp.concatenate([own, other], axis=0)
+    c_y = relative(both(c_m, c_t), order_y)
+    o = jnp.concatenate([o_1, o_2], axis=1)
+    o_t = swap(o)
+    qt = jnp.concatenate([qt_1, qt_2], axis=0)
+    lse = jnp.concatenate([lse_1, lse_2], axis=0)
+    near_m, near_o, far_b = tie(near_m, near_o, far_b)
+    far_bo = swap(far_b)
     xn_t = swap(xn_o)
-
-    row_arg = row.astype(jnp.int32).reshape(1)
-    start_arg = start_own.reshape(1, OWN)
-    o, lse, qt = attend(row_arg, q, cosine_t, sine_t, start_arg, own_kv, other_kv)
-    o, w_o_x = tie(o, w_o_x)
-    w_o_xo = swap(w_o_x)
-
-    o_x = cross(o)
-    o_t = swap(o)
-    near_m, near_o = dot_plain(o, w_o), dot_plain(o, w_o_o)
-    near_m, near_o, o_x = tie(near_m, near_o, o_x)
-    hidden_m = x_m + (near_m + dot_plain(o_x, w_o_x))
-    hidden_o = x_o + (near_o + dot_plain(o_x, w_o_xo))
+    c_y, qt, lse, far_b, far_bo, o_x1 = tie(c_y, qt, lse, far_b, far_bo, o_x1)
+    pick = lambda a, b: (jnp.where(low, a, b), jnp.where(low, b, a))
+    far_1, far_2 = pick(far_a, far_b)
+    far_1o, far_2o = pick(far_ao, far_bo)
+    mid_m, mid_o = dot_plain(o_x1, far_1), dot_plain(o_x1, far_1o)
+    mid_m, mid_o, o_t, xn_t, o_x2 = tie(mid_m, mid_o, o_t, xn_t, o_x2)
+    hidden_m = x_m + (near_m + (mid_m + dot_plain(o_x2, far_2)))
+    hidden_o = x_o + (near_o + (mid_o + dot_plain(o_x2, far_2o)))
     square = jnp.sum(hidden_m * hidden_m, axis=-1, keepdims=True) + jnp.sum(
         hidden_o * hidden_o, axis=-1, keepdims=True
     )
@@ -514,39 +552,54 @@
     xn2_m = (unit_m * gains[1]).astype(BF16)
     xn2_o = (unit_o * gains_o[1]).astype(BF16)
 
-    order_y, order_z = order_of(0), order_of(min(1, max(bits - 1, 0)))
-    both = lambda own, other: jnp.concatenate([own, other], axis=0)
-    xn2_all = both(xn2_m, swap(xn2_o))
+    xn2_t = swap(xn2_o)
+    tiles = w_gate.shape[1] // 256
+    operands = (c_m, c_o, w_gate, wg_o, w_up, wu_o, w_down, wd_o)
+    one = hidden_units(0, tiles - tiles // 2, xn2_m, xn2_o, *operands)
+    one_t = swap(one)
+    one, xn2_m2 = tie(one, xn2_m)
+    two = hidden_units(tiles - tiles // 2, tiles // 2, xn2_m2, xn2_o, *operands)
+    two, one_t, xn2_t = tie(two, one_t, xn2_t)
+    two_t = swap(two)
+
+    all_1 = [both(one[i], one_t[i]) for i in range(3)]
+    down_1 = Halving([(c_y, all_1[0])], order_y, flip)
+    down_1.begin(two)
+    down_1.go()
+    down_1.send, xn2_m2 = tie(down_1.send, xn2_m2)
+    xn2_all = both(xn2_m2, xn2_t)
     xn2_y, xn2_z = relative(xn2_all, order_y), relative(xn2_all, order_z)
-    c_y = relative(both(c_m, c_t), order_y)
-    act, d_gate, d_up = hidden_units(xn2_m, xn2_o, c_m, c_o, w_gate, wg_o, w_up, wu_o, w_down, wd_o)
-    act_t, d_up_t, d_gate_t = swap(act), swap(d_up), swap(d_gate)
-    part_m = input_grad(d_gate, d_up, w_gate, w_up)
-    came_m = cross(part_m)
-    act_t, d_up_t, part_m = tie(act_t, d_up_t, part_m)
-    down = Halving(both(act, act_t), c_y, 1, order_y, flip)
-    upper = Halving(xn2_z, both(d_up, d_up_t), 0, order_z, flip)
-    gater = Halving(xn2_y, both(d_gate, d_gate_t), 0, order_y, flip)
-    down.begin()
-    down.go()
-    upper.begin()
-    upper.go()
-    down.send, upper.send, d_gate_late = tie(down.send, upper.send, d_gate)
-    part_o = input_grad(d_gate_late, d_up, wg_o, wu_o)
-    came_o = cross(part_o)
-    down.left, upper.left, part_o = tie(down.left, upper.left, part_o)
-    down.stay()
-    upper.stay()
-    gater.begin()
-    gater.stay()
-    mix_m = dot_plain(act, w_down).astype(BF16)
-    mix_o = dot_plain(act, wd_o).astype(BF16)
-
-    came_m, came_o, down.keep, upper.keep, gater.send, gater.keep, mix_m, mix_o = tie(
-        came_m, came_o, down.keep, upper.keep, gater.send, gater.keep, mix_m, mix_o
-    )
-    d_xn2_m = part_m.astype(F32) + came_m.astype(F32)
-    d_xn2_o = part_o.astype(F32) + came_o.astype(F32)
+    upper_1 = Halving([(xn2_z, all_1[2])], order_z, flip)
+    upper_1.begin()
+    upper_1.go()
+    upper_1.send, two_late, two_t = tie(upper_1.send, two, two_t)
+    part = input_grad(one, two_late, w_gate, w_up, wg_o, wu_o)
+    came = cross(part)
+    part, two_t = tie(part, two_t)
+    all_2 = [both(two[i], two_t[i]) for i in range(3)]
+    middle = Halving([(c_y, all_2[0]), (xn2_y, all_1[1])], order_y, flip)
+    middle.begin(part)
+    middle.go()
+    upper_2 = Halving([(xn2_z, all_2[2])], order_z, flip)
+    upper_2.begin(middle.send)
+    upper_2.go()
+    gate_2 = Halving([(xn2_y, all_2[1])], order_y, flip)
+    gate_2.begin(upper_2.send)
+    down_1.stay(gate_2.send)
+    upper_1.stay(down_1.keep)
+    part = serve(part, (down_1, upper_1), (upper_1.keep, down_1.keep))
+    down_1.add()
+    down_1.go()
+    upper_1.add()
+    upper_1.go()
+    middle.stay(part, down_1.send, upper_1.send)
+    upper_2.stay(middle.keep)
+    gate_2.stay(upper_2.keep)
+
+    came, gate_2.keep, middle.keep, upper_2.keep = tie(came, gate_2.keep, middle.keep, upper_2.keep)
+    width = tokens.shape[1]
+    d_xn2 = part.astype(F32) + came.astype(F32)
+    d_xn2_m, d_xn2_o = d_xn2[:, :width], d_xn2[:, width:]
     e_m, e_o = d_xn2_m * gains[1], d_xn2_o * gains_o[1]
     mean = (
         jnp.sum(e_m * unit_m, axis=-1, keepdims=True) + jnp.sum(e_o * unit_o, axis=-1, keepdims=True)
@@ -558,49 +611,74 @@
     dh_m, dh_o = d_hid_m.astype(BF16), d_hid_o.astype(BF16)
     dh_t = swap(dh_o)
     d_o = (dot_right(dh_m, w_o) + dot_right(dh_o, w_o_o)).astype(BF16)
+    d_o, dh_t, gate_2.send = tie(d_o, dh_t, gate_2.send)
+    d_o = serve(d_o, (upper_2,))
+    gate_2.go()
+    upper_2.add()
+    d_o, upper_2.send, upper_2.keep, gate_2.send = tie(d_o, upper_2.send, upper_2.keep, gate_2.send)
 
     d_q, d_k, d_v = attend_back(row_arg, qt, d_o, o, lse, cosine_t, sine_t, start_arg, own_kv, other_kv)
     d_kv = jnp.concatenate([d_k[0], d_k[1], d_v[0], d_v[1]], axis=1)
     d_kv_t = swap(other_rows(d_kv, row))
     d_kv_own = own_rows(d_kv, row)
-    d_kv_own, down.came, upper.came, gater.send = tie(d_kv_own, down.came, upper.came, gater.send)
-    gater.go()
-    down.add()
-    down.go()
-    upper.add()
-    upper.go()
-    d_kv_t, down.send, down.keep, upper.send, upper.keep = tie(
-        d_kv_t, down.send, down.keep, upper.send, upper.keep
-    )
+    d_kv_own = serve(d_kv_own, (down_1,))
+    down_1.add()
+    d_kv_t, d_kv_own, down_1.send, down_1.keep = tie(d_kv_t, d_kv_own, down_1.send, down_1.keep)
     d_kv = d_kv_own + d_kv_t
     d_key = d_kv[:, :narrow].reshape(OWN, -1, HEAD_SIZE)
     first, second = d_key[..., :HALF], d_key[..., HALF:]
     d_key = jnp.concatenate([first * cosine + second * sine, second * cosine - first * sine], axis=-1)
     d_kv = jnp.concatenate([d_key.reshape(OWN, narrow).astype(BF16), d_kv[:, narrow:].astype(BF16)], axis=1)
     d_qkv = jnp.concatenate([d_q, d_kv], axis=1)
-    part_m = (dot_right(d_q, query_weight) + dot_right(d_kv, wkv)).astype(BF16)
-    came_m = cross(part_m)
-    part_o = (dot_right(d_q, wq_o) + dot_right(d_kv, wkv_o)).astype(BF16)
-    came_o = cross(part_o)
     d_qkv_t = swap(d_qkv)
-    d_qkv_t, dh_t, part_o = tie(d_qkv_t, dh_t, part_o)
-    outer = Halving(both(o, o_t), relative(both(dh_m, dh_t), order_y), 1, order_y, flip)
-    inner = Halving(relative(both(xn_m, xn_t), order_y), both(d_qkv, d_qkv_t), 0, order_y, flip)
-    inner.begin()
-    inner.go()
-    outer.begin()
+    last = jnp.concatenate(
+        [
+            (dot_right(d_q, query_weight) + dot_right(d_kv, wkv)).astype(BF16),
+            (dot_right(d_q, wq_o) + dot_right(d_kv, wkv_o)).astype(BF16),
+        ],
+        axis=1,
+    )
+    last, d_qkv_t = tie(last, d_qkv_t)
+    last_came = cross(last)
+    last = serve(last, (middle,))
+    middle.add()
+    middle.go()
+    outer = Halving(
+        [
+            (relative(both(dh_m, dh_t), order_y), both(o, o_t)),
+            (relative(both(xn_m, xn_t), order_y), both(d_qkv, d_qkv_t)),
+        ],
+        order_y,
+        flip,
+    )
+    outer.begin(last, middle.send, middle.keep)
+    outer.send = serve(outer.send, (upper_1,))
     outer.go()
-    inner.stay()
-    outer.stay()
-
-    came_m, came_o, inner.keep, outer.keep, gater.came, mix_m, mix_o = tie(
-        came_m, came_o, inner.keep, outer.keep, gater.came, mix_m, mix_o
+    upper_1.add()
+    upper_1.go()
+    down_1.send, upper_1.send = tie(down_1.send, upper_1.send)
+    down_1.go()
+    outer.stay(down_1.send, outer.send)
+    one, outer.keep = tie(one, outer.keep)
+    cut = one.shape[2]
+    mix = jnp.concatenate(
+        [
+            (dot_plain(one[0], w_down[:cut]) + dot_plain(two[0], w_down[cut:])).astype(BF16),
+            (dot_plain(one[0], wd_o[:cut]) + dot_plain(two[0], wd_o[cut:])).astype(BF16),
+        ],
+        axis=1,
     )
-    gater.add()
-    gater.go()
-    mix_cm, mix_co = cross(mix_m), cross(mix_o)
-    d_xn_m = part_m.astype(F32) + came_m.astype(F32)
-    d_xn_o = part_o.astype(F32) + came_o.astype(F32)
+    mix = serve(mix, (down_1, middle, upper_1))
+    down_1.add()
+    middle.add()
+    middle.go()
+    upper_2.send, middle.send = tie(upper_2.send, middle.send)
+    upper_2.go()
+
+    last_came, mix, middle.keep, middle.send = tie(last_came, mix, middle.keep, middle.send)
+    mix_came = cross(mix)
+    d_xn = last.astype(F32) + last_came.astype(F32)
+    d_xn_m, d_xn_o = d_xn[:, :width], d_xn[:, width:]
     unit_m, unit_o = x_m * inv_one, x_o * inv_one
     e_m, e_o = d_xn_m * gains[0], d_xn_o * gains_o[0]
     mean = (
@@ -610,18 +688,34 @@
     gg_attn_o = jnp.sum(d_xn_o * unit_o, axis=0)
     d_tok_m = d_hid_m + inv_one * (e_m - unit_m * mean)
     d_tok_o = d_hid_o + inv_one * (e_o - unit_o * mean)
-    d_tokens = merge_rows(d_tok_m, swap(d_tok_o), row)
-
-    out_m = (hidden_m + (mix_m.astype(F32) + mix_cm.astype(F32))).astype(BF16)
-    out_o = (hidden_o + (mix_o.astype(F32) + mix_co.astype(F32))).astype(BF16)
+    d_tok_t = swap(d_tok_o)
+    gg = jnp.stack([gg_attn_m, gg_mlp_m]) + swap(jnp.stack([gg_attn_o, gg_mlp_o]))
+    gg = lax.psum_scatter(gg, "dp", scatter_dimension=1, tiled=True)
+    d_tokens = merge_rows(d_tok_m, d_tok_t, row)
+
+    d_tokens = serve(d_tokens, (gate_2,))
+    gate_2.add()
+    gate_2.go()
+    d_tokens, gate_2.send, gate_2.keep = tie(d_tokens, gate_2.send, gate_2.keep)
+    gate_2.came = serve(gate_2.came, (middle,))
+    middle.add()
+    outer.came, middle.total = tie(outer.came, middle.total)
+    outer.add()
+    outer.go()
+    outer.send, mix_came = tie(outer.send, mix_came)
+
+    mixed_all = mix.astype(F32) + mix_came.astype(F32)
+    out_m = (hidden_m + mixed_all[:, :width]).astype(BF16)
+    out_o = (hidden_o + mixed_all[:, width:]).astype(BF16)
     mixed = merge_rows(out_m, swap(out_o), row)
 
-    gg = jnp.stack([gg_attn_m, gg_mlp_m]) + swap(jnp.stack([gg_attn_o, gg_mlp_o]))
-    gg = relative(gg, order_y)
-    for bit in order_y:
-        gg = half_of(gg, 1, False) + flip(half_of(gg, 1, True), bit)
-
-    gw_down, gw_up, gw_gate, gw_o, gw_qkv = (h.rest() for h in (down, upper, gater, outer, inner))
+    cut = one.shape[2]
+    down_1, upper_1, middle = down_1.rest(), upper_1.rest(), middle.rest()
+    gate_2, upper_2, outer = gate_2.rest(), upper_2.rest(), outer.rest()
+    gw_down = jnp.concatenate([down_1.T, middle[:, : w_gate.shape[1] - cut].T], axis=0)
+    gw_gate = jnp.concatenate([middle[:, w_gate.shape[1] - cut :], gate_2], axis=1)
+    gw_up = jnp.concatenate([upper_1, upper_2], axis=1)
+    gw_o, gw_qkv = outer[:, : o.shape[1]].T, outer[:, o.shape[1] :]
     return (
         mixed,
         d_tokens,

time: 520 us -> 573 us (1.10)
  other arithmetic: 54.6 us -> 71.1 us
  local copies, waits for them, and re-layouts: 38.1 us -> 54.2 us
  between operations: 2.55 us -> 16.5 us
    ppermute x18 -> x19, waiting for transfers between devices: 184 us -> 142 us  [flip(): return lax.ppermute(value, 'dp', [(i, i ^ 1 << bit) for i in range(count)])]
    unnamed x0 -> x2, waiting for transfers between devices: none -> 21.9 us
    unnamed x208 -> x284, local copies, waits for them, and re-layouts: 15.8 us -> 32.2 us
    ppermute x23, waiting for transfers between devices: 0.06 us -> 13 us  [swap(): return lax.ppermute(value, 'row', [(0, 1), (1, 0)])]
    concatenate x3 -> x11, other arithmetic: 2.85 us -> 14.5 us  [the longest x4 9.01 us: part(): return parts[0] if len(parts) == 1 else jnp.concatenate(parts, axis=1)]
    ppermute x8 -> x6, waiting for transfers between devices: 24.7 us -> 32.9 us  [cross(): return lax.ppermute(value, 'col', [(0, 1), (1, 0)])]
    squeeze x1 -> x4, local copies, waits for them, and re-layouts: 0.52 us -> 7.06 us  [the longest x2 4.1 us: shards(): all_2 = [both(two[i], two_t[i]) for i in range(3)]]
    pallas_call x4 -> x5, Pallas kernels: 64.1 us -> 68.3 us  [the longest x2 27.7 us: hidden_units(): pl.pallas_call(hidden_units_kernel, grid=(tiles,), in_specs=[full] * 4 +...]
  transfers between devices with their start and end apart: 49 -> 49, of which waited for: 13 -> 15; matrix products, arithmetic and copies ran while one was open for 31% -> 32% of each run, Pallas kernels for 11% -> 13%
where the time goes in v3:
time: 573 us; the launch traced here: 566 us
  waiting for transfers between devices  210 us (37%)
  Pallas kernels  87.6 us (15%)
  matrix products  86.4 us (15%)
  other arithmetic  71.1 us (12%)
  local copies, waits for them, and re-layouts  54.2 us (9%)
  starting transfers between devices  40.4 us (7%)
  between operations  16.5 us (3%)
    ppermute x19, waiting for transfers between devices, flip(): return lax.ppermute(value, 'dp', [(i, i ^ 1 << bit) for i in range(count)])  142 us
    dot_general x16, matrix products, dot_left(): lax.dot_general(left, right, (((0,), (0,)), ((), ())), preferred_element_...  38.5 us
    dot_general x16, matrix products, dot_plain(): return jnp.dot(left, right, preferred_element_type=F32)  35.3 us
    ppermute x6, waiting for transfers between devices, cross(): return lax.ppermute(value, 'col', [(0, 1), (1, 0)])  32.9 us
    unnamed x284, local copies, waits for them, and re-layouts  32.2 us
    pallas_call x2, Pallas kernels, hidden_units(): pl.pallas_call(hidden_units_kernel, grid=(tiles,), in_specs=[full] * 4 +...  27.7 us
    ppermute x19, starting transfers between devices, flip(): return lax.ppermute(value, 'dp', [(i, i ^ 1 << bit) for i in range(count)])  24.9 us
    unnamed x2, waiting for transfers between devices  21.9 us
  transfers between devices with their start and end apart: 49, of which 15 were waited for; matrix products, arithmetic and copies ran while one was open for 32% of the time, Pallas kernels for 13%

profile of v3, /device:TPU:0, one launch (start us, length us, event | category | flops | bytes accessed | tf_op | source)
XLA Modules:
  0.0 565.9 jit_solution(5054521888831692874)
XLA Ops:
  26.6 11.3 %collective-permute-done.3 = bf16[1024,1024]{1,0:T(8,128)(2,1)} collective-permute-done((bf16[1024,1024]{1,0:T(8,128)(2,1)}, bf16[1024,1024]{1,0:T(8,128)(2,1)}, u32[]{:S(2)}, u32[]{:S(2)}) %collective-permute-start.3) | collective-permute-done | bytes 2097184 | tf_op jit(solution)/shard_map/ppermute | solution.py:450
  41.0 5.2 collective-permute-done.4
  46.1 10.1 %attend.2 = (bf16[512,512]{1,0:T(8,128)(2,1)S(1)}, f32[4,2,512]{2,1,0:T(2,128)S(1)}, bf16[512,512]{1,0:T(8,128)(2,1)S(1)}) custom-call(s32[1]{0:T(128)} %bitcast.row_ref, f32[512,1024]{1,0:T(8,128)S(1)} %fusion.149.q_ref, f32[32,512]{1,0:T(8,128)S(1)} %get-tuple-element.390.cos_ref, f32[32,512]{1,0:T(8,128)S(1)} %get-tuple-element.389.sin_ref, ...), custom_call_target="tpu_custom_call" | custom-call | flops 1000 | bytes 1000 | tf_op jit(solution)/shard_map/attend/pallas_call | solution.py:143
  59.6 10.6 %attend.3 = (bf16[512,512]{1,0:T(8,128)(2,1)S(1)}, f32[4,2,512]{2,1,0:T(2,128)S(1)}, bf16[512,512]{1,0:T(8,128)(2,1)S(1)}) custom-call(s32[1]{0:T(128)} %bitcast.row_ref, f32[512,1024]{1,0:T(8,128)S(1)} %copy-done.2, f32[32,512]{1,0:T(8,128)S(1)} %get-tuple-element.390.cos_ref, f32[32,512]{1,0:T(8,128)S(1)} %get-tuple-element.389.sin_ref, ...), custom_call_target="tpu_custom_call" | custom-call | flops 1000 | bytes 1000 | tf_op jit(solution)/shard_map/attend/pallas_call | solution.py:143
  90.9 8.5 %collective-permute-done.17 = bf16[512,512]{1,0:T(8,128)(2,1)S(1)} collective-permute-done((bf16[512,512]{1,0:T(8,128)(2,1)S(1)}, bf16[512,512]{1,0:T(8,128)(2,1)S(1)}, u32[]{:S(2)}, u32[]{:S(2)}) %collective-permute-start.17) | collective-permute-done | bytes 524320 | tf_op jit(solution)/shard_map/ppermute | solution.py:453
  105.2 14.9 %hidden_units.2.a_ref = bf16[3,512,1536]{2,1,0:T(8,128)(2,1)} custom-call(bf16[512,1024]{1,0:T(8,128)(2,1)S(1)} %get-tuple-element.180.xm_ref, bf16[512,1024]{1,0:T(8,128)(2,1)S(1)} %get-tuple-element.393.xo_ref, bf16[512,1024]{1,0:T(8,128)(2,1)S(1)} %pad_maximum_fusion.42.cm_ref, bf16[512,1024]{1,0:T(8,128)(2,1)S(1)} %collective-permute-done.9.co_ref, ...), custom_call_target="tpu_custom_call" | custom-call | flops 1000 | bytes 1000 | tf_op jit(solution)/shard_map/hidden_units/pallas_call | solution.py:319
  120.6 12.9 %hidden_units.3.b_ref = bf16[3,512,1280]{2,1,0:T(8,128)(2,1)} custom-call(bf16[512,1024]{1,0:T(8,128)(2,1)S(1)} %get-tuple-element.180.xm_ref, bf16[512,1024]{1,0:T(8,128)(2,1)S(1)} %get-tuple-element.393.xo_ref, bf16[512,1024]{1,0:T(8,128)(2,1)S(1)} %pad_maximum_fusion.42.cm_ref, bf16[512,1024]{1,0:T(8,128)(2,1)S(1)} %collective-permute-done.9.co_ref, ...), custom_call_target="tpu_custom_call" | custom-call | flops 1000 | bytes 1000 | tf_op jit(solution)/shard_map/hidden_units/pallas_call | solution.py:319
  145.6 4.2 collective-permute-start.21
  165.5 4.6 fusion.14
  171.8 19.9 %input_grad.1 = bf16[512,2048]{1,0:T(8,128)(2,1)S(1)} custom-call(bf16[3,512,1536]{2,1,0:T(8,128)(2,1)} %hidden_units.2.a_ref, bf16[3,512,1280]{2,1,0:T(8,128)(2,1)S(1)} %copy-done, bf16[1024,2816]{1,0:T(8,128)(2,1)} %gm_ref.2, bf16[1024,2816]{1,0:T(8,128)(2,1)} %um_ref.2, bf16[1024,2816]{1,0:T(8,128)(2,1)} %collective-permute-done.6.go_ref, ...), custom_call_target="tpu_custom_call" | custom-call | flops 1000 | bytes 1000 | tf_op jit(solution)/shard_map/input_grad/pallas_call | solution.py:352
  221.8 4.6 fusion.36
  229.7 9.6 %collective-permute-done.23 = bf16[512,2048]{1,0:T(8,128)(2,1)} collective-permute-done((bf16[512,2048]{1,0:T(8,128)(2,1)S(1)}, bf16[512,2048]{1,0:T(8,128)(2,1)}, u32[]{:S(2)}, u32[]{:S(2)}) %collective-permute-start.23) | collective-permute-done | bytes 2097184 | tf_op jit(solution)/shard_map/ppermute | solution.py:453
  245.2 4.6 fusion.12
  260.9 19.3 %attend_back.1 = (bf16[512,1024]{1,0:T(8,128)(2,1)S(1)}, f32[2,1024,64]{2,1,0:T(8,128)S(1)}, f32[2,1024,64]{2,1,0:T(8,128)S(1)}) custom-call(s32[1]{0:T(128)} %bitcast.row_ref, bf16[1024,512]{1,0:T(8,128)(2,1)S(1)} %pad_maximum_fusion.44.qt_ref, bf16[512,1024]{1,0:T(8,128)(2,1)S(1)} %add_convert_fusion.4.do_ref, ...), custom_call_target="tpu_custom_call" | custom-call | flops 1000 | bytes 1000 | tf_op jit(solution)/shard_map/attend_back/pallas_call | solution.py:261
  298.5 17.3 %collective-permute-done.30 = bf16[512,2816]{1,0:T(8,128)(2,1)} collective-permute-done((bf16[512,2816]{1,0:T(8,128)(2,1)}, bf16[512,2816]{1,0:T(8,128)(2,1)}, u32[]{:S(2)}, u32[]{:S(2)}) %collective-permute-start.30) | collective-permute-done | bytes 2883616 | tf_op jit(solution)/shard_map/ppermute | solution.py:456
  325.4 7.4 %collective-permute-done.31 = bf16[256,1536]{1,0:T(8,128)(2,1)} collective-permute-done((bf16[256,1536]{1,0:T(8,128)(2,1)}, bf16[256,1536]{1,0:T(8,128)(2,1)}, u32[]{:S(2)}, u32[]{:S(2)}) %collective-permute-start.31) | collective-permute-done | bytes 786464 | tf_op jit(solution)/shard_map/ppermute | solution.py:456
  352.3 17.9 %collective-permute-done.32 = bf16[128,1536]{1,0:T(8,128)(2,1)S(1)} collective-permute-done((bf16[128,1536]{1,0:T(8,128)(2,1)S(1)}, bf16[128,1536]{1,0:T(8,128)(2,1)S(1)}, u32[]{:S(2)}, u32[]{:S(2)}) %collective-permute-start.32) | collective-permute-done | bytes 393248 | tf_op jit(solution)/shard_map/ppermute | solution.py:456
  378.2 4.8 fusion.27
  388.4 45.8 %collective-permute-done.46 = bf16[256,1280]{1,0:T(8,128)(2,1)} collective-permute-done((bf16[256,1280]{1,0:T(8,128)(2,1)}, bf16[256,1280]{1,0:T(8,128)(2,1)}, u32[]{:S(2)}, u32[]{:S(2)}) %collective-permute-start.46) | collective-permute-done | bytes 655392 | tf_op jit(solution)/shard_map/ppermute | solution.py:456
  440.2 21.9 %reduce-scatter.4.cloned.1.call-done = f32[128,2]{1,0:T(8,128)} async-done(((f32[1024,2]{1,0:T(8,128)}), f32[128,2]{1,0:T(8,128)}) %reduce-scatter.4.cloned.1.call-update) | async-done | bytes 1040
  474.1 12.3 %collective-permute-done.38 = bf16[256,1280]{1,0:T(8,128)(2,1)S(1)} collective-permute-done((bf16[256,1280]{1,0:T(8,128)(2,1)S(1)}, bf16[256,1280]{1,0:T(8,128)(2,1)S(1)}, u32[]{:S(2)}, u32[]{:S(2)}) %collective-permute-start.38) | collective-permute-done | bytes 655392 | tf_op jit(solution)/shard_map/ppermute | solution.py:456
  500.0 9.6 %collective-permute-done.40 = bf16[512,2048]{1,0:T(8,128)(2,1)} collective-permute-done((bf16[512,2048]{1,0:T(8,128)(2,1)}, bf16[512,2048]{1,0:T(8,128)(2,1)}, u32[]{:S(2)}, u32[]{:S(2)}) %collective-permute-start.40) | collective-permute-done | bytes 2097184 | tf_op jit(solution)/shard_map/ppermute | solution.py:453
  514.0 16.1 %collective-permute-done.43 = bf16[256,2304]{1,0:T(8,128)(2,1)S(1)} collective-permute-done((bf16[256,2304]{1,0:T(8,128)(2,1)S(1)}, bf16[256,2304]{1,0:T(8,128)(2,1)S(1)}, u32[]{:S(2)}, u32[]{:S(2)}) %collective-permute-start.43) | collective-permute-done | bytes 1179680 | tf_op jit(solution)/shard_map/ppermute | solution.py:456
  533.3 22.9 %collective-permute-done.44 = bf16[128,2304]{1,0:T(8,128)(2,1)S(1)} collective-permute-done((bf16[128,2304]{1,0:T(8,128)(2,1)S(1)}, bf16[128,2304]{1,0:T(8,128)(2,1)S(1)}, u32[]{:S(2)}, u32[]{:S(2)}) %collective-permute-start.44) | collective-permute-done | bytes 589856 | tf_op jit(solution)/shard_map/ppermute | solution.py:456
  (543 shorter events, 233.2 us)
Async XLA Ops:
  7.2 454.9 %reduce-scatter.4.cloned.1.call-start = ((), (), s32[]{:S(2)}) async-start(), calls=%async_computation.1 | async-start | bytes 589824
  16.9 40.1 %collective-permute-start.6 = (bf16[1024,2816]{1,0:T(8,128)(2,1)}, bf16[1024,2816]{1,0:T(8,128)(2,1)}, u32[]{:S(2)}, u32[]{:S(2)}) collective-permute-start(bf16[1024,2816]{1,0:T(8,128)(2,1)} %gm_ref.2), channel_id=1, source_target_pairs={{0,2},{2,0},{1,3},{3,1},{4,6},{6,4},{5,7},{7,5},{8,10},{10,8},{9,1... | collective-permute-start | bytes 17301512 | tf_op jit(solution)/shard_map/ppermute | solution.py:450
  17.0 40.0 %collective-permute-start.7 = (bf16[1024,2816]{1,0:T(8,128)(2,1)}, bf16[1024,2816]{1,0:T(8,128)(2,1)}, u32[]{:S(2)}, u32[]{:S(2)}) collective-permute-start(bf16[1024,2816]{1,0:T(8,128)(2,1)} %um_ref.2), channel_id=1, source_target_pairs={{0,2},{2,0},{1,3},{3,1},{4,6},{6,4},{5,7},{7,5},{8,10},{10,8},{9,1... | collective-permute-start | bytes 17301512 | tf_op jit(solution)/shard_map/ppermute | solution.py:450
  17.6 39.5 %collective-permute-start.8 = (bf16[1024,1024]{1,0:T(8,128)(2,1)}, bf16[1024,1024]{1,0:T(8,128)(2,1)}, u32[]{:S(2)}, u32[]{:S(2)}) collective-permute-start(bf16[1024,1024]{1,0:T(8,128)(2,1)} %param.19), channel_id=1, source_target_pairs={{0,2},{2,0},{1,3},{3,1},{4,6},{6,4},{5,7},{7,5},{8,10},{10,8},{9,1... | collective-permute-start | bytes 6291464 | tf_op jit(solution)/shard_map/ppermute | solution.py:450
  139.9 32.0 %collective-permute-start.20 = (bf16[3,512,1280]{2,1,0:T(8,128)(2,1)S(1)}, bf16[3,512,1280]{2,1,0:T(8,128)(2,1)}, u32[]{:S(2)}, u32[]{:S(2)}) collective-permute-start(bf16[3,512,1280]{2,1,0:T(8,128)(2,1)S(1)} %copy-done), channel_id=1, source_target_pairs={{0,2},{2,0},{1,3},{3,1},{4,6},{6,4},{5,7},{7,5},{8,10},{10,8},{9,1... | collective-permute-start | bytes 11796488 | tf_op jit(solution)/shard_map/ppermute | solution.py:450
  145.6 65.4 %collective-permute-start.21 = (bf16[512,1536]{1,0:T(8,128)(2,1)}, bf16[512,1536]{1,0:T(8,128)(2,1)}, u32[]{:S(2)}, u32[]{:S(2)}) collective-permute-start(bf16[512,1536]{1,0:T(8,128)(2,1)} %convolution_convert_fusion.6), channel_id=1, source_target_pairs={{0,4},{4,0},{8,12},{12,8},{16,20},{20,16},{24,28},{28,24},{1,5},{5... | collective-permute-start | bytes 4718600 | tf_op jit(solution)/shard_map/ppermute | solution.py:456
  156.8 54.2 %collective-permute-start.22 = (bf16[512,1536]{1,0:T(8,128)(2,1)}, bf16[512,1536]{1,0:T(8,128)(2,1)}, u32[]{:S(2)}, u32[]{:S(2)}) collective-permute-start(bf16[512,1536]{1,0:T(8,128)(2,1)} %convolution_convert_fusion.5), channel_id=1, source_target_pairs={{0,8},{4,12},{8,0},{12,4},{16,24},{20,28},{24,16},{28,20},{1,9},{5... | collective-permute-start | bytes 4718600 | tf_op jit(solution)/shard_map/ppermute | solution.py:456
  191.7 47.6 %collective-permute-start.23 = (bf16[512,2048]{1,0:T(8,128)(2,1)S(1)}, bf16[512,2048]{1,0:T(8,128)(2,1)}, u32[]{:S(2)}, u32[]{:S(2)}) collective-permute-start(bf16[512,2048]{1,0:T(8,128)(2,1)S(1)} %input_grad.1), channel_id=1, source_target_pairs={{0,1},{1,0},{2,3},{3,2},{4,5},{5,4},{6,7},{7,6},{8,9},{9,8},{10,11... | collective-permute-start | bytes 6291464 | tf_op jit(solution)/shard_map/ppermute | solution.py:453
  204.0 54.2 %collective-permute-start.25 = (bf16[512,1280]{1,0:T(8,128)(2,1)}, bf16[512,1280]{1,0:T(8,128)(2,1)}, u32[]{:S(2)}, u32[]{:S(2)}) collective-permute-start(bf16[512,1280]{1,0:T(8,128)(2,1)} %convolution_convert_fusion.2), channel_id=1, source_target_pairs={{0,8},{4,12},{8,0},{12,4},{16,24},{20,28},{24,16},{28,20},{1,9},{5... | collective-permute-start | bytes 3932168 | tf_op jit(solution)/shard_map/ppermute | solution.py:456
  249.8 31.1 %collective-permute-start.27 = (bf16[256,1536]{1,0:T(8,128)(2,1)S(1)}, bf16[256,1536]{1,0:T(8,128)(2,1)S(1)}, u32[]{:S(2)}, u32[]{:S(2)}) collective-permute-start(bf16[256,1536]{1,0:T(8,128)(2,1)S(1)} %slice.754), channel_id=1, source_target_pairs={{0,8},{4,12},{8,0},{12,4},{16,24},{20,28},{24,16},{28,20},{1,9},{5... | collective-permute-start | bytes 2359304 | tf_op jit(solution)/shard_map/ppermute | solution.py:456
  250.3 65.6 %collective-permute-start.30 = (bf16[512,2816]{1,0:T(8,128)(2,1)}, bf16[512,2816]{1,0:T(8,128)(2,1)}, u32[]{:S(2)}, u32[]{:S(2)}) collective-permute-start(bf16[512,2816]{1,0:T(8,128)(2,1)} %pad_maximum_fusion.6), channel_id=1, source_target_pairs={{0,4},{4,0},{8,12},{12,8},{16,20},{20,16},{24,28},{28,24},{1,5},{5... | collective-permute-start | bytes 8650760 | tf_op jit(solution)/shard_map/ppermute | solution.py:456
  250.5 82.2 %collective-permute-start.31 = (bf16[256,1536]{1,0:T(8,128)(2,1)}, bf16[256,1536]{1,0:T(8,128)(2,1)}, u32[]{:S(2)}, u32[]{:S(2)}) collective-permute-start(bf16[256,1536]{1,0:T(8,128)(2,1)} %slice.753), channel_id=1, source_target_pairs={{0,4},{4,0},{8,12},{12,8},{16,20},{20,16},{24,28},{28,24},{1,5},{5... | collective-permute-start | bytes 2359304 | tf_op jit(solution)/shard_map/ppermute | solution.py:456
  282.0 187.5 %collective-permute-start.37 = (bf16[512,1280]{1,0:T(8,128)(2,1)}, bf16[512,1280]{1,0:T(8,128)(2,1)}, u32[]{:S(2)}, u32[]{:S(2)}) collective-permute-start(bf16[512,1280]{1,0:T(8,128)(2,1)} %convolution_convert_fusion.1), channel_id=1, source_target_pairs={{0,4},{4,0},{8,12},{12,8},{16,20},{20,16},{24,28},{28,24},{1,5},{5... | collective-permute-start | bytes 3932168 | tf_op jit(solution)/shard_map/ppermute | solution.py:456
  297.0 77.5 %collective-permute-start.29 = (bf16[512,2048]{1,0:T(8,128)(2,1)S(1)}, bf16[512,2048]{1,0:T(8,128)(2,1)S(1)}, u32[]{:S(2)}, u32[]{:S(2)}) collective-permute-start(bf16[512,2048]{1,0:T(8,128)(2,1)S(1)} %pad_maximum_fusion.12), channel_id=1, source_target_pairs={{0,1},{1,0},{2,3},{3,2},{4,5},{5,4},{6,7},{7,6},{8,9},{9,8},{10,11... | collective-permute-start | bytes 6291464 | tf_op jit(solution)/shard_map/ppermute | solution.py:453
  318.6 51.9 %collective-permute-start.33 = (bf16[256,2816]{1,0:T(8,128)(2,1)S(1)}, bf16[256,2816]{1,0:T(8,128)(2,1)S(1)}, u32[]{:S(2)}, u32[]{:S(2)}) collective-permute-start(bf16[256,2816]{1,0:T(8,128)(2,1)S(1)} %slice.751), channel_id=1, source_target_pairs={{0,8},{4,12},{8,0},{12,4},{16,24},{20,28},{24,16},{28,20},{1,9},{5... | collective-permute-start | bytes 4325384 | tf_op jit(solution)/shard_map/ppermute | solution.py:456
  334.2 36.3 %collective-permute-start.34 = (bf16[128,1536]{1,0:T(8,128)(2,1)S(1)}, bf16[128,1536]{1,0:T(8,128)(2,1)S(1)}, u32[]{:S(2)}, u32[]{:S(2)}) collective-permute-start(bf16[128,1536]{1,0:T(8,128)(2,1)S(1)} %slice.759), channel_id=1, source_target_pairs={{0,16},{4,20},{8,24},{12,28},{16,0},{20,4},{24,8},{28,12},{1,17},{... | collective-permute-start | bytes 1179656 | tf_op jit(solution)/shard_map/ppermute | solution.py:456
  336.9 33.3 %collective-permute-start.32 = (bf16[128,1536]{1,0:T(8,128)(2,1)S(1)}, bf16[128,1536]{1,0:T(8,128)(2,1)S(1)}, u32[]{:S(2)}, u32[]{:S(2)}) collective-permute-start(bf16[128,1536]{1,0:T(8,128)(2,1)S(1)} %copy-done.85), channel_id=1, source_target_pairs={{0,16},{4,20},{8,24},{12,28},{16,0},{20,4},{24,8},{28,12},{1,17},{... | collective-permute-start | bytes 1179656 | tf_op jit(solution)/shard_map/ppermute | solution.py:456
  370.2 117.7 %collective-permute-start.35 = (bf16[512,2304]{1,0:T(8,128)(2,1)}, bf16[512,2304]{1,0:T(8,128)(2,1)}, u32[]{:S(2)}, u32[]{:S(2)}) collective-permute-start(bf16[512,2304]{1,0:T(8,128)(2,1)} %pad_maximum_fusion.11), channel_id=1, source_target_pairs={{0,4},{4,0},{8,12},{12,8},{16,20},{20,16},{24,28},{28,24},{1,5},{5... | collective-permute-start | bytes 7077896 | tf_op jit(solution)/shard_map/ppermute | solution.py:456
  372.7 61.6 %collective-permute-start.46 = (bf16[256,1280]{1,0:T(8,128)(2,1)}, bf16[256,1280]{1,0:T(8,128)(2,1)}, u32[]{:S(2)}, u32[]{:S(2)}) collective-permute-start(bf16[256,1280]{1,0:T(8,128)(2,1)} %slice.757), channel_id=1, source_target_pairs={{0,4},{4,0},{8,12},{12,8},{16,20},{20,16},{24,28},{28,24},{1,5},{5... | collective-permute-start | bytes 1966088 | tf_op jit(solution)/shard_map/ppermute | solution.py:456
  383.0 81.3 %collective-permute-start.36 = (f32[512,1024]{1,0:T(8,128)}, f32[512,1024]{1,0:T(8,128)}, u32[]{:S(2)}, u32[]{:S(2)}) collective-permute-start(f32[512,1024]{1,0:T(8,128)} %get-tuple-element.325), channel_id=1, source_target_pairs={{0,2},{2,0},{1,3},{3,1},{4,6},{6,4},{5,7},{7,5},{8,10},{10,8},{9,1... | collective-permute-start | bytes 6291464 | tf_op jit(solution)/shard_map/ppermute | solution.py:450
  387.2 86.9 %collective-permute-start.39 = (bf16[128,2816]{1,0:T(8,128)(2,1)}, bf16[128,2816]{1,0:T(8,128)(2,1)}, u32[]{:S(2)}, u32[]{:S(2)}) collective-permute-start(bf16[128,2816]{1,0:T(8,128)(2,1)} %slice.755), channel_id=1, source_target_pairs={{0,16},{4,20},{8,24},{12,28},{16,0},{20,4},{24,8},{28,12},{1,17},{... | collective-permute-start | bytes 2162696 | tf_op jit(solution)/shard_map/ppermute | solution.py:456
  436.6 36.0 %collective-permute-start.47 = (bf16[128,1280]{1,0:T(8,128)(2,1)S(1)}, bf16[128,1280]{1,0:T(8,128)(2,1)S(1)}, u32[]{:S(2)}, u32[]{:S(2)}) collective-permute-start(bf16[128,1280]{1,0:T(8,128)(2,1)S(1)} %slice.761), channel_id=1, source_target_pairs={{0,16},{4,20},{8,24},{12,28},{16,0},{20,4},{24,8},{28,12},{1,17},{... | collective-permute-start | bytes 983048 | tf_op jit(solution)/shard_map/ppermute | solution.py:456
  464.3 45.4 %collective-permute-start.40 = (bf16[512,2048]{1,0:T(8,128)(2,1)}, bf16[512,2048]{1,0:T(8,128)(2,1)}, u32[]{:S(2)}, u32[]{:S(2)}) collective-permute-start(bf16[512,2048]{1,0:T(8,128)(2,1)} %pad_maximum_fusion.14), channel_id=1, source_target_pairs={{0,1},{1,0},{2,3},{3,2},{4,5},{5,4},{6,7},{7,6},{8,9},{9,8},{10,11... | collective-permute-start | bytes 6291464 | tf_op jit(solution)/shard_map/ppermute | solution.py:453
  498.6 31.5 %collective-permute-start.43 = (bf16[256,2304]{1,0:T(8,128)(2,1)S(1)}, bf16[256,2304]{1,0:T(8,128)(2,1)S(1)}, u32[]{:S(2)}, u32[]{:S(2)}) collective-permute-start(bf16[256,2304]{1,0:T(8,128)(2,1)S(1)} %slice.752), channel_id=1, source_target_pairs={{0,8},{4,12},{8,0},{12,4},{16,24},{20,28},{24,16},{28,20},{1,9},{5... | collective-permute-start | bytes 3538952 | tf_op jit(solution)/shard_map/ppermute | solution.py:456
  (157 other events, 1379.3 us)
Sparse Core Ops, SparseCore 0:
  388.5 73.5 reduce-scatter.3

commit v4 on v3

--- a/solution.py
+++ b/solution.py
@@ -361,54 +361,101 @@
     )(a, b, gm, um, go, uo)
 
 
-class Halving:
-    def __init__(self, pairs, order, flip):
-        self.pairs, self.order, self.flip, self.at, self.open = pairs, list(order), flip, 0, False
-
-    def part(self, upper):
-        parts = [dot_left(half_of(a, upper, 1) if self.order else a, b) for a, b in self.pairs]
-        if upper:
-            parts = [p.astype(BF16) for p in parts]
-        return parts[0] if len(parts) == 1 else jnp.concatenate(parts, axis=1)
+def product_kernel(counts, *refs):
+    pieces = len(counts)
+    lefts, owns, others = (refs[i * pieces : (i + 1) * pieces] for i in range(3))
+    send_ref, keep_ref = refs[3 * pieces :]
+    step, first = pl.program_id(0), 0
+    for left, own, other, count in zip(lefts, owns, others, counts):
+
+        @pl.when((step >= first) & (step < first + count))
+        def _(left=left, own=own, other=other):
+            tokens, half = own.shape[1], left.shape[0] // 2
+            total = dot_plain(left[:, :tokens], own[0]) + dot_plain(left[:, tokens:], other[0])
+            send_ref[...] = total[:half].astype(BF16)
+            keep_ref[...] = total[half:].astype(BF16)
+
+        first += count
+
+
+def product(pieces):
+    tile = 256
+    counts = [own.shape[2] // tile for _, own, _, _ in pieces]
+    rows, tokens = pieces[0][0].shape
+    owns, others = [], []
+    first = 0
+    for (_, own, other, index), count in zip(pieces, counts):
+        place = lambda i, first=first, count=count: jnp.clip(i - first, 0, count - 1)
+        owns.append(pl.BlockSpec((1, own.shape[1], tile), lambda i, index=index, place=place: (index, 0, place(i))))
+        others.append(pl.BlockSpec((1, other.shape[1], tile), lambda i, index=index, place=place: (index, 0, place(i))))
+        first += count
+    return pl.pallas_call(
+        functools.partial(product_kernel, counts),
+        grid=(first,),
+        in_specs=[pl.BlockSpec((rows, tokens), lambda i: (0, 0))] * len(pieces) + owns + others,
+        out_specs=[pl.BlockSpec((rows // 2, tile), lambda i: (0, i))] * 2,
+        out_shape=[jax.ShapeDtypeStruct((rows // 2, first * tile), BF16)] * 2,
+        compiler_params=pltpu.CompilerParams(vmem_limit_bytes=40 * 1024 * 1024),
+        cost_estimate=pl.CostEstimate(flops=1000, bytes_accessed=1000, transcendentals=0),
+        name="product",
+    )(*[p[0] for p in pieces], *[p[1] for p in pieces], *[p[2] for p in pieces])
+
+
+def sided_kernel(side_ref, own_ref, other_ref, out_ref):
+    tokens = own_ref.shape[0]
+    out_ref[:, :tokens] = jnp.transpose(own_ref[...])
+    out_ref[:, tokens:] = jnp.transpose(other_ref[...])
+
+
+def sided(own, other, side, count):
+    tokens, wide = own.shape
+    width = wide // count
+    if width % 128:
+        blocks = jnp.concatenate([own, other], axis=0).T.reshape(count // 2, 2, width, 2 * tokens)
+        near = jnp.where(side == 0, blocks[:, 0], blocks[:, 1])
+        far = jnp.where(side == 0, blocks[:, 1], blocks[:, 0])
+        return jnp.concatenate([far, near], axis=0).reshape(wide, 2 * tokens)
+    column = pl.BlockSpec((tokens, width), lambda i, side: (0, i))
+    return pl.pallas_call(
+        sided_kernel,
+        grid_spec=pltpu.PrefetchScalarGridSpec(
+            num_scalar_prefetch=1,
+            grid=(count,),
+            in_specs=[column, column],
+            out_specs=pl.BlockSpec(
+                (width, 2 * tokens), lambda i, side: (i // 2 + jnp.where(i % 2 == side[0], count // 2, 0), 0)
+            ),
+        ),
+        out_shape=jax.ShapeDtypeStruct((wide, 2 * tokens), BF16),
+        compiler_params=pltpu.CompilerParams(vmem_limit_bytes=40 * 1024 * 1024),
+        cost_estimate=pl.CostEstimate(flops=1000, bytes_accessed=1000, transcendentals=0),
+        name="sided",
+    )(side.astype(jnp.int32).reshape(1), own, other)
+
+
+class Summed:
+    def __init__(self, pieces, flip, count):
+        self.pieces, self.flip, self.count = pieces, flip, count
 
     def begin(self, *deps):
-        if deps:
-            a, b = self.pairs[0]
-            a, *_ = tie(a, *deps)
-            self.pairs[0] = (a, b)
-        self.send = self.part(True)
-        return self.send
-
-    def stay(self, *deps):
-        if deps:
-            a, b = self.pairs[0]
-            a, *_ = tie(a, *deps)
-            self.pairs[0] = (a, b)
-        self.keep = self.part(False)
+        left, *others = self.pieces[0]
+        left, *_ = tie(left, *deps)
+        self.send, self.keep = product([(left, *others), *self.pieces[1:]])
         return self.keep
 
-    def go(self):
-        self.came, self.open = self.send, self.at < len(self.order)
-        if self.open:
-            self.came = self.flip(self.send, self.order[self.at])
-
-    def add(self):
-        if self.open:
-            self.open = False
-            self.total = self.keep + self.came.astype(F32)
-            self.at += 1
-            if self.at < len(self.order):
-                self.send = half_of(self.total, True).astype(BF16)
-                self.keep = half_of(self.total, False)
-        elif not self.order:
-            self.total = self.keep
-
-    def rest(self):
-        self.add()
-        while self.at < len(self.order):
-            self.go()
-            self.add()
-        return self.total
+    def go(self, after=None):
+        if after is not None:
+            self.send, after.came = tie(self.send, after.came)
+        self.came = self.flip(self.send)
+
+    def scatter(self, value):
+        groups = [list(range(side, self.count, 2)) for side in range(2)]
+        return lax.psum_scatter(value, "dp", scatter_dimension=0, axis_index_groups=groups, tiled=True)
+
+    def finish(self):
+        total = (self.keep.astype(F32) + self.came.astype(F32)).astype(BF16)
+        self.total = self.scatter(total)
+        return total
 
 
 def half_of(value, upper, axis=0):
@@ -443,8 +490,8 @@
     w_down,
 ):
     row = lax.axis_index("row")
-    dp = lax.axis_index("dp")
-    bits = count.bit_length() - 1
+    side = lax.axis_index("dp") & 1
+    low = side == 0
 
     def swap(value):
         return lax.ppermute(value, "row", [(0, 1), (1, 0)])
@@ -452,23 +499,9 @@
     def cross(value):
         return lax.ppermute(value, "col", [(0, 1), (1, 0)])
 
-    def flip(value, bit):
-        return lax.ppermute(value, "dp", [(i, i ^ (1 << bit)) for i in range(count)])
-
-    def order_of(first):
-        return ([first] + [b for b in range(bits) if b != first]) if bits else []
-
-    def relative(value, order):
-        width = value.shape[1] // count
-        blocks = []
-        for place in range(count):
-            differs = 0
-            for at, bit in enumerate(order):
-                differs |= ((place >> (len(order) - 1 - at)) & 1) << bit
-            blocks.append(lax.dynamic_slice_in_dim(value, (dp ^ differs) * width, width, axis=1))
-        return jnp.concatenate(blocks, axis=1)
-
-    low = (dp & 1) == 0
+    def flip(value):
+        return lax.ppermute(value, "dp", [(i, i ^ 1) for i in range(count)])
+
     half = w_o.shape[0] // 2
     far_a = cross(jnp.where(low, w_o[:half], w_o[half:]))
     x_m = own_rows(tokens, row)
@@ -511,7 +544,7 @@
     c_m = own_rows(cotangent, row)
     c_t = other_rows(cotangent, row)
     q, far_a, other_kv, c_m, c_t = tie(q, far_a, other_kv, c_m, c_t)
-    far_b = flip(far_a, 0)
+    far_b = flip(far_a)
     row_arg = row.astype(jnp.int32).reshape(1)
     start_arg = start_own.reshape(1, OWN)
     o_1, lse_1, qt_1 = attend(0, row_arg, q, cosine_t, sine_t, start_arg, own_kv, other_kv)
@@ -526,9 +559,8 @@
 
     near_m = dot_plain(o_1, w_o[:half]) + dot_plain(o_2, w_o[half:])
     near_o = dot_plain(o_1, w_o_o[:half]) + dot_plain(o_2, w_o_o[half:])
-    order_y, order_z = order_of(0), order_of(min(1, max(bits - 1, 0)))
     both = lambda own, other: jnp.concatenate([own, other], axis=0)
-    c_y = relative(both(c_m, c_t), order_y)
+    c_y = sided(c_m, c_t, side, count)
     o = jnp.concatenate([o_1, o_2], axis=1)
     o_t = swap(o)
     qt = jnp.concatenate([qt_1, qt_2], axis=0)
@@ -562,41 +594,35 @@
     two, one_t, xn2_t = tie(two, one_t, xn2_t)
     two_t = swap(two)
 
-    all_1 = [both(one[i], one_t[i]) for i in range(3)]
-    down_1 = Halving([(c_y, all_1[0])], order_y, flip)
-    down_1.begin(two)
-    down_1.go()
-    down_1.send, xn2_m2 = tie(down_1.send, xn2_m2)
-    xn2_all = both(xn2_m2, xn2_t)
-    xn2_y, xn2_z = relative(xn2_all, order_y), relative(xn2_all, order_z)
-    upper_1 = Halving([(xn2_z, all_1[2])], order_z, flip)
-    upper_1.begin()
-    upper_1.go()
-    upper_1.send, two_late, two_t = tie(upper_1.send, two, two_t)
+    send_1 = Summed([(c_y, one, one_t, 0)], flip, count)
+    send_1.begin(two)
+    send_1.go()
+    send_1.keep, xn2_m2 = tie(send_1.keep, xn2_m2)
+    xn2_y = sided(xn2_m2, xn2_t, side, count)
+    first_z = Summed([(xn2_y, one, one_t, 2)], flip, count)
+    first_z.begin()
+    first_z.send = first_z.scatter(first_z.send)
+    first_z.keep, two_late = tie(first_z.keep, two)
     part = input_grad(one, two_late, w_gate, w_up, wg_o, wu_o)
     came = cross(part)
-    part, two_t = tie(part, two_t)
-    all_2 = [both(two[i], two_t[i]) for i in range(3)]
-    middle = Halving([(c_y, all_2[0]), (xn2_y, all_1[1])], order_y, flip)
-    middle.begin(part)
-    middle.go()
-    upper_2 = Halving([(xn2_z, all_2[2])], order_z, flip)
-    upper_2.begin(middle.send)
-    upper_2.go()
-    gate_2 = Halving([(xn2_y, all_2[1])], order_y, flip)
-    gate_2.begin(upper_2.send)
-    down_1.stay(gate_2.send)
-    upper_1.stay(down_1.keep)
-    part = serve(part, (down_1, upper_1), (upper_1.keep, down_1.keep))
-    down_1.add()
-    down_1.go()
-    upper_1.add()
-    upper_1.go()
-    middle.stay(part, down_1.send, upper_1.send)
-    upper_2.stay(middle.keep)
-    gate_2.stay(upper_2.keep)
-
-    came, gate_2.keep, middle.keep, upper_2.keep = tie(came, gate_2.keep, middle.keep, upper_2.keep)
+    two_t, part = tie(two_t, part)
+    send_2 = Summed([(c_y, two, two_t, 0)], flip, count)
+    send_2.begin(part)
+    part = serve(part, (send_1,), (send_2.keep,))
+    send_2.go(send_1)
+    part, first_z.keep, total = tie(part, first_z.keep, send_1.finish())
+    first_z.keep = first_z.scatter(first_z.keep)
+    send_3 = Summed([(xn2_y, one, one_t, 1)], flip, count)
+    send_3.begin(part)
+    send_4 = Summed([(xn2_y, two, two_t, 1)], flip, count)
+    send_4.begin(send_3.keep)
+    send_6 = Summed([(xn2_y, two, two_t, 2)], flip, count)
+    send_6.begin(send_4.keep)
+    came, first_z.send, part = tie(came, first_z.send, part, send_6.keep)[:3]
+    came = serve(came, (send_2,))
+    send_3.go(send_2)
+    came, _ = tie(came, send_2.finish())
+
     width = tokens.shape[1]
     d_xn2 = part.astype(F32) + came.astype(F32)
     d_xn2_m, d_xn2_o = d_xn2[:, :width], d_xn2[:, width:]
@@ -611,19 +637,15 @@
     dh_m, dh_o = d_hid_m.astype(BF16), d_hid_o.astype(BF16)
     dh_t = swap(dh_o)
     d_o = (dot_right(dh_m, w_o) + dot_right(dh_o, w_o_o)).astype(BF16)
-    d_o, dh_t, gate_2.send = tie(d_o, dh_t, gate_2.send)
-    d_o = serve(d_o, (upper_2,))
-    gate_2.go()
-    upper_2.add()
-    d_o, upper_2.send, upper_2.keep, gate_2.send = tie(d_o, upper_2.send, upper_2.keep, gate_2.send)
+    d_o, dh_t = tie(d_o, dh_t)
 
     d_q, d_k, d_v = attend_back(row_arg, qt, d_o, o, lse, cosine_t, sine_t, start_arg, own_kv, other_kv)
+    d_q = serve(d_q, (send_3,))
+    send_4.go(send_3)
+    d_q, d_k, _ = tie(d_q, d_k, send_3.finish())
     d_kv = jnp.concatenate([d_k[0], d_k[1], d_v[0], d_v[1]], axis=1)
     d_kv_t = swap(other_rows(d_kv, row))
     d_kv_own = own_rows(d_kv, row)
-    d_kv_own = serve(d_kv_own, (down_1,))
-    down_1.add()
-    d_kv_t, d_kv_own, down_1.send, down_1.keep = tie(d_kv_t, d_kv_own, down_1.send, down_1.keep)
     d_kv = d_kv_own + d_kv_t
     d_key = d_kv[:, :narrow].reshape(OWN, -1, HEAD_SIZE)
     first, second = d_key[..., :HALF], d_key[..., HALF:]
@@ -640,26 +662,17 @@
     )
     last, d_qkv_t = tie(last, d_qkv_t)
     last_came = cross(last)
-    last = serve(last, (middle,))
-    middle.add()
-    middle.go()
-    outer = Halving(
+    last, first_z.keep, send_1.total = tie(last, first_z.keep, send_1.total)
+    send_5 = Summed(
         [
-            (relative(both(dh_m, dh_t), order_y), both(o, o_t)),
-            (relative(both(xn_m, xn_t), order_y), both(d_qkv, d_qkv_t)),
-        ],
-        order_y,
+            (sided(dh_m, dh_t, side, count), o[None], o_t[None], 0),
+            (sided(xn_m, xn_t, side, count), d_qkv[None], d_qkv_t[None], 0),
+        ],
         flip,
+        count,
     )
-    outer.begin(last, middle.send, middle.keep)
-    outer.send = serve(outer.send, (upper_1,))
-    outer.go()
-    upper_1.add()
-    upper_1.go()
-    down_1.send, upper_1.send = tie(down_1.send, upper_1.send)
-    down_1.go()
-    outer.stay(down_1.send, outer.send)
-    one, outer.keep = tie(one, outer.keep)
+    send_5.begin(last)
+    one, send_5.keep = tie(one, send_5.keep)
     cut = one.shape[2]
     mix = jnp.concatenate(
         [
@@ -668,14 +681,11 @@
         ],
         axis=1,
     )
-    mix = serve(mix, (down_1, middle, upper_1))
-    down_1.add()
-    middle.add()
-    middle.go()
-    upper_2.send, middle.send = tie(upper_2.send, middle.send)
-    upper_2.go()
-
-    last_came, mix, middle.keep, middle.send = tie(last_came, mix, middle.keep, middle.send)
+    mix = serve(mix, (send_4,))
+    send_5.go(send_4)
+    mix, send_2.total, _ = tie(mix, send_2.total, send_4.finish())
+
+    last_came, mix, send_3.total = tie(last_came, mix, send_3.total)
     mix_came = cross(mix)
     d_xn = last.astype(F32) + last_came.astype(F32)
     d_xn_m, d_xn_o = d_xn[:, :width], d_xn[:, width:]
@@ -690,32 +700,28 @@
     d_tok_o = d_hid_o + inv_one * (e_o - unit_o * mean)
     d_tok_t = swap(d_tok_o)
     gg = jnp.stack([gg_attn_m, gg_mlp_m]) + swap(jnp.stack([gg_attn_o, gg_mlp_o]))
+    gg, send_4.total = tie(gg, send_4.total)
     gg = lax.psum_scatter(gg, "dp", scatter_dimension=1, tiled=True)
     d_tokens = merge_rows(d_tok_m, d_tok_t, row)
 
-    d_tokens = serve(d_tokens, (gate_2,))
-    gate_2.add()
-    gate_2.go()
-    d_tokens, gate_2.send, gate_2.keep = tie(d_tokens, gate_2.send, gate_2.keep)
-    gate_2.came = serve(gate_2.came, (middle,))
-    middle.add()
-    outer.came, middle.total = tie(outer.came, middle.total)
-    outer.add()
-    outer.go()
-    outer.send, mix_came = tie(outer.send, mix_came)
+    d_tokens = serve(d_tokens, (send_5,))
+    first_z.go(send_5)
+    send_6.go(send_5)
+    d_tokens, mix_came, _ = tie(d_tokens, mix_came, send_5.finish())
 
     mixed_all = mix.astype(F32) + mix_came.astype(F32)
     out_m = (hidden_m + mixed_all[:, :width]).astype(BF16)
     out_o = (hidden_o + mixed_all[:, width:]).astype(BF16)
     mixed = merge_rows(out_m, swap(out_o), row)
 
-    cut = one.shape[2]
-    down_1, upper_1, middle = down_1.rest(), upper_1.rest(), middle.rest()
-    gate_2, upper_2, outer = gate_2.rest(), upper_2.rest(), outer.rest()
-    gw_down = jnp.concatenate([down_1.T, middle[:, : w_gate.shape[1] - cut].T], axis=0)
-    gw_gate = jnp.concatenate([middle[:, w_gate.shape[1] - cut :], gate_2], axis=1)
-    gw_up = jnp.concatenate([upper_1, upper_2], axis=1)
-    gw_o, gw_qkv = outer[:, : o.shape[1]].T, outer[:, o.shape[1] :]
+    mixed, send_6.came = tie(mixed, send_6.came)
+    send_6.finish()
+    first_z.total = first_z.keep.astype(F32) + first_z.came.astype(F32)
+    got = [h.total.astype(F32) for h in (send_1, send_2, send_3, send_4, first_z, send_6, send_5)]
+    gw_down = jnp.concatenate([got[0].T, got[1].T], axis=0)
+    gw_gate = jnp.concatenate([got[2], got[3]], axis=1)
+    gw_up = jnp.concatenate([got[4], got[5]], axis=1)
+    gw_o, gw_qkv = got[6][:, : o.shape[1]].T, got[6][:, o.shape[1] :]
     return (
         mixed,
         d_tokens,

time: 573 us -> 608 us (1.061)
  Pallas kernels: 87.6 us -> 139 us
  waiting for transfers between devices: 210 us -> 249 us
  matrix products: 86.4 us -> 53.1 us
  starting transfers between devices: 40.4 us -> 24 us
    reduce_scatter x0 -> x8, waiting for transfers between devices: none -> 78.1 us  [scatter(): lax.psum_scatter(value, 'dp', scatter_dimension=0, axis_index_groups=grou...]
    ppermute x19 -> x8, waiting for transfers between devices: 142 us -> 85.2 us  [flip(): return lax.ppermute(value, 'dp', [(i, i ^ 1) for i in range(count)])]
    pallas_call x0 -> x11, Pallas kernels: none -> 53.3 us  [the longest x7 43.3 us: product(): pl.pallas_call(functools.partial(product_kernel, counts), grid=(first,),...]
    dot_general x16 -> x0, matrix products: 38.5 us -> none  [dot_left(): lax.dot_general(left, right, (((0,), (0,)), ((), ())), preferred_element_...]
    add x17 -> x1, other arithmetic: 19.4 us -> 0.09 us  [shards(): first_z.total = first_z.keep.astype(F32) + first_z.came.astype(F32)]
    convert_element_type x0 -> x8, other arithmetic: none -> 18.6 us  [the longest x6 16.4 us: finish(): total = (self.keep.astype(F32) + self.came.astype(F32)).astype(BF16)]
    ppermute x19 -> x8, starting transfers between devices: 24.9 us -> 8.19 us  [flip(): return lax.ppermute(value, 'dp', [(i, i ^ 1) for i in range(count)])]
    ppermute x6, waiting for transfers between devices: 32.9 us -> 44.7 us  [cross(): return lax.ppermute(value, 'col', [(0, 1), (1, 0)])]
  transfers between devices with their start and end apart: 49 -> 46, of which waited for: 15 -> 17; matrix products, arithmetic and copies ran while one was open for 32% -> 18% of each run, Pallas kernels for 13% -> 21%
where the time goes in v4:
time: 608 us; the launch traced here: 600 us
  waiting for transfers between devices  249 us (41%)
  Pallas kernels  139 us (23%)
  other arithmetic  69.7 us (11%)
  matrix products  53.1 us (9%)
  local copies, waits for them, and re-layouts  48.7 us (8%)
  starting transfers between devices  24 us (4%)
  between operations  15.9 us (3%)
    ppermute x8, waiting for transfers between devices, flip(): return lax.ppermute(value, 'dp', [(i, i ^ 1) for i in range(count)])  85.2 us
    reduce_scatter x8, waiting for transfers between devices, scatter(): lax.psum_scatter(value, 'dp', scatter_dimension=0, axis_index_groups=grou...  78.1 us
    ppermute x6, waiting for transfers between devices, cross(): return lax.ppermute(value, 'col', [(0, 1), (1, 0)])  44.7 us
    unnamed x255, local copies, waits for them, and re-layouts  43.4 us
    pallas_call x7, Pallas kernels, product(): pl.pallas_call(functools.partial(product_kernel, counts), grid=(first,),...  43.3 us
    dot_general x16, matrix products, dot_plain(): return jnp.dot(left, right, preferred_element_type=F32)  37.8 us
    pallas_call x2, Pallas kernels, hidden_units(): pl.pallas_call(hidden_units_kernel, grid=(tiles,), in_specs=[full] * 4 +...  27.6 us
    unnamed x10, waiting for transfers between devices  27.2 us
  transfers between devices with their start and end apart: 46, of which 17 were waited for; matrix products, arithmetic and copies ran while one was open for 18% of the time, Pallas kernels for 21%

profile of v4, /device:TPU:0, one launch (start us, length us, event | category | flops | bytes accessed | tf_op | source)
XLA Modules:
  0.0 600.1 jit_solution(17936086676056912884)
XLA Ops:
  26.1 11.7 %collective-permute-done.3 = bf16[1024,1024]{1,0:T(8,128)(2,1)} collective-permute-done((bf16[1024,1024]{1,0:T(8,128)(2,1)}, bf16[1024,1024]{1,0:T(8,128)(2,1)}, u32[]{:S(2)}, u32[]{:S(2)}) %collective-permute-start.3) | collective-permute-done | bytes 2097184 | tf_op jit(solution)/shard_map/ppermute | solution.py:497
  40.8 5.0 collective-permute-done.4
  45.9 10.0 %attend.2 = (bf16[512,512]{1,0:T(8,128)(2,1)S(1)}, f32[4,2,512]{2,1,0:T(2,128)S(1)}, bf16[512,512]{1,0:T(8,128)(2,1)S(1)}) custom-call(s32[1]{0:T(128)} %bitcast.row_ref, f32[512,1024]{1,0:T(8,128)S(1)} %fusion.76.q_ref, f32[32,512]{1,0:T(8,128)S(1)} %get-tuple-element.380.cos_ref, f32[32,512]{1,0:T(8,128)S(1)} %get-tuple-element.379.sin_ref, ...), custom_call_target="tpu_custom_call" | custom-call | flops 1000 | bytes 1000 | tf_op jit(solution)/shard_map/attend/pallas_call | solution.py:143
  58.4 10.0 %attend.3 = (bf16[512,512]{1,0:T(8,128)(2,1)S(1)}, f32[4,2,512]{2,1,0:T(2,128)S(1)}, bf16[512,512]{1,0:T(8,128)(2,1)S(1)}) custom-call(s32[1]{0:T(128)} %bitcast.row_ref, f32[512,1024]{1,0:T(8,128)S(1)} %fusion.76.q_ref, f32[32,512]{1,0:T(8,128)S(1)} %get-tuple-element.380.cos_ref, f32[32,512]{1,0:T(8,128)S(1)} %get-tuple-element.379.sin_ref, ...), custom_call_target="tpu_custom_call" | custom-call | flops 1000 | bytes 1000 | tf_op jit(solution)/shard_map/attend/pallas_call | solution.py:143
  88.9 8.2 %collective-permute-done.14 = bf16[512,512]{1,0:T(8,128)(2,1)S(1)} collective-permute-done((bf16[512,512]{1,0:T(8,128)(2,1)S(1)}, bf16[512,512]{1,0:T(8,128)(2,1)S(1)}, u32[]{:S(2)}, u32[]{:S(2)}) %collective-permute-start.14) | collective-permute-done | bytes 524320 | tf_op jit(solution)/shard_map/ppermute | solution.py:500
  98.7 9.1 %collective-permute-done.17 = bf16[512,512]{1,0:T(8,128)(2,1)S(1)} collective-permute-done((bf16[512,512]{1,0:T(8,128)(2,1)S(1)}, bf16[512,512]{1,0:T(8,128)(2,1)S(1)}, u32[]{:S(2)}, u32[]{:S(2)}) %collective-permute-start.17) | collective-permute-done | bytes 524320 | tf_op jit(solution)/shard_map/ppermute | solution.py:500
  115.8 14.7 %hidden_units.2.refs_1_.a_ref = bf16[3,512,1536]{2,1,0:T(8,128)(2,1)} custom-call(bf16[512,1024]{1,0:T(8,128)(2,1)S(1)} %get-tuple-element.194.xm_ref.own_ref, bf16[512,1024]{1,0:T(8,128)(2,1)S(1)} %get-tuple-element.383.xo_ref, bf16[512,1024]{1,0:T(8,128)(2,1)S(1)} %pad_maximum_fusion.8.own_ref.cm_ref, bf16[512,1024]{1,0:T(8,128)(2,1)S(1)} %collective-permute-done.9.co_ref, ...), custom_call_target="tpu_custom_call" | custom-call | flops 1000 | bytes 1000 | tf_op jit(solution)/shard_map/hidden_units/pallas_call | solution.py:319
  131.0 12.9 %hidden_units.3.b_ref.refs_1_ = bf16[3,512,1280]{2,1,0:T(8,128)(2,1)} custom-call(bf16[512,1024]{1,0:T(8,128)(2,1)S(1)} %get-tuple-element.194.xm_ref.own_ref, bf16[512,1024]{1,0:T(8,128)(2,1)S(1)} %get-tuple-element.383.xo_ref, bf16[512,1024]{1,0:T(8,128)(2,1)S(1)} %pad_maximum_fusion.8.own_ref.cm_ref, bf16[512,1024]{1,0:T(8,128)(2,1)S(1)} %collective-permute-done.9.co_ref, ...), custom_call_target="tpu_custom_call" | custom-call | flops 1000 | bytes 1000 | tf_op jit(solution)/shard_map/hidden_units/pallas_call | solution.py:319
  144.0 6.0 %product.7 = (bf16[512,1536]{1,0:T(8,128)(2,1)S(1)}, bf16[512,1536]{1,0:T(8,128)(2,1)S(1)}) custom-call(bf16[1024,1024]{1,0:T(8,128)(2,1)S(1)} %sided.4.refs_0_, bf16[3,512,1536]{2,1,0:T(8,128)(2,1)S(1)} %copy-done, bf16[3,512,1536]{2,1,0:T(8,128)(2,1)} %collective-permute-done.18.refs_2_), custom_call_target="tpu_custom_call" | custom-call | flops 1000 | bytes 1000 | tf_op jit(solution)/shard_map/product/pallas_call | solution.py:392
  154.0 6.1 %product.8 = (bf16[512,1536]{1,0:T(8,128)(2,1)S(1)}, bf16[512,1536]{1,0:T(8,128)(2,1)S(1)}) custom-call(bf16[1024,1024]{1,0:T(8,128)(2,1)S(1)} %sided.5.refs_0_, bf16[3,512,1536]{2,1,0:T(8,128)(2,1)S(1)} %copy-done, bf16[3,512,1536]{2,1,0:T(8,128)(2,1)} %collective-permute-done.18.refs_2_), custom_call_target="tpu_custom_call" | custom-call | flops 1000 | bytes 1000 | tf_op jit(solution)/shard_map/product/pallas_call | solution.py:392
  165.0 19.5 %input_grad.1 = bf16[512,2048]{1,0:T(8,128)(2,1)S(1)} custom-call(bf16[3,512,1536]{2,1,0:T(8,128)(2,1)} %hidden_units.2.refs_1_.a_ref, bf16[3,512,1280]{2,1,0:T(8,128)(2,1)S(1)} %copy-done.2, bf16[1024,2816]{1,0:T(8,128)(2,1)} %gm_ref.2, bf16[1024,2816]{1,0:T(8,128)(2,1)} %um_ref.2, bf16[1024,2816]{1,0:T(8,128)(2,1)} %collective-permute-done.6.go_ref, ...), custom_call_target="tpu_custom_call" | custom-call | flops 1000 | bytes 1000 | tf_op jit(solution)/shard_map/input_grad/pallas_call | solution.py:352
  185.8 5.3 product.9
  193.3 6.3 %collective-permute-done.22 = bf16[512,1536]{1,0:T(8,128)(2,1)} collective-permute-done((bf16[512,1536]{1,0:T(8,128)(2,1)}, bf16[512,1536]{1,0:T(8,128)(2,1)}, u32[]{:S(2)}, u32[]{:S(2)}) %collective-permute-start.22) | collective-permute-done | bytes 1572896 | tf_op jit(solution)/shard_map/ppermute | solution.py:503
  207.1 6.4 %product.10 = (bf16[512,1536]{1,0:T(8,128)(2,1)S(1)}, bf16[512,1536]{1,0:T(8,128)(2,1)S(1)}) custom-call(bf16[1024,1024]{1,0:T(8,128)(2,1)S(1)} %sided.5.refs_0_, bf16[3,512,1536]{2,1,0:T(8,128)(2,1)S(1)} %copy-done.1, bf16[3,512,1536]{2,1,0:T(8,128)(2,1)} %collective-permute-done.18.refs_2_), custom_call_target="tpu_custom_call" | custom-call | flops 1000 | bytes 1000 | tf_op jit(solution)/shard_map/product/pallas_call | solution.py:392
  214.7 6.2 %product.11 = (bf16[512,1280]{1,0:T(8,128)(2,1)}, bf16[512,1280]{1,0:T(8,128)(2,1)S(1)}) custom-call(bf16[1024,1024]{1,0:T(8,128)(2,1)S(1)} %sided.5.refs_0_, bf16[3,512,1280]{2,1,0:T(8,128)(2,1)S(1)} %copy-done.4, bf16[3,512,1280]{2,1,0:T(8,128)(2,1)} %collective-permute-done.21.refs_2_), custom_call_target="tpu_custom_call" | custom-call | flops 1000 | bytes 1000 | tf_op jit(solution)/shard_map/product/pallas_call | solution.py:392
  221.9 5.2 product.12
  229.3 20.8 %collective-permute-done.20 = bf16[512,2048]{1,0:T(8,128)(2,1)} collective-permute-done((bf16[512,2048]{1,0:T(8,128)(2,1)}, bf16[512,2048]{1,0:T(8,128)(2,1)}, u32[]{:S(2)}, u32[]{:S(2)}) %collective-permute-start.20) | collective-permute-done | bytes 2097184 | tf_op jit(solution)/shard_map/ppermute | solution.py:500
  270.8 18.9 %attend_back.1 = (bf16[512,1024]{1,0:T(8,128)(2,1)S(1)}, f32[2,1024,64]{2,1,0:T(8,128)S(1)}, f32[2,1024,64]{2,1,0:T(8,128)S(1)}) custom-call(s32[1]{0:T(128)} %bitcast.row_ref, bf16[1024,512]{1,0:T(8,128)(2,1)S(1)} %copy-done.22, bf16[512,1024]{1,0:T(8,128)(2,1)S(1)} %add_convert_fusion.10.do_ref, bf16[512,1024]{1,0:T(8,128)(2,1)S(1)} %copy-done.18, ...), custom_call_target="tpu_custom_call" | custom-call | flops 1000 | bytes 1000 | tf_op jit(solution)/shard_map/attend_back/pallas_call | solution.py:261
  341.7 8.1 %product.13 = (bf16[512,2304]{1,0:T(8,128)(2,1)}, bf16[512,2304]{1,0:T(8,128)(2,1)S(1)}) custom-call(bf16[1024,1024]{1,0:T(8,128)(2,1)S(1)} %copy-done.14, bf16[1024,1024]{1,0:T(8,128)(2,1)S(1)} %copy-done.12, bf16[1,512,1024]{2,1,0:T(8,128)(2,1)S(1)} %bitcast.78, bf16[1,512,1280]{2,1,0:T(8,128)(2,1)S(1)} %copy-done.20, bf16[1,512,1024]{2,1,0:T(8,128)(2,1)S(1)} %bitcast.80, ...), custom_call_target="tpu_custom_call" | custom-call | flops 1000 | bytes 1000 | tf_op jit(solution)/shard_map/product/pallas_call | solution.py:392
  388.6 43.7 %collective-permute-done.31 = bf16[512,2304]{1,0:T(8,128)(2,1)S(1)} collective-permute-done((bf16[512,2304]{1,0:T(8,128)(2,1)}, bf16[512,2304]{1,0:T(8,128)(2,1)S(1)}, u32[]{:S(2)}, u32[]{:S(2)}) %collective-permute-start.31) | collective-permute-done | bytes 2359328 | tf_op jit(solution)/shard_map/ppermute | solution.py:503
  445.0 27.4 %collective-permute-done.34 = bf16[512,1280]{1,0:T(8,128)(2,1)} collective-permute-done((bf16[512,1280]{1,0:T(8,128)(2,1)S(1)}, bf16[512,1280]{1,0:T(8,128)(2,1)}, u32[]{:S(2)}, u32[]{:S(2)}) %collective-permute-start.34) | collective-permute-done | bytes 1310752 | tf_op jit(solution)/shard_map/ppermute | solution.py:503
  480.4 26.4 %reduce-scatter.28.cloned.1.call-done = f32[128,2]{1,0:T(8,128)} async-done(((f32[1024,2]{1,0:T(8,128)}), f32[128,2]{1,0:T(8,128)}) %reduce-scatter.28.cloned.1.call-update) | async-done | bytes 1040
  509.1 31.0 %reduce-scatter.26.cloned.1.call-done = bf16[128,1280]{1,0:T(8,128)(2,1)} async-done(((bf16[512,1280]{1,0:T(8,128)(2,1)}), bf16[128,1280]{1,0:T(8,128)(2,1)}) %reduce-scatter.26.cloned.1.call-update) | async-done | bytes 327696 | tf_op jit(solution)/shard_map/reduce_scatter | solution.py:453
  542.2 47.1 %reduce-scatter.24.cloned.1.call-done = bf16[128,2304]{1,0:T(8,128)(2,1)} async-done(((bf16[512,2304]{1,0:T(8,128)(2,1)}), bf16[128,2304]{1,0:T(8,128)(2,1)}) %reduce-scatter.24.cloned.1.call-update) | async-done | bytes 589840 | tf_op jit(solution)/shard_map/reduce_scatter | solution.py:453
  (456 shorter events, 218.1 us)
Async XLA Ops:
  7.2 243.0 %reduce-scatter.12.cloned.1.call-start = ((), (), s32[]{:S(2)}) async-start(), calls=%async_computation.9 | async-start | bytes 1966080 | tf_op jit(solution)/shard_map/reduce_scatter | solution.py:453
  16.8 39.2 %collective-permute-start.6 = (bf16[1024,2816]{1,0:T(8,128)(2,1)}, bf16[1024,2816]{1,0:T(8,128)(2,1)}, u32[]{:S(2)}, u32[]{:S(2)}) collective-permute-start(bf16[1024,2816]{1,0:T(8,128)(2,1)} %gm_ref.2), channel_id=1, source_target_pairs={{0,2},{2,0},{1,3},{3,1},{4,6},{6,4},{5,7},{7,5},{8,10},{10,8},{9,1... | collective-permute-start | bytes 17301512 | tf_op jit(solution)/shard_map/ppermute | solution.py:497
  16.9 39.1 %collective-permute-start.7 = (bf16[1024,2816]{1,0:T(8,128)(2,1)}, bf16[1024,2816]{1,0:T(8,128)(2,1)}, u32[]{:S(2)}, u32[]{:S(2)}) collective-permute-start(bf16[1024,2816]{1,0:T(8,128)(2,1)} %um_ref.2), channel_id=1, source_target_pairs={{0,2},{2,0},{1,3},{3,1},{4,6},{6,4},{5,7},{7,5},{8,10},{10,8},{9,1... | collective-permute-start | bytes 17301512 | tf_op jit(solution)/shard_map/ppermute | solution.py:497
  17.4 38.5 %collective-permute-start.8 = (bf16[1024,1024]{1,0:T(8,128)(2,1)}, bf16[1024,1024]{1,0:T(8,128)(2,1)}, u32[]{:S(2)}, u32[]{:S(2)}) collective-permute-start(bf16[1024,1024]{1,0:T(8,128)(2,1)} %param.19), channel_id=1, source_target_pairs={{0,2},{2,0},{1,3},{3,1},{4,6},{6,4},{5,7},{7,5},{8,10},{10,8},{9,1... | collective-permute-start | bytes 6291464 | tf_op jit(solution)/shard_map/ppermute | solution.py:497
  19.5 26.4 %collective-permute-start.4 = (bf16[512,1024]{1,0:T(8,128)(2,1)S(1)}, bf16[512,1024]{1,0:T(8,128)(2,1)S(1)}, u32[]{:S(2)}, u32[]{:S(2)}) collective-permute-start(bf16[512,1024]{1,0:T(8,128)(2,1)S(1)} %slice_select_fusion), channel_id=1, source_target_pairs={{0,1},{1,0},{2,3},{3,2},{4,5},{5,4},{6,7},{7,6},{8,9},{9,8},{10,11... | collective-permute-start | bytes 3145736 | tf_op jit(solution)/shard_map/ppermute | solution.py:500
  143.9 41.9 %collective-permute-start.21 = (bf16[3,512,1280]{2,1,0:T(8,128)(2,1)}, bf16[3,512,1280]{2,1,0:T(8,128)(2,1)}, u32[]{:S(2)}, u32[]{:S(2)}) collective-permute-start(bf16[3,512,1280]{2,1,0:T(8,128)(2,1)} %hidden_units.3.b_ref.refs_1_), channel_id=1, source_target_pairs={{0,2},{2,0},{1,3},{3,1},{4,6},{6,4},{5,7},{7,5},{8,10},{10,8},{9,1... | collective-permute-start | bytes 11796488 | tf_op jit(solution)/shard_map/ppermute | solution.py:497
  162.4 170.9 %reduce-scatter.14.cloned.1.call-start = ((), (), s32[]{:S(2)}) async-start(), calls=%async_computation.10 | async-start | bytes 1966080 | tf_op jit(solution)/shard_map/reduce_scatter | solution.py:453
  162.5 37.1 %collective-permute-start.22 = (bf16[512,1536]{1,0:T(8,128)(2,1)}, bf16[512,1536]{1,0:T(8,128)(2,1)}, u32[]{:S(2)}, u32[]{:S(2)}) collective-permute-start(bf16[512,1536]{1,0:T(8,128)(2,1)} %copy-done.49), channel_id=1, source_target_pairs={{0,4},{4,0},{8,12},{12,8},{16,20},{20,16},{24,28},{28,24},{1,5},{5... | collective-permute-start | bytes 4718600 | tf_op jit(solution)/shard_map/ppermute | solution.py:503
  202.6 130.8 %reduce-scatter.16.cloned.1.call-start = ((), (), s32[]{:S(2)}) async-start(), calls=%async_computation.11 | async-start | bytes 1966080 | tf_op jit(solution)/shard_map/reduce_scatter | solution.py:453
  202.6 47.6 %collective-permute-start.20 = (bf16[512,2048]{1,0:T(8,128)(2,1)}, bf16[512,2048]{1,0:T(8,128)(2,1)}, u32[]{:S(2)}, u32[]{:S(2)}) collective-permute-start(bf16[512,2048]{1,0:T(8,128)(2,1)} %copy-done.15), channel_id=1, source_target_pairs={{0,1},{1,0},{2,3},{3,2},{4,5},{5,4},{6,7},{7,6},{8,9},{9,8},{10,11... | collective-permute-start | bytes 6291464 | tf_op jit(solution)/shard_map/ppermute | solution.py:500
  204.4 45.8 %collective-permute-start.23 = (bf16[512,1280]{1,0:T(8,128)(2,1)}, bf16[512,1280]{1,0:T(8,128)(2,1)}, u32[]{:S(2)}, u32[]{:S(2)}) collective-permute-start(bf16[512,1280]{1,0:T(8,128)(2,1)} %copy-done.52), channel_id=1, source_target_pairs={{0,4},{4,0},{8,12},{12,8},{16,20},{20,16},{24,28},{28,24},{1,5},{5... | collective-permute-start | bytes 3932168 | tf_op jit(solution)/shard_map/ppermute | solution.py:503
  204.7 161.5 %reduce-scatter.18.cloned.1.call-start = ((), (), s32[]{:S(2)}) async-start(), calls=%async_computation.12 | async-start | bytes 1638400 | tf_op jit(solution)/shard_map/reduce_scatter | solution.py:453
  253.3 38.3 %collective-permute-start.25 = (bf16[512,1536]{1,0:T(8,128)(2,1)}, bf16[512,1536]{1,0:T(8,128)(2,1)}, u32[]{:S(2)}, u32[]{:S(2)}) collective-permute-start(bf16[512,1536]{1,0:T(8,128)(2,1)} %copy-done.48), channel_id=1, source_target_pairs={{0,4},{4,0},{8,12},{12,8},{16,20},{20,16},{24,28},{28,24},{1,5},{5... | collective-permute-start | bytes 4718600 | tf_op jit(solution)/shard_map/ppermute | solution.py:503
  264.0 102.3 %reduce-scatter.20.cloned.1.call-start = ((), (), s32[]{:S(2)}) async-start(), calls=%async_computation.13 | async-start | bytes 1966080 | tf_op jit(solution)/shard_map/reduce_scatter | solution.py:453
  302.2 140.0 %reduce-scatter.22.cloned.1.call-start = ((), (), s32[]{:S(2)}) async-start(), calls=%async_computation.14 | async-start | bytes 1638400 | tf_op jit(solution)/shard_map/reduce_scatter | solution.py:453
  319.2 48.5 %collective-permute-start.28 = (bf16[512,2048]{1,0:T(8,128)(2,1)}, bf16[512,2048]{1,0:T(8,128)(2,1)}, u32[]{:S(2)}, u32[]{:S(2)}) collective-permute-start(bf16[512,2048]{1,0:T(8,128)(2,1)} %pad_maximum_fusion.1), channel_id=1, source_target_pairs={{0,1},{1,0},{2,3},{3,2},{4,5},{5,4},{6,7},{7,6},{8,9},{9,8},{10,11... | collective-permute-start | bytes 6291464 | tf_op jit(solution)/shard_map/ppermute | solution.py:500
  332.0 31.5 %collective-permute-start.29 = (bf16[512,1280]{1,0:T(8,128)(2,1)}, bf16[512,1280]{1,0:T(8,128)(2,1)}, u32[]{:S(2)}, u32[]{:S(2)}) collective-permute-start(bf16[512,1280]{1,0:T(8,128)(2,1)} %get-tuple-element.247), channel_id=1, source_target_pairs={{0,4},{4,0},{8,12},{12,8},{16,20},{20,16},{24,28},{28,24},{1,5},{5... | collective-permute-start | bytes 3932168 | tf_op jit(solution)/shard_map/ppermute | solution.py:503
  378.5 53.9 %collective-permute-start.31 = (bf16[512,2304]{1,0:T(8,128)(2,1)}, bf16[512,2304]{1,0:T(8,128)(2,1)S(1)}, u32[]{:S(2)}, u32[]{:S(2)}) collective-permute-start(bf16[512,2304]{1,0:T(8,128)(2,1)} %get-tuple-element.255), channel_id=1, source_target_pairs={{0,4},{4,0},{8,12},{12,8},{16,20},{20,16},{24,28},{28,24},{1,5},{5... | collective-permute-start | bytes 7077896 | tf_op jit(solution)/shard_map/ppermute | solution.py:503
  379.8 54.5 %collective-permute-start.32 = (bf16[512,2048]{1,0:T(8,128)(2,1)}, bf16[512,2048]{1,0:T(8,128)(2,1)}, u32[]{:S(2)}, u32[]{:S(2)}) collective-permute-start(bf16[512,2048]{1,0:T(8,128)(2,1)} %pad_maximum_fusion.2), channel_id=1, source_target_pairs={{0,1},{1,0},{2,3},{3,2},{4,5},{5,4},{6,7},{7,6},{8,9},{9,8},{10,11... | collective-permute-start | bytes 6291464 | tf_op jit(solution)/shard_map/ppermute | solution.py:500
  381.5 125.3 %reduce-scatter.28.cloned.1.call-start = ((), (), s32[]{:S(2)}) async-start(), calls=%async_computation.17 | async-start | bytes 589824
  439.5 32.9 %collective-permute-start.34 = (bf16[512,1280]{1,0:T(8,128)(2,1)S(1)}, bf16[512,1280]{1,0:T(8,128)(2,1)}, u32[]{:S(2)}, u32[]{:S(2)}) collective-permute-start(bf16[512,1280]{1,0:T(8,128)(2,1)S(1)} %copy-done.51), channel_id=1, source_target_pairs={{0,4},{4,0},{8,12},{12,8},{16,20},{20,16},{24,28},{28,24},{1,5},{5... | collective-permute-start | bytes 3932168 | tf_op jit(solution)/shard_map/ppermute | solution.py:503
  443.2 96.8 %reduce-scatter.26.cloned.1.call-start = ((), (), s32[]{:S(2)}) async-start(), calls=%async_computation.16 | async-start | bytes 1638400 | tf_op jit(solution)/shard_map/reduce_scatter | solution.py:453
  475.1 114.2 %reduce-scatter.24.cloned.1.call-start = ((), (), s32[]{:S(2)}) async-start(), calls=%async_computation.15 | async-start | bytes 2949120 | tf_op jit(solution)/shard_map/reduce_scatter | solution.py:453
  477.8 31.2 %collective-permute-start.36 = (bf16[128,1536]{1,0:T(8,128)(2,1)S(1)}, bf16[128,1536]{1,0:T(8,128)(2,1)S(1)}, u32[]{:S(2)}, u32[]{:S(2)}) collective-permute-start(bf16[128,1536]{1,0:T(8,128)(2,1)S(1)} %copy-done.117), channel_id=1, source_target_pairs={{0,4},{4,0},{8,12},{12,8},{16,20},{20,16},{24,28},{28,24},{1,5},{5... | collective-permute-start | bytes 1179656 | tf_op jit(solution)/shard_map/ppermute | solution.py:503
  (146 other events, 1076.4 us)
Sparse Core Ops, SparseCore 0:
  162.5 35.9 reduce-scatter.11
  202.7 35.8 reduce-scatter.13
  240.9 34.2 reduce-scatter.15
  277.3 30.1 reduce-scatter.17
  309.7 34.0 reduce-scatter.19
  381.6 30.7 reduce-scatter.21
  443.4 63.3 reduce-scatter.27
  509.8 30.2 reduce-scatter.25
  542.4 46.8 reduce-scatter.23

commit v5 on v4

--- a/solution.py
+++ b/solution.py
@@ -168,7 +168,7 @@
             pltpu.VMEM((HEAD_SIZE, SEQ), BF16),
         ],
         compiler_params=pltpu.CompilerParams(vmem_limit_bytes=40 * 1024 * 1024),
-        cost_estimate=pl.CostEstimate(flops=1000, bytes_accessed=1000, transcendentals=0),
+        cost_estimate=pl.CostEstimate(flops=10_000_000_000, bytes_accessed=4_000_000, transcendentals=0),
         name="attend",
     )(row, q, cosine, sine, start, own_kv, other_kv)
 
@@ -290,7 +290,7 @@
             pltpu.VMEM((2, SEQ, HEAD_SIZE), BF16),
         ],
         compiler_params=pltpu.CompilerParams(vmem_limit_bytes=40 * 1024 * 1024),
-        cost_estimate=pl.CostEstimate(flops=1000, bytes_accessed=1000, transcendentals=0),
+        cost_estimate=pl.CostEstimate(flops=20_000_000_000, bytes_accessed=8_000_000, transcendentals=0),
         name="attend_back",
     )(row, qt, d_o, o, lse, cosine, sine, start, own_kv, other_kv)
 
@@ -323,7 +323,7 @@
         out_specs=out,
         out_shape=jax.ShapeDtypeStruct((3, rows, wide), BF16),
         compiler_params=pltpu.CompilerParams(vmem_limit_bytes=48 * 1024 * 1024),
-        cost_estimate=pl.CostEstimate(flops=1000, bytes_accessed=1000, transcendentals=0),
+        cost_estimate=pl.CostEstimate(flops=12 * rows * depth * wide, bytes_accessed=12 * depth * wide, transcendentals=0),
         name="hidden_units",
     )(xm, xo, cm, co, gm, go, um, uo, dm, do)
 
@@ -356,7 +356,7 @@
         out_specs=pl.BlockSpec((rows, tile), lambda i: (0, i)),
         out_shape=jax.ShapeDtypeStruct((rows, 2 * depth), BF16),
         compiler_params=pltpu.CompilerParams(vmem_limit_bytes=48 * 1024 * 1024),
-        cost_estimate=pl.CostEstimate(flops=1000, bytes_accessed=1000, transcendentals=0),
+        cost_estimate=pl.CostEstimate(flops=8 * rows * depth * wide, bytes_accessed=8 * depth * wide, transcendentals=0),
         name="input_grad",
     )(a, b, gm, um, go, uo)
 
@@ -396,7 +396,7 @@
         out_specs=[pl.BlockSpec((rows // 2, tile), lambda i: (0, i))] * 2,
         out_shape=[jax.ShapeDtypeStruct((rows // 2, first * tile), BF16)] * 2,
         compiler_params=pltpu.CompilerParams(vmem_limit_bytes=40 * 1024 * 1024),
-        cost_estimate=pl.CostEstimate(flops=1000, bytes_accessed=1000, transcendentals=0),
+        cost_estimate=pl.CostEstimate(flops=4 * rows * tokens * first * tile, bytes_accessed=6 * rows * first * tile, transcendentals=0),
         name="product",
     )(*[p[0] for p in pieces], *[p[1] for p in pieces], *[p[2] for p in pieces])
 
@@ -428,7 +428,7 @@
         ),
         out_shape=jax.ShapeDtypeStruct((wide, 2 * tokens), BF16),
         compiler_params=pltpu.CompilerParams(vmem_limit_bytes=40 * 1024 * 1024),
-        cost_estimate=pl.CostEstimate(flops=1000, bytes_accessed=1000, transcendentals=0),
+        cost_estimate=pl.CostEstimate(flops=1000, bytes_accessed=8 * tokens * wide, transcendentals=0),
         name="sided",
     )(side.astype(jnp.int32).reshape(1), own, other)
 
@@ -511,6 +511,7 @@
     wq_o = swap(query_weight)
     gains = jnp.stack([g_attn, g_mlp])
     gains_o = swap(gains)
+    x_o, wkv_o, wq_o, gains_o = tie(x_o, wkv_o, wq_o, gains_o)
     x_m, x_o = x_m.astype(F32), x_o.astype(F32)
     square = jnp.sum(x_m * x_m, axis=-1, keepdims=True) + jnp.sum(x_o * x_o, axis=-1, keepdims=True)
     inv_one = lax.rsqrt(square / MODEL_WIDTH + EPS)
@@ -594,34 +595,27 @@
     two, one_t, xn2_t = tie(two, one_t, xn2_t)
     two_t = swap(two)
 
-    send_1 = Summed([(c_y, one, one_t, 0)], flip, count)
-    send_1.begin(two)
-    send_1.go()
-    send_1.keep, xn2_m2 = tie(send_1.keep, xn2_m2)
+    two, xn2_m2 = tie(two, xn2_m2)
     xn2_y = sided(xn2_m2, xn2_t, side, count)
     first_z = Summed([(xn2_y, one, one_t, 2)], flip, count)
     first_z.begin()
     first_z.send = first_z.scatter(first_z.send)
-    first_z.keep, two_late = tie(first_z.keep, two)
+    first_z.keep, two_t = tie(first_z.keep, two_t)
+    send_1 = Summed([(c_y, one, one_t, 0), (c_y, two, two_t, 0)], flip, count)
+    send_1.begin(first_z.keep)
+    send_1.go()
+    send_1.keep, two_late, first_z.keep = tie(send_1.keep, two, first_z.keep)
+    first_z.keep = first_z.scatter(first_z.keep)
     part = input_grad(one, two_late, w_gate, w_up, wg_o, wu_o)
     came = cross(part)
-    two_t, part = tie(two_t, part)
-    send_2 = Summed([(c_y, two, two_t, 0)], flip, count)
+    send_2 = Summed([(xn2_y, one, one_t, 1)], flip, count)
     send_2.begin(part)
-    part = serve(part, (send_1,), (send_2.keep,))
+    send_3 = Summed([(xn2_y, two, two_t, 1), (xn2_y, two, two_t, 2)], flip, count)
+    send_3.begin(send_2.keep)
+    came, first_z.send, part = tie(came, first_z.send, part, send_3.keep)[:3]
+    came = serve(came, (send_1,))
     send_2.go(send_1)
-    part, first_z.keep, total = tie(part, first_z.keep, send_1.finish())
-    first_z.keep = first_z.scatter(first_z.keep)
-    send_3 = Summed([(xn2_y, one, one_t, 1)], flip, count)
-    send_3.begin(part)
-    send_4 = Summed([(xn2_y, two, two_t, 1)], flip, count)
-    send_4.begin(send_3.keep)
-    send_6 = Summed([(xn2_y, two, two_t, 2)], flip, count)
-    send_6.begin(send_4.keep)
-    came, first_z.send, part = tie(came, first_z.send, part, send_6.keep)[:3]
-    came = serve(came, (send_2,))
-    send_3.go(send_2)
-    came, _ = tie(came, send_2.finish())
+    came, _ = tie(came, send_1.finish())
 
     width = tokens.shape[1]
     d_xn2 = part.astype(F32) + came.astype(F32)
@@ -637,12 +631,12 @@
     dh_m, dh_o = d_hid_m.astype(BF16), d_hid_o.astype(BF16)
     dh_t = swap(dh_o)
     d_o = (dot_right(dh_m, w_o) + dot_right(dh_o, w_o_o)).astype(BF16)
-    d_o, dh_t = tie(d_o, dh_t)
+    d_o, dh_t, first_z.keep = tie(d_o, dh_t, first_z.keep)
+    d_o = serve(d_o, (send_2,))
+    send_3.go(send_2)
+    d_o, _ = tie(d_o, send_2.finish())
 
     d_q, d_k, d_v = attend_back(row_arg, qt, d_o, o, lse, cosine_t, sine_t, start_arg, own_kv, other_kv)
-    d_q = serve(d_q, (send_3,))
-    send_4.go(send_3)
-    d_q, d_k, _ = tie(d_q, d_k, send_3.finish())
     d_kv = jnp.concatenate([d_k[0], d_k[1], d_v[0], d_v[1]], axis=1)
     d_kv_t = swap(other_rows(d_kv, row))
     d_kv_own = own_rows(d_kv, row)
@@ -662,7 +656,7 @@
     )
     last, d_qkv_t = tie(last, d_qkv_t)
     last_came = cross(last)
-    last, first_z.keep, send_1.total = tie(last, first_z.keep, send_1.total)
+    last, send_1.total = tie(last, send_1.total)
     send_5 = Summed(
         [
             (sided(dh_m, dh_t, side, count), o[None], o_t[None], 0),
@@ -673,6 +667,10 @@
     )
     send_5.begin(last)
     one, send_5.keep = tie(one, send_5.keep)
+    one = serve(one, (send_3,))
+    send_5.go(send_3)
+    first_z.go(send_3)
+    one, _ = tie(one, send_3.finish())
     cut = one.shape[2]
     mix = jnp.concatenate(
         [
@@ -681,11 +679,11 @@
         ],
         axis=1,
     )
-    mix = serve(mix, (send_4,))
-    send_5.go(send_4)
-    mix, send_2.total, _ = tie(mix, send_2.total, send_4.finish())
-
-    last_came, mix, send_3.total = tie(last_came, mix, send_3.total)
+
+    last_came, mix, send_2.total = tie(last_came, mix, send_2.total)
+    last_came, first_z.came = tie(last_came, first_z.came)
+    last_came = serve(last_came, (send_5,))
+    last_came, mix, _ = tie(last_came, mix, send_5.finish())
     mix_came = cross(mix)
     d_xn = last.astype(F32) + last_came.astype(F32)
     d_xn_m, d_xn_o = d_xn[:, :width], d_xn[:, width:]
@@ -700,28 +698,23 @@
     d_tok_o = d_hid_o + inv_one * (e_o - unit_o * mean)
     d_tok_t = swap(d_tok_o)
     gg = jnp.stack([gg_attn_m, gg_mlp_m]) + swap(jnp.stack([gg_attn_o, gg_mlp_o]))
-    gg, send_4.total = tie(gg, send_4.total)
-    gg = lax.psum_scatter(gg, "dp", scatter_dimension=1, tiled=True)
+    for bit in range(count.bit_length() - 1):
+        gg = gg + lax.ppermute(gg, "dp", [(i, i ^ (1 << bit)) for i in range(count)])
+    gg = lax.dynamic_slice_in_dim(gg, lax.axis_index("dp") * (width // count), width // count, axis=1)
     d_tokens = merge_rows(d_tok_m, d_tok_t, row)
-
-    d_tokens = serve(d_tokens, (send_5,))
-    first_z.go(send_5)
-    send_6.go(send_5)
-    d_tokens, mix_came, _ = tie(d_tokens, mix_came, send_5.finish())
 
     mixed_all = mix.astype(F32) + mix_came.astype(F32)
     out_m = (hidden_m + mixed_all[:, :width]).astype(BF16)
     out_o = (hidden_o + mixed_all[:, width:]).astype(BF16)
     mixed = merge_rows(out_m, swap(out_o), row)
 
-    mixed, send_6.came = tie(mixed, send_6.came)
-    send_6.finish()
     first_z.total = first_z.keep.astype(F32) + first_z.came.astype(F32)
-    got = [h.total.astype(F32) for h in (send_1, send_2, send_3, send_4, first_z, send_6, send_5)]
-    gw_down = jnp.concatenate([got[0].T, got[1].T], axis=0)
-    gw_gate = jnp.concatenate([got[2], got[3]], axis=1)
-    gw_up = jnp.concatenate([got[4], got[5]], axis=1)
-    gw_o, gw_qkv = got[6][:, : o.shape[1]].T, got[6][:, o.shape[1] :]
+    got = [h.total.astype(F32) for h in (send_1, send_2, send_3, first_z, send_5)]
+    rest = two.shape[2]
+    gw_down = got[0].T
+    gw_gate = jnp.concatenate([got[1], got[2][:, :rest]], axis=1)
+    gw_up = jnp.concatenate([got[3], got[2][:, rest:]], axis=1)
+    gw_o, gw_qkv = got[4][:, : o.shape[1]].T, got[4][:, o.shape[1] :]
     return (
         mixed,
         d_tokens,

time: 608 us -> 535 us (0.88)
  waiting for transfers between devices: 249 us -> 165 us
    reduce_scatter x8 -> x6, waiting for transfers between devices: 78.1 us -> 0.01 us  [scatter(): lax.psum_scatter(value, 'dp', scatter_dimension=0, axis_index_groups=grou...]
    ppermute x6, waiting for transfers between devices: 44.7 us -> 85 us  [cross(): return lax.ppermute(value, 'col', [(0, 1), (1, 0)])]
    unnamed x10 -> x6, waiting for transfers between devices: 27.2 us -> 0.1 us
    ppermute x23, waiting for transfers between devices: 14.2 us -> 1.01 us  [swap(): return lax.ppermute(value, 'row', [(0, 1), (1, 0)])]
    ppermute x8 -> x6, waiting for transfers between devices: 85.2 us -> 77.9 us  [flip(): return lax.ppermute(value, 'dp', [(i, i ^ 1) for i in range(count)])]
    unnamed x255 -> x236, local copies, waits for them, and re-layouts: 43.4 us -> 47.2 us
    convert_element_type x6 -> x4, other arithmetic: 16.4 us -> 16.8 us  [finish(): total = (self.keep.astype(F32) + self.came.astype(F32)).astype(BF16)]
    pallas_call x7 -> x5, Pallas kernels: 43.3 us -> 43 us  [product(): pl.pallas_call(functools.partial(product_kernel, counts), grid=(first,),...]
  transfers between devices with their start and end apart: 46 -> 44, of which waited for: 17 -> 11; matrix products, arithmetic and copies ran while one was open for 18% -> 23% of each run, Pallas kernels for 21% -> 24%
where the time goes in v5:
time: 535 us; the launch traced here: 528 us
  waiting for transfers between devices  165 us (31%)
  Pallas kernels  139 us (26%)
  other arithmetic  72.7 us (14%)
  matrix products  53.3 us (10%)
  local copies, waits for them, and re-layouts  52 us (10%)
  starting transfers between devices  29.1 us (5%)
  between operations  16.1 us (3%)
    ppermute x6, waiting for transfers between devices, cross(): return lax.ppermute(value, 'col', [(0, 1), (1, 0)])  85 us
    ppermute x6, waiting for transfers between devices, flip(): return lax.ppermute(value, 'dp', [(i, i ^ 1) for i in range(count)])  77.9 us
    unnamed x236, local copies, waits for them, and re-layouts  47.2 us
    pallas_call x5, Pallas kernels, product(): pl.pallas_call(functools.partial(product_kernel, counts), grid=(first,),...  43 us
    dot_general x16, matrix products, dot_plain(): return jnp.dot(left, right, preferred_element_type=F32)  38 us
    pallas_call x2, Pallas kernels, hidden_units(): pl.pallas_call(hidden_units_kernel, grid=(tiles,), in_specs=[full] * 4 +...  27.4 us
    pallas_call x2, Pallas kernels, attend(): pl.pallas_call(functools.partial(attend_kernel, group), grid=(pairs,), in...  20.1 us
    pallas_call x1, Pallas kernels, input_grad(): pl.pallas_call(input_grad_kernel, grid=(2 * tiles,), in_specs=[full(a), f...  20.1 us
  transfers between devices with their start and end apart: 44, of which 11 were waited for; matrix products, arithmetic and copies ran while one was open for 23% of the time, Pallas kernels for 24%

profile of v5, /device:TPU:0, one launch (start us, length us, event | category | flops | bytes accessed | tf_op | source)
XLA Modules:
  0.0 527.5 jit_solution(6747767214015070250)
XLA Ops:
  29.5 15.4 %collective-permute-done.4 = bf16[512,1024]{1,0:T(8,128)(2,1)S(1)} collective-permute-done((bf16[512,1024]{1,0:T(8,128)(2,1)S(1)}, bf16[512,1024]{1,0:T(8,128)(2,1)S(1)}, u32[]{:S(2)}, u32[]{:S(2)}) %collective-permute-start.4) | collective-permute-done | bytes 1048608 | tf_op jit(solution)/shard_map/ppermute | solution.py:500
  45.0 10.1 %attend.2 = (bf16[512,512]{1,0:T(8,128)(2,1)S(1)}, f32[4,2,512]{2,1,0:T(2,128)S(1)}, bf16[512,512]{1,0:T(8,128)(2,1)S(1)}) custom-call(s32[1]{0:T(128)} %bitcast.row_ref, f32[512,1024]{1,0:T(8,128)S(1)} %convolution_add_fusion.2.q_ref, f32[32,512]{1,0:T(8,128)S(1)} %get-tuple-element.343.cos_ref, f32[32,512]{1,0:T(8,128)S(1)} %get-tuple-element.342.sin_ref, ...), custom_call_target="tpu_custom_call" | custom-call | flops 10000000000 | bytes 4000000 | tf_op jit(solution)/shard_map/attend/pallas_call | solution.py:143
  58.7 10.0 %attend.3 = (bf16[512,512]{1,0:T(8,128)(2,1)S(1)}, f32[4,2,512]{2,1,0:T(2,128)S(1)}, bf16[512,512]{1,0:T(8,128)(2,1)S(1)}) custom-call(s32[1]{0:T(128)} %bitcast.row_ref, f32[512,1024]{1,0:T(8,128)S(1)} %convolution_add_fusion.2.q_ref, f32[32,512]{1,0:T(8,128)S(1)} %get-tuple-element.343.cos_ref, f32[32,512]{1,0:T(8,128)S(1)} %get-tuple-element.342.sin_ref, ...), custom_call_target="tpu_custom_call" | custom-call | flops 10000000000 | bytes 4000000 | tf_op jit(solution)/shard_map/attend/pallas_call | solution.py:143
  89.1 8.2 %collective-permute-done.14 = bf16[512,512]{1,0:T(8,128)(2,1)S(1)} collective-permute-done((bf16[512,512]{1,0:T(8,128)(2,1)S(1)}, bf16[512,512]{1,0:T(8,128)(2,1)S(1)}, u32[]{:S(2)}, u32[]{:S(2)}) %collective-permute-start.14) | collective-permute-done | bytes 524320 | tf_op jit(solution)/shard_map/ppermute | solution.py:500
  98.8 9.4 %collective-permute-done.17 = bf16[512,512]{1,0:T(8,128)(2,1)S(1)} collective-permute-done((bf16[512,512]{1,0:T(8,128)(2,1)S(1)}, bf16[512,512]{1,0:T(8,128)(2,1)S(1)}, u32[]{:S(2)}, u32[]{:S(2)}) %collective-permute-start.17) | collective-permute-done | bytes 524320 | tf_op jit(solution)/shard_map/ppermute | solution.py:500
  116.8 14.7 %hidden_units.2.refs_1_.refs_2_.a_ref = bf16[3,512,1536]{2,1,0:T(8,128)(2,1)} custom-call(bf16[512,1024]{1,0:T(8,128)(2,1)S(1)} %get-tuple-element.182.xm_ref.own_ref, bf16[512,1024]{1,0:T(8,128)(2,1)S(1)} %get-tuple-element.346.xo_ref, bf16[512,1024]{1,0:T(8,128)(2,1)S(1)} %pad_maximum_fusion.9.own_ref.cm_ref, ...), custom_call_target="tpu_custom_call" | custom-call | flops 9663676416 | bytes 18874368 | tf_op jit(solution)/shard_map/hidden_units/pallas_call | solution.py:319
  131.9 12.8 %hidden_units.3.refs_3_.b_ref.refs_2_ = bf16[3,512,1280]{2,1,0:T(8,128)(2,1)} custom-call(bf16[512,1024]{1,0:T(8,128)(2,1)S(1)} %get-tuple-element.182.xm_ref.own_ref, bf16[512,1024]{1,0:T(8,128)(2,1)S(1)} %get-tuple-element.346.xo_ref, bf16[512,1024]{1,0:T(8,128)(2,1)S(1)} %pad_maximum_fusion.9.own_ref.cm_ref, ...), custom_call_target="tpu_custom_call" | custom-call | flops 8053063680 | bytes 15728640 | tf_op jit(solution)/shard_map/hidden_units/pallas_call | solution.py:319
  146.5 6.3 %product.5 = (bf16[512,1536]{1,0:T(8,128)(2,1)S(1)}, bf16[512,1536]{1,0:T(8,128)(2,1)S(1)}) custom-call(bf16[1024,1024]{1,0:T(8,128)(2,1)S(1)} %sided.5.refs_0_.refs_1_, bf16[3,512,1536]{2,1,0:T(8,128)(2,1)S(1)} %copy-done, bf16[3,512,1536]{2,1,0:T(8,128)(2,1)} %collective-permute-done.18.refs_2_.refs_4_), custom_call_target="tpu_custom_call" | custom-call | flops 6442450944 | bytes 9437184 | tf_op jit(solution)/shard_map/product/pallas_call | solution.py:392
  158.9 11.7 %product.6 = (bf16[512,2816]{1,0:T(8,128)(2,1)}, bf16[512,2816]{1,0:T(8,128)(2,1)S(1)}) custom-call(bf16[1024,1024]{1,0:T(8,128)(2,1)S(1)} %copy-done.14, bf16[1024,1024]{1,0:T(8,128)(2,1)S(1)} %copy-done.14, bf16[3,512,1536]{2,1,0:T(8,128)(2,1)} %hidden_units.2.refs_1_.refs_2_.a_ref, bf16[3,512,1280]{2,1,0:T(8,128)(2,1)S(1)} %copy-done.4, ...), custom_call_target="tpu_custom_call" | custom-call | flops 11811160064 | bytes 17301504 | tf_op jit(solution)/shard_map/product/pallas_call | solution.py:392
  172.5 20.1 %input_grad.1 = bf16[512,2048]{1,0:T(8,128)(2,1)} custom-call(bf16[3,512,1536]{2,1,0:T(8,128)(2,1)} %hidden_units.2.refs_1_.refs_2_.a_ref, bf16[3,512,1280]{2,1,0:T(8,128)(2,1)S(1)} %copy-done.5, bf16[1024,2816]{1,0:T(8,128)(2,1)} %gm_ref.2, bf16[1024,2816]{1,0:T(8,128)(2,1)} %um_ref.2, bf16[1024,2816]{1,0:T(8,128)(2,1)} %collective-permute-done.6.go_ref, ...), custom_call_target="tpu_custom_call" | custom-call | flops 11811160064 | bytes 23068672 | tf_op jit(solution)/shard_map/input_grad/pallas_call | solution.py:352
  198.1 6.4 %product.7 = (bf16[512,1536]{1,0:T(8,128)(2,1)S(1)}, bf16[512,1536]{1,0:T(8,128)(2,1)S(1)}) custom-call(bf16[1024,1024]{1,0:T(8,128)(2,1)S(1)} %copy-done.18, bf16[3,512,1536]{2,1,0:T(8,128)(2,1)S(1)} %copy-done.1, bf16[3,512,1536]{2,1,0:T(8,128)(2,1)} %collective-permute-done.18.refs_2_.refs_4_), custom_call_target="tpu_custom_call" | custom-call | flops 6442450944 | bytes 9437184 | tf_op jit(solution)/shard_map/product/pallas_call | solution.py:392
  206.8 10.5 %product.8 = (bf16[512,2560]{1,0:T(8,128)(2,1)}, bf16[512,2560]{1,0:T(8,128)(2,1)S(1)}) custom-call(bf16[1024,1024]{1,0:T(8,128)(2,1)S(1)} %copy-done.19, bf16[1024,1024]{1,0:T(8,128)(2,1)S(1)} %copy-done.19, bf16[3,512,1280]{2,1,0:T(8,128)(2,1)S(1)} %copy-done.6, bf16[3,512,1280]{2,1,0:T(8,128)(2,1)S(1)} %copy-done.6, ...), custom_call_target="tpu_custom_call" | custom-call | flops 10737418240 | bytes 15728640 | tf_op jit(solution)/shard_map/product/pallas_call | solution.py:392
  218.8 21.8 %collective-permute-done.21 = bf16[512,2048]{1,0:T(8,128)(2,1)} collective-permute-done((bf16[512,2048]{1,0:T(8,128)(2,1)}, bf16[512,2048]{1,0:T(8,128)(2,1)}, u32[]{:S(2)}, u32[]{:S(2)}) %collective-permute-start.21) | collective-permute-done | bytes 2097184 | tf_op jit(solution)/shard_map/ppermute | solution.py:500
  240.6 5.0 add_convert_fusion
  254.8 6.0 %fusion.72 = (bf16[512,1024]{1,0:T(8,128)(2,1)}, bf16[512,1024]{1,0:T(8,128)(2,1)}) fusion(f32[512]{0:T(512)S(1)} %add_multiply_fusion.1, f32[512,1024]{1,0:T(8,128)} %copy-done.45, f32[1024]{0:T(1024)S(1)} %bitcast.93, f32[512,2048]{1,0:T(8,128)} %copy-done.49, f32[512]{0:T(512)S(1)} %add_rsqrt_fusion, ...), kind=kLoop, calls=%fused_computation.182 | loop fusion | flops 8388608 | bytes 12595200 | tf_op jit(solution)/shard_map/convert_element_type | solution.py:631
  271.0 10.5 %collective-permute-done.24 = bf16[512,1536]{1,0:T(8,128)(2,1)} collective-permute-done((bf16[512,1536]{1,0:T(8,128)(2,1)}, bf16[512,1536]{1,0:T(8,128)(2,1)}, u32[]{:S(2)}, u32[]{:S(2)}) %collective-permute-start.24) | collective-permute-done | bytes 1572896 | tf_op jit(solution)/shard_map/ppermute | solution.py:503
  289.2 18.7 %attend_back.1 = (bf16[512,1024]{1,0:T(8,128)(2,1)S(1)}, f32[2,1024,64]{2,1,0:T(8,128)S(1)}, f32[2,1024,64]{2,1,0:T(8,128)S(1)}) custom-call(s32[1]{0:T(128)} %bitcast.row_ref, bf16[1024,512]{1,0:T(8,128)(2,1)S(1)} %copy-done.25, bf16[512,1024]{1,0:T(8,128)(2,1)S(1)} %copy-done.40, bf16[512,1024]{1,0:T(8,128)(2,1)S(1)} %copy-done.30, ...), custom_call_target="tpu_custom_call" | custom-call | flops 20000000000 | bytes 8000000 | tf_op jit(solution)/shard_map/attend_back/pallas_call | solution.py:261
  310.9 5.1 fusion.14
  316.0 4.6 sided.6.refs_0_
  349.3 8.2 %product.9 = (bf16[512,2304]{1,0:T(8,128)(2,1)}, bf16[512,2304]{1,0:T(8,128)(2,1)S(1)}) custom-call(bf16[1024,1024]{1,0:T(8,128)(2,1)S(1)} %copy-done.16, bf16[1024,1024]{1,0:T(8,128)(2,1)S(1)} %copy-done.12, bf16[1,512,1024]{2,1,0:T(8,128)(2,1)S(1)} %bitcast.76, bf16[1,512,1280]{2,1,0:T(8,128)(2,1)S(1)} %get-tuple-element.320.refs_3_, ...), custom_call_target="tpu_custom_call" | custom-call | flops 9663676416 | bytes 14155776 | tf_op jit(solution)/shard_map/product/pallas_call | solution.py:392
  358.8 22.6 %collective-permute-done.28 = bf16[512,2560]{1,0:T(8,128)(2,1)} collective-permute-done((bf16[512,2560]{1,0:T(8,128)(2,1)}, bf16[512,2560]{1,0:T(8,128)(2,1)}, u32[]{:S(2)}, u32[]{:S(2)}) %collective-permute-start.28) | collective-permute-done | bytes 2621472 | tf_op jit(solution)/shard_map/ppermute | solution.py:503
  400.9 41.9 %collective-permute-done.29 = bf16[128,1536]{1,0:T(8,128)(2,1)S(1)} collective-permute-done((bf16[128,1536]{1,0:T(8,128)(2,1)S(1)}, bf16[128,1536]{1,0:T(8,128)(2,1)S(1)}, u32[]{:S(2)}, u32[]{:S(2)}) %collective-permute-start.29) | collective-permute-done | bytes 393248 | tf_op jit(solution)/shard_map/ppermute | solution.py:503
  455.7 4.9 fusion.27
  470.2 30.3 %collective-permute-done.31 = bf16[512,2048]{1,0:T(8,128)(2,1)} collective-permute-done((bf16[512,2048]{1,0:T(8,128)(2,1)}, bf16[512,2048]{1,0:T(8,128)(2,1)}, u32[]{:S(2)}, u32[]{:S(2)}) %collective-permute-start.31) | collective-permute-done | bytes 2097184 | tf_op jit(solution)/shard_map/ppermute | solution.py:500
  (430 shorter events, 196.5 us)
Async XLA Ops:
  7.2 211.6 %reduce-scatter.7.cloned.1.call-start = ((), (), s32[]{:S(2)}) async-start(), calls=%async_computation.6 | async-start | bytes 1966080 | tf_op jit(solution)/shard_map/reduce_scatter | solution.py:453
  16.3 38.7 %collective-permute-start.6 = (bf16[1024,2816]{1,0:T(8,128)(2,1)}, bf16[1024,2816]{1,0:T(8,128)(2,1)}, u32[]{:S(2)}, u32[]{:S(2)}) collective-permute-start(bf16[1024,2816]{1,0:T(8,128)(2,1)} %gm_ref.2), channel_id=1, source_target_pairs={{0,2},{2,0},{1,3},{3,1},{4,6},{6,4},{5,7},{7,5},{8,10},{10,8},{9,1... | collective-permute-start | bytes 17301512 | tf_op jit(solution)/shard_map/ppermute | solution.py:497
  16.8 38.3 %collective-permute-start.7 = (bf16[1024,2816]{1,0:T(8,128)(2,1)}, bf16[1024,2816]{1,0:T(8,128)(2,1)}, u32[]{:S(2)}, u32[]{:S(2)}) collective-permute-start(bf16[1024,2816]{1,0:T(8,128)(2,1)} %um_ref.2), channel_id=1, source_target_pairs={{0,2},{2,0},{1,3},{3,1},{4,6},{6,4},{5,7},{7,5},{8,10},{10,8},{9,1... | collective-permute-start | bytes 17301512 | tf_op jit(solution)/shard_map/ppermute | solution.py:497
  18.6 26.4 %collective-permute-start.4 = (bf16[512,1024]{1,0:T(8,128)(2,1)S(1)}, bf16[512,1024]{1,0:T(8,128)(2,1)S(1)}, u32[]{:S(2)}, u32[]{:S(2)}) collective-permute-start(bf16[512,1024]{1,0:T(8,128)(2,1)S(1)} %slice_select_fusion), channel_id=1, source_target_pairs={{0,1},{1,0},{2,3},{3,2},{4,5},{5,4},{6,7},{7,6},{8,9},{9,8},{10,11... | collective-permute-start | bytes 3145736 | tf_op jit(solution)/shard_map/ppermute | solution.py:500
  21.8 23.1 %collective-permute-start.5 = (bf16[512,256]{1,0:T(8,128)(2,1)S(1)}, bf16[512,256]{1,0:T(8,128)(2,1)S(1)}, u32[]{:S(2)}, u32[]{:S(2)}) collective-permute-start(bf16[512,256]{1,0:T(8,128)(2,1)S(1)} %pad_maximum_fusion.14.own_ref), channel_id=1, source_target_pairs={{0,2},{2,0},{1,3},{3,1},{4,6},{6,4},{5,7},{7,5},{8,10},{10,8},{9,1... | collective-permute-start | bytes 786440 | tf_op jit(solution)/shard_map/ppermute | solution.py:497
  21.9 33.1 %collective-permute-start.8 = (bf16[1024,1024]{1,0:T(8,128)(2,1)}, bf16[1024,1024]{1,0:T(8,128)(2,1)S(1)}, u32[]{:S(2)}, u32[]{:S(2)}) collective-permute-start(bf16[1024,1024]{1,0:T(8,128)(2,1)} %param.19), channel_id=1, source_target_pairs={{0,2},{2,0},{1,3},{3,1},{4,6},{6,4},{5,7},{7,5},{8,10},{10,8},{9,1... | collective-permute-start | bytes 6291464 | tf_op jit(solution)/shard_map/ppermute | solution.py:497
  56.9 25.6 %collective-permute-start.12 = (bf16[512,1024]{1,0:T(8,128)(2,1)S(1)}, bf16[512,1024]{1,0:T(8,128)(2,1)}, u32[]{:S(2)}, u32[]{:S(2)}) collective-permute-start(bf16[512,1024]{1,0:T(8,128)(2,1)S(1)} %collective-permute-done.4), channel_id=1, source_target_pairs={{0,4},{4,0},{8,12},{12,8},{16,20},{20,16},{24,28},{28,24},{1,5},{5... | collective-permute-start | bytes 3145736 | tf_op jit(solution)/shard_map/ppermute | solution.py:503
  84.4 23.7 %collective-permute-start.15 = (bf16[512,1024]{1,0:T(8,128)(2,1)S(1)}, bf16[512,1024]{1,0:T(8,128)(2,1)S(1)}, u32[]{:S(2)}, u32[]{:S(2)}) collective-permute-start(bf16[512,1024]{1,0:T(8,128)(2,1)S(1)} %constant_dynamic-update-slice_fusion.2.o_ref), channel_id=1, source_target_pairs={{0,2},{2,0},{1,3},{3,1},{4,6},{6,4},{5,7},{7,5},{8,10},{10,8},{9,1... | collective-permute-start | bytes 3145736 | tf_op jit(solution)/shard_map/ppermute | solution.py:497
  84.7 23.4 %collective-permute-start.16 = (bf16[512,1024]{1,0:T(8,128)(2,1)S(1)}, bf16[512,1024]{1,0:T(8,128)(2,1)S(1)}, u32[]{:S(2)}, u32[]{:S(2)}) collective-permute-start(bf16[512,1024]{1,0:T(8,128)(2,1)S(1)} %copy-done.66), channel_id=1, source_target_pairs={{0,2},{2,0},{1,3},{3,1},{4,6},{6,4},{5,7},{7,5},{8,10},{10,8},{9,1... | collective-permute-start | bytes 3145736 | tf_op jit(solution)/shard_map/ppermute | solution.py:497
  88.8 19.3 %collective-permute-start.17 = (bf16[512,512]{1,0:T(8,128)(2,1)S(1)}, bf16[512,512]{1,0:T(8,128)(2,1)S(1)}, u32[]{:S(2)}, u32[]{:S(2)}) collective-permute-start(bf16[512,512]{1,0:T(8,128)(2,1)S(1)} %get-tuple-element.155), channel_id=1, source_target_pairs={{0,1},{1,0},{2,3},{3,2},{4,5},{5,4},{6,7},{7,6},{8,9},{9,8},{10,11... | collective-permute-start | bytes 1572872 | tf_op jit(solution)/shard_map/ppermute | solution.py:500
  155.1 115.8 %reduce-scatter.9.cloned.1.call-start = ((), (), s32[]{:S(2)}) async-start(), calls=%async_computation.7 | async-start | bytes 1966080 | tf_op jit(solution)/shard_map/reduce_scatter | solution.py:453
  172.2 68.4 %collective-permute-start.22 = (bf16[512,2816]{1,0:T(8,128)(2,1)}, bf16[512,2816]{1,0:T(8,128)(2,1)}, u32[]{:S(2)}, u32[]{:S(2)}) collective-permute-start(bf16[512,2816]{1,0:T(8,128)(2,1)} %get-tuple-element.199), channel_id=1, source_target_pairs={{0,4},{4,0},{8,12},{12,8},{16,20},{20,16},{24,28},{28,24},{1,5},{5... | collective-permute-start | bytes 8650760 | tf_op jit(solution)/shard_map/ppermute | solution.py:503
  192.6 48.0 %collective-permute-start.21 = (bf16[512,2048]{1,0:T(8,128)(2,1)}, bf16[512,2048]{1,0:T(8,128)(2,1)}, u32[]{:S(2)}, u32[]{:S(2)}) collective-permute-start(bf16[512,2048]{1,0:T(8,128)(2,1)} %input_grad.1), channel_id=1, source_target_pairs={{0,1},{1,0},{2,3},{3,2},{4,5},{5,4},{6,7},{7,6},{8,9},{9,8},{10,11... | collective-permute-start | bytes 6291464 | tf_op jit(solution)/shard_map/ppermute | solution.py:500
  194.1 148.2 %reduce-scatter.11.cloned.1.call-start = ((), (), s32[]{:S(2)}) async-start(), calls=%async_computation.8 | async-start | bytes 3604480 | tf_op jit(solution)/shard_map/reduce_scatter | solution.py:453
  245.6 35.9 %collective-permute-start.24 = (bf16[512,1536]{1,0:T(8,128)(2,1)}, bf16[512,1536]{1,0:T(8,128)(2,1)}, u32[]{:S(2)}, u32[]{:S(2)}) collective-permute-start(bf16[512,1536]{1,0:T(8,128)(2,1)} %copy-done.33), channel_id=1, source_target_pairs={{0,4},{4,0},{8,12},{12,8},{16,20},{20,16},{24,28},{28,24},{1,5},{5... | collective-permute-start | bytes 4718600 | tf_op jit(solution)/shard_map/ppermute | solution.py:503
  254.1 146.8 %reduce-scatter.13.cloned.1.call-start = ((), (), s32[]{:S(2)}) async-start(), calls=%async_computation.9 | async-start | bytes 1966080 | tf_op jit(solution)/shard_map/reduce_scatter | solution.py:453
  321.9 59.5 %collective-permute-start.28 = (bf16[512,2560]{1,0:T(8,128)(2,1)}, bf16[512,2560]{1,0:T(8,128)(2,1)}, u32[]{:S(2)}, u32[]{:S(2)}) collective-permute-start(bf16[512,2560]{1,0:T(8,128)(2,1)} %get-tuple-element.227), channel_id=1, source_target_pairs={{0,4},{4,0},{8,12},{12,8},{16,20},{20,16},{24,28},{28,24},{1,5},{5... | collective-permute-start | bytes 7864328 | tf_op jit(solution)/shard_map/ppermute | solution.py:503
  323.6 186.2 %reduce-scatter.17.cloned.1.call-start = ((), (), s32[]{:S(2)}) async-start(), calls=%async_computation.11 | async-start | bytes 3276800 | tf_op jit(solution)/shard_map/reduce_scatter | solution.py:453
  340.5 60.5 %collective-permute-start.27 = (bf16[512,2048]{1,0:T(8,128)(2,1)}, bf16[512,2048]{1,0:T(8,128)(2,1)}, u32[]{:S(2)}, u32[]{:S(2)}) collective-permute-start(bf16[512,2048]{1,0:T(8,128)(2,1)} %pad_maximum_fusion.1), channel_id=1, source_target_pairs={{0,1},{1,0},{2,3},{3,2},{4,5},{5,4},{6,7},{7,6},{8,9},{9,8},{10,11... | collective-permute-start | bytes 6291464 | tf_op jit(solution)/shard_map/ppermute | solution.py:500
  381.4 61.4 %collective-permute-start.30 = (bf16[512,2304]{1,0:T(8,128)(2,1)}, bf16[512,2304]{1,0:T(8,128)(2,1)}, u32[]{:S(2)}, u32[]{:S(2)}) collective-permute-start(bf16[512,2304]{1,0:T(8,128)(2,1)} %get-tuple-element.238), channel_id=1, source_target_pairs={{0,4},{4,0},{8,12},{12,8},{16,20},{20,16},{24,28},{28,24},{1,5},{5... | collective-permute-start | bytes 7077896 | tf_op jit(solution)/shard_map/ppermute | solution.py:503
  387.1 129.3 %reduce-scatter.15.cloned.1.call-start = ((), (), s32[]{:S(2)}) async-start(), calls=%async_computation.10 | async-start | bytes 2949120 | tf_op jit(solution)/shard_map/reduce_scatter | solution.py:453
  391.2 51.6 %collective-permute-start.29 = (bf16[128,1536]{1,0:T(8,128)(2,1)S(1)}, bf16[128,1536]{1,0:T(8,128)(2,1)S(1)}, u32[]{:S(2)}, u32[]{:S(2)}) collective-permute-start(bf16[128,1536]{1,0:T(8,128)(2,1)S(1)} %copy-done.110), channel_id=1, source_target_pairs={{0,4},{4,0},{8,12},{12,8},{16,20},{20,16},{24,28},{28,24},{1,5},{5... | collective-permute-start | bytes 1179656 | tf_op jit(solution)/shard_map/ppermute | solution.py:503
  452.0 48.6 %collective-permute-start.31 = (bf16[512,2048]{1,0:T(8,128)(2,1)}, bf16[512,2048]{1,0:T(8,128)(2,1)}, u32[]{:S(2)}, u32[]{:S(2)}) collective-permute-start(bf16[512,2048]{1,0:T(8,128)(2,1)} %pad_maximum_fusion.2), channel_id=1, source_target_pairs={{0,1},{1,0},{2,3},{3,2},{4,5},{5,4},{6,7},{7,6},{8,9},{9,8},{10,11... | collective-permute-start | bytes 6291464 | tf_op jit(solution)/shard_map/ppermute | solution.py:500
  460.6 44.6 %collective-permute-start.33 = (f32[512,1024]{1,0:T(8,128)}, f32[512,1024]{1,0:T(8,128)}, u32[]{:S(2)}, u32[]{:S(2)}) collective-permute-start(f32[512,1024]{1,0:T(8,128)} %get-tuple-element.298), channel_id=1, source_target_pairs={{0,2},{2,0},{1,3},{3,1},{4,6},{6,4},{5,7},{7,5},{8,10},{10,8},{9,1... | collective-permute-start | bytes 6291464 | tf_op jit(solution)/shard_map/ppermute | solution.py:497
  (136 other events, 697.1 us)
Sparse Core Ops, SparseCore 0:
  155.3 35.8 reduce-scatter.6
  194.2 36.0 reduce-scatter.8
  254.2 56.7 reduce-scatter.10
  323.8 35.8 reduce-scatter.12
  387.2 52.7 reduce-scatter.16
  460.8 48.0 reduce-scatter.14

commit v6 on v5

--- a/solution.py
+++ b/solution.py
@@ -85,9 +85,10 @@
 
 
 def attend_kernel(
-    group, row_ref, q_ref, cos_ref, sin_ref, start_ref, own_ref, other_ref, o_ref, lse_ref, qt_ref, bias, keys, values_t
+    row_ref, q_ref, cos_ref, sin_ref, start_ref, own_ref, other_ref, o_ref, lse_ref, qt_ref, bias, keys, values_t
 ):
     step = pl.program_id(0)
+    kv = step // 4
     row = row_ref[0]
 
     @pl.when(step == 0)
@@ -96,9 +97,11 @@
 
         def put(i, block):
             span = slice(i * CHUNK, (i + 1) * CHUNK)
-            lanes = slice(group * HEAD_SIZE, (group + 1) * HEAD_SIZE)
-            keys[span, :] = block[:, lanes]
-            values_t[:, span] = jnp.transpose(block[:, PAIR:].astype(F32)).astype(BF16)[lanes]
+            for h in range(2):
+                keys[h, span, :] = block[:, h * HEAD_SIZE : (h + 1) * HEAD_SIZE]
+            turned = jnp.transpose(block[:, PAIR:].astype(F32)).astype(BF16)
+            for h in range(2):
+                values_t[h, :, span] = turned[h * HEAD_SIZE : (h + 1) * HEAD_SIZE]
 
         place_keys(own_ref, other_ref, row, put)
 
@@ -116,11 +119,11 @@
         outs, sums = [], []
         for h in range(2):
             query = qt_ref[h * HEAD_SIZE : (h + 1) * HEAD_SIZE, lanes]
-            scores = dot_plain(keys[:count, :], query) + bias[:count, lanes]
+            scores = dot_plain(keys[kv, :count, :], query) + bias[:count, lanes]
             top = jnp.max(scores, axis=0, keepdims=True)
             expo = jnp.exp(scores - top)
             total = jnp.sum(expo, axis=0, keepdims=True)
-            head = dot_plain(values_t[:, :count], expo.astype(BF16))
+            head = dot_plain(values_t[kv, :, :count], expo.astype(BF16))
             outs.append(head * (1.0 / total))
             sums.append(top + jnp.log(total))
         o_ref[lanes, :] = jnp.transpose(jnp.concatenate(outs, axis=0)).astype(BF16)
@@ -137,15 +140,16 @@
         unit(1, 3)
 
 
-def attend(group, row, q, cosine, sine, start, own_kv, other_kv):
-    pairs = q.shape[1] // (2 * PAIR)
+def attend(row, q, cosine, sine, start, own_kv, other_kv):
+    heads = q.shape[1] // HEAD_SIZE
+    pairs = heads // 2
     whole = lambda shape: pl.BlockSpec(shape, lambda i: (0,) * len(shape))
     return pl.pallas_call(
-        functools.partial(attend_kernel, group),
+        attend_kernel,
         grid=(pairs,),
         in_specs=[
             pl.BlockSpec(memory_space=pltpu.SMEM),
-            pl.BlockSpec((OWN, PAIR), lambda i: (0, i + group * pairs)),
+            pl.BlockSpec((OWN, PAIR), lambda i: (0, i)),
             whole((HALF, OWN)),
             whole((HALF, OWN)),
             whole((1, OWN)),
@@ -158,17 +162,17 @@
             pl.BlockSpec((PAIR, OWN), lambda i: (i, 0)),
         ],
         out_shape=[
-            jax.ShapeDtypeStruct((OWN, pairs * PAIR), BF16),
+            jax.ShapeDtypeStruct((OWN, heads * HEAD_SIZE), BF16),
             jax.ShapeDtypeStruct((pairs, 2, OWN), F32),
-            jax.ShapeDtypeStruct((pairs * PAIR, OWN), BF16),
+            jax.ShapeDtypeStruct((heads * HEAD_SIZE, OWN), BF16),
         ],
         scratch_shapes=[
             pltpu.VMEM((SEQ, OWN), F32),
-            pltpu.VMEM((SEQ, HEAD_SIZE), BF16),
-            pltpu.VMEM((HEAD_SIZE, SEQ), BF16),
-        ],
-        compiler_params=pltpu.CompilerParams(vmem_limit_bytes=40 * 1024 * 1024),
-        cost_estimate=pl.CostEstimate(flops=10_000_000_000, bytes_accessed=4_000_000, transcendentals=0),
+            pltpu.VMEM((2, SEQ, HEAD_SIZE), BF16),
+            pltpu.VMEM((2, HEAD_SIZE, SEQ), BF16),
+        ],
+        compiler_params=pltpu.CompilerParams(vmem_limit_bytes=60 * 1024 * 1024),
+        cost_estimate=pl.CostEstimate(flops=20_000_000_000, bytes_accessed=8_000_000, transcendentals=0),
         name="attend",
     )(row, q, cosine, sine, start, own_kv, other_kv)
 
@@ -289,8 +293,8 @@
             pltpu.VMEM((2, HEAD_SIZE, SEQ), BF16),
             pltpu.VMEM((2, SEQ, HEAD_SIZE), BF16),
         ],
-        compiler_params=pltpu.CompilerParams(vmem_limit_bytes=40 * 1024 * 1024),
-        cost_estimate=pl.CostEstimate(flops=20_000_000_000, bytes_accessed=8_000_000, transcendentals=0),
+        compiler_params=pltpu.CompilerParams(vmem_limit_bytes=60 * 1024 * 1024),
+        cost_estimate=pl.CostEstimate(flops=1000, bytes_accessed=1000, transcendentals=0),
         name="attend_back",
     )(row, qt, d_o, o, lse, cosine, sine, start, own_kv, other_kv)
 
@@ -322,7 +326,7 @@
         in_specs=[full] * 4 + [column] * 4 + [line] * 2,
         out_specs=out,
         out_shape=jax.ShapeDtypeStruct((3, rows, wide), BF16),
-        compiler_params=pltpu.CompilerParams(vmem_limit_bytes=48 * 1024 * 1024),
+        compiler_params=pltpu.CompilerParams(vmem_limit_bytes=60 * 1024 * 1024),
         cost_estimate=pl.CostEstimate(flops=12 * rows * depth * wide, bytes_accessed=12 * depth * wide, transcendentals=0),
         name="hidden_units",
     )(xm, xo, cm, co, gm, go, um, uo, dm, do)
@@ -355,7 +359,7 @@
         in_specs=[full(a), full(b), line_m, line_m, line_o, line_o],
         out_specs=pl.BlockSpec((rows, tile), lambda i: (0, i)),
         out_shape=jax.ShapeDtypeStruct((rows, 2 * depth), BF16),
-        compiler_params=pltpu.CompilerParams(vmem_limit_bytes=48 * 1024 * 1024),
+        compiler_params=pltpu.CompilerParams(vmem_limit_bytes=60 * 1024 * 1024),
         cost_estimate=pl.CostEstimate(flops=8 * rows * depth * wide, bytes_accessed=8 * depth * wide, transcendentals=0),
         name="input_grad",
     )(a, b, gm, um, go, uo)
@@ -395,10 +399,61 @@
         in_specs=[pl.BlockSpec((rows, tokens), lambda i: (0, 0))] * len(pieces) + owns + others,
         out_specs=[pl.BlockSpec((rows // 2, tile), lambda i: (0, i))] * 2,
         out_shape=[jax.ShapeDtypeStruct((rows // 2, first * tile), BF16)] * 2,
-        compiler_params=pltpu.CompilerParams(vmem_limit_bytes=40 * 1024 * 1024),
+        compiler_params=pltpu.CompilerParams(vmem_limit_bytes=60 * 1024 * 1024),
         cost_estimate=pl.CostEstimate(flops=4 * rows * tokens * first * tile, bytes_accessed=6 * rows * first * tile, transcendentals=0),
         name="product",
     )(*[p[0] for p in pieces], *[p[1] for p in pieces], *[p[2] for p in pieces])
+
+
+def blend_kernel(sizes, halves, counts, transposed, *refs):
+    total_a = sum(len(g) for g in sizes)
+    a_refs, w_refs, out_ref = refs[:total_a], refs[total_a:-1], refs[-1]
+    step, first = pl.program_id(0), 0
+    for half in range(halves):
+
+        @pl.when((step >= first) & (step < first + counts[half]))
+        def _(half=half):
+            total, at = None, 0
+            for g, group in enumerate(sizes):
+                w, low = w_refs[half * len(sizes) + g], 0
+                for size in group:
+                    if transposed:
+                        part = dot_right(a_refs[at][0], w[:, low : low + size])
+                    else:
+                        part = dot_plain(a_refs[at][0], w[low : low + size, :])
+                    total = part if total is None else total + part
+                    low, at = low + size, at + 1
+            out_ref[...] = total.astype(out_ref.dtype)
+
+        first += counts[half]
+
+
+def blend(groups, weights, transposed, dtype, flops=1000):
+    tile = 256
+    arrays = [v if v.ndim == 3 else v[None] for g in groups for v in g]
+    sizes = [[v.shape[-1] for v in g] for g in groups]
+    rows = arrays[0].shape[1]
+    counts = [ws[0].shape[0 if transposed else 1] // tile for ws in weights]
+    specs = [pl.BlockSpec((1, rows, v.shape[2]), lambda i: (0, 0, 0)) for v in arrays]
+    first = 0
+    for ws, count in zip(weights, counts):
+        for w in ws:
+            place = lambda i, first=first, count=count: jnp.clip(i - first, 0, count - 1)
+            if transposed:
+                specs.append(pl.BlockSpec((tile, w.shape[1]), lambda i, place=place: (place(i), 0)))
+            else:
+                specs.append(pl.BlockSpec((w.shape[0], tile), lambda i, place=place: (0, place(i))))
+        first += count
+    return pl.pallas_call(
+        functools.partial(blend_kernel, sizes, len(weights), counts, transposed),
+        grid=(first,),
+        in_specs=specs,
+        out_specs=pl.BlockSpec((rows, tile), lambda i: (0, i)),
+        out_shape=jax.ShapeDtypeStruct((rows, first * tile), dtype),
+        compiler_params=pltpu.CompilerParams(vmem_limit_bytes=60 * 1024 * 1024),
+        cost_estimate=pl.CostEstimate(flops=flops, bytes_accessed=1000, transcendentals=0),
+        name="blend",
+    )(*arrays, *[w for ws in weights for w in ws])
 
 
 def sided_kernel(side_ref, own_ref, other_ref, out_ref):
@@ -427,8 +482,8 @@
             ),
         ),
         out_shape=jax.ShapeDtypeStruct((wide, 2 * tokens), BF16),
-        compiler_params=pltpu.CompilerParams(vmem_limit_bytes=40 * 1024 * 1024),
-        cost_estimate=pl.CostEstimate(flops=1000, bytes_accessed=8 * tokens * wide, transcendentals=0),
+        compiler_params=pltpu.CompilerParams(vmem_limit_bytes=60 * 1024 * 1024),
+        cost_estimate=pl.CostEstimate(flops=1000, bytes_accessed=1000, transcendentals=0),
         name="sided",
     )(side.astype(jnp.int32).reshape(1), own, other)
 
@@ -502,8 +557,8 @@
     def flip(value):
         return lax.ppermute(value, "dp", [(i, i ^ 1) for i in range(count)])
 
-    half = w_o.shape[0] // 2
-    far_a = cross(jnp.where(low, w_o[:half], w_o[half:]))
+    part_rows = w_o.shape[0] // 4
+    far_0 = cross(w_o[:part_rows])
     x_m = own_rows(tokens, row)
     x_o = swap(other_rows(tokens, row))
     wkv = jnp.concatenate([key_weight, value_weight], axis=1)
@@ -511,7 +566,8 @@
     wq_o = swap(query_weight)
     gains = jnp.stack([g_attn, g_mlp])
     gains_o = swap(gains)
-    x_o, wkv_o, wq_o, gains_o = tie(x_o, wkv_o, wq_o, gains_o)
+    x_o, wkv_o, wq_o, gains_o, far_0, w_o = tie(x_o, wkv_o, wq_o, gains_o, far_0, w_o)
+    far_1 = cross(w_o[part_rows : 2 * part_rows])
     x_m, x_o = x_m.astype(F32), x_o.astype(F32)
     square = jnp.sum(x_m * x_m, axis=-1, keepdims=True) + jnp.sum(x_o * x_o, axis=-1, keepdims=True)
     inv_one = lax.rsqrt(square / MODEL_WIDTH + EPS)
@@ -541,42 +597,28 @@
     cotangent, w_gate, w_up, w_down, w_o, xn_o = tie(cotangent, w_gate, w_up, w_down, w_o, xn_o)
     wg_o = swap(w_gate)
     wu_o = swap(w_up)
+    row_arg = row.astype(jnp.int32).reshape(1)
+    start_arg = start_own.reshape(1, OWN)
+    q, other_kv, far_1, w_o = tie(q, other_kv, far_1, w_o)
+    far_2 = cross(w_o[2 * part_rows :])
+    o, lse, qt = attend(row_arg, q, cosine_t, sine_t, start_arg, own_kv, other_kv)
+    o, far_2, w_o, w_down, cotangent, wg_o, wu_o = tie(o, far_2, w_o, w_down, cotangent, wg_o, wu_o)
     w_o_o = swap(w_o)
+    far = jnp.concatenate([far_0, far_1, far_2], axis=0)
+    o_x = cross(o)
+
     c_m = own_rows(cotangent, row)
     c_t = other_rows(cotangent, row)
-    q, far_a, other_kv, c_m, c_t = tie(q, far_a, other_kv, c_m, c_t)
-    far_b = flip(far_a)
-    row_arg = row.astype(jnp.int32).reshape(1)
-    start_arg = start_own.reshape(1, OWN)
-    o_1, lse_1, qt_1 = attend(0, row_arg, q, cosine_t, sine_t, start_arg, own_kv, other_kv)
-    o_1, q, wg_o, wu_o, w_o_o, w_down, c_t, far_a = tie(o_1, q, wg_o, wu_o, w_o_o, w_down, c_t, far_a)
-    o_x1 = cross(o_1)
     c_o = swap(c_t)
+    far_o = swap(far)
     wd_o = swap(w_down)
-    far_ao = swap(far_a)
-    o_2, lse_2, qt_2 = attend(1, row_arg, q, cosine_t, sine_t, start_arg, own_kv, other_kv)
-    o_2, o_1, c_o, wd_o, far_ao, xn_o = tie(o_2, o_1, c_o, wd_o, far_ao, xn_o)
-    o_x2 = cross(o_2)
-
-    near_m = dot_plain(o_1, w_o[:half]) + dot_plain(o_2, w_o[half:])
-    near_o = dot_plain(o_1, w_o_o[:half]) + dot_plain(o_2, w_o_o[half:])
+    near = blend([[o]], [[w_o], [w_o_o]], False, F32)
     both = lambda own, other: jnp.concatenate([own, other], axis=0)
     c_y = sided(c_m, c_t, side, count)
-    o = jnp.concatenate([o_1, o_2], axis=1)
-    o_t = swap(o)
-    qt = jnp.concatenate([qt_1, qt_2], axis=0)
-    lse = jnp.concatenate([lse_1, lse_2], axis=0)
-    near_m, near_o, far_b = tie(near_m, near_o, far_b)
-    far_bo = swap(far_b)
-    xn_t = swap(xn_o)
-    c_y, qt, lse, far_b, far_bo, o_x1 = tie(c_y, qt, lse, far_b, far_bo, o_x1)
-    pick = lambda a, b: (jnp.where(low, a, b), jnp.where(low, b, a))
-    far_1, far_2 = pick(far_a, far_b)
-    far_1o, far_2o = pick(far_ao, far_bo)
-    mid_m, mid_o = dot_plain(o_x1, far_1), dot_plain(o_x1, far_1o)
-    mid_m, mid_o, o_t, xn_t, o_x2 = tie(mid_m, mid_o, o_t, xn_t, o_x2)
-    hidden_m = x_m + (near_m + (mid_m + dot_plain(o_x2, far_2)))
-    hidden_o = x_o + (near_o + (mid_o + dot_plain(o_x2, far_2o)))
+    near, c_y, c_o, far_o, o_x, wd_o = tie(near, c_y, c_o, far_o, o_x, wd_o)
+    width = tokens.shape[1]
+    total = near + blend([[o_x]], [[far], [far_o]], False, F32)
+    hidden_m, hidden_o = x_m + total[:, :width], x_o + total[:, width:]
     square = jnp.sum(hidden_m * hidden_m, axis=-1, keepdims=True) + jnp.sum(
         hidden_o * hidden_o, axis=-1, keepdims=True
     )
@@ -590,9 +632,10 @@
     operands = (c_m, c_o, w_gate, wg_o, w_up, wu_o, w_down, wd_o)
     one = hidden_units(0, tiles - tiles // 2, xn2_m, xn2_o, *operands)
     one_t = swap(one)
-    one, xn2_m2 = tie(one, xn2_m)
+    one, xn2_m2, o_late, xn_o = tie(one, xn2_m, o, xn_o)
+    o_t, xn_t = swap(o_late), swap(xn_o)
     two = hidden_units(tiles - tiles // 2, tiles // 2, xn2_m2, xn2_o, *operands)
-    two, one_t, xn2_t = tie(two, one_t, xn2_t)
+    two, one_t, xn2_t, o_t, xn_t = tie(two, one_t, xn2_t, o_t, xn_t)
     two_t = swap(two)
 
     two, xn2_m2 = tie(two, xn2_m2)
@@ -610,9 +653,11 @@
     came = cross(part)
     send_2 = Summed([(xn2_y, one, one_t, 1)], flip, count)
     send_2.begin(part)
-    send_3 = Summed([(xn2_y, two, two_t, 1), (xn2_y, two, two_t, 2)], flip, count)
+    send_3 = Summed([(xn2_y, two, two_t, 1)], flip, count)
     send_3.begin(send_2.keep)
-    came, first_z.send, part = tie(came, first_z.send, part, send_3.keep)[:3]
+    send_4 = Summed([(xn2_y, two, two_t, 2)], flip, count)
+    send_4.begin(send_3.keep)
+    came, first_z.send, part = tie(came, first_z.send, part, send_4.keep)[:3]
     came = serve(came, (send_1,))
     send_2.go(send_1)
     came, _ = tie(came, send_1.finish())
@@ -630,13 +675,17 @@
     d_hid_o = c_o.astype(F32) + inv_two * (e_o - unit_o * mean)
     dh_m, dh_o = d_hid_m.astype(BF16), d_hid_o.astype(BF16)
     dh_t = swap(dh_o)
-    d_o = (dot_right(dh_m, w_o) + dot_right(dh_o, w_o_o)).astype(BF16)
-    d_o, dh_t, first_z.keep = tie(d_o, dh_t, first_z.keep)
+    d_o = blend([[dh_m], [dh_o]], [[w_o, w_o_o]], True, BF16)
+    dh_y, xn_y = sided(dh_m, dh_t, side, count), sided(xn_m, xn_t, side, count)
+    d_o, dh_y, xn_y, first_z.keep = tie(d_o, dh_y, xn_y, first_z.keep)
     d_o = serve(d_o, (send_2,))
     send_3.go(send_2)
     d_o, _ = tie(d_o, send_2.finish())
 
     d_q, d_k, d_v = attend_back(row_arg, qt, d_o, o, lse, cosine_t, sine_t, start_arg, own_kv, other_kv)
+    d_q = serve(d_q, (send_3,))
+    send_4.go(send_3)
+    d_q, d_k, _ = tie(d_q, d_k, send_3.finish())
     d_kv = jnp.concatenate([d_k[0], d_k[1], d_v[0], d_v[1]], axis=1)
     d_kv_t = swap(other_rows(d_kv, row))
     d_kv_own = own_rows(d_kv, row)
@@ -647,44 +696,31 @@
     d_kv = jnp.concatenate([d_key.reshape(OWN, narrow).astype(BF16), d_kv[:, narrow:].astype(BF16)], axis=1)
     d_qkv = jnp.concatenate([d_q, d_kv], axis=1)
     d_qkv_t = swap(d_qkv)
-    last = jnp.concatenate(
-        [
-            (dot_right(d_q, query_weight) + dot_right(d_kv, wkv)).astype(BF16),
-            (dot_right(d_q, wq_o) + dot_right(d_kv, wkv_o)).astype(BF16),
-        ],
-        axis=1,
-    )
+    last = blend([[d_q], [d_kv]], [[query_weight, wkv], [wq_o, wkv_o]], True, BF16)
     last, d_qkv_t = tie(last, d_qkv_t)
     last_came = cross(last)
     last, send_1.total = tie(last, send_1.total)
+    last = serve(last, (send_4,))
+    last, _ = tie(last, send_4.finish())
     send_5 = Summed(
         [
-            (sided(dh_m, dh_t, side, count), o[None], o_t[None], 0),
-            (sided(xn_m, xn_t, side, count), d_qkv[None], d_qkv_t[None], 0),
+            (dh_y, o[None], o_t[None], 0),
+            (xn_y, d_qkv[None], d_qkv_t[None], 0),
         ],
         flip,
         count,
     )
     send_5.begin(last)
     one, send_5.keep = tie(one, send_5.keep)
-    one = serve(one, (send_3,))
-    send_5.go(send_3)
-    first_z.go(send_3)
-    one, _ = tie(one, send_3.finish())
-    cut = one.shape[2]
-    mix = jnp.concatenate(
-        [
-            (dot_plain(one[0], w_down[:cut]) + dot_plain(two[0], w_down[cut:])).astype(BF16),
-            (dot_plain(one[0], wd_o[:cut]) + dot_plain(two[0], wd_o[cut:])).astype(BF16),
-        ],
-        axis=1,
-    )
-
-    last_came, mix, send_2.total = tie(last_came, mix, send_2.total)
-    last_came, first_z.came = tie(last_came, first_z.came)
+    one, send_2.total = tie(one, send_2.total)
+    send_5.go()
+    first_z.go()
+    mix = blend([[one, two]], [[w_down], [wd_o]], False, BF16)
+
+    last_came, mix, send_3.total = tie(last_came, mix, send_3.total)
+    mix_came = cross(mix)
     last_came = serve(last_came, (send_5,))
-    last_came, mix, _ = tie(last_came, mix, send_5.finish())
-    mix_came = cross(mix)
+    last_came, _ = tie(last_came, send_5.finish())
     d_xn = last.astype(F32) + last_came.astype(F32)
     d_xn_m, d_xn_o = d_xn[:, :width], d_xn[:, width:]
     unit_m, unit_o = x_m * inv_one, x_o * inv_one
@@ -701,6 +737,7 @@
     for bit in range(count.bit_length() - 1):
         gg = gg + lax.ppermute(gg, "dp", [(i, i ^ (1 << bit)) for i in range(count)])
     gg = lax.dynamic_slice_in_dim(gg, lax.axis_index("dp") * (width // count), width // count, axis=1)
+    d_tok_t, send_5.total = tie(d_tok_t, send_5.total)
     d_tokens = merge_rows(d_tok_m, d_tok_t, row)
 
     mixed_all = mix.astype(F32) + mix_came.astype(F32)
@@ -709,12 +746,11 @@
     mixed = merge_rows(out_m, swap(out_o), row)
 
     first_z.total = first_z.keep.astype(F32) + first_z.came.astype(F32)
-    got = [h.total.astype(F32) for h in (send_1, send_2, send_3, first_z, send_5)]
-    rest = two.shape[2]
+    got = [h.total.astype(F32) for h in (send_1, send_2, send_3, first_z, send_4, send_5)]
     gw_down = got[0].T
-    gw_gate = jnp.concatenate([got[1], got[2][:, :rest]], axis=1)
-    gw_up = jnp.concatenate([got[3], got[2][:, rest:]], axis=1)
-    gw_o, gw_qkv = got[4][:, : o.shape[1]].T, got[4][:, o.shape[1] :]
+    gw_gate = jnp.concatenate([got[1], got[2]], axis=1)
+    gw_up = jnp.concatenate([got[3], got[4]], axis=1)
+    gw_o, gw_qkv = got[5][:, : o.shape[1]].T, got[5][:, o.shape[1] :]
     return (
         mixed,
         d_tokens,

time: 535 us -> 522 us (0.976)
  Pallas kernels: 139 us -> 220 us
  matrix products: 53.3 us -> 8.27 us
  waiting for transfers between devices: 165 us -> 137 us
  local copies, waits for them, and re-layouts: 52 us -> 27.1 us
    pallas_call x2 -> x6, Pallas kernels: 20.1 us -> 67 us  [the longest x5 45.5 us: blend(): pl.pallas_call(functools.partial(blend_kernel, sizes, len(weights), count...]
    ppermute x6, waiting for transfers between devices: 77.9 us -> 35.2 us  [flip(): return lax.ppermute(value, 'dp', [(i, i ^ 1) for i in range(count)])]
    unnamed x236 -> x99, local copies, waits for them, and re-layouts: 47.2 us -> 8.8 us
    dot_general x16 -> x4, matrix products: 38 us -> 8.27 us  [dot_plain(): return jnp.dot(left, right, preferred_element_type=F32)]
    dot_general x6 -> x0, matrix products: 15.3 us -> none  [dot_right(): lax.dot_general(left, right, (((1,), (1,)), ((), ())), preferred_element_...]
    pallas_call x4, Pallas kernels: 9.86 us -> 24.7 us  [sided(): pl.pallas_call(sided_kernel, grid_spec=pltpu.PrefetchScalarGridSpec(num_s...]
    pallas_call x5 -> x6, Pallas kernels: 43 us -> 56.3 us  [product(): pl.pallas_call(functools.partial(product_kernel, counts), grid=(first,),...]
    ppermute x6 -> x7, waiting for transfers between devices: 85 us -> 96.7 us  [cross(): return lax.ppermute(value, 'col', [(0, 1), (1, 0)])]
  transfers between devices with their start and end apart: 44 -> 45, of which waited for: 11 -> 15; matrix products, arithmetic and copies ran while one was open for 23% -> 17% of each run, Pallas kernels for 24% -> 38%
where the time goes in v6:
time: 522 us; the launch traced here: 513 us
  Pallas kernels  220 us (42%)
  waiting for transfers between devices  137 us (26%)
  other arithmetic  77.3 us (15%)
  starting transfers between devices  27.8 us (5%)
  local copies, waits for them, and re-layouts  27.1 us (5%)
  between operations  15.4 us (3%)
  matrix products  8.27 us (2%)
    ppermute x7, waiting for transfers between devices, cross(): return lax.ppermute(value, 'col', [(0, 1), (1, 0)])  96.7 us
    pallas_call x6, Pallas kernels, product(): pl.pallas_call(functools.partial(product_kernel, counts), grid=(first,),...  56.3 us
    pallas_call x5, Pallas kernels, blend(): pl.pallas_call(functools.partial(blend_kernel, sizes, len(weights), count...  45.5 us
    ppermute x6, waiting for transfers between devices, flip(): return lax.ppermute(value, 'dp', [(i, i ^ 1) for i in range(count)])  35.2 us
    pallas_call x2, Pallas kernels, hidden_units(): pl.pallas_call(hidden_units_kernel, grid=(tiles,), in_specs=[full] * 4 +...  30.6 us
    pallas_call x4, Pallas kernels, sided(): pl.pallas_call(sided_kernel, grid_spec=pltpu.PrefetchScalarGridSpec(num_s...  24.7 us
    pallas_call x1, Pallas kernels, attend(): pl.pallas_call(attend_kernel, grid=(pairs,), in_specs=[pl.BlockSpec(memor...  21.6 us
    pallas_call x1, Pallas kernels, attend_back(): pl.pallas_call(attend_back_kernel, grid=(pairs,), in_specs=[pl.BlockSpec(...  20.8 us
  transfers between devices with their start and end apart: 45, of which 15 were waited for; matrix products, arithmetic and copies ran while one was open for 17% of the time, Pallas kernels for 38%

profile of v6, /device:TPU:0, one launch (start us, length us, event | category | flops | bytes accessed | tf_op | source)
XLA Modules:
  0.0 513.5 jit_solution(5211843740819063580)
XLA Ops:
  51.6 21.6 %attend.1 = (bf16[512,1024]{1,0:T(8,128)(2,1)}, f32[8,2,512]{2,1,0:T(2,128)}, bf16[1024,512]{1,0:T(8,128)(2,1)}) custom-call(s32[1]{0:T(128)} %bitcast.row_ref, f32[512,1024]{1,0:T(8,128)} %convolution_add_fusion.q_ref, f32[32,512]{1,0:T(8,128)} %get-tuple-element.334.cos_ref, f32[32,512]{1,0:T(8,128)} %get-tuple-element.333.sin_ref, s32[1,512]{1,0:T(1,128)} %bitcast.71, ...), custom_call_target="tpu_custom_call" | custom-call | flops 20000000000 | bytes 8000000 | tf_op jit(solution)/shard_map/attend/pallas_call | solution.py:147
  93.0 8.5 %blend.5 = f32[512,2048]{1,0:T(8,128)} custom-call(bf16[1,512,1024]{2,1,0:T(8,128)(2,1)} %bitcast.7.refs_0_.refs_2_, bf16[1024,1024]{1,0:T(8,128)(2,1)} %refs_2_.1, bf16[1024,1024]{1,0:T(8,128)(2,1)} %collective-permute-done.10.refs_2_.refs_3_), custom_call_target="tpu_custom_call" | custom-call | flops 1000 | bytes 1000 | tf_op jit(solution)/shard_map/blend/pallas_call | solution.py:447
  106.4 8.6 %blend.6 = f32[512,2048]{1,0:T(8,128)} custom-call(bf16[1,512,1024]{2,1,0:T(8,128)(2,1)} %bitcast.9.refs_0_, bf16[1024,1024]{1,0:T(8,128)(2,1)} %constant_dynamic-update-slice_fusion.2.refs_1_, bf16[1024,1024]{1,0:T(8,128)(2,1)} %collective-permute-done.12.refs_2_), custom_call_target="tpu_custom_call" | custom-call | flops 1000 | bytes 1000 | tf_op jit(solution)/shard_map/blend/pallas_call | solution.py:447
  122.0 16.3 %hidden_units.2.refs_1_.refs_2_.a_ref.refs_0_ = bf16[3,512,1536]{2,1,0:T(8,128)(2,1)} custom-call(bf16[512,1024]{1,0:T(8,128)(2,1)} %get-tuple-element.163.xm_ref.own_ref, bf16[512,1024]{1,0:T(8,128)(2,1)} %get-tuple-element.337.xo_ref, bf16[512,1024]{1,0:T(8,128)(2,1)} %pad_maximum_fusion.6.own_ref.cm_ref, ...), custom_call_target="tpu_custom_call" | custom-call | flops 9663676416 | bytes 18874368 | tf_op jit(solution)/shard_map/hidden_units/pallas_call | solution.py:323
  139.3 14.3 %hidden_units.3.refs_3_.b_ref.refs_1_ = bf16[3,512,1280]{2,1,0:T(8,128)(2,1)} custom-call(bf16[512,1024]{1,0:T(8,128)(2,1)} %get-tuple-element.163.xm_ref.own_ref, bf16[512,1024]{1,0:T(8,128)(2,1)} %get-tuple-element.337.xo_ref, bf16[512,1024]{1,0:T(8,128)(2,1)} %pad_maximum_fusion.6.own_ref.cm_ref, bf16[512,1024]{1,0:T(8,128)(2,1)} %collective-permute-done.11.co_ref, ...), custom_call_target="tpu_custom_call" | custom-call | flops 8053063680 | bytes 15728640 | tf_op jit(solution)/shard_map/hidden_units/pallas_call | solution.py:323
  153.8 6.2 %sided.5.refs_0_ = bf16[1024,1024]{1,0:T(8,128)(2,1)} custom-call(s32[1]{0:T(128)} %bitcast.8.side_ref, bf16[512,1024]{1,0:T(8,128)(2,1)} %get-tuple-element.163.xm_ref.own_ref, bf16[512,1024]{1,0:T(8,128)(2,1)} %collective-permute-done.16.other_ref), custom_call_target="tpu_custom_call" | custom-call | flops 1000 | bytes 1000 | tf_op jit(solution)/shard_map/sided/pallas_call | solution.py:474
  159.9 8.3 %product.6 = (bf16[512,1536]{1,0:T(8,128)(2,1)}, bf16[512,1536]{1,0:T(8,128)(2,1)}) custom-call(bf16[1024,1024]{1,0:T(8,128)(2,1)} %sided.5.refs_0_, bf16[3,512,1536]{2,1,0:T(8,128)(2,1)} %hidden_units.2.refs_1_.refs_2_.a_ref.refs_0_, bf16[3,512,1536]{2,1,0:T(8,128)(2,1)} %collective-permute-done.15.refs_2_.refs_4_), custom_call_target="tpu_custom_call" | custom-call | flops 6442450944 | bytes 9437184 | tf_op jit(solution)/shard_map/product/pallas_call | solution.py:396
  168.3 13.7 %product.7 = (bf16[512,2816]{1,0:T(8,128)(2,1)}, bf16[512,2816]{1,0:T(8,128)(2,1)}) custom-call(bf16[1024,1024]{1,0:T(8,128)(2,1)} %sided.4.refs_0_.refs_1_, bf16[1024,1024]{1,0:T(8,128)(2,1)} %sided.4.refs_0_.refs_1_, bf16[3,512,1536]{2,1,0:T(8,128)(2,1)} %hidden_units.2.refs_1_.refs_2_.a_ref.refs_0_, ...), custom_call_target="tpu_custom_call" | custom-call | flops 11811160064 | bytes 17301504 | tf_op jit(solution)/shard_map/product/pallas_call | solution.py:396
  183.8 20.8 %input_grad.1 = bf16[512,2048]{1,0:T(8,128)(2,1)} custom-call(bf16[3,512,1536]{2,1,0:T(8,128)(2,1)} %hidden_units.2.refs_1_.refs_2_.a_ref.refs_0_, bf16[3,512,1280]{2,1,0:T(8,128)(2,1)} %hidden_units.3.refs_3_.b_ref.refs_1_, bf16[1024,2816]{1,0:T(8,128)(2,1)} %gm_ref.2, bf16[1024,2816]{1,0:T(8,128)(2,1)} %um_ref.2, ...), custom_call_target="tpu_custom_call" | custom-call | flops 11811160064 | bytes 23068672 | tf_op jit(solution)/shard_map/input_grad/pallas_call | solution.py:356
  206.1 8.1 %product.8 = (bf16[512,1536]{1,0:T(8,128)(2,1)}, bf16[512,1536]{1,0:T(8,128)(2,1)}) custom-call(bf16[1024,1024]{1,0:T(8,128)(2,1)} %sided.5.refs_0_, bf16[3,512,1536]{2,1,0:T(8,128)(2,1)} %hidden_units.2.refs_1_.refs_2_.a_ref.refs_0_, bf16[3,512,1536]{2,1,0:T(8,128)(2,1)} %collective-permute-done.15.refs_2_.refs_4_), custom_call_target="tpu_custom_call" | custom-call | flops 6442450944 | bytes 9437184 | tf_op jit(solution)/shard_map/product/pallas_call | solution.py:396
  214.2 7.2 %product.9 = (bf16[512,1280]{1,0:T(8,128)(2,1)}, bf16[512,1280]{1,0:T(8,128)(2,1)}) custom-call(bf16[1024,1024]{1,0:T(8,128)(2,1)} %sided.5.refs_0_, bf16[3,512,1280]{2,1,0:T(8,128)(2,1)} %hidden_units.3.refs_3_.b_ref.refs_1_, bf16[3,512,1280]{2,1,0:T(8,128)(2,1)} %collective-permute-done.19.refs_5_.refs_2_), custom_call_target="tpu_custom_call" | custom-call | flops 5368709120 | bytes 7864320 | tf_op jit(solution)/shard_map/product/pallas_call | solution.py:396
  221.4 7.3 %product.10 = (bf16[512,1280]{1,0:T(8,128)(2,1)}, bf16[512,1280]{1,0:T(8,128)(2,1)}) custom-call(bf16[1024,1024]{1,0:T(8,128)(2,1)} %sided.5.refs_0_, bf16[3,512,1280]{2,1,0:T(8,128)(2,1)} %hidden_units.3.refs_3_.b_ref.refs_1_, bf16[3,512,1280]{2,1,0:T(8,128)(2,1)} %collective-permute-done.19.refs_5_.refs_2_), custom_call_target="tpu_custom_call" | custom-call | flops 5368709120 | bytes 7864320 | tf_op jit(solution)/shard_map/product/pallas_call | solution.py:396
  228.7 23.8 %collective-permute-done.20 = bf16[512,2048]{1,0:T(8,128)(2,1)} collective-permute-done((bf16[512,2048]{1,0:T(8,128)(2,1)}, bf16[512,2048]{1,0:T(8,128)(2,1)}, u32[]{:S(2)}, u32[]{:S(2)}) %collective-permute-start.20) | collective-permute-done | bytes 2097184 | tf_op jit(solution)/shard_map/ppermute | solution.py:555
  268.0 6.2 %sided.7.refs_1_ = bf16[1024,1024]{1,0:T(8,128)(2,1)} custom-call(s32[1]{0:T(128)} %bitcast.8.side_ref, bf16[512,1024]{1,0:T(8,128)(2,1)} %copy-done.12, bf16[512,1024]{1,0:T(8,128)(2,1)} %collective-permute-done.18.other_ref), custom_call_target="tpu_custom_call" | custom-call | flops 1000 | bytes 1000 | tf_op jit(solution)/shard_map/sided/pallas_call | solution.py:474
  274.2 6.3 %blend.7.do_ref = bf16[512,1024]{1,0:T(8,128)(2,1)} custom-call(bf16[1,512,1024]{2,1,0:T(8,128)(2,1)} %bitcast.50, bf16[1,512,1024]{2,1,0:T(8,128)(2,1)} %bitcast.12.refs_1_, bf16[1024,1024]{1,0:T(8,128)(2,1)} %refs_2_.1, bf16[1024,1024]{1,0:T(8,128)(2,1)} %collective-permute-done.10.refs_2_.refs_3_), custom_call_target="tpu_custom_call" | custom-call | flops 1000 | bytes 1000 | tf_op jit(solution)/shard_map/blend/pallas_call | solution.py:447
  280.5 6.2 %sided.6.refs_0_ = bf16[1024,1024]{1,0:T(8,128)(2,1)} custom-call(s32[1]{0:T(128)} %bitcast.8.side_ref, bf16[512,1024]{1,0:T(8,128)(2,1)} %get-tuple-element.282.own_ref, bf16[512,1024]{1,0:T(8,128)(2,1)} %collective-permute-done.22.other_ref), custom_call_target="tpu_custom_call" | custom-call | flops 1000 | bytes 1000 | tf_op jit(solution)/shard_map/sided/pallas_call | solution.py:474
  286.7 7.0 %collective-permute-done.23 = bf16[512,1536]{1,0:T(8,128)(2,1)} collective-permute-done((bf16[512,1536]{1,0:T(8,128)(2,1)}, bf16[512,1536]{1,0:T(8,128)(2,1)}, u32[]{:S(2)}, u32[]{:S(2)}) %collective-permute-start.23) | collective-permute-done | bytes 1572896 | tf_op jit(solution)/shard_map/ppermute | solution.py:558
  297.5 20.8 %attend_back.1 = (bf16[512,1024]{1,0:T(8,128)(2,1)}, f32[2,1024,64]{2,1,0:T(8,128)}, f32[2,1024,64]{2,1,0:T(8,128)}) custom-call(s32[1]{0:T(128)} %bitcast.row_ref, bf16[1024,512]{1,0:T(8,128)(2,1)} %get-tuple-element.151.qt_ref, bf16[512,1024]{1,0:T(8,128)(2,1)} %blend.7.do_ref, bf16[512,1024]{1,0:T(8,128)(2,1)} %get-tuple-element.160.o_ref, ...), custom_call_target="tpu_custom_call" | custom-call | flops 1000 | bytes 1000 | tf_op jit(solution)/shard_map/attend_back/pallas_call | solution.py:265
  337.4 9.1 %blend.8 = bf16[512,2048]{1,0:T(8,128)(2,1)} custom-call(bf16[1,512,1024]{2,1,0:T(8,128)(2,1)} %bitcast.51, bf16[1,512,256]{2,1,0:T(8,128)(2,1)} %maximum_bitcast_fusion.refs_1_, bf16[1024,1024]{1,0:T(8,128)(2,1)} %refs_2_.2, bf16[1024,256]{1,0:T(8,128)(2,1)} %copy-done.21, bf16[1024,1024]{1,0:T(8,128)(2,1)} %collective-permute-done.2.refs_4_, ...), custom_call_target="tpu_custom_call" | custom-call | flops 1000 | bytes 1000 | tf_op jit(solution)/shard_map/blend/pallas_call | solution.py:447
  346.5 20.7 %collective-permute-done.28 = bf16[512,1280]{1,0:T(8,128)(2,1)} collective-permute-done((bf16[512,1280]{1,0:T(8,128)(2,1)}, bf16[512,1280]{1,0:T(8,128)(2,1)}, u32[]{:S(2)}, u32[]{:S(2)}) %collective-permute-start.28) | collective-permute-done | bytes 1310752 | tf_op jit(solution)/shard_map/ppermute | solution.py:558
  370.3 11.7 %product.11 = (bf16[512,2304]{1,0:T(8,128)(2,1)}, bf16[512,2304]{1,0:T(8,128)(2,1)}) custom-call(bf16[1024,1024]{1,0:T(8,128)(2,1)} %sided.6.refs_0_, bf16[1024,1024]{1,0:T(8,128)(2,1)} %sided.7.refs_1_, bf16[1,512,1024]{2,1,0:T(8,128)(2,1)} %bitcast.7.refs_0_.refs_2_, bf16[1,512,1280]{2,1,0:T(8,128)(2,1)} %get-tuple-element.313.refs_3_, ...), custom_call_target="tpu_custom_call" | custom-call | flops 9663676416 | bytes 14155776 | tf_op jit(solution)/shard_map/product/pallas_call | solution.py:396
  385.7 12.9 %blend.9 = bf16[512,2048]{1,0:T(8,128)(2,1)} custom-call(bf16[3,512,1536]{2,1,0:T(8,128)(2,1)} %hidden_units.2.refs_1_.refs_2_.a_ref.refs_0_, bf16[3,512,1280]{2,1,0:T(8,128)(2,1)} %hidden_units.3.refs_3_.b_ref.refs_1_, bf16[2816,1024]{1,0:T(8,128)(2,1)} %refs_2_.3, bf16[2816,1024]{1,0:T(8,128)(2,1)} %collective-permute-done.14.do_ref.refs_3_), custom_call_target="tpu_custom_call" | custom-call | flops 1000 | bytes 1000 | tf_op jit(solution)/shard_map/blend/pallas_call | solution.py:447
  398.6 31.2 %collective-permute-done.27 = bf16[512,2048]{1,0:T(8,128)(2,1)} collective-permute-done((bf16[512,2048]{1,0:T(8,128)(2,1)}, bf16[512,2048]{1,0:T(8,128)(2,1)}, u32[]{:S(2)}, u32[]{:S(2)}) %collective-permute-start.27) | collective-permute-done | bytes 2097184 | tf_op jit(solution)/shard_map/ppermute | solution.py:555
  452.0 24.0 %collective-permute-done.29 = bf16[512,2048]{1,0:T(8,128)(2,1)} collective-permute-done((bf16[512,2048]{1,0:T(8,128)(2,1)}, bf16[512,2048]{1,0:T(8,128)(2,1)}, u32[]{:S(2)}, u32[]{:S(2)}) %collective-permute-start.29) | collective-permute-done | bytes 2097184 | tf_op jit(solution)/shard_map/ppermute | solution.py:555
  (279 shorter events, 177.3 us)
Async XLA Ops:
  7.2 221.6 %reduce-scatter.8.cloned.1.call-start = ((), (), s32[]{:S(2)}) async-start(), calls=%async_computation.7 | async-start | bytes 1966080 | tf_op jit(solution)/shard_map/reduce_scatter | solution.py:508
  32.8 42.1 %collective-permute-start.8 = (bf16[1024,2816]{1,0:T(8,128)(2,1)}, bf16[1024,2816]{1,0:T(8,128)(2,1)}, u32[]{:S(2)}, u32[]{:S(2)}) collective-permute-start(bf16[1024,2816]{1,0:T(8,128)(2,1)} %gm_ref.2), channel_id=1, source_target_pairs={{0,2},{2,0},{1,3},{3,1},{4,6},{6,4},{5,7},{7,5},{8,10},{10,8},{9,1... | collective-permute-start | bytes 17301512 | tf_op jit(solution)/shard_map/ppermute | solution.py:552
  32.9 42.0 %collective-permute-start.9 = (bf16[1024,2816]{1,0:T(8,128)(2,1)}, bf16[1024,2816]{1,0:T(8,128)(2,1)}, u32[]{:S(2)}, u32[]{:S(2)}) collective-permute-start(bf16[1024,2816]{1,0:T(8,128)(2,1)} %um_ref.2), channel_id=1, source_target_pairs={{0,2},{2,0},{1,3},{3,1},{4,6},{6,4},{5,7},{7,5},{8,10},{10,8},{9,1... | collective-permute-start | bytes 17301512 | tf_op jit(solution)/shard_map/ppermute | solution.py:552
  49.9 25.0 %collective-permute-start.7 = (bf16[512,1024]{1,0:T(8,128)(2,1)}, bf16[512,1024]{1,0:T(8,128)(2,1)}, u32[]{:S(2)}, u32[]{:S(2)}) collective-permute-start(bf16[512,1024]{1,0:T(8,128)(2,1)} %slice.216), channel_id=1, source_target_pairs={{0,1},{1,0},{2,3},{3,2},{4,5},{5,4},{6,7},{7,6},{8,9},{9,8},{10,11... | collective-permute-start | bytes 3145736 | tf_op jit(solution)/shard_map/ppermute | solution.py:555
  74.9 31.4 %collective-permute-start.14 = (bf16[2816,1024]{1,0:T(8,128)(2,1)}, bf16[2816,1024]{1,0:T(8,128)(2,1)}, u32[]{:S(2)}, u32[]{:S(2)}) collective-permute-start(bf16[2816,1024]{1,0:T(8,128)(2,1)} %refs_2_.3), channel_id=1, source_target_pairs={{0,2},{2,0},{1,3},{3,1},{4,6},{6,4},{5,7},{7,5},{8,10},{10,8},{9,1... | collective-permute-start | bytes 17301512 | tf_op jit(solution)/shard_map/ppermute | solution.py:552
  80.5 25.9 %collective-permute-start.12 = (bf16[1024,1024]{1,0:T(8,128)(2,1)}, bf16[1024,1024]{1,0:T(8,128)(2,1)}, u32[]{:S(2)}, u32[]{:S(2)}) collective-permute-start(bf16[1024,1024]{1,0:T(8,128)(2,1)} %constant_dynamic-update-slice_fusion.2.refs_1_), channel_id=1, source_target_pairs={{0,2},{2,0},{1,3},{3,1},{4,6},{6,4},{5,7},{7,5},{8,10},{10,8},{9,1... | collective-permute-start | bytes 6291464 | tf_op jit(solution)/shard_map/ppermute | solution.py:552
  80.6 25.7 %collective-permute-start.13 = (bf16[512,1024]{1,0:T(8,128)(2,1)}, bf16[512,1024]{1,0:T(8,128)(2,1)}, u32[]{:S(2)}, u32[]{:S(2)}) collective-permute-start(bf16[512,1024]{1,0:T(8,128)(2,1)} %get-tuple-element.160.o_ref), channel_id=1, source_target_pairs={{0,1},{1,0},{2,3},{3,2},{4,5},{5,4},{6,7},{7,6},{8,9},{9,8},{10,11... | collective-permute-start | bytes 3145736 | tf_op jit(solution)/shard_map/ppermute | solution.py:555
  84.5 21.8 %collective-permute-start.11 = (bf16[512,1024]{1,0:T(8,128)(2,1)}, bf16[512,1024]{1,0:T(8,128)(2,1)}, u32[]{:S(2)}, u32[]{:S(2)}) collective-permute-start(bf16[512,1024]{1,0:T(8,128)(2,1)} %pad_maximum_fusion.7.other_ref), channel_id=1, source_target_pairs={{0,2},{2,0},{1,3},{3,1},{4,6},{6,4},{5,7},{7,5},{8,10},{10,8},{9,1... | collective-permute-start | bytes 3145736 | tf_op jit(solution)/shard_map/ppermute | solution.py:552
  168.2 118.5 %reduce-scatter.10.cloned.1.call-start = ((), (), s32[]{:S(2)}) async-start(), calls=%async_computation.8 | async-start | bytes 1966080 | tf_op jit(solution)/shard_map/reduce_scatter | solution.py:508
  181.9 70.7 %collective-permute-start.21 = (bf16[512,2816]{1,0:T(8,128)(2,1)}, bf16[512,2816]{1,0:T(8,128)(2,1)}, u32[]{:S(2)}, u32[]{:S(2)}) collective-permute-start(bf16[512,2816]{1,0:T(8,128)(2,1)} %get-tuple-element.182), channel_id=1, source_target_pairs={{0,4},{4,0},{8,12},{12,8},{16,20},{20,16},{24,28},{28,24},{1,5},{5... | collective-permute-start | bytes 8650760 | tf_op jit(solution)/shard_map/ppermute | solution.py:558
  183.8 162.8 %reduce-scatter.12.cloned.1.call-start = ((), (), s32[]{:S(2)}) async-start(), calls=%async_computation.9 | async-start | bytes 3604480 | tf_op jit(solution)/shard_map/reduce_scatter | solution.py:508
  204.6 48.0 %collective-permute-start.20 = (bf16[512,2048]{1,0:T(8,128)(2,1)}, bf16[512,2048]{1,0:T(8,128)(2,1)}, u32[]{:S(2)}, u32[]{:S(2)}) collective-permute-start(bf16[512,2048]{1,0:T(8,128)(2,1)} %input_grad.1), channel_id=1, source_target_pairs={{0,1},{1,0},{2,3},{3,2},{4,5},{5,4},{6,7},{7,6},{8,9},{9,8},{10,11... | collective-permute-start | bytes 6291464 | tf_op jit(solution)/shard_map/ppermute | solution.py:555
  257.6 128.1 %reduce-scatter.14.cloned.1.call-start = ((), (), s32[]{:S(2)}) async-start(), calls=%async_computation.10 | async-start | bytes 1966080 | tf_op jit(solution)/shard_map/reduce_scatter | solution.py:508
  257.6 36.0 %collective-permute-start.23 = (bf16[512,1536]{1,0:T(8,128)(2,1)}, bf16[512,1536]{1,0:T(8,128)(2,1)}, u32[]{:S(2)}, u32[]{:S(2)}) collective-permute-start(bf16[512,1536]{1,0:T(8,128)(2,1)} %get-tuple-element.192), channel_id=1, source_target_pairs={{0,4},{4,0},{8,12},{12,8},{16,20},{20,16},{24,28},{28,24},{1,5},{5... | collective-permute-start | bytes 4718600 | tf_op jit(solution)/shard_map/ppermute | solution.py:558
  293.6 29.4 %collective-permute-start.24 = (bf16[512,1280]{1,0:T(8,128)(2,1)}, bf16[512,1280]{1,0:T(8,128)(2,1)}, u32[]{:S(2)}, u32[]{:S(2)}) collective-permute-start(bf16[512,1280]{1,0:T(8,128)(2,1)} %get-tuple-element.200), channel_id=1, source_target_pairs={{0,4},{4,0},{8,12},{12,8},{16,20},{20,16},{24,28},{28,24},{1,5},{5... | collective-permute-start | bytes 3932168 | tf_op jit(solution)/shard_map/ppermute | solution.py:558
  297.5 101.1 %reduce-scatter.16.cloned.1.call-start = ((), (), s32[]{:S(2)}) async-start(), calls=%async_computation.11 | async-start | bytes 1638400 | tf_op jit(solution)/shard_map/reduce_scatter | solution.py:508
  335.9 31.4 %collective-permute-start.28 = (bf16[512,1280]{1,0:T(8,128)(2,1)}, bf16[512,1280]{1,0:T(8,128)(2,1)}, u32[]{:S(2)}, u32[]{:S(2)}) collective-permute-start(bf16[512,1280]{1,0:T(8,128)(2,1)} %get-tuple-element.212), channel_id=1, source_target_pairs={{0,4},{4,0},{8,12},{12,8},{16,20},{20,16},{24,28},{28,24},{1,5},{5... | collective-permute-start | bytes 3932168 | tf_op jit(solution)/shard_map/ppermute | solution.py:558
  336.6 154.2 %reduce-scatter.20.cloned.1.call-start = ((), (), s32[]{:S(2)}) async-start(), calls=%async_computation.13 | async-start | bytes 1638400 | tf_op jit(solution)/shard_map/reduce_scatter | solution.py:508
  382.0 54.5 %collective-permute-start.31 = (bf16[512,2304]{1,0:T(8,128)(2,1)}, bf16[512,2304]{1,0:T(8,128)(2,1)}, u32[]{:S(2)}, u32[]{:S(2)}) collective-permute-start(bf16[512,2304]{1,0:T(8,128)(2,1)} %get-tuple-element.225), channel_id=1, source_target_pairs={{0,4},{4,0},{8,12},{12,8},{16,20},{20,16},{24,28},{28,24},{1,5},{5... | collective-permute-start | bytes 7077896 | tf_op jit(solution)/shard_map/ppermute | solution.py:558
  382.7 47.1 %collective-permute-start.27 = (bf16[512,2048]{1,0:T(8,128)(2,1)}, bf16[512,2048]{1,0:T(8,128)(2,1)}, u32[]{:S(2)}, u32[]{:S(2)}) collective-permute-start(bf16[512,2048]{1,0:T(8,128)(2,1)} %blend.8), channel_id=1, source_target_pairs={{0,1},{1,0},{2,3},{3,2},{4,5},{5,4},{6,7},{7,6},{8,9},{9,8},{10,11... | collective-permute-start | bytes 6291464 | tf_op jit(solution)/shard_map/ppermute | solution.py:555
  384.3 111.5 %reduce-scatter.18.cloned.1.call-start = ((), (), s32[]{:S(2)}) async-start(), calls=%async_computation.12 | async-start | bytes 2949120 | tf_op jit(solution)/shard_map/reduce_scatter | solution.py:508
  384.3 61.0 %collective-permute-start.37 = (bf16[128,1536]{1,0:T(8,128)(2,1)}, bf16[128,1536]{1,0:T(8,128)(2,1)S(1)}, u32[]{:S(2)}, u32[]{:S(2)}) collective-permute-start(bf16[128,1536]{1,0:T(8,128)(2,1)} %reduce-scatter.8.cloned.1.call-done), channel_id=1, source_target_pairs={{0,4},{4,0},{8,12},{12,8},{16,20},{20,16},{24,28},{28,24},{1,5},{5... | collective-permute-start | bytes 1179656 | tf_op jit(solution)/shard_map/ppermute | solution.py:558
  429.8 46.2 %collective-permute-start.29 = (bf16[512,2048]{1,0:T(8,128)(2,1)}, bf16[512,2048]{1,0:T(8,128)(2,1)}, u32[]{:S(2)}, u32[]{:S(2)}) collective-permute-start(bf16[512,2048]{1,0:T(8,128)(2,1)} %blend.9), channel_id=1, source_target_pairs={{0,1},{1,0},{2,3},{3,2},{4,5},{5,4},{6,7},{7,6},{8,9},{9,8},{10,11... | collective-permute-start | bytes 6291464 | tf_op jit(solution)/shard_map/ppermute | solution.py:555
  450.3 35.3 %collective-permute-start.35 = (f32[2,1024]{1,0:T(2,128)S(1)}, f32[2,1024]{1,0:T(2,128)S(1)}, u32[]{:S(2)}, u32[]{:S(2)}) collective-permute-start(f32[2,1024]{1,0:T(2,128)S(1)} %fusion.40), channel_id=1, source_target_pairs={{0,8},{4,12},{8,0},{12,4},{16,24},{20,28},{24,16},{28,20},{1,9},{5... | collective-permute-start | bytes 24584 | tf_op jit(solution)/shard_map/ppermute | solution.py:738
  (68 other events, 511.9 us)
Sparse Core Ops, SparseCore 0:
  168.3 36.9 reduce-scatter.7
  207.6 34.2 reduce-scatter.9
  257.7 56.5 reduce-scatter.11
  316.4 35.1 reduce-scatter.13
  354.3 30.1 reduce-scatter.15
  387.2 29.9 reduce-scatter.19
  441.0 48.7 reduce-scatter.17

commit v7 on v6

--- a/solution.py
+++ b/solution.py
@@ -557,8 +557,6 @@
     def flip(value):
         return lax.ppermute(value, "dp", [(i, i ^ 1) for i in range(count)])
 
-    part_rows = w_o.shape[0] // 4
-    far_0 = cross(w_o[:part_rows])
     x_m = own_rows(tokens, row)
     x_o = swap(other_rows(tokens, row))
     wkv = jnp.concatenate([key_weight, value_weight], axis=1)
@@ -566,8 +564,6 @@
     wq_o = swap(query_weight)
     gains = jnp.stack([g_attn, g_mlp])
     gains_o = swap(gains)
-    x_o, wkv_o, wq_o, gains_o, far_0, w_o = tie(x_o, wkv_o, wq_o, gains_o, far_0, w_o)
-    far_1 = cross(w_o[part_rows : 2 * part_rows])
     x_m, x_o = x_m.astype(F32), x_o.astype(F32)
     square = jnp.sum(x_m * x_m, axis=-1, keepdims=True) + jnp.sum(x_o * x_o, axis=-1, keepdims=True)
     inv_one = lax.rsqrt(square / MODEL_WIDTH + EPS)
@@ -595,30 +591,25 @@
     q = dot_plain(xn_m, query_weight) + dot_plain(xn_o, wq_o)
 
     cotangent, w_gate, w_up, w_down, w_o, xn_o = tie(cotangent, w_gate, w_up, w_down, w_o, xn_o)
+    w_o_o = swap(w_o)
     wg_o = swap(w_gate)
     wu_o = swap(w_up)
-    row_arg = row.astype(jnp.int32).reshape(1)
-    start_arg = start_own.reshape(1, OWN)
-    q, other_kv, far_1, w_o = tie(q, other_kv, far_1, w_o)
-    far_2 = cross(w_o[2 * part_rows :])
-    o, lse, qt = attend(row_arg, q, cosine_t, sine_t, start_arg, own_kv, other_kv)
-    o, far_2, w_o, w_down, cotangent, wg_o, wu_o = tie(o, far_2, w_o, w_down, cotangent, wg_o, wu_o)
-    w_o_o = swap(w_o)
-    far = jnp.concatenate([far_0, far_1, far_2], axis=0)
-    o_x = cross(o)
-
     c_m = own_rows(cotangent, row)
     c_t = other_rows(cotangent, row)
     c_o = swap(c_t)
-    far_o = swap(far)
     wd_o = swap(w_down)
-    near = blend([[o]], [[w_o], [w_o_o]], False, F32)
-    both = lambda own, other: jnp.concatenate([own, other], axis=0)
-    c_y = sided(c_m, c_t, side, count)
-    near, c_y, c_o, far_o, o_x, wd_o = tie(near, c_y, c_o, far_o, o_x, wd_o)
-    width = tokens.shape[1]
-    total = near + blend([[o_x]], [[far], [far_o]], False, F32)
-    hidden_m, hidden_o = x_m + total[:, :width], x_o + total[:, width:]
+    xn_t = swap(xn_o)
+
+    row_arg = row.astype(jnp.int32).reshape(1)
+    start_arg = start_own.reshape(1, OWN)
+    o, lse, qt = attend(row_arg, q, cosine_t, sine_t, start_arg, own_kv, other_kv)
+    part_m = dot_plain(o, w_o).astype(BF16)
+    came_m = cross(part_m)
+    part_o = dot_plain(o, w_o_o).astype(BF16)
+    came_o = cross(part_o)
+    o_t = swap(o)
+    hidden_m = x_m + (part_m.astype(F32) + came_m.astype(F32))
+    hidden_o = x_o + (part_o.astype(F32) + came_o.astype(F32))
     square = jnp.sum(hidden_m * hidden_m, axis=-1, keepdims=True) + jnp.sum(
         hidden_o * hidden_o, axis=-1, keepdims=True
     )
@@ -627,18 +618,19 @@
     xn2_m = (unit_m * gains[1]).astype(BF16)
     xn2_o = (unit_o * gains_o[1]).astype(BF16)
 
+    width = tokens.shape[1]
     xn2_t = swap(xn2_o)
     tiles = w_gate.shape[1] // 256
     operands = (c_m, c_o, w_gate, wg_o, w_up, wu_o, w_down, wd_o)
     one = hidden_units(0, tiles - tiles // 2, xn2_m, xn2_o, *operands)
     one_t = swap(one)
-    one, xn2_m2, o_late, xn_o = tie(one, xn2_m, o, xn_o)
-    o_t, xn_t = swap(o_late), swap(xn_o)
+    one, xn2_m2 = tie(one, xn2_m)
     two = hidden_units(tiles - tiles // 2, tiles // 2, xn2_m2, xn2_o, *operands)
-    two, one_t, xn2_t, o_t, xn_t = tie(two, one_t, xn2_t, o_t, xn_t)
+    two, one_t, xn2_t = tie(two, one_t, xn2_t)
     two_t = swap(two)
 
-    two, xn2_m2 = tie(two, xn2_m2)
+    two, xn2_m2, c_m2 = tie(two, xn2_m2, c_m)
+    c_y = sided(c_m2, c_t, side, count)
     xn2_y = sided(xn2_m2, xn2_t, side, count)
     first_z = Summed([(xn2_y, one, one_t, 2)], flip, count)
     first_z.begin()
@@ -657,7 +649,11 @@
     send_3.begin(send_2.keep)
     send_4 = Summed([(xn2_y, two, two_t, 2)], flip, count)
     send_4.begin(send_3.keep)
-    came, first_z.send, part = tie(came, first_z.send, part, send_4.keep)[:3]
+    one_late, xn_late, _ = tie(one, xn_m, send_4.keep)
+    mix = blend([[one_late, two]], [[w_down], [wd_o]], False, BF16)
+    xn_y = sided(xn_late, xn_t, side, count)
+    mix_came = cross(mix)
+    came, first_z.send, part = tie(came, first_z.send, part, mix, xn_y)[:3]
     came = serve(came, (send_1,))
     send_2.go(send_1)
     came, _ = tie(came, send_1.finish())
@@ -676,13 +672,13 @@
     dh_m, dh_o = d_hid_m.astype(BF16), d_hid_o.astype(BF16)
     dh_t = swap(dh_o)
     d_o = blend([[dh_m], [dh_o]], [[w_o, w_o_o]], True, BF16)
-    dh_y, xn_y = sided(dh_m, dh_t, side, count), sided(xn_m, xn_t, side, count)
-    d_o, dh_y, xn_y, first_z.keep = tie(d_o, dh_y, xn_y, first_z.keep)
+    d_o, dh_t, first_z.keep = tie(d_o, dh_t, first_z.keep)
     d_o = serve(d_o, (send_2,))
     send_3.go(send_2)
     d_o, _ = tie(d_o, send_2.finish())
 
     d_q, d_k, d_v = attend_back(row_arg, qt, d_o, o, lse, cosine_t, sine_t, start_arg, own_kv, other_kv)
+    d_q, mix_came = tie(d_q, mix_came)
     d_q = serve(d_q, (send_3,))
     send_4.go(send_3)
     d_q, d_k, _ = tie(d_q, d_k, send_3.finish())
@@ -696,29 +692,19 @@
     d_kv = jnp.concatenate([d_key.reshape(OWN, narrow).astype(BF16), d_kv[:, narrow:].astype(BF16)], axis=1)
     d_qkv = jnp.concatenate([d_q, d_kv], axis=1)
     d_qkv_t = swap(d_qkv)
-    last = blend([[d_q], [d_kv]], [[query_weight, wkv], [wq_o, wkv_o]], True, BF16)
-    last, d_qkv_t = tie(last, d_qkv_t)
+    dh_y = sided(dh_m, dh_t, side, count)
+    send_5 = Summed([(dh_y, o[None], o_t[None], 0), (xn_y, d_qkv[None], d_qkv_t[None], 0)], flip, count)
+    d_q_late, send_5.keep = tie(d_q, send_5.begin())
+    last = blend([[d_q_late], [d_kv]], [[query_weight, wkv], [wq_o, wkv_o]], True, BF16)
     last_came = cross(last)
-    last, send_1.total = tie(last, send_1.total)
-    last = serve(last, (send_4,))
-    last, _ = tie(last, send_4.finish())
-    send_5 = Summed(
-        [
-            (dh_y, o[None], o_t[None], 0),
-            (xn_y, d_qkv[None], d_qkv_t[None], 0),
-        ],
-        flip,
-        count,
-    )
-    send_5.begin(last)
-    one, send_5.keep = tie(one, send_5.keep)
-    one, send_2.total = tie(one, send_2.total)
-    send_5.go()
+    last, send_1.total, send_5.keep = tie(last, send_1.total, send_5.keep)
+    send_5.keep = serve(send_5.keep, (send_4,))
+    send_5.go(send_4)
     first_z.go()
-    mix = blend([[one, two]], [[w_down], [wd_o]], False, BF16)
-
-    last_came, mix, send_3.total = tie(last_came, mix, send_3.total)
-    mix_came = cross(mix)
+    send_5.keep, send_2.total, _ = tie(send_5.keep, send_2.total, send_4.finish())
+    last_came, send_5.keep = tie(last_came, send_5.keep)
+
+    last_came, send_3.total = tie(last_came, send_3.total)
     last_came = serve(last_came, (send_5,))
     last_came, _ = tie(last_came, send_5.finish())
     d_xn = last.astype(F32) + last_came.astype(F32)

time: 522 us -> 508 us (0.973)
  Pallas kernels: 220 us -> 203 us
  waiting for transfers between devices: 137 us -> 153 us
  matrix products: 8.27 us -> 16.6 us
  local copies, waits for them, and re-layouts: 27.1 us -> 19.8 us
  starting transfers between devices: 27.8 us -> 21.2 us
  other arithmetic: 77.3 us -> 70.9 us
    ppermute x7 -> x5, waiting for transfers between devices: 96.7 us -> 44.9 us  [cross(): return lax.ppermute(value, 'col', [(0, 1), (1, 0)])]
    ppermute x6, waiting for transfers between devices: 35.2 us -> 77.6 us  [flip(): return lax.ppermute(value, 'dp', [(i, i ^ 1) for i in range(count)])]
    reduce_scatter x7, waiting for transfers between devices: 0.03 us -> 21.5 us  [scatter(): lax.psum_scatter(value, 'dp', scatter_dimension=0, axis_index_groups=grou...]
    pallas_call x5 -> x3, Pallas kernels: 45.5 us -> 28.1 us  [blend(): pl.pallas_call(functools.partial(blend_kernel, sizes, len(weights), count...]
    dot_general x4 -> x6, matrix products: 8.27 us -> 16.6 us  [dot_plain(): return jnp.dot(left, right, preferred_element_type=F32)]
    ppermute x7 -> x5, starting transfers between devices: 12.7 us -> 7.74 us  [cross(): return lax.ppermute(value, 'col', [(0, 1), (1, 0)])]
  transfers between devices with their start and end apart: 45 -> 42, of which waited for: 15 -> 14; matrix products, arithmetic and copies ran while one was open for 17% -> 18% of each run, Pallas kernels for 38% -> 37%
where the time goes in v7:
time: 508 us; the launch traced here: 500 us
  Pallas kernels  203 us (40%)
  waiting for transfers between devices  153 us (30%)
  other arithmetic  70.9 us (14%)
  starting transfers between devices  21.2 us (4%)
  local copies, waits for them, and re-layouts  19.8 us (4%)
  matrix products  16.6 us (3%)
  between operations  15.3 us (3%)
    ppermute x6, waiting for transfers between devices, flip(): return lax.ppermute(value, 'dp', [(i, i ^ 1) for i in range(count)])  77.6 us
    pallas_call x6, Pallas kernels, product(): pl.pallas_call(functools.partial(product_kernel, counts), grid=(first,),...  56.9 us
    ppermute x5, waiting for transfers between devices, cross(): return lax.ppermute(value, 'col', [(0, 1), (1, 0)])  44.9 us
    pallas_call x2, Pallas kernels, hidden_units(): pl.pallas_call(hidden_units_kernel, grid=(tiles,), in_specs=[full] * 4 +...  30.6 us
    pallas_call x3, Pallas kernels, blend(): pl.pallas_call(functools.partial(blend_kernel, sizes, len(weights), count...  28.1 us
    pallas_call x4, Pallas kernels, sided(): pl.pallas_call(sided_kernel, grid_spec=pltpu.PrefetchScalarGridSpec(num_s...  24.8 us
    reduce_scatter x7, waiting for transfers between devices, scatter(): lax.psum_scatter(value, 'dp', scatter_dimension=0, axis_index_groups=grou...  21.5 us
    pallas_call x1, Pallas kernels, attend(): pl.pallas_call(attend_kernel, grid=(pairs,), in_specs=[pl.BlockSpec(memor...  21.4 us
  transfers between devices with their start and end apart: 42, of which 14 were waited for; matrix products, arithmetic and copies ran while one was open for 18% of the time, Pallas kernels for 37%

profile of v7, /device:TPU:0, one launch (start us, length us, event | category | flops | bytes accessed | tf_op | source)
XLA Modules:
  0.0 499.9 jit_solution(11734000295321482934)
XLA Ops:
  32.9 21.4 %attend.1 = (bf16[512,1024]{1,0:T(8,128)(2,1)}, f32[8,2,512]{2,1,0:T(2,128)}, bf16[1024,512]{1,0:T(8,128)(2,1)}) custom-call(s32[1]{0:T(128)} %bitcast.row_ref, f32[512,1024]{1,0:T(8,128)} %fusion.30.q_ref, f32[32,512]{1,0:T(8,128)} %get-tuple-element.286.cos_ref, f32[32,512]{1,0:T(8,128)} %get-tuple-element.285.sin_ref, s32[1,512]{1,0:T(1,128)} %bitcast.75, ...), custom_call_target="tpu_custom_call" | custom-call | flops 20000000000 | bytes 8000000 | tf_op jit(solution)/shard_map/attend/pallas_call | solution.py:147
  65.0 19.5 %collective-permute-done.5 = bf16[512,1024]{1,0:T(8,128)(2,1)S(1)} collective-permute-done((bf16[512,1024]{1,0:T(8,128)(2,1)S(1)}, bf16[512,1024]{1,0:T(8,128)(2,1)S(1)}, u32[]{:S(2)}, u32[]{:S(2)}) %collective-permute-start.5) | collective-permute-done | bytes 1048608 | tf_op jit(solution)/shard_map/ppermute | solution.py:555
  85.1 20.4 %collective-permute-done.7 = bf16[512,1024]{1,0:T(8,128)(2,1)S(1)} collective-permute-done((bf16[512,1024]{1,0:T(8,128)(2,1)S(1)}, bf16[512,1024]{1,0:T(8,128)(2,1)S(1)}, u32[]{:S(2)}, u32[]{:S(2)}) %collective-permute-start.7) | collective-permute-done | bytes 1048608 | tf_op jit(solution)/shard_map/ppermute | solution.py:555
  109.0 16.3 %hidden_units.2.refs_1_.refs_2_.a_ref.refs_0_ = bf16[3,512,1536]{2,1,0:T(8,128)(2,1)} custom-call(bf16[512,1024]{1,0:T(8,128)(2,1)} %get-tuple-element.113.xm_ref.own_ref, bf16[512,1024]{1,0:T(8,128)(2,1)} %get-tuple-element.289.xo_ref, bf16[512,1024]{1,0:T(8,128)(2,1)} %pad_maximum_fusion.6.cm_ref.own_ref, bf16[512,1024]{1,0:T(8,128)(2,1)} %copy-done.12, ...), custom_call_target="tpu_custom_call" | custom-call | flops 9663676416 | bytes 18874368 | tf_op jit(solution)/shard_map/hidden_units/pallas_call | solution.py:323
  125.9 14.2 %hidden_units.3.refs_3_.b_ref.refs_1_ = bf16[3,512,1280]{2,1,0:T(8,128)(2,1)} custom-call(bf16[512,1024]{1,0:T(8,128)(2,1)} %get-tuple-element.113.xm_ref.own_ref, bf16[512,1024]{1,0:T(8,128)(2,1)} %get-tuple-element.289.xo_ref, bf16[512,1024]{1,0:T(8,128)(2,1)} %pad_maximum_fusion.6.cm_ref.own_ref, bf16[512,1024]{1,0:T(8,128)(2,1)} %copy-done.12, ...), custom_call_target="tpu_custom_call" | custom-call | flops 8053063680 | bytes 15728640 | tf_op jit(solution)/shard_map/hidden_units/pallas_call | solution.py:323
  140.3 6.2 %sided.4.refs_0_ = bf16[1024,1024]{1,0:T(8,128)(2,1)} custom-call(s32[1]{0:T(128)} %bitcast.8.side_ref, bf16[512,1024]{1,0:T(8,128)(2,1)} %get-tuple-element.113.xm_ref.own_ref, bf16[512,1024]{1,0:T(8,128)(2,1)} %collective-permute-done.13.other_ref), custom_call_target="tpu_custom_call" | custom-call | flops 1000 | bytes 1000 | tf_op jit(solution)/shard_map/sided/pallas_call | solution.py:474
  146.4 8.6 %product.6 = (bf16[512,1536]{1,0:T(8,128)(2,1)}, bf16[512,1536]{1,0:T(8,128)(2,1)}) custom-call(bf16[1024,1024]{1,0:T(8,128)(2,1)} %sided.4.refs_0_, bf16[3,512,1536]{2,1,0:T(8,128)(2,1)} %hidden_units.2.refs_1_.refs_2_.a_ref.refs_0_, bf16[3,512,1536]{2,1,0:T(8,128)(2,1)} %collective-permute-done.12.refs_2_.refs_4_), custom_call_target="tpu_custom_call" | custom-call | flops 6442450944 | bytes 9437184 | tf_op jit(solution)/shard_map/product/pallas_call | solution.py:396
  155.1 6.2 %sided.5.refs_0_.refs_1_ = bf16[1024,1024]{1,0:T(8,128)(2,1)} custom-call(s32[1]{0:T(128)} %bitcast.8.side_ref, bf16[512,1024]{1,0:T(8,128)(2,1)} %pad_maximum_fusion.6.cm_ref.own_ref, bf16[512,1024]{1,0:T(8,128)(2,1)} %copy-done.23), custom_call_target="tpu_custom_call" | custom-call | flops 1000 | bytes 1000 | tf_op jit(solution)/shard_map/sided/pallas_call | solution.py:474
  161.3 14.0 %product.7 = (bf16[512,2816]{1,0:T(8,128)(2,1)}, bf16[512,2816]{1,0:T(8,128)(2,1)}) custom-call(bf16[1024,1024]{1,0:T(8,128)(2,1)} %sided.5.refs_0_.refs_1_, bf16[1024,1024]{1,0:T(8,128)(2,1)} %sided.5.refs_0_.refs_1_, bf16[3,512,1536]{2,1,0:T(8,128)(2,1)} %hidden_units.2.refs_1_.refs_2_.a_ref.refs_0_, ...), custom_call_target="tpu_custom_call" | custom-call | flops 11811160064 | bytes 17301504 | tf_op jit(solution)/shard_map/product/pallas_call | solution.py:396
  177.1 20.7 %input_grad.1 = bf16[512,2048]{1,0:T(8,128)(2,1)} custom-call(bf16[3,512,1536]{2,1,0:T(8,128)(2,1)} %hidden_units.2.refs_1_.refs_2_.a_ref.refs_0_, bf16[3,512,1280]{2,1,0:T(8,128)(2,1)} %hidden_units.3.refs_3_.b_ref.refs_1_, bf16[1024,2816]{1,0:T(8,128)(2,1)} %gm_ref.2, bf16[1024,2816]{1,0:T(8,128)(2,1)} %um_ref.2, ...), custom_call_target="tpu_custom_call" | custom-call | flops 11811160064 | bytes 23068672 | tf_op jit(solution)/shard_map/input_grad/pallas_call | solution.py:356
  199.4 8.1 %product.8 = (bf16[512,1536]{1,0:T(8,128)(2,1)}, bf16[512,1536]{1,0:T(8,128)(2,1)}) custom-call(bf16[1024,1024]{1,0:T(8,128)(2,1)} %sided.4.refs_0_, bf16[3,512,1536]{2,1,0:T(8,128)(2,1)} %hidden_units.2.refs_1_.refs_2_.a_ref.refs_0_, bf16[3,512,1536]{2,1,0:T(8,128)(2,1)} %collective-permute-done.12.refs_2_.refs_4_), custom_call_target="tpu_custom_call" | custom-call | flops 6442450944 | bytes 9437184 | tf_op jit(solution)/shard_map/product/pallas_call | solution.py:396
  207.5 7.2 %product.9 = (bf16[512,1280]{1,0:T(8,128)(2,1)}, bf16[512,1280]{1,0:T(8,128)(2,1)}) custom-call(bf16[1024,1024]{1,0:T(8,128)(2,1)} %sided.4.refs_0_, bf16[3,512,1280]{2,1,0:T(8,128)(2,1)} %hidden_units.3.refs_3_.b_ref.refs_1_, bf16[3,512,1280]{2,1,0:T(8,128)(2,1)} %collective-permute-done.14.refs_5_.refs_2_), custom_call_target="tpu_custom_call" | custom-call | flops 5368709120 | bytes 7864320 | tf_op jit(solution)/shard_map/product/pallas_call | solution.py:396
  214.7 7.3 %product.10 = (bf16[512,1280]{1,0:T(8,128)(2,1)}, bf16[512,1280]{1,0:T(8,128)(2,1)}) custom-call(bf16[1024,1024]{1,0:T(8,128)(2,1)} %sided.4.refs_0_, bf16[3,512,1280]{2,1,0:T(8,128)(2,1)} %hidden_units.3.refs_3_.b_ref.refs_1_, bf16[3,512,1280]{2,1,0:T(8,128)(2,1)} %collective-permute-done.14.refs_5_.refs_2_), custom_call_target="tpu_custom_call" | custom-call | flops 5368709120 | bytes 7864320 | tf_op jit(solution)/shard_map/product/pallas_call | solution.py:396
  222.0 12.7 %blend.3 = bf16[512,2048]{1,0:T(8,128)(2,1)} custom-call(bf16[3,512,1536]{2,1,0:T(8,128)(2,1)} %hidden_units.2.refs_1_.refs_2_.a_ref.refs_0_, bf16[3,512,1280]{2,1,0:T(8,128)(2,1)} %hidden_units.3.refs_3_.b_ref.refs_1_, bf16[2816,1024]{1,0:T(8,128)(2,1)} %refs_2_.1, bf16[2816,1024]{1,0:T(8,128)(2,1)} %collective-permute-done.11.do_ref.refs_3_), custom_call_target="tpu_custom_call" | custom-call | flops 1000 | bytes 1000 | tf_op jit(solution)/shard_map/blend/pallas_call | solution.py:447
  234.7 6.2 %sided.6.refs_1_ = bf16[1024,1024]{1,0:T(8,128)(2,1)} custom-call(s32[1]{0:T(128)} %bitcast.8.side_ref, bf16[512,1024]{1,0:T(8,128)(2,1)} %copy-done.15, bf16[512,1024]{1,0:T(8,128)(2,1)} %collective-permute-done.16.other_ref), custom_call_target="tpu_custom_call" | custom-call | flops 1000 | bytes 1000 | tf_op jit(solution)/shard_map/sided/pallas_call | solution.py:474
  240.9 5.0 %collective-permute-done.15 = bf16[512,2048]{1,0:T(8,128)(2,1)} collective-permute-done((bf16[512,2048]{1,0:T(8,128)(2,1)}, bf16[512,2048]{1,0:T(8,128)(2,1)}, u32[]{:S(2)}, u32[]{:S(2)}) %collective-permute-start.15) | collective-permute-done | bytes 2097184 | tf_op jit(solution)/shard_map/ppermute | solution.py:555
  262.8 6.3 %blend.4.do_ref = bf16[512,1024]{1,0:T(8,128)(2,1)} custom-call(bf16[1,512,1024]{2,1,0:T(8,128)(2,1)} %bitcast.53, bf16[1,512,1024]{2,1,0:T(8,128)(2,1)} %bitcast.10.refs_1_, bf16[1024,1024]{1,0:T(8,128)(2,1)} %refs_2_.2, bf16[1024,1024]{1,0:T(8,128)(2,1)} %collective-permute-done.6.refs_3_), custom_call_target="tpu_custom_call" | custom-call | flops 1000 | bytes 1000 | tf_op jit(solution)/shard_map/blend/pallas_call | solution.py:447
  269.1 17.9 %collective-permute-done.19 = bf16[512,1536]{1,0:T(8,128)(2,1)} collective-permute-done((bf16[512,1536]{1,0:T(8,128)(2,1)}, bf16[512,1536]{1,0:T(8,128)(2,1)}, u32[]{:S(2)}, u32[]{:S(2)}) %collective-permute-start.19) | collective-permute-done | bytes 1572896 | tf_op jit(solution)/shard_map/ppermute | solution.py:558
  290.7 20.6 %attend_back.1 = (bf16[512,1024]{1,0:T(8,128)(2,1)}, f32[2,1024,64]{2,1,0:T(8,128)}, f32[2,1024,64]{2,1,0:T(8,128)}) custom-call(s32[1]{0:T(128)} %bitcast.row_ref, bf16[1024,512]{1,0:T(8,128)(2,1)} %get-tuple-element.131.qt_ref, bf16[512,1024]{1,0:T(8,128)(2,1)} %blend.4.do_ref, bf16[512,1024]{1,0:T(8,128)(2,1)} %get-tuple-element.104.o_ref, ...), custom_call_target="tpu_custom_call" | custom-call | flops 1000 | bytes 1000 | tf_op jit(solution)/shard_map/attend_back/pallas_call | solution.py:265
  330.2 6.2 %sided.7.refs_0_ = bf16[1024,1024]{1,0:T(8,128)(2,1)} custom-call(s32[1]{0:T(128)} %bitcast.8.side_ref, bf16[512,1024]{1,0:T(8,128)(2,1)} %get-tuple-element.236.own_ref, bf16[512,1024]{1,0:T(8,128)(2,1)} %collective-permute-done.18.other_ref), custom_call_target="tpu_custom_call" | custom-call | flops 1000 | bytes 1000 | tf_op jit(solution)/shard_map/sided/pallas_call | solution.py:474
  337.1 11.7 %product.11 = (bf16[512,2304]{1,0:T(8,128)(2,1)}, bf16[512,2304]{1,0:T(8,128)(2,1)}) custom-call(bf16[1024,1024]{1,0:T(8,128)(2,1)} %sided.7.refs_0_, bf16[1024,1024]{1,0:T(8,128)(2,1)} %sided.6.refs_1_, bf16[1,512,1024]{2,1,0:T(8,128)(2,1)} %bitcast.55, bf16[1,512,1280]{2,1,0:T(8,128)(2,1)} %get-tuple-element.266.refs_3_, ...), custom_call_target="tpu_custom_call" | custom-call | flops 9663676416 | bytes 14155776 | tf_op jit(solution)/shard_map/product/pallas_call | solution.py:396
  348.9 9.2 %blend.5 = bf16[512,2048]{1,0:T(8,128)(2,1)} custom-call(bf16[1,512,1024]{2,1,0:T(8,128)(2,1)} %bitcast.54, bf16[1,512,256]{2,1,0:T(8,128)(2,1)} %maximum_bitcast_fusion.refs_1_, bf16[1024,1024]{1,0:T(8,128)(2,1)} %refs_2_.3, bf16[1024,256]{1,0:T(8,128)(2,1)} %constant_dynamic-update-slice_fusion.refs_3_, bf16[1024,1024]{1,0:T(8,128)(2,1)} %collective-permute-done.3.refs_4_, ...), custom_call_target="tpu_custom_call" | custom-call | flops 1000 | bytes 1000 | tf_op jit(solution)/shard_map/blend/pallas_call | solution.py:447
  367.8 54.2 %collective-permute-done.34 = bf16[128,1536]{1,0:T(8,128)(2,1)} collective-permute-done((bf16[128,1536]{1,0:T(8,128)(2,1)}, bf16[128,1536]{1,0:T(8,128)(2,1)}, u32[]{:S(2)}, u32[]{:S(2)}) %collective-permute-start.34) | collective-permute-done | bytes 393248 | tf_op jit(solution)/shard_map/ppermute | solution.py:558
  460.8 21.5 %reduce-scatter.18.cloned.1.call-done = bf16[128,2304]{1,0:T(8,128)(2,1)} async-done(((bf16[512,2304]{1,0:T(8,128)(2,1)}), bf16[128,2304]{1,0:T(8,128)(2,1)}) %reduce-scatter.18.cloned.1.call-update) | async-done | bytes 589840 | tf_op jit(solution)/shard_map/reduce_scatter | solution.py:508
  (271 shorter events, 143.2 us)
Async XLA Ops:
  7.2 233.7 %reduce-scatter.8.cloned.1.call-start = ((), (), s32[]{:S(2)}) async-start(), calls=%async_computation.7 | async-start | bytes 1966080 | tf_op jit(solution)/shard_map/reduce_scatter | solution.py:508
  21.9 87.1 %collective-permute-start.9 = (bf16[1024,2816]{1,0:T(8,128)(2,1)}, bf16[1024,2816]{1,0:T(8,128)(2,1)}, u32[]{:S(2)}, u32[]{:S(2)}) collective-permute-start(bf16[1024,2816]{1,0:T(8,128)(2,1)} %gm_ref.2), channel_id=1, source_target_pairs={{0,2},{2,0},{1,3},{3,1},{4,6},{6,4},{5,7},{7,5},{8,10},{10,8},{9,1... | collective-permute-start | bytes 17301512 | tf_op jit(solution)/shard_map/ppermute | solution.py:552
  22.4 86.7 %collective-permute-start.10 = (bf16[1024,2816]{1,0:T(8,128)(2,1)}, bf16[1024,2816]{1,0:T(8,128)(2,1)}, u32[]{:S(2)}, u32[]{:S(2)}) collective-permute-start(bf16[1024,2816]{1,0:T(8,128)(2,1)} %um_ref.2), channel_id=1, source_target_pairs={{0,2},{2,0},{1,3},{3,1},{4,6},{6,4},{5,7},{7,5},{8,10},{10,8},{9,1... | collective-permute-start | bytes 17301512 | tf_op jit(solution)/shard_map/ppermute | solution.py:552
  22.5 86.5 %collective-permute-start.11 = (bf16[2816,1024]{1,0:T(8,128)(2,1)}, bf16[2816,1024]{1,0:T(8,128)(2,1)}, u32[]{:S(2)}, u32[]{:S(2)}) collective-permute-start(bf16[2816,1024]{1,0:T(8,128)(2,1)} %refs_2_.1), channel_id=1, source_target_pairs={{0,2},{2,0},{1,3},{3,1},{4,6},{6,4},{5,7},{7,5},{8,10},{10,8},{9,1... | collective-permute-start | bytes 17301512 | tf_op jit(solution)/shard_map/ppermute | solution.py:552
  26.9 33.5 %collective-permute-start.6 = (bf16[1024,1024]{1,0:T(8,128)(2,1)}, bf16[1024,1024]{1,0:T(8,128)(2,1)}, u32[]{:S(2)}, u32[]{:S(2)}) collective-permute-start(bf16[1024,1024]{1,0:T(8,128)(2,1)} %refs_2_.2), channel_id=1, source_target_pairs={{0,2},{2,0},{1,3},{3,1},{4,6},{6,4},{5,7},{7,5},{8,10},{10,8},{9,1... | collective-permute-start | bytes 6291464 | tf_op jit(solution)/shard_map/ppermute | solution.py:552
  57.5 27.0 %collective-permute-start.5 = (bf16[512,1024]{1,0:T(8,128)(2,1)S(1)}, bf16[512,1024]{1,0:T(8,128)(2,1)S(1)}, u32[]{:S(2)}, u32[]{:S(2)}) collective-permute-start(bf16[512,1024]{1,0:T(8,128)(2,1)S(1)} %convolution_convert_fusion.1), channel_id=1, source_target_pairs={{0,1},{1,0},{2,3},{3,2},{4,5},{5,4},{6,7},{7,6},{8,9},{9,8},{10,11... | collective-permute-start | bytes 3145736 | tf_op jit(solution)/shard_map/ppermute | solution.py:555
  63.3 42.1 %collective-permute-start.7 = (bf16[512,1024]{1,0:T(8,128)(2,1)S(1)}, bf16[512,1024]{1,0:T(8,128)(2,1)S(1)}, u32[]{:S(2)}, u32[]{:S(2)}) collective-permute-start(bf16[512,1024]{1,0:T(8,128)(2,1)S(1)} %convolution_convert_fusion), channel_id=1, source_target_pairs={{0,1},{1,0},{2,3},{3,2},{4,5},{5,4},{6,7},{7,6},{8,9},{9,8},{10,11... | collective-permute-start | bytes 3145736 | tf_op jit(solution)/shard_map/ppermute | solution.py:555
  84.5 23.5 %collective-permute-start.8 = (bf16[512,1024]{1,0:T(8,128)(2,1)S(1)}, bf16[512,1024]{1,0:T(8,128)(2,1)S(1)}, u32[]{:S(2)}, u32[]{:S(2)}) collective-permute-start(bf16[512,1024]{1,0:T(8,128)(2,1)S(1)} %pad_maximum_fusion.7.other_ref), channel_id=1, source_target_pairs={{0,2},{2,0},{1,3},{3,1},{4,6},{6,4},{5,7},{7,5},{8,10},{10,8},{9,1... | collective-permute-start | bytes 3145736 | tf_op jit(solution)/shard_map/ppermute | solution.py:552
  155.0 114.0 %reduce-scatter.10.cloned.1.call-start = ((), (), s32[]{:S(2)}) async-start(), calls=%async_computation.8 | async-start | bytes 1966080 | tf_op jit(solution)/shard_map/reduce_scatter | solution.py:508
  175.3 70.6 %collective-permute-start.17 = (bf16[512,2816]{1,0:T(8,128)(2,1)}, bf16[512,2816]{1,0:T(8,128)(2,1)}, u32[]{:S(2)}, u32[]{:S(2)}) collective-permute-start(bf16[512,2816]{1,0:T(8,128)(2,1)} %get-tuple-element.137), channel_id=1, source_target_pairs={{0,4},{4,0},{8,12},{12,8},{16,20},{20,16},{24,28},{28,24},{1,5},{5... | collective-permute-start | bytes 8650760 | tf_op jit(solution)/shard_map/ppermute | solution.py:558
  177.1 181.0 %reduce-scatter.12.cloned.1.call-start = ((), (), s32[]{:S(2)}) async-start(), calls=%async_computation.9 | async-start | bytes 3604480 | tf_op jit(solution)/shard_map/reduce_scatter | solution.py:508
  197.9 48.0 %collective-permute-start.15 = (bf16[512,2048]{1,0:T(8,128)(2,1)}, bf16[512,2048]{1,0:T(8,128)(2,1)}, u32[]{:S(2)}, u32[]{:S(2)}) collective-permute-start(bf16[512,2048]{1,0:T(8,128)(2,1)} %input_grad.1), channel_id=1, source_target_pairs={{0,1},{1,0},{2,3},{3,2},{4,5},{5,4},{6,7},{7,6},{8,9},{9,8},{10,11... | collective-permute-start | bytes 6291464 | tf_op jit(solution)/shard_map/ppermute | solution.py:555
  199.4 35.3 %collective-permute-start.16 = (bf16[512,1024]{1,0:T(8,128)(2,1)}, bf16[512,1024]{1,0:T(8,128)(2,1)}, u32[]{:S(2)}, u32[]{:S(2)}) collective-permute-start(bf16[512,1024]{1,0:T(8,128)(2,1)} %copy-done.24), channel_id=1, source_target_pairs={{0,2},{2,0},{1,3},{3,1},{4,6},{6,4},{5,7},{7,5},{8,10},{10,8},{9,1... | collective-permute-start | bytes 3145736 | tf_op jit(solution)/shard_map/ppermute | solution.py:552
  250.8 178.2 %reduce-scatter.14.cloned.1.call-start = ((), (), s32[]{:S(2)}) async-start(), calls=%async_computation.10 | async-start | bytes 1966080 | tf_op jit(solution)/shard_map/reduce_scatter | solution.py:508
  250.9 36.0 %collective-permute-start.19 = (bf16[512,1536]{1,0:T(8,128)(2,1)}, bf16[512,1536]{1,0:T(8,128)(2,1)}, u32[]{:S(2)}, u32[]{:S(2)}) collective-permute-start(bf16[512,1536]{1,0:T(8,128)(2,1)} %get-tuple-element.146), channel_id=1, source_target_pairs={{0,4},{4,0},{8,12},{12,8},{16,20},{20,16},{24,28},{28,24},{1,5},{5... | collective-permute-start | bytes 4718600 | tf_op jit(solution)/shard_map/ppermute | solution.py:558
  261.2 52.4 %collective-permute-start.20 = (bf16[512,2048]{1,0:T(8,128)(2,1)}, bf16[512,2048]{1,0:T(8,128)(2,1)}, u32[]{:S(2)}, u32[]{:S(2)}) collective-permute-start(bf16[512,2048]{1,0:T(8,128)(2,1)} %blend.3), channel_id=1, source_target_pairs={{0,1},{1,0},{2,3},{3,2},{4,5},{5,4},{6,7},{7,6},{8,9},{9,8},{10,11... | collective-permute-start | bytes 6291464 | tf_op jit(solution)/shard_map/ppermute | solution.py:555
  286.9 29.4 %collective-permute-start.22 = (bf16[512,1280]{1,0:T(8,128)(2,1)}, bf16[512,1280]{1,0:T(8,128)(2,1)}, u32[]{:S(2)}, u32[]{:S(2)}) collective-permute-start(bf16[512,1280]{1,0:T(8,128)(2,1)} %get-tuple-element.156), channel_id=1, source_target_pairs={{0,4},{4,0},{8,12},{12,8},{16,20},{20,16},{24,28},{28,24},{1,5},{5... | collective-permute-start | bytes 3932168 | tf_op jit(solution)/shard_map/ppermute | solution.py:558
  290.7 138.4 %reduce-scatter.16.cloned.1.call-start = ((), (), s32[]{:S(2)}) async-start(), calls=%async_computation.11 | async-start | bytes 1638400 | tf_op jit(solution)/shard_map/reduce_scatter | solution.py:508
  329.2 126.5 %reduce-scatter.20.cloned.1.call-start = ((), (), s32[]{:S(2)}) async-start(), calls=%async_computation.13 | async-start | bytes 1638400 | tf_op jit(solution)/shard_map/reduce_scatter | solution.py:508
  329.7 31.1 %collective-permute-start.27 = (bf16[512,1280]{1,0:T(8,128)(2,1)}, bf16[512,1280]{1,0:T(8,128)(2,1)}, u32[]{:S(2)}, u32[]{:S(2)}) collective-permute-start(bf16[512,1280]{1,0:T(8,128)(2,1)} %get-tuple-element.171), channel_id=1, source_target_pairs={{0,4},{4,0},{8,12},{12,8},{16,20},{20,16},{24,28},{28,24},{1,5},{5... | collective-permute-start | bytes 3932168 | tf_op jit(solution)/shard_map/ppermute | solution.py:558
  360.8 68.2 %collective-permute-start.28 = (bf16[512,2304]{1,0:T(8,128)(2,1)}, bf16[512,2304]{1,0:T(8,128)(2,1)}, u32[]{:S(2)}, u32[]{:S(2)}) collective-permute-start(bf16[512,2304]{1,0:T(8,128)(2,1)} %get-tuple-element.179), channel_id=1, source_target_pairs={{0,4},{4,0},{8,12},{12,8},{16,20},{20,16},{24,28},{28,24},{1,5},{5... | collective-permute-start | bytes 7077896 | tf_op jit(solution)/shard_map/ppermute | solution.py:558
  361.3 67.8 %collective-permute-start.26 = (bf16[512,2048]{1,0:T(8,128)(2,1)}, bf16[512,2048]{1,0:T(8,128)(2,1)}, u32[]{:S(2)}, u32[]{:S(2)}) collective-permute-start(bf16[512,2048]{1,0:T(8,128)(2,1)} %blend.5), channel_id=1, source_target_pairs={{0,1},{1,0},{2,3},{3,2},{4,5},{5,4},{6,7},{7,6},{8,9},{9,8},{10,11... | collective-permute-start | bytes 6291464 | tf_op jit(solution)/shard_map/ppermute | solution.py:555
  366.0 116.4 %reduce-scatter.18.cloned.1.call-start = ((), (), s32[]{:S(2)}) async-start(), calls=%async_computation.12 | async-start | bytes 2949120 | tf_op jit(solution)/shard_map/reduce_scatter | solution.py:508
  366.2 55.8 %collective-permute-start.34 = (bf16[128,1536]{1,0:T(8,128)(2,1)}, bf16[128,1536]{1,0:T(8,128)(2,1)}, u32[]{:S(2)}, u32[]{:S(2)}) collective-permute-start(bf16[128,1536]{1,0:T(8,128)(2,1)} %reduce-scatter.8.cloned.1.call-done), channel_id=1, source_target_pairs={{0,4},{4,0},{8,12},{12,8},{16,20},{20,16},{24,28},{28,24},{1,5},{5... | collective-permute-start | bytes 1179656 | tf_op jit(solution)/shard_map/ppermute | solution.py:558
  (67 other events, 482.4 us)
Sparse Core Ops, SparseCore 0:
  155.1 36.8 reduce-scatter.7
  194.4 34.2 reduce-scatter.9
  250.9 56.4 reduce-scatter.11
  309.6 35.1 reduce-scatter.13
  347.5 30.1 reduce-scatter.15
  380.4 29.9 reduce-scatter.19
  433.7 48.6 reduce-scatter.17

commit v8 on v7

--- a/solution.py
+++ b/solution.py
@@ -608,6 +608,10 @@
     part_o = dot_plain(o, w_o_o).astype(BF16)
     came_o = cross(part_o)
     o_t = swap(o)
+    c_late, xn_late, _ = tie(c_m, xn_m, part_o)
+    c_y = sided(c_late, c_t, side, count)
+    xn_y = sided(xn_late, xn_t, side, count)
+    came_o, c_y, xn_y = tie(came_o, c_y, xn_y)
     hidden_m = x_m + (part_m.astype(F32) + came_m.astype(F32))
     hidden_o = x_o + (part_o.astype(F32) + came_o.astype(F32))
     square = jnp.sum(hidden_m * hidden_m, axis=-1, keepdims=True) + jnp.sum(
@@ -629,31 +633,30 @@
     two, one_t, xn2_t = tie(two, one_t, xn2_t)
     two_t = swap(two)
 
-    two, xn2_m2, c_m2 = tie(two, xn2_m2, c_m)
-    c_y = sided(c_m2, c_t, side, count)
+    two, xn2_m2 = tie(two, xn2_m2)
     xn2_y = sided(xn2_m2, xn2_t, side, count)
-    first_z = Summed([(xn2_y, one, one_t, 2)], flip, count)
-    first_z.begin()
-    first_z.send = first_z.scatter(first_z.send)
-    first_z.keep, two_t = tie(first_z.keep, two_t)
+    c_y, xn2_y = tie(c_y, xn2_y)
     send_1 = Summed([(c_y, one, one_t, 0), (c_y, two, two_t, 0)], flip, count)
-    send_1.begin(first_z.keep)
+    send_1.begin()
     send_1.go()
-    send_1.keep, two_late, first_z.keep = tie(send_1.keep, two, first_z.keep)
-    first_z.keep = first_z.scatter(first_z.keep)
+    send_1.keep, two_late = tie(send_1.keep, two)
     part = input_grad(one, two_late, w_gate, w_up, wg_o, wu_o)
     came = cross(part)
+    first_z = Summed([(xn2_y, one, one_t, 2)], flip, count)
+    first_z.begin(part)
+    first_z.send = first_z.scatter(first_z.send)
+    part, first_z.keep = tie(part, first_z.keep)
+    first_z.keep = first_z.scatter(first_z.keep)
     send_2 = Summed([(xn2_y, one, one_t, 1)], flip, count)
     send_2.begin(part)
     send_3 = Summed([(xn2_y, two, two_t, 1)], flip, count)
     send_3.begin(send_2.keep)
     send_4 = Summed([(xn2_y, two, two_t, 2)], flip, count)
     send_4.begin(send_3.keep)
-    one_late, xn_late, _ = tie(one, xn_m, send_4.keep)
+    one_late, _ = tie(one, send_4.keep)
     mix = blend([[one_late, two]], [[w_down], [wd_o]], False, BF16)
-    xn_y = sided(xn_late, xn_t, side, count)
     mix_came = cross(mix)
-    came, first_z.send, part = tie(came, first_z.send, part, mix, xn_y)[:3]
+    came, first_z.send, part = tie(came, first_z.send, part, mix)[:3]
     came = serve(came, (send_1,))
     send_2.go(send_1)
     came, _ = tie(came, send_1.finish())
@@ -706,7 +709,7 @@
 
     last_came, send_3.total = tie(last_came, send_3.total)
     last_came = serve(last_came, (send_5,))
-    last_came, _ = tie(last_came, send_5.finish())
+    last_came, mix, mix_came, first_z.keep, _ = tie(last_came, mix, mix_came, first_z.keep, send_5.finish())
     d_xn = last.astype(F32) + last_came.astype(F32)
     d_xn_m, d_xn_o = d_xn[:, :width], d_xn[:, width:]
     unit_m, unit_o = x_m * inv_one, x_o * inv_one
@@ -722,8 +725,8 @@
     gg = jnp.stack([gg_attn_m, gg_mlp_m]) + swap(jnp.stack([gg_attn_o, gg_mlp_o]))
     for bit in range(count.bit_length() - 1):
         gg = gg + lax.ppermute(gg, "dp", [(i, i ^ (1 << bit)) for i in range(count)])
+    gg, send_5.total = tie(gg, send_5.total)
     gg = lax.dynamic_slice_in_dim(gg, lax.axis_index("dp") * (width // count), width // count, axis=1)
-    d_tok_t, send_5.total = tie(d_tok_t, send_5.total)
     d_tokens = merge_rows(d_tok_m, d_tok_t, row)
 
     mixed_all = mix.astype(F32) + mix_came.astype(F32)

time: 508 us -> 499 us (0.982)
  waiting for transfers between devices: 153 us -> 139 us
  other arithmetic: 70.9 us -> 77.7 us
    ppermute x6, waiting for transfers between devices: 77.6 us -> 41.9 us  [flip(): return lax.ppermute(value, 'dp', [(i, i ^ 1) for i in range(count)])]
    ppermute x5, waiting for transfers between devices: 44.9 us -> 75.5 us  [cross(): return lax.ppermute(value, 'col', [(0, 1), (1, 0)])]
    reduce_scatter x7, waiting for transfers between devices: 21.5 us -> 9.69 us  [scatter(): lax.psum_scatter(value, 'dp', scatter_dimension=0, axis_index_groups=grou...]
  transfers between devices with their start and end apart: 42 -> 42, of which waited for: 14 -> 16; matrix products, arithmetic and copies ran while one was open for 18% -> 20% of each run, Pallas kernels for 37% -> 29%
where the time goes in v8:
time: 499 us; the launch traced here: 492 us
  Pallas kernels  203 us (41%)
  waiting for transfers between devices  139 us (28%)
  other arithmetic  77.7 us (16%)
  starting transfers between devices  25.5 us (5%)
  matrix products  16.3 us (3%)
  local copies, waits for them, and re-layouts  15.5 us (3%)
  between operations  15.3 us (3%)
    ppermute x5, waiting for transfers between devices, cross(): return lax.ppermute(value, 'col', [(0, 1), (1, 0)])  75.5 us
    pallas_call x6, Pallas kernels, product(): pl.pallas_call(functools.partial(product_kernel, counts), grid=(first,),...  56.7 us
    ppermute x6, waiting for transfers between devices, flip(): return lax.ppermute(value, 'dp', [(i, i ^ 1) for i in range(count)])  41.9 us
    pallas_call x2, Pallas kernels, hidden_units(): pl.pallas_call(hidden_units_kernel, grid=(tiles,), in_specs=[full] * 4 +...  30.5 us
    pallas_call x3, Pallas kernels, blend(): pl.pallas_call(functools.partial(blend_kernel, sizes, len(weights), count...  28.1 us
    pallas_call x4, Pallas kernels, sided(): pl.pallas_call(sided_kernel, grid_spec=pltpu.PrefetchScalarGridSpec(num_s...  24.7 us
    pallas_call x1, Pallas kernels, attend(): pl.pallas_call(attend_kernel, grid=(pairs,), in_specs=[pl.BlockSpec(memor...  21.3 us
    pallas_call x1, Pallas kernels, input_grad(): pl.pallas_call(input_grad_kernel, grid=(2 * tiles,), in_specs=[full(a), f...  20.6 us
  transfers between devices with their start and end apart: 42, of which 16 were waited for; matrix products, arithmetic and copies ran while one was open for 20% of the time, Pallas kernels for 29%

profile of v8, /device:TPU:0, one launch (start us, length us, event | category | flops | bytes accessed | tf_op | source)
XLA Modules:
  0.0 491.7 jit_solution(17581939772736438345)
XLA Ops:
  26.7 21.3 %attend.1 = (bf16[512,1024]{1,0:T(8,128)(2,1)}, f32[8,2,512]{2,1,0:T(2,128)}, bf16[1024,512]{1,0:T(8,128)(2,1)}) custom-call(s32[1]{0:T(128)} %bitcast.row_ref, f32[512,1024]{1,0:T(8,128)} %fusion.30.q_ref, f32[32,512]{1,0:T(8,128)} %get-tuple-element.300.cos_ref, f32[32,512]{1,0:T(8,128)} %get-tuple-element.299.sin_ref, s32[1,512]{1,0:T(1,128)} %bitcast.74, ...), custom_call_target="tpu_custom_call" | custom-call | flops 20000000000 | bytes 8000000 | tf_op jit(solution)/shard_map/attend/pallas_call | solution.py:147
  63.9 15.5 %collective-permute-done.5 = bf16[512,1024]{1,0:T(8,128)(2,1)} collective-permute-done((bf16[512,1024]{1,0:T(8,128)(2,1)}, bf16[512,1024]{1,0:T(8,128)(2,1)}, u32[]{:S(2)}, u32[]{:S(2)}) %collective-permute-start.5) | collective-permute-done | bytes 1048608 | tf_op jit(solution)/shard_map/ppermute | solution.py:555
  81.5 6.2 %sided.4.refs_0_.refs_1_ = bf16[1024,1024]{1,0:T(8,128)(2,1)} custom-call(s32[1]{0:T(128)} %bitcast.7.side_ref, bf16[512,1024]{1,0:T(8,128)(2,1)} %pad_maximum_fusion.6.own_ref.cm_ref, bf16[512,1024]{1,0:T(8,128)(2,1)} %pad_maximum_fusion.7.other_ref), custom_call_target="tpu_custom_call" | custom-call | flops 1000 | bytes 1000 | tf_op jit(solution)/shard_map/sided/pallas_call | solution.py:474
  93.9 6.5 %collective-permute-done.7 = bf16[512,1024]{1,0:T(8,128)(2,1)} collective-permute-done((bf16[512,1024]{1,0:T(8,128)(2,1)}, bf16[512,1024]{1,0:T(8,128)(2,1)}, u32[]{:S(2)}, u32[]{:S(2)}) %collective-permute-start.7) | collective-permute-done | bytes 1048608 | tf_op jit(solution)/shard_map/ppermute | solution.py:555
  104.4 16.3 %hidden_units.2.refs_2_.a_ref.refs_1_.refs_0_ = bf16[3,512,1536]{2,1,0:T(8,128)(2,1)} custom-call(bf16[512,1024]{1,0:T(8,128)(2,1)} %get-tuple-element.126.xm_ref.own_ref, bf16[512,1024]{1,0:T(8,128)(2,1)} %get-tuple-element.303.xo_ref, bf16[512,1024]{1,0:T(8,128)(2,1)} %pad_maximum_fusion.6.own_ref.cm_ref, bf16[512,1024]{1,0:T(8,128)(2,1)} %collective-permute-done.9.co_ref, ...), custom_call_target="tpu_custom_call" | custom-call | flops 9663676416 | bytes 18874368 | tf_op jit(solution)/shard_map/hidden_units/pallas_call | solution.py:323
  121.3 14.2 %hidden_units.3.refs_3_.b_ref.refs_1_ = bf16[3,512,1280]{2,1,0:T(8,128)(2,1)} custom-call(bf16[512,1024]{1,0:T(8,128)(2,1)} %get-tuple-element.126.xm_ref.own_ref, bf16[512,1024]{1,0:T(8,128)(2,1)} %get-tuple-element.303.xo_ref, bf16[512,1024]{1,0:T(8,128)(2,1)} %pad_maximum_fusion.6.own_ref.cm_ref, bf16[512,1024]{1,0:T(8,128)(2,1)} %collective-permute-done.9.co_ref, ...), custom_call_target="tpu_custom_call" | custom-call | flops 8053063680 | bytes 15728640 | tf_op jit(solution)/shard_map/hidden_units/pallas_call | solution.py:323
  142.7 14.3 %product.6 = (bf16[512,2816]{1,0:T(8,128)(2,1)}, bf16[512,2816]{1,0:T(8,128)(2,1)}) custom-call(bf16[1024,1024]{1,0:T(8,128)(2,1)} %sided.4.refs_0_.refs_1_, bf16[1024,1024]{1,0:T(8,128)(2,1)} %sided.4.refs_0_.refs_1_, bf16[3,512,1536]{2,1,0:T(8,128)(2,1)} %hidden_units.2.refs_2_.a_ref.refs_1_.refs_0_, ...), custom_call_target="tpu_custom_call" | custom-call | flops 11811160064 | bytes 17301504 | tf_op jit(solution)/shard_map/product/pallas_call | solution.py:396
  157.0 20.6 %input_grad.1 = bf16[512,2048]{1,0:T(8,128)(2,1)} custom-call(bf16[3,512,1536]{2,1,0:T(8,128)(2,1)} %hidden_units.2.refs_2_.a_ref.refs_1_.refs_0_, bf16[3,512,1280]{2,1,0:T(8,128)(2,1)} %hidden_units.3.refs_3_.b_ref.refs_1_, bf16[1024,2816]{1,0:T(8,128)(2,1)} %gm_ref.2, bf16[1024,2816]{1,0:T(8,128)(2,1)} %um_ref.2, ...), custom_call_target="tpu_custom_call" | custom-call | flops 11811160064 | bytes 23068672 | tf_op jit(solution)/shard_map/input_grad/pallas_call | solution.py:356
  177.6 8.1 %product.7 = (bf16[512,1536]{1,0:T(8,128)(2,1)}, bf16[512,1536]{1,0:T(8,128)(2,1)}) custom-call(bf16[1024,1024]{1,0:T(8,128)(2,1)} %sided.6.refs_0_, bf16[3,512,1536]{2,1,0:T(8,128)(2,1)} %hidden_units.2.refs_2_.a_ref.refs_1_.refs_0_, bf16[3,512,1536]{2,1,0:T(8,128)(2,1)} %collective-permute-done.13.refs_4_.refs_2_), custom_call_target="tpu_custom_call" | custom-call | flops 6442450944 | bytes 9437184 | tf_op jit(solution)/shard_map/product/pallas_call | solution.py:396
  189.2 8.2 %product.8 = (bf16[512,1536]{1,0:T(8,128)(2,1)}, bf16[512,1536]{1,0:T(8,128)(2,1)}) custom-call(bf16[1024,1024]{1,0:T(8,128)(2,1)} %sided.6.refs_0_, bf16[3,512,1536]{2,1,0:T(8,128)(2,1)} %hidden_units.2.refs_2_.a_ref.refs_1_.refs_0_, bf16[3,512,1536]{2,1,0:T(8,128)(2,1)} %collective-permute-done.13.refs_4_.refs_2_), custom_call_target="tpu_custom_call" | custom-call | flops 6442450944 | bytes 9437184 | tf_op jit(solution)/shard_map/product/pallas_call | solution.py:396
  197.3 7.2 %product.9 = (bf16[512,1280]{1,0:T(8,128)(2,1)}, bf16[512,1280]{1,0:T(8,128)(2,1)}) custom-call(bf16[1024,1024]{1,0:T(8,128)(2,1)} %sided.6.refs_0_, bf16[3,512,1280]{2,1,0:T(8,128)(2,1)} %hidden_units.3.refs_3_.b_ref.refs_1_, bf16[3,512,1280]{2,1,0:T(8,128)(2,1)} %collective-permute-done.15.refs_5_.refs_2_), custom_call_target="tpu_custom_call" | custom-call | flops 5368709120 | bytes 7864320 | tf_op jit(solution)/shard_map/product/pallas_call | solution.py:396
  204.6 7.3 %product.10 = (bf16[512,1280]{1,0:T(8,128)(2,1)}, bf16[512,1280]{1,0:T(8,128)(2,1)}) custom-call(bf16[1024,1024]{1,0:T(8,128)(2,1)} %sided.6.refs_0_, bf16[3,512,1280]{2,1,0:T(8,128)(2,1)} %hidden_units.3.refs_3_.b_ref.refs_1_, bf16[3,512,1280]{2,1,0:T(8,128)(2,1)} %collective-permute-done.15.refs_5_.refs_2_), custom_call_target="tpu_custom_call" | custom-call | flops 5368709120 | bytes 7864320 | tf_op jit(solution)/shard_map/product/pallas_call | solution.py:396
  211.9 12.7 %blend.3 = bf16[512,2048]{1,0:T(8,128)(2,1)} custom-call(bf16[3,512,1536]{2,1,0:T(8,128)(2,1)} %hidden_units.2.refs_2_.a_ref.refs_1_.refs_0_, bf16[3,512,1280]{2,1,0:T(8,128)(2,1)} %hidden_units.3.refs_3_.b_ref.refs_1_, bf16[2816,1024]{1,0:T(8,128)(2,1)} %refs_2_.1, bf16[2816,1024]{1,0:T(8,128)(2,1)} %collective-permute-done.12.do_ref.refs_3_), custom_call_target="tpu_custom_call" | custom-call | flops 1000 | bytes 1000 | tf_op jit(solution)/shard_map/blend/pallas_call | solution.py:447
  224.5 10.9 %collective-permute-done.16 = bf16[512,2048]{1,0:T(8,128)(2,1)} collective-permute-done((bf16[512,2048]{1,0:T(8,128)(2,1)}, bf16[512,2048]{1,0:T(8,128)(2,1)}, u32[]{:S(2)}, u32[]{:S(2)}) %collective-permute-start.16) | collective-permute-done | bytes 2097184 | tf_op jit(solution)/shard_map/ppermute | solution.py:555
  235.4 15.3 %collective-permute-done.17 = bf16[512,2816]{1,0:T(8,128)(2,1)} collective-permute-done((bf16[512,2816]{1,0:T(8,128)(2,1)}, bf16[512,2816]{1,0:T(8,128)(2,1)}, u32[]{:S(2)}, u32[]{:S(2)}) %collective-permute-start.17) | collective-permute-done | bytes 2883616 | tf_op jit(solution)/shard_map/ppermute | solution.py:558
  268.8 6.3 %blend.4.do_ref = bf16[512,1024]{1,0:T(8,128)(2,1)} custom-call(bf16[1,512,1024]{2,1,0:T(8,128)(2,1)} %bitcast.53, bf16[1,512,1024]{2,1,0:T(8,128)(2,1)} %bitcast.10.refs_1_, bf16[1024,1024]{1,0:T(8,128)(2,1)} %refs_2_.2, bf16[1024,1024]{1,0:T(8,128)(2,1)} %collective-permute-done.6.refs_3_), custom_call_target="tpu_custom_call" | custom-call | flops 1000 | bytes 1000 | tf_op jit(solution)/shard_map/blend/pallas_call | solution.py:447
  275.1 18.0 %collective-permute-done.19 = bf16[512,1536]{1,0:T(8,128)(2,1)} collective-permute-done((bf16[512,1536]{1,0:T(8,128)(2,1)}, bf16[512,1536]{1,0:T(8,128)(2,1)}, u32[]{:S(2)}, u32[]{:S(2)}) %collective-permute-start.19) | collective-permute-done | bytes 1572896 | tf_op jit(solution)/shard_map/ppermute | solution.py:558
  298.1 20.6 %attend_back.1 = (bf16[512,1024]{1,0:T(8,128)(2,1)}, f32[2,1024,64]{2,1,0:T(8,128)}, f32[2,1024,64]{2,1,0:T(8,128)}) custom-call(s32[1]{0:T(128)} %bitcast.row_ref, bf16[1024,512]{1,0:T(8,128)(2,1)} %get-tuple-element.113.qt_ref, bf16[512,1024]{1,0:T(8,128)(2,1)} %blend.4.do_ref, bf16[512,1024]{1,0:T(8,128)(2,1)} %get-tuple-element.111.o_ref, ...), custom_call_target="tpu_custom_call" | custom-call | flops 1000 | bytes 1000 | tf_op jit(solution)/shard_map/attend_back/pallas_call | solution.py:265
  337.1 6.2 %sided.7.refs_0_ = bf16[1024,1024]{1,0:T(8,128)(2,1)} custom-call(s32[1]{0:T(128)} %bitcast.7.side_ref, bf16[512,1024]{1,0:T(8,128)(2,1)} %get-tuple-element.250.own_ref, bf16[512,1024]{1,0:T(8,128)(2,1)} %collective-permute-done.18.other_ref), custom_call_target="tpu_custom_call" | custom-call | flops 1000 | bytes 1000 | tf_op jit(solution)/shard_map/sided/pallas_call | solution.py:474
  344.1 11.7 %product.11 = (bf16[512,2304]{1,0:T(8,128)(2,1)}, bf16[512,2304]{1,0:T(8,128)(2,1)}) custom-call(bf16[1024,1024]{1,0:T(8,128)(2,1)} %sided.7.refs_0_, bf16[1024,1024]{1,0:T(8,128)(2,1)} %sided.5.refs_1_, bf16[1,512,1024]{2,1,0:T(8,128)(2,1)} %bitcast.11.refs_2_, bf16[1,512,1280]{2,1,0:T(8,128)(2,1)} %get-tuple-element.280.refs_3_, ...), custom_call_target="tpu_custom_call" | custom-call | flops 9663676416 | bytes 14155776 | tf_op jit(solution)/shard_map/product/pallas_call | solution.py:396
  355.8 9.2 %blend.5 = bf16[512,2048]{1,0:T(8,128)(2,1)} custom-call(bf16[1,512,1024]{2,1,0:T(8,128)(2,1)} %bitcast.54, bf16[1,512,256]{2,1,0:T(8,128)(2,1)} %maximum_bitcast_fusion.refs_1_, bf16[1024,1024]{1,0:T(8,128)(2,1)} %refs_2_.3, bf16[1024,256]{1,0:T(8,128)(2,1)} %copy-done.23, bf16[1024,1024]{1,0:T(8,128)(2,1)} %collective-permute-done.3.refs_4_, ...), custom_call_target="tpu_custom_call" | custom-call | flops 1000 | bytes 1000 | tf_op jit(solution)/shard_map/blend/pallas_call | solution.py:447
  372.4 42.7 %collective-permute-done.25 = bf16[512,2048]{1,0:T(8,128)(2,1)} collective-permute-done((bf16[512,2048]{1,0:T(8,128)(2,1)}, bf16[512,2048]{1,0:T(8,128)(2,1)}, u32[]{:S(2)}, u32[]{:S(2)}) %collective-permute-start.25) | collective-permute-done | bytes 2097184 | tf_op jit(solution)/shard_map/ppermute | solution.py:555
  435.6 6.5 %fusion.19 = (f32[512,1024]{1,0:T(8,128)}, f32[512,1024]{1,0:T(8,128)}, bf16[512,1024]{1,0:T(8,128)(2,1)}, bf16[512,1024]{1,0:T(8,128)(2,1)}) fusion(bf16[512,1024]{1,0:T(8,128)(2,1)S(1)} %collective-permute-done, f32[512,2048]{1,0:T(8,128)} %copy-done.5, f32[512]{0:T(512)S(1)} %add_multiply_fusion, f32[1024]{0:T(1024)S(1)} %bitcast.66, ...), kind=kLoop, calls=%fused_computation.35 | loop fusion | flops 14680064 | bytes 26234880 | tf_op jit(solution)/shard_map/add | solution.py:723
  470.6 9.7 %reduce-scatter.18.cloned.1.call-done = bf16[128,2304]{1,0:T(8,128)(2,1)} async-done(((bf16[512,2304]{1,0:T(8,128)(2,1)}), bf16[128,2304]{1,0:T(8,128)(2,1)}) %reduce-scatter.18.cloned.1.call-update) | async-done | bytes 589840 | tf_op jit(solution)/shard_map/reduce_scatter | solution.py:508
  (290 shorter events, 161.3 us)
Async XLA Ops:
  7.2 228.2 %reduce-scatter.8.cloned.1.call-start = ((), (), s32[]{:S(2)}) async-start(), calls=%async_computation.7 | async-start | bytes 1966080 | tf_op jit(solution)/shard_map/reduce_scatter | solution.py:508
  15.7 88.8 %collective-permute-start.10 = (bf16[1024,2816]{1,0:T(8,128)(2,1)}, bf16[1024,2816]{1,0:T(8,128)(2,1)}, u32[]{:S(2)}, u32[]{:S(2)}) collective-permute-start(bf16[1024,2816]{1,0:T(8,128)(2,1)} %gm_ref.2), channel_id=1, source_target_pairs={{0,2},{2,0},{1,3},{3,1},{4,6},{6,4},{5,7},{7,5},{8,10},{10,8},{9,1... | collective-permute-start | bytes 17301512 | tf_op jit(solution)/shard_map/ppermute | solution.py:552
  16.2 88.3 %collective-permute-start.11 = (bf16[1024,2816]{1,0:T(8,128)(2,1)}, bf16[1024,2816]{1,0:T(8,128)(2,1)}, u32[]{:S(2)}, u32[]{:S(2)}) collective-permute-start(bf16[1024,2816]{1,0:T(8,128)(2,1)} %um_ref.2), channel_id=1, source_target_pairs={{0,2},{2,0},{1,3},{3,1},{4,6},{6,4},{5,7},{7,5},{8,10},{10,8},{9,1... | collective-permute-start | bytes 17301512 | tf_op jit(solution)/shard_map/ppermute | solution.py:552
  16.2 88.2 %collective-permute-start.12 = (bf16[2816,1024]{1,0:T(8,128)(2,1)}, bf16[2816,1024]{1,0:T(8,128)(2,1)}, u32[]{:S(2)}, u32[]{:S(2)}) collective-permute-start(bf16[2816,1024]{1,0:T(8,128)(2,1)} %refs_2_.1), channel_id=1, source_target_pairs={{0,2},{2,0},{1,3},{3,1},{4,6},{6,4},{5,7},{7,5},{8,10},{10,8},{9,1... | collective-permute-start | bytes 17301512 | tf_op jit(solution)/shard_map/ppermute | solution.py:552
  20.7 31.5 %collective-permute-start.6 = (bf16[1024,1024]{1,0:T(8,128)(2,1)}, bf16[1024,1024]{1,0:T(8,128)(2,1)}, u32[]{:S(2)}, u32[]{:S(2)}) collective-permute-start(bf16[1024,1024]{1,0:T(8,128)(2,1)} %refs_2_.2), channel_id=1, source_target_pairs={{0,2},{2,0},{1,3},{3,1},{4,6},{6,4},{5,7},{7,5},{8,10},{10,8},{9,1... | collective-permute-start | bytes 6291464 | tf_op jit(solution)/shard_map/ppermute | solution.py:552
  26.0 33.2 %collective-permute-start.8 = (bf16[512,1024]{1,0:T(8,128)(2,1)S(1)}, bf16[512,1024]{1,0:T(8,128)(2,1)S(1)}, u32[]{:S(2)}, u32[]{:S(2)}) collective-permute-start(bf16[512,1024]{1,0:T(8,128)(2,1)S(1)} %copy-done.22), channel_id=1, source_target_pairs={{0,2},{2,0},{1,3},{3,1},{4,6},{6,4},{5,7},{7,5},{8,10},{10,8},{9,1... | collective-permute-start | bytes 3145736 | tf_op jit(solution)/shard_map/ppermute | solution.py:552
  52.1 27.3 %collective-permute-start.5 = (bf16[512,1024]{1,0:T(8,128)(2,1)}, bf16[512,1024]{1,0:T(8,128)(2,1)}, u32[]{:S(2)}, u32[]{:S(2)}) collective-permute-start(bf16[512,1024]{1,0:T(8,128)(2,1)} %convolution_convert_fusion.1), channel_id=1, source_target_pairs={{0,1},{1,0},{2,3},{3,2},{4,5},{5,4},{6,7},{7,6},{8,9},{9,8},{10,11... | collective-permute-start | bytes 3145736 | tf_op jit(solution)/shard_map/ppermute | solution.py:555
  59.1 41.2 %collective-permute-start.7 = (bf16[512,1024]{1,0:T(8,128)(2,1)}, bf16[512,1024]{1,0:T(8,128)(2,1)}, u32[]{:S(2)}, u32[]{:S(2)}) collective-permute-start(bf16[512,1024]{1,0:T(8,128)(2,1)} %convolution_convert_fusion), channel_id=1, source_target_pairs={{0,1},{1,0},{2,3},{3,2},{4,5},{5,4},{6,7},{7,6},{8,9},{9,8},{10,11... | collective-permute-start | bytes 3145736 | tf_op jit(solution)/shard_map/ppermute | solution.py:555
  79.4 25.0 %collective-permute-start.9 = (bf16[512,1024]{1,0:T(8,128)(2,1)}, bf16[512,1024]{1,0:T(8,128)(2,1)}, u32[]{:S(2)}, u32[]{:S(2)}) collective-permute-start(bf16[512,1024]{1,0:T(8,128)(2,1)} %pad_maximum_fusion.7.other_ref), channel_id=1, source_target_pairs={{0,2},{2,0},{1,3},{3,1},{4,6},{6,4},{5,7},{7,5},{8,10},{10,8},{9,1... | collective-permute-start | bytes 3145736 | tf_op jit(solution)/shard_map/ppermute | solution.py:552
  185.7 89.5 %reduce-scatter.10.cloned.1.call-start = ((), (), s32[]{:S(2)}) async-start(), calls=%async_computation.8 | async-start | bytes 1966080 | tf_op jit(solution)/shard_map/reduce_scatter | solution.py:508
  185.7 64.9 %collective-permute-start.17 = (bf16[512,2816]{1,0:T(8,128)(2,1)}, bf16[512,2816]{1,0:T(8,128)(2,1)}, u32[]{:S(2)}, u32[]{:S(2)}) collective-permute-start(bf16[512,2816]{1,0:T(8,128)(2,1)} %get-tuple-element.147), channel_id=1, source_target_pairs={{0,4},{4,0},{8,12},{12,8},{16,20},{20,16},{24,28},{28,24},{1,5},{5... | collective-permute-start | bytes 8650760 | tf_op jit(solution)/shard_map/ppermute | solution.py:558
  187.6 177.4 %reduce-scatter.12.cloned.1.call-start = ((), (), s32[]{:S(2)}) async-start(), calls=%async_computation.9 | async-start | bytes 3604480 | tf_op jit(solution)/shard_map/reduce_scatter | solution.py:508
  187.6 47.8 %collective-permute-start.16 = (bf16[512,2048]{1,0:T(8,128)(2,1)}, bf16[512,2048]{1,0:T(8,128)(2,1)}, u32[]{:S(2)}, u32[]{:S(2)}) collective-permute-start(bf16[512,2048]{1,0:T(8,128)(2,1)} %input_grad.1), channel_id=1, source_target_pairs={{0,1},{1,0},{2,3},{3,2},{4,5},{5,4},{6,7},{7,6},{8,9},{9,8},{10,11... | collective-permute-start | bytes 6291464 | tf_op jit(solution)/shard_map/ppermute | solution.py:555
  255.6 116.8 %reduce-scatter.14.cloned.1.call-start = ((), (), s32[]{:S(2)}) async-start(), calls=%async_computation.10 | async-start | bytes 1966080 | tf_op jit(solution)/shard_map/reduce_scatter | solution.py:508
  255.7 63.0 %collective-permute-start.20 = (bf16[512,2048]{1,0:T(8,128)(2,1)}, bf16[512,2048]{1,0:T(8,128)(2,1)}, u32[]{:S(2)}, u32[]{:S(2)}) collective-permute-start(bf16[512,2048]{1,0:T(8,128)(2,1)} %blend.3), channel_id=1, source_target_pairs={{0,1},{1,0},{2,3},{3,2},{4,5},{5,4},{6,7},{7,6},{8,9},{9,8},{10,11... | collective-permute-start | bytes 6291464 | tf_op jit(solution)/shard_map/ppermute | solution.py:555
  257.5 35.6 %collective-permute-start.19 = (bf16[512,1536]{1,0:T(8,128)(2,1)}, bf16[512,1536]{1,0:T(8,128)(2,1)}, u32[]{:S(2)}, u32[]{:S(2)}) collective-permute-start(bf16[512,1536]{1,0:T(8,128)(2,1)} %get-tuple-element.156), channel_id=1, source_target_pairs={{0,4},{4,0},{8,12},{12,8},{16,20},{20,16},{24,28},{28,24},{1,5},{5... | collective-permute-start | bytes 4718600 | tf_op jit(solution)/shard_map/ppermute | solution.py:558
  293.1 29.1 %collective-permute-start.21 = (bf16[512,1280]{1,0:T(8,128)(2,1)}, bf16[512,1280]{1,0:T(8,128)(2,1)}, u32[]{:S(2)}, u32[]{:S(2)}) collective-permute-start(bf16[512,1280]{1,0:T(8,128)(2,1)} %get-tuple-element.165), channel_id=1, source_target_pairs={{0,4},{4,0},{8,12},{12,8},{16,20},{20,16},{24,28},{28,24},{1,5},{5... | collective-permute-start | bytes 3932168 | tf_op jit(solution)/shard_map/ppermute | solution.py:558
  318.7 96.4 %reduce-scatter.16.cloned.1.call-start = ((), (), s32[]{:S(2)}) async-start(), calls=%async_computation.11 | async-start | bytes 1638400 | tf_op jit(solution)/shard_map/reduce_scatter | solution.py:508
  335.5 31.1 %collective-permute-start.26 = (bf16[512,1280]{1,0:T(8,128)(2,1)}, bf16[512,1280]{1,0:T(8,128)(2,1)}, u32[]{:S(2)}, u32[]{:S(2)}) collective-permute-start(bf16[512,1280]{1,0:T(8,128)(2,1)} %get-tuple-element.180), channel_id=1, source_target_pairs={{0,4},{4,0},{8,12},{12,8},{16,20},{20,16},{24,28},{28,24},{1,5},{5... | collective-permute-start | bytes 3932168 | tf_op jit(solution)/shard_map/ppermute | solution.py:558
  343.3 116.4 %reduce-scatter.20.cloned.1.call-start = ((), (), s32[]{:S(2)}) async-start(), calls=%async_computation.13 | async-start | bytes 1638400 | tf_op jit(solution)/shard_map/reduce_scatter | solution.py:508
  366.6 54.5 %collective-permute-start.27 = (bf16[512,2304]{1,0:T(8,128)(2,1)}, bf16[512,2304]{1,0:T(8,128)(2,1)}, u32[]{:S(2)}, u32[]{:S(2)}) collective-permute-start(bf16[512,2304]{1,0:T(8,128)(2,1)} %get-tuple-element.188), channel_id=1, source_target_pairs={{0,4},{4,0},{8,12},{12,8},{16,20},{20,16},{24,28},{28,24},{1,5},{5... | collective-permute-start | bytes 7077896 | tf_op jit(solution)/shard_map/ppermute | solution.py:558
  368.2 46.9 %collective-permute-start.25 = (bf16[512,2048]{1,0:T(8,128)(2,1)}, bf16[512,2048]{1,0:T(8,128)(2,1)}, u32[]{:S(2)}, u32[]{:S(2)}) collective-permute-start(bf16[512,2048]{1,0:T(8,128)(2,1)} %blend.5), channel_id=1, source_target_pairs={{0,1},{1,0},{2,3},{3,2},{4,5},{5,4},{6,7},{7,6},{8,9},{9,8},{10,11... | collective-permute-start | bytes 6291464 | tf_op jit(solution)/shard_map/ppermute | solution.py:555
  371.7 108.6 %reduce-scatter.18.cloned.1.call-start = ((), (), s32[]{:S(2)}) async-start(), calls=%async_computation.12 | async-start | bytes 2949120 | tf_op jit(solution)/shard_map/reduce_scatter | solution.py:508
  371.9 82.4 %collective-permute-start.34 = (bf16[128,1536]{1,0:T(8,128)(2,1)}, bf16[128,1536]{1,0:T(8,128)(2,1)S(1)}, u32[]{:S(2)}, u32[]{:S(2)}) collective-permute-start(bf16[128,1536]{1,0:T(8,128)(2,1)} %reduce-scatter.8.cloned.1.call-done), channel_id=1, source_target_pairs={{0,4},{4,0},{8,12},{12,8},{16,20},{20,16},{24,28},{28,24},{1,5},{5... | collective-permute-start | bytes 1179656 | tf_op jit(solution)/shard_map/ppermute | solution.py:558
  (76 other events, 377.6 us)
Sparse Core Ops, SparseCore 0:
  185.8 36.7 reduce-scatter.7
  224.9 34.2 reduce-scatter.9
  262.1 55.1 reduce-scatter.11
  319.5 35.1 reduce-scatter.13
  357.4 30.1 reduce-scatter.15
  390.3 29.9 reduce-scatter.19
  431.4 48.8 reduce-scatter.17

commit v9 on v8

--- a/solution.py
+++ b/solution.py
@@ -650,10 +650,8 @@
     send_2 = Summed([(xn2_y, one, one_t, 1)], flip, count)
     send_2.begin(part)
     send_3 = Summed([(xn2_y, two, two_t, 1)], flip, count)
-    send_3.begin(send_2.keep)
     send_4 = Summed([(xn2_y, two, two_t, 2)], flip, count)
-    send_4.begin(send_3.keep)
-    one_late, _ = tie(one, send_4.keep)
+    one_late, _ = tie(one, send_2.keep)
     mix = blend([[one_late, two]], [[w_down], [wd_o]], False, BF16)
     mix_came = cross(mix)
     came, first_z.send, part = tie(came, first_z.send, part, mix)[:3]
@@ -675,7 +673,9 @@
     dh_m, dh_o = d_hid_m.astype(BF16), d_hid_o.astype(BF16)
     dh_t = swap(dh_o)
     d_o = blend([[dh_m], [dh_o]], [[w_o, w_o_o]], True, BF16)
-    d_o, dh_t, first_z.keep = tie(d_o, dh_t, first_z.keep)
+    send_3.begin(d_o)
+    send_4.begin(send_3.keep)
+    d_o, dh_t, first_z.keep, send_4.keep = tie(d_o, dh_t, first_z.keep, send_4.keep)
     d_o = serve(d_o, (send_2,))
     send_3.go(send_2)
     d_o, _ = tie(d_o, send_2.finish())

time: 499 us -> 502 us (level)
    ppermute x6, waiting for transfers between devices: 41.9 us -> 27.4 us  [flip(): return lax.ppermute(value, 'dp', [(i, i ^ 1) for i in range(count)])]
    ppermute x5, waiting for transfers between devices: 75.5 us -> 89.8 us  [cross(): return lax.ppermute(value, 'col', [(0, 1), (1, 0)])]
    ppermute x3, waiting for transfers between devices: 8.11 us -> 2.99 us  [shards(): gg = gg + lax.ppermute(gg, 'dp', [(i, i ^ 1 << bit) for i in range(count)])]
where the time goes in v9:
time: 502 us; the launch traced here: 495 us
  Pallas kernels  203 us (40%)
  waiting for transfers between devices  136 us (27%)
  other arithmetic  77.8 us (15%)
  starting transfers between devices  26.8 us (5%)
  local copies, waits for them, and re-layouts  19.5 us (4%)
  matrix products  16.2 us (3%)
  between operations  15.3 us (3%)
    ppermute x5, waiting for transfers between devices, cross(): return lax.ppermute(value, 'col', [(0, 1), (1, 0)])  89.8 us
    pallas_call x6, Pallas kernels, product(): pl.pallas_call(functools.partial(product_kernel, counts), grid=(first,),...  56.5 us
    pallas_call x2, Pallas kernels, hidden_units(): pl.pallas_call(hidden_units_kernel, grid=(tiles,), in_specs=[full] * 4 +...  30.5 us
    pallas_call x3, Pallas kernels, blend(): pl.pallas_call(functools.partial(blend_kernel, sizes, len(weights), count...  28.2 us
    ppermute x6, waiting for transfers between devices, flip(): return lax.ppermute(value, 'dp', [(i, i ^ 1) for i in range(count)])  27.4 us
    pallas_call x4, Pallas kernels, sided(): pl.pallas_call(sided_kernel, grid_spec=pltpu.PrefetchScalarGridSpec(num_s...  24.7 us
    pallas_call x1, Pallas kernels, attend(): pl.pallas_call(attend_kernel, grid=(pairs,), in_specs=[pl.BlockSpec(memor...  21.5 us
    pallas_call x1, Pallas kernels, input_grad(): pl.pallas_call(input_grad_kernel, grid=(2 * tiles,), in_specs=[full(a), f...  20.6 us
  transfers between devices with their start and end apart: 42, of which 16 were waited for; matrix products, arithmetic and copies ran while one was open for 20% of the time, Pallas kernels for 29%

profile of v9, /device:TPU:0, one launch (start us, length us, event | category | flops | bytes accessed | tf_op | source)
XLA Modules:
  0.0 494.5 jit_solution(8742427300042379838)
XLA Ops:
  30.2 21.5 %attend.1 = (bf16[512,1024]{1,0:T(8,128)(2,1)}, f32[8,2,512]{2,1,0:T(2,128)}, bf16[1024,512]{1,0:T(8,128)(2,1)}) custom-call(s32[1]{0:T(128)} %bitcast.row_ref, f32[512,1024]{1,0:T(8,128)} %fusion.30.q_ref, f32[32,512]{1,0:T(8,128)} %get-tuple-element.302.cos_ref, f32[32,512]{1,0:T(8,128)} %get-tuple-element.301.sin_ref, s32[1,512]{1,0:T(1,128)} %bitcast.74, ...), custom_call_target="tpu_custom_call" | custom-call | flops 20000000000 | bytes 8000000 | tf_op jit(solution)/shard_map/attend/pallas_call | solution.py:147
  67.7 15.4 %collective-permute-done.5 = bf16[512,1024]{1,0:T(8,128)(2,1)} collective-permute-done((bf16[512,1024]{1,0:T(8,128)(2,1)}, bf16[512,1024]{1,0:T(8,128)(2,1)}, u32[]{:S(2)}, u32[]{:S(2)}) %collective-permute-start.5) | collective-permute-done | bytes 1048608 | tf_op jit(solution)/shard_map/ppermute | solution.py:555
  85.2 6.2 %sided.4.refs_0_.refs_1_ = bf16[1024,1024]{1,0:T(8,128)(2,1)} custom-call(s32[1]{0:T(128)} %bitcast.7.side_ref, bf16[512,1024]{1,0:T(8,128)(2,1)} %pad_maximum_fusion.6.own_ref.cm_ref, bf16[512,1024]{1,0:T(8,128)(2,1)} %pad_maximum_fusion.7.other_ref), custom_call_target="tpu_custom_call" | custom-call | flops 1000 | bytes 1000 | tf_op jit(solution)/shard_map/sided/pallas_call | solution.py:474
  91.4 6.2 %sided.5.refs_1_ = bf16[1024,1024]{1,0:T(8,128)(2,1)} custom-call(s32[1]{0:T(128)} %bitcast.7.side_ref, bf16[512,1024]{1,0:T(8,128)(2,1)} %copy-done.14, bf16[512,1024]{1,0:T(8,128)(2,1)} %copy-done.28), custom_call_target="tpu_custom_call" | custom-call | flops 1000 | bytes 1000 | tf_op jit(solution)/shard_map/sided/pallas_call | solution.py:474
  97.6 6.5 %collective-permute-done.7 = bf16[512,1024]{1,0:T(8,128)(2,1)} collective-permute-done((bf16[512,1024]{1,0:T(8,128)(2,1)}, bf16[512,1024]{1,0:T(8,128)(2,1)}, u32[]{:S(2)}, u32[]{:S(2)}) %collective-permute-start.7) | collective-permute-done | bytes 1048608 | tf_op jit(solution)/shard_map/ppermute | solution.py:555
  108.2 16.3 %hidden_units.2.refs_2_.a_ref.refs_1_.refs_0_ = bf16[3,512,1536]{2,1,0:T(8,128)(2,1)} custom-call(bf16[512,1024]{1,0:T(8,128)(2,1)} %get-tuple-element.127.xm_ref.own_ref, bf16[512,1024]{1,0:T(8,128)(2,1)} %get-tuple-element.305.xo_ref, bf16[512,1024]{1,0:T(8,128)(2,1)} %pad_maximum_fusion.6.own_ref.cm_ref, bf16[512,1024]{1,0:T(8,128)(2,1)} %collective-permute-done.9.co_ref, ...), custom_call_target="tpu_custom_call" | custom-call | flops 9663676416 | bytes 18874368 | tf_op jit(solution)/shard_map/hidden_units/pallas_call | solution.py:323
  125.0 14.2 %hidden_units.3.refs_3_.b_ref.refs_1_ = bf16[3,512,1280]{2,1,0:T(8,128)(2,1)} custom-call(bf16[512,1024]{1,0:T(8,128)(2,1)} %get-tuple-element.127.xm_ref.own_ref, bf16[512,1024]{1,0:T(8,128)(2,1)} %get-tuple-element.305.xo_ref, bf16[512,1024]{1,0:T(8,128)(2,1)} %pad_maximum_fusion.6.own_ref.cm_ref, bf16[512,1024]{1,0:T(8,128)(2,1)} %collective-permute-done.9.co_ref, ...), custom_call_target="tpu_custom_call" | custom-call | flops 8053063680 | bytes 15728640 | tf_op jit(solution)/shard_map/hidden_units/pallas_call | solution.py:323
  146.4 13.9 %product.6 = (bf16[512,2816]{1,0:T(8,128)(2,1)}, bf16[512,2816]{1,0:T(8,128)(2,1)}) custom-call(bf16[1024,1024]{1,0:T(8,128)(2,1)} %sided.4.refs_0_.refs_1_, bf16[1024,1024]{1,0:T(8,128)(2,1)} %sided.4.refs_0_.refs_1_, bf16[3,512,1536]{2,1,0:T(8,128)(2,1)} %hidden_units.2.refs_2_.a_ref.refs_1_.refs_0_, ...), custom_call_target="tpu_custom_call" | custom-call | flops 11811160064 | bytes 17301504 | tf_op jit(solution)/shard_map/product/pallas_call | solution.py:396
  160.2 20.6 %input_grad.1 = bf16[512,2048]{1,0:T(8,128)(2,1)} custom-call(bf16[3,512,1536]{2,1,0:T(8,128)(2,1)} %hidden_units.2.refs_2_.a_ref.refs_1_.refs_0_, bf16[3,512,1280]{2,1,0:T(8,128)(2,1)} %hidden_units.3.refs_3_.b_ref.refs_1_, bf16[1024,2816]{1,0:T(8,128)(2,1)} %gm_ref.2, bf16[1024,2816]{1,0:T(8,128)(2,1)} %um_ref.2, ...), custom_call_target="tpu_custom_call" | custom-call | flops 11811160064 | bytes 23068672 | tf_op jit(solution)/shard_map/input_grad/pallas_call | solution.py:356
  180.9 8.1 %product.7 = (bf16[512,1536]{1,0:T(8,128)(2,1)}, bf16[512,1536]{1,0:T(8,128)(2,1)}) custom-call(bf16[1024,1024]{1,0:T(8,128)(2,1)} %sided.6.refs_0_, bf16[3,512,1536]{2,1,0:T(8,128)(2,1)} %hidden_units.2.refs_2_.a_ref.refs_1_.refs_0_, bf16[3,512,1536]{2,1,0:T(8,128)(2,1)} %collective-permute-done.13.refs_4_.refs_2_), custom_call_target="tpu_custom_call" | custom-call | flops 6442450944 | bytes 9437184 | tf_op jit(solution)/shard_map/product/pallas_call | solution.py:396
  192.5 8.2 %product.8 = (bf16[512,1536]{1,0:T(8,128)(2,1)}, bf16[512,1536]{1,0:T(8,128)(2,1)}) custom-call(bf16[1024,1024]{1,0:T(8,128)(2,1)} %sided.6.refs_0_, bf16[3,512,1536]{2,1,0:T(8,128)(2,1)} %hidden_units.2.refs_2_.a_ref.refs_1_.refs_0_, bf16[3,512,1536]{2,1,0:T(8,128)(2,1)} %collective-permute-done.13.refs_4_.refs_2_), custom_call_target="tpu_custom_call" | custom-call | flops 6442450944 | bytes 9437184 | tf_op jit(solution)/shard_map/product/pallas_call | solution.py:396
  200.7 12.7 %blend.3 = bf16[512,2048]{1,0:T(8,128)(2,1)} custom-call(bf16[3,512,1536]{2,1,0:T(8,128)(2,1)} %hidden_units.2.refs_2_.a_ref.refs_1_.refs_0_, bf16[3,512,1280]{2,1,0:T(8,128)(2,1)} %hidden_units.3.refs_3_.b_ref.refs_1_, bf16[2816,1024]{1,0:T(8,128)(2,1)} %refs_2_.1, bf16[2816,1024]{1,0:T(8,128)(2,1)} %collective-permute-done.12.do_ref.refs_3_), custom_call_target="tpu_custom_call" | custom-call | flops 1000 | bytes 1000 | tf_op jit(solution)/shard_map/blend/pallas_call | solution.py:447
  213.4 25.3 %collective-permute-done.16 = bf16[512,2048]{1,0:T(8,128)(2,1)} collective-permute-done((bf16[512,2048]{1,0:T(8,128)(2,1)}, bf16[512,2048]{1,0:T(8,128)(2,1)}, u32[]{:S(2)}, u32[]{:S(2)}) %collective-permute-start.16) | collective-permute-done | bytes 2097184 | tf_op jit(solution)/shard_map/ppermute | solution.py:555
  238.7 15.3 %collective-permute-done.17 = bf16[512,2816]{1,0:T(8,128)(2,1)} collective-permute-done((bf16[512,2816]{1,0:T(8,128)(2,1)}, bf16[512,2816]{1,0:T(8,128)(2,1)}, u32[]{:S(2)}, u32[]{:S(2)}) %collective-permute-start.17) | collective-permute-done | bytes 2883616 | tf_op jit(solution)/shard_map/ppermute | solution.py:558
  272.2 6.3 %blend.4.do_ref = bf16[512,1024]{1,0:T(8,128)(2,1)} custom-call(bf16[1,512,1024]{2,1,0:T(8,128)(2,1)} %bitcast.53, bf16[1,512,1024]{2,1,0:T(8,128)(2,1)} %bitcast.10.refs_1_, bf16[1024,1024]{1,0:T(8,128)(2,1)} %refs_2_.2, bf16[1024,1024]{1,0:T(8,128)(2,1)} %collective-permute-done.6.refs_3_), custom_call_target="tpu_custom_call" | custom-call | flops 1000 | bytes 1000 | tf_op jit(solution)/shard_map/blend/pallas_call | solution.py:447
  278.5 7.2 %product.9 = (bf16[512,1280]{1,0:T(8,128)(2,1)}, bf16[512,1280]{1,0:T(8,128)(2,1)}) custom-call(bf16[1024,1024]{1,0:T(8,128)(2,1)} %sided.6.refs_0_, bf16[3,512,1280]{2,1,0:T(8,128)(2,1)} %hidden_units.3.refs_3_.b_ref.refs_1_, bf16[3,512,1280]{2,1,0:T(8,128)(2,1)} %collective-permute-done.15.refs_5_.refs_2_), custom_call_target="tpu_custom_call" | custom-call | flops 5368709120 | bytes 7864320 | tf_op jit(solution)/shard_map/product/pallas_call | solution.py:396
  285.7 7.3 %product.10 = (bf16[512,1280]{1,0:T(8,128)(2,1)}, bf16[512,1280]{1,0:T(8,128)(2,1)}) custom-call(bf16[1024,1024]{1,0:T(8,128)(2,1)} %sided.6.refs_0_, bf16[3,512,1280]{2,1,0:T(8,128)(2,1)} %hidden_units.3.refs_3_.b_ref.refs_1_, bf16[3,512,1280]{2,1,0:T(8,128)(2,1)} %collective-permute-done.15.refs_5_.refs_2_), custom_call_target="tpu_custom_call" | custom-call | flops 5368709120 | bytes 7864320 | tf_op jit(solution)/shard_map/product/pallas_call | solution.py:396
  301.3 20.5 %attend_back.1 = (bf16[512,1024]{1,0:T(8,128)(2,1)}, f32[2,1024,64]{2,1,0:T(8,128)}, f32[2,1024,64]{2,1,0:T(8,128)}) custom-call(s32[1]{0:T(128)} %bitcast.row_ref, bf16[1024,512]{1,0:T(8,128)(2,1)} %get-tuple-element.114.qt_ref, bf16[512,1024]{1,0:T(8,128)(2,1)} %blend.4.do_ref, bf16[512,1024]{1,0:T(8,128)(2,1)} %get-tuple-element.112.o_ref, ...), custom_call_target="tpu_custom_call" | custom-call | flops 1000 | bytes 1000 | tf_op jit(solution)/shard_map/attend_back/pallas_call | solution.py:265
  340.2 6.2 %sided.7.refs_0_ = bf16[1024,1024]{1,0:T(8,128)(2,1)} custom-call(s32[1]{0:T(128)} %bitcast.7.side_ref, bf16[512,1024]{1,0:T(8,128)(2,1)} %get-tuple-element.252.own_ref, bf16[512,1024]{1,0:T(8,128)(2,1)} %collective-permute-done.18.other_ref), custom_call_target="tpu_custom_call" | custom-call | flops 1000 | bytes 1000 | tf_op jit(solution)/shard_map/sided/pallas_call | solution.py:474
  347.2 11.9 %product.11 = (bf16[512,2304]{1,0:T(8,128)(2,1)}, bf16[512,2304]{1,0:T(8,128)(2,1)}) custom-call(bf16[1024,1024]{1,0:T(8,128)(2,1)} %sided.7.refs_0_, bf16[1024,1024]{1,0:T(8,128)(2,1)} %sided.5.refs_1_, bf16[1,512,1024]{2,1,0:T(8,128)(2,1)} %bitcast.11.refs_2_, bf16[1,512,1280]{2,1,0:T(8,128)(2,1)} %get-tuple-element.282.refs_3_, ...), custom_call_target="tpu_custom_call" | custom-call | flops 9663676416 | bytes 14155776 | tf_op jit(solution)/shard_map/product/pallas_call | solution.py:396
  359.1 9.2 %blend.5 = bf16[512,2048]{1,0:T(8,128)(2,1)} custom-call(bf16[1,512,1024]{2,1,0:T(8,128)(2,1)} %bitcast.54, bf16[1,512,256]{2,1,0:T(8,128)(2,1)} %maximum_bitcast_fusion.refs_1_, bf16[1024,1024]{1,0:T(8,128)(2,1)} %refs_2_.3, bf16[1024,256]{1,0:T(8,128)(2,1)} %copy-done.21, bf16[1024,1024]{1,0:T(8,128)(2,1)} %collective-permute-done.3.refs_4_, ...), custom_call_target="tpu_custom_call" | custom-call | flops 1000 | bytes 1000 | tf_op jit(solution)/shard_map/blend/pallas_call | solution.py:447
  375.7 42.5 %collective-permute-done.25 = bf16[512,2048]{1,0:T(8,128)(2,1)} collective-permute-done((bf16[512,2048]{1,0:T(8,128)(2,1)}, bf16[512,2048]{1,0:T(8,128)(2,1)}, u32[]{:S(2)}, u32[]{:S(2)}) %collective-permute-start.25) | collective-permute-done | bytes 2097184 | tf_op jit(solution)/shard_map/ppermute | solution.py:555
  438.3 6.4 %fusion.19 = (f32[512,1024]{1,0:T(8,128)}, f32[512,1024]{1,0:T(8,128)}, bf16[512,1024]{1,0:T(8,128)(2,1)}, bf16[512,1024]{1,0:T(8,128)(2,1)}) fusion(bf16[512,1024]{1,0:T(8,128)(2,1)S(1)} %collective-permute-done, f32[512,2048]{1,0:T(8,128)} %copy-done.5, f32[512]{0:T(512)S(1)} %add_multiply_fusion, f32[1024]{0:T(1024)S(1)} %bitcast.66, ...), kind=kLoop, calls=%fused_computation.35 | loop fusion | flops 14680064 | bytes 26234880 | tf_op jit(solution)/shard_map/add | solution.py:723
  470.6 12.5 %reduce-scatter.18.cloned.1.call-done = bf16[128,2304]{1,0:T(8,128)(2,1)} async-done(((bf16[512,2304]{1,0:T(8,128)(2,1)}), bf16[128,2304]{1,0:T(8,128)(2,1)}) %reduce-scatter.18.cloned.1.call-update) | async-done | bytes 589840 | tf_op jit(solution)/shard_map/reduce_scatter | solution.py:508
  (276 shorter events, 158.8 us)
Async XLA Ops:
  7.2 231.5 %reduce-scatter.8.cloned.1.call-start = ((), (), s32[]{:S(2)}) async-start(), calls=%async_computation.7 | async-start | bytes 1966080 | tf_op jit(solution)/shard_map/reduce_scatter | solution.py:508
  19.2 88.9 %collective-permute-start.10 = (bf16[1024,2816]{1,0:T(8,128)(2,1)}, bf16[1024,2816]{1,0:T(8,128)(2,1)}, u32[]{:S(2)}, u32[]{:S(2)}) collective-permute-start(bf16[1024,2816]{1,0:T(8,128)(2,1)} %gm_ref.2), channel_id=1, source_target_pairs={{0,2},{2,0},{1,3},{3,1},{4,6},{6,4},{5,7},{7,5},{8,10},{10,8},{9,1... | collective-permute-start | bytes 17301512 | tf_op jit(solution)/shard_map/ppermute | solution.py:552
  19.7 88.4 %collective-permute-start.11 = (bf16[1024,2816]{1,0:T(8,128)(2,1)}, bf16[1024,2816]{1,0:T(8,128)(2,1)}, u32[]{:S(2)}, u32[]{:S(2)}) collective-permute-start(bf16[1024,2816]{1,0:T(8,128)(2,1)} %um_ref.2), channel_id=1, source_target_pairs={{0,2},{2,0},{1,3},{3,1},{4,6},{6,4},{5,7},{7,5},{8,10},{10,8},{9,1... | collective-permute-start | bytes 17301512 | tf_op jit(solution)/shard_map/ppermute | solution.py:552
  19.8 88.3 %collective-permute-start.12 = (bf16[2816,1024]{1,0:T(8,128)(2,1)}, bf16[2816,1024]{1,0:T(8,128)(2,1)}, u32[]{:S(2)}, u32[]{:S(2)}) collective-permute-start(bf16[2816,1024]{1,0:T(8,128)(2,1)} %refs_2_.1), channel_id=1, source_target_pairs={{0,2},{2,0},{1,3},{3,1},{4,6},{6,4},{5,7},{7,5},{8,10},{10,8},{9,1... | collective-permute-start | bytes 17301512 | tf_op jit(solution)/shard_map/ppermute | solution.py:552
  24.1 31.7 %collective-permute-start.6 = (bf16[1024,1024]{1,0:T(8,128)(2,1)}, bf16[1024,1024]{1,0:T(8,128)(2,1)}, u32[]{:S(2)}, u32[]{:S(2)}) collective-permute-start(bf16[1024,1024]{1,0:T(8,128)(2,1)} %refs_2_.2), channel_id=1, source_target_pairs={{0,2},{2,0},{1,3},{3,1},{4,6},{6,4},{5,7},{7,5},{8,10},{10,8},{9,1... | collective-permute-start | bytes 6291464 | tf_op jit(solution)/shard_map/ppermute | solution.py:552
  29.5 33.4 %collective-permute-start.8 = (bf16[512,1024]{1,0:T(8,128)(2,1)S(1)}, bf16[512,1024]{1,0:T(8,128)(2,1)S(1)}, u32[]{:S(2)}, u32[]{:S(2)}) collective-permute-start(bf16[512,1024]{1,0:T(8,128)(2,1)S(1)} %get-tuple-element.118), channel_id=1, source_target_pairs={{0,2},{2,0},{1,3},{3,1},{4,6},{6,4},{5,7},{7,5},{8,10},{10,8},{9,1... | collective-permute-start | bytes 3145736 | tf_op jit(solution)/shard_map/ppermute | solution.py:552
  55.9 27.3 %collective-permute-start.5 = (bf16[512,1024]{1,0:T(8,128)(2,1)}, bf16[512,1024]{1,0:T(8,128)(2,1)}, u32[]{:S(2)}, u32[]{:S(2)}) collective-permute-start(bf16[512,1024]{1,0:T(8,128)(2,1)} %convolution_convert_fusion.1), channel_id=1, source_target_pairs={{0,1},{1,0},{2,3},{3,2},{4,5},{5,4},{6,7},{7,6},{8,9},{9,8},{10,11... | collective-permute-start | bytes 3145736 | tf_op jit(solution)/shard_map/ppermute | solution.py:555
  63.9 40.2 %collective-permute-start.7 = (bf16[512,1024]{1,0:T(8,128)(2,1)}, bf16[512,1024]{1,0:T(8,128)(2,1)}, u32[]{:S(2)}, u32[]{:S(2)}) collective-permute-start(bf16[512,1024]{1,0:T(8,128)(2,1)} %convolution_convert_fusion), channel_id=1, source_target_pairs={{0,1},{1,0},{2,3},{3,2},{4,5},{5,4},{6,7},{7,6},{8,9},{9,8},{10,11... | collective-permute-start | bytes 3145736 | tf_op jit(solution)/shard_map/ppermute | solution.py:555
  83.1 25.0 %collective-permute-start.9 = (bf16[512,1024]{1,0:T(8,128)(2,1)}, bf16[512,1024]{1,0:T(8,128)(2,1)}, u32[]{:S(2)}, u32[]{:S(2)}) collective-permute-start(bf16[512,1024]{1,0:T(8,128)(2,1)} %pad_maximum_fusion.7.other_ref), channel_id=1, source_target_pairs={{0,2},{2,0},{1,3},{3,1},{4,6},{6,4},{5,7},{7,5},{8,10},{10,8},{9,1... | collective-permute-start | bytes 3145736 | tf_op jit(solution)/shard_map/ppermute | solution.py:552
  188.9 104.0 %reduce-scatter.10.cloned.1.call-start = ((), (), s32[]{:S(2)}) async-start(), calls=%async_computation.8 | async-start | bytes 1966080 | tf_op jit(solution)/shard_map/reduce_scatter | solution.py:508
  189.0 64.9 %collective-permute-start.17 = (bf16[512,2816]{1,0:T(8,128)(2,1)}, bf16[512,2816]{1,0:T(8,128)(2,1)}, u32[]{:S(2)}, u32[]{:S(2)}) collective-permute-start(bf16[512,2816]{1,0:T(8,128)(2,1)} %get-tuple-element.144), channel_id=1, source_target_pairs={{0,4},{4,0},{8,12},{12,8},{16,20},{20,16},{24,28},{28,24},{1,5},{5... | collective-permute-start | bytes 8650760 | tf_op jit(solution)/shard_map/ppermute | solution.py:558
  190.9 177.5 %reduce-scatter.12.cloned.1.call-start = ((), (), s32[]{:S(2)}) async-start(), calls=%async_computation.9 | async-start | bytes 3604480 | tf_op jit(solution)/shard_map/reduce_scatter | solution.py:508
  190.9 47.8 %collective-permute-start.16 = (bf16[512,2048]{1,0:T(8,128)(2,1)}, bf16[512,2048]{1,0:T(8,128)(2,1)}, u32[]{:S(2)}, u32[]{:S(2)}) collective-permute-start(bf16[512,2048]{1,0:T(8,128)(2,1)} %input_grad.1), channel_id=1, source_target_pairs={{0,1},{1,0},{2,3},{3,2},{4,5},{5,4},{6,7},{7,6},{8,9},{9,8},{10,11... | collective-permute-start | bytes 6291464 | tf_op jit(solution)/shard_map/ppermute | solution.py:555
  258.9 116.8 %reduce-scatter.14.cloned.1.call-start = ((), (), s32[]{:S(2)}) async-start(), calls=%async_computation.10 | async-start | bytes 1966080 | tf_op jit(solution)/shard_map/reduce_scatter | solution.py:508
  259.0 62.9 %collective-permute-start.20 = (bf16[512,2048]{1,0:T(8,128)(2,1)}, bf16[512,2048]{1,0:T(8,128)(2,1)}, u32[]{:S(2)}, u32[]{:S(2)}) collective-permute-start(bf16[512,2048]{1,0:T(8,128)(2,1)} %blend.3), channel_id=1, source_target_pairs={{0,1},{1,0},{2,3},{3,2},{4,5},{5,4},{6,7},{7,6},{8,9},{9,8},{10,11... | collective-permute-start | bytes 6291464 | tf_op jit(solution)/shard_map/ppermute | solution.py:555
  260.8 35.6 %collective-permute-start.19 = (bf16[512,1536]{1,0:T(8,128)(2,1)}, bf16[512,1536]{1,0:T(8,128)(2,1)}, u32[]{:S(2)}, u32[]{:S(2)}) collective-permute-start(bf16[512,1536]{1,0:T(8,128)(2,1)} %get-tuple-element.157), channel_id=1, source_target_pairs={{0,4},{4,0},{8,12},{12,8},{16,20},{20,16},{24,28},{28,24},{1,5},{5... | collective-permute-start | bytes 4718600 | tf_op jit(solution)/shard_map/ppermute | solution.py:558
  296.4 29.1 %collective-permute-start.21 = (bf16[512,1280]{1,0:T(8,128)(2,1)}, bf16[512,1280]{1,0:T(8,128)(2,1)}, u32[]{:S(2)}, u32[]{:S(2)}) collective-permute-start(bf16[512,1280]{1,0:T(8,128)(2,1)} %get-tuple-element.166), channel_id=1, source_target_pairs={{0,4},{4,0},{8,12},{12,8},{16,20},{20,16},{24,28},{28,24},{1,5},{5... | collective-permute-start | bytes 3932168 | tf_op jit(solution)/shard_map/ppermute | solution.py:558
  321.9 96.3 %reduce-scatter.16.cloned.1.call-start = ((), (), s32[]{:S(2)}) async-start(), calls=%async_computation.11 | async-start | bytes 1638400 | tf_op jit(solution)/shard_map/reduce_scatter | solution.py:508
  338.7 31.1 %collective-permute-start.26 = (bf16[512,1280]{1,0:T(8,128)(2,1)}, bf16[512,1280]{1,0:T(8,128)(2,1)}, u32[]{:S(2)}, u32[]{:S(2)}) collective-permute-start(bf16[512,1280]{1,0:T(8,128)(2,1)} %get-tuple-element.181), channel_id=1, source_target_pairs={{0,4},{4,0},{8,12},{12,8},{16,20},{20,16},{24,28},{28,24},{1,5},{5... | collective-permute-start | bytes 3932168 | tf_op jit(solution)/shard_map/ppermute | solution.py:558
  346.4 113.3 %reduce-scatter.20.cloned.1.call-start = ((), (), s32[]{:S(2)}) async-start(), calls=%async_computation.13 | async-start | bytes 1638400 | tf_op jit(solution)/shard_map/reduce_scatter | solution.py:508
  369.8 54.5 %collective-permute-start.27 = (bf16[512,2304]{1,0:T(8,128)(2,1)}, bf16[512,2304]{1,0:T(8,128)(2,1)}, u32[]{:S(2)}, u32[]{:S(2)}) collective-permute-start(bf16[512,2304]{1,0:T(8,128)(2,1)} %get-tuple-element.190), channel_id=1, source_target_pairs={{0,4},{4,0},{8,12},{12,8},{16,20},{20,16},{24,28},{28,24},{1,5},{5... | collective-permute-start | bytes 7077896 | tf_op jit(solution)/shard_map/ppermute | solution.py:558
  371.4 46.9 %collective-permute-start.25 = (bf16[512,2048]{1,0:T(8,128)(2,1)}, bf16[512,2048]{1,0:T(8,128)(2,1)}, u32[]{:S(2)}, u32[]{:S(2)}) collective-permute-start(bf16[512,2048]{1,0:T(8,128)(2,1)} %blend.5), channel_id=1, source_target_pairs={{0,1},{1,0},{2,3},{3,2},{4,5},{5,4},{6,7},{7,6},{8,9},{9,8},{10,11... | collective-permute-start | bytes 6291464 | tf_op jit(solution)/shard_map/ppermute | solution.py:555
  375.2 107.9 %reduce-scatter.18.cloned.1.call-start = ((), (), s32[]{:S(2)}) async-start(), calls=%async_computation.12 | async-start | bytes 2949120 | tf_op jit(solution)/shard_map/reduce_scatter | solution.py:508
  375.3 80.9 %collective-permute-start.34 = (bf16[128,1536]{1,0:T(8,128)(2,1)}, bf16[128,1536]{1,0:T(8,128)(2,1)}, u32[]{:S(2)}, u32[]{:S(2)}) collective-permute-start(bf16[128,1536]{1,0:T(8,128)(2,1)} %reduce-scatter.8.cloned.1.call-done), channel_id=1, source_target_pairs={{0,4},{4,0},{8,12},{12,8},{16,20},{20,16},{24,28},{28,24},{1,5},{5... | collective-permute-start | bytes 1179656 | tf_op jit(solution)/shard_map/ppermute | solution.py:558
  (69 other events, 356.9 us)
Sparse Core Ops, SparseCore 0:
  189.1 36.7 reduce-scatter.7
  228.2 34.2 reduce-scatter.9
  264.8 55.1 reduce-scatter.11
  322.1 35.1 reduce-scatter.13
  360.0 30.1 reduce-scatter.15
  393.0 29.9 reduce-scatter.19
  434.1 48.9 reduce-scatter.17
